TPU v7x, 32 devices: a whole 2x2x4 slice. The times are simulated.
32 devices in a mesh: fsdp: 16 (over z, y, core), ctx: 2 (over x).
Axes of the slice: x: 2, y: 2, z: 4, core: 2. Of those that a mesh axis runs over, the one named last changes fastest.
Arguments:
- activations: bfloat16 [4096, 1280], P('fsdp', 'ctx'), may hold values from -500 to 500
- norm_gain: float32 [4096], P('fsdp'), may hold values from 0.25 to 1.75
- w_in: bfloat16 [3, 4096, 4096], P(None, 'fsdp'), may hold values from -0.09375 to 0.09375
- w_short: float32 [3, 4096, 3], P(None, 'fsdp'), may hold values from -3.5 to 3.5
- long_filter: bfloat16 [4096, 1280], P('fsdp'), may hold values from -1.1 to 1.1
- skip_gain: float32 [4096], P('fsdp'), may hold values from -4 to 4
- w_out: bfloat16 [4096, 4096], P('fsdp'), may hold values from -0.09375 to 0.09375
Outputs:
- mixer_out: bfloat16 [4096, 1280], P('fsdp', 'ctx')
All inputs are finite; a program needn't handle non-finite values.
Results may differ from a plain program's by a relative error of at most 0.035.
Values may be sent and summed in bfloat16 or wider, within the bound.
No kernel may reach another device: no remote copies, remote signals or barrier semaphores. Data moves between devices by JAX's collectives and lax.ppermute only.
A program may use at most 64 MiB of HBM per device.

v0:
```python
import math

import jax
import jax.numpy as jnp
from jax import lax
from jax.sharding import PartitionSpec as P

epsilon = 1e-05
highest_precision = lax.Precision.HIGHEST


def shifted(block, axis, distance):
    devices = range(lax.axis_size(axis))
    route = [(i - distance, i) for i in devices if i - distance in devices]
    return lax.ppermute(block, axis, route)


def dft_tables(block_len):
    size = 2 * block_len
    sample = jnp.arange(size, dtype=jnp.int32)
    turns = sample[:, None] * sample[None, :] % size
    angle = turns.astype(jnp.float32) * (2.0 * math.pi / size)
    forward_pass = jnp.concatenate([jnp.cos(angle), -jnp.sin(angle)], axis=1)
    places = block_len + jnp.arange(block_len, dtype=jnp.int32)
    back_turns = sample[:, None] * places[None, :] % size
    back_angle = back_turns.astype(jnp.float32) * (2.0 * math.pi / size)
    inverse = jnp.concatenate([jnp.cos(back_angle), -jnp.sin(back_angle)], axis=0) / size
    return (forward_pass, inverse)


def complex_product(left, right):
    half = left.shape[-1] // 2
    left_re = left[..., :half]
    left_im = left[..., half:]
    right_re = right[..., :half]
    right_im = right[..., half:]
    return jnp.concatenate(
        [left_re * right_re - left_im * right_im, left_re * right_im + left_im * right_re], axis=-1
    )


def add_portion(running, portion, anchor, padded_spec, forward_pass, first_block, block_len):
    channels = portion.shape[0]
    count = portion.shape[1] // block_len
    local_blocks = running.shape[1]
    block_list = portion.astype(jnp.float32).reshape(channels, count, block_len)
    block_list = jnp.concatenate([block_list, jnp.zeros(block_list.shape, jnp.float32)], axis=2)
    filter_spectra = jnp.einsum(
        "grs,si->gri", block_list, forward_pass, precision=highest_precision
    )
    anchor_block = anchor // block_len

    def one_block(index, current):
        source = anchor_block + index
        spectrum = lax.dynamic_index_in_dim(filter_spectra, index, 1, keepdims=False)

        def apply_block(inner):
            start = local_blocks + first_block - source
            chosen = lax.dynamic_slice_in_dim(padded_spec, start, local_blocks, 1)
            return inner + complex_product(chosen, spectrum[:, None, :])

        def keep_block(inner):
            return inner

        return lax.cond(source < first_block + local_blocks, apply_block, keep_block, current)

    return lax.fori_loop(0, count, one_block, running)


def shards(activations, norm_gain, w_in, w_short, long_filter, skip_gain, w_out):
    channels = activations.shape[0]
    tok_rows = activations.shape[1]
    gathered, gains = (
        lax.all_gather(activations, "fsdp", axis=0, tiled=True),
        lax.all_gather(norm_gain.astype(jnp.bfloat16), "fsdp", axis=0, tiled=True).astype(
            norm_gain.dtype
        ),
    )
    factor = lax.rsqrt(jnp.mean(jnp.square(gathered.astype(jnp.float32)), axis=0) + epsilon)
    normed = (gathered.astype(jnp.float32) * factor[None, :] * gains[:, None]).astype(jnp.bfloat16)
    projected = jnp.einsum("sci,it->sct", w_in, normed, preferred_element_type=jnp.float32)
    projected = projected.astype(jnp.bfloat16)
    taps = w_short.shape[2]
    earlier = shifted(projected[:, :, tok_rows - (taps - 1) :], "ctx", 1)
    padded = jnp.concatenate([earlier, projected], axis=2).astype(jnp.float32)
    smoothed = jnp.zeros((3, channels, tok_rows), jnp.float32)
    for tap_index in range(taps):
        begin = taps - 1 - tap_index
        smoothed = (
            smoothed + w_short[:, :, tap_index][:, :, None] * padded[:, :, begin : begin + tok_rows]
        )
    query = smoothed[0]
    gated = (smoothed[1] * smoothed[2]).astype(jnp.bfloat16)
    block_len = 128
    local_blocks = tok_rows // block_len
    total_len = long_filter.shape[1]
    total_blocks = total_len // block_len
    forward_pass, inverse = dft_tables(block_len)
    edge = jnp.zeros((channels, block_len), jnp.float32)
    filter_wide = jnp.concatenate([edge, long_filter.astype(jnp.float32), edge], axis=1)
    filter_rows = filter_wide.reshape(channels, total_blocks + 2, block_len)
    segments = jnp.concatenate(
        [filter_rows[:, :total_blocks], filter_rows[:, 1 : total_blocks + 1]], axis=2
    )
    filter_spec = jnp.einsum("ckn,nf->ckf", segments, forward_pass, precision=highest_precision)
    padded_spec = jnp.concatenate(
        [jnp.zeros((channels, local_blocks, filter_spec.shape[2]), jnp.float32), filter_spec],
        axis=1,
    )
    my_index = lax.axis_index("ctx")
    first_token = my_index * tok_rows
    first_block = my_index * local_blocks
    empty = jnp.zeros((channels, local_blocks, 4 * block_len), jnp.float32)
    cycle_size = lax.axis_size("ctx")
    running = add_portion(
        empty, gated, first_token, padded_spec, forward_pass, first_block, block_len
    )

    def turn(turn_index, carried):
        current, moving = carried
        moving = shifted(moving, "ctx", 1)
        source = (my_index - turn_index + cycle_size) % cycle_size
        current = add_portion(
            current, moving, source * tok_rows, padded_spec, forward_pass, first_block, block_len
        )
        return (current, moving)

    accumulated, moved = lax.fori_loop(1, cycle_size, turn, (running, gated))
    filtered = jnp.einsum("caf,fi->cai", accumulated, inverse, precision=highest_precision).reshape(
        channels, tok_rows
    )
    mixed = (query * (filtered + skip_gain[:, None] * gated.astype(jnp.float32))).astype(
        jnp.bfloat16
    )
    result = jnp.dot(
        w_out, lax.all_gather(mixed, "fsdp", axis=0, tiled=True), preferred_element_type=jnp.float32
    )
    return result.astype(jnp.bfloat16)


def solution(mesh):
    placed = (
        P("fsdp", "ctx"),
        P("fsdp"),
        P(None, "fsdp", None),
        P(None, "fsdp", None),
        P("fsdp", None),
        P("fsdp"),
        P("fsdp", None),
    )
    return jax.shard_map(
        shards, mesh=mesh, in_specs=placed, out_specs=P("fsdp", "ctx"), check_vma=False
    )
```

profile of v0, /device:TPU:0, one launch (start us, length us, event | category | flops | bytes accessed | tf_op | source)
XLA Modules:
  0.0 284.2 jit_solution(9009154656110349167)
XLA Ops:
  8.0 23.1 %all-gather = bf16[16,1,256]{2,1,0:T(2,128)(2,1)S(1)} all-gather(bf16[1,1,256]{2,1,0:T(2,128)(2,1)S(1)} %reshape.38), channel_id=1, replica_groups=mesh['fsdp'=16,'ctx'=2] {'fsdp'}, dimensions={0}, use_global_device_ids=true | all-gather | bytes 8704 | tf_op jit(solution)/shard_map/all_gather | solution.py:75
  34.1 2.8 copy.36
  40.8 7.8 %fusion.8 = f32[256,10,512]{2,0,1:T(8,128)} fusion(f32[256,10,128]{2,0,1:T(8,128)} %copy.37, f32[256,10,128]{2,0,1:T(8,128)} %copy.36, f32[256,256]{1,0:T(8,128)S(1)} %get-tuple-element.546, f32[256,256]{1,0:T(8,128)S(1)} %get-tuple-element.547), kind=kOutput, calls=%fused_computation.19 | convolution fusion | flops 4027318272 | bytes 8388608 | tf_op jit(solution)/shard_map/ckn,nf->ckf/dot_general | solution.py:105
  48.6 19.8 %all-gather.4.cloned.1.call-done = bf16[4096,640]{1,0:T(8,128)(2,1)} async-done(((bf16[256,640]{1,0:T(8,128)(2,1)}), bf16[4096,640]{1,0:T(8,128)(2,1)}) %all-gather.4.cloned.1.call-update) | async-done | bytes 5242896 | tf_op jit(solution)/shard_map/all_gather | solution.py:74
  68.4 3.7 %fusion = f32[640]{0:T(1024)S(1)} fusion(bf16[4096,640]{1,0:T(8,128)(2,1)} %all-gather.4.cloned.1.call-done), kind=kLoop, calls=%fused_computation.12 | loop fusion | flops 7863680 | bytes 5245440 | tf_op jit(solution)/shard_map/reduce_sum | solution.py:79
  72.4 7.9 %fusion.19 = bf16[3,256,640]{1,2,0:T(8,128)(2,1)S(1)} fusion(bf16[3,256,4096]{2,1,0:T(8,128)(2,1)} %param.17, bf16[4096,640]{1,0:T(8,128)(2,1)S(1)} %copy-done.3, f32[4096]{0:T(1024)S(1)} %bitcast.57, f32[640]{0:T(1024)S(1)} %add_rsqrt_fusion), kind=kOutput, calls=%fused_computation.32 | convolution fusion | flops 4037509120 | bytes 12536320 | tf_op jit(solution)/shard_map/sci,it->sct/dot_general | solution.py:81
  81.3 3.5 %collective-permute-start = (bf16[3,256,2]{1,2,0:T(2,128)(2,1)S(1)}, bf16[3,256,2]{1,2,0:T(2,128)(2,1)S(1)}, u32[]{:S(2)}, u32[]{:S(2)}) collective-permute-start(bf16[3,256,2]{1,2,0:T(2,128)(2,1)S(1)} %slice.88), channel_id=1, source_target_pairs={{0,1},{2,3},{4,5},{6,7},{8,9},{10,11},{12,13},{14,15},{16,17},{18,... | collective-permute-start | bytes 9224 | tf_op jit(solution)/shard_map/ppermute | solution.py:15
  84.9 5.7 %copy.38 = f32[256,10,512]{2,1,0:T(8,128)S(1)} copy(f32[256,10,512]{2,0,1:T(8,128)} %fusion.8) | data formatting | bytes 10485760
  90.6 4.9 %concatenate.43.clone = f32[256,15,512]{2,1,0:T(8,128)} pad(f32[256,10,512]{2,1,0:T(8,128)S(1)} %copy.38, f32[]{:T(128)} %constant.170.clone.1), padding=0_0x5_0x0_0 | pad | bytes 13107204 | tf_op jit(solution)/shard_map/concatenate | solution.py:106
  98.4 2.0 collective-permute-start.1
  100.7 2.7 fusion.28
  103.4 2.5 broadcast.43
  105.9 51.9 %while.43 = (s32[]{:T(128)}, f32[256,5,512]{2,1,0:T(8,128)}, s32[]{:T(128)}, s32[]{:T(128)}, s32[]{:T(128)}, /*index=5*/f32[256,15,512]{2,1,0:T(8,128)}, f32[256,5,512]{2,0,1:T(8,128)}, s32[]{:T(128)}) while((s32[]{:T(128)}, f32[256,5,512]{2,1,0:T(8,128)}, s32[]{:T(128)}, s32[]{:T(128)}, s32[]{:T(128)}, /*index=5*/f32[256,15,512]{2,1,0:T(8,128)}, ...), condition=%wide.region_4.5_spmd, body=%wide.region_1.4_spmd.sunk | while | flops 3276814 | bytes 14680351 | solution.py:67
  105.9 10.4 %conditional.4 = (f32[256,5,512]{2,1,0:T(8,128)}) conditional(s32[]{:T(128)} %convert_element_type.149, f32[256,5,512]{2,1,0:T(8,128)} %get-tuple-element.643, (s32[]{:T(128)}, s32[]{:T(128)}, f32[256,15,512]{2,1,0:T(8,128)}, s32[]{:T(128)}, f32[256,5,512]{2,0,1:T(8,128)}, /*index=5*/f32[256,5,512]{2,1,0:T(8,128)}) %tuple.113), branch_computations={%region_2.2_spmd, %region_3.3_spmd} | conditional | flops 3276809 | bytes 14680192 | solution.py:65
  107.0 4.3 %multiply_subtract_fusion = (f32[256,5,256]{2,1,0:T(8,128)S(1)}, f32[256,5,256]{2,1,0:T(8,128)S(1)}) fusion(f32[256,15,512]{2,1,0:T(8,128)} %get-tuple-element.428, s32[]{:T(128)S(6)} %select_n.55, s32[]{:T(128)S(6)} %add.215, f32[256,256]{1,0:T(8,128)S(1)} %get-tuple-element.532, f32[256,256]{1,0:T(8,128)S(1)} %get-tuple-element.531), kind=kLoop, calls=%fused_computation.2 | loop fusion | flops 1966080 | bytes 5767176 | tf_op jit(solution)/shard_map/while/body/eval_jaxpr/cond/branch_1_fun/sub | solution.py:38
  111.3 5.0 %maximum_add_fusion = f32[256,5,512]{2,1,0:T(8,128)} fusion(f32[256,5,512]{2,1,0:T(8,128)} %get-tuple-element.427, f32[256,5,256]{2,1,0:T(8,128)S(1)} %get-tuple-element.530, f32[256,5,256]{2,1,0:T(8,128)S(1)} %get-tuple-element.529), kind=kLoop, calls=%fused_computation | loop fusion | flops 1310720 | bytes 7864320 | tf_op jit(solution)/shard_map/while/body/eval_jaxpr/cond/branch_1_fun/add | solution.py:60
  116.3 10.4 %conditional.4 = (f32[256,5,512]{2,1,0:T(8,128)}) conditional(s32[]{:T(128)} %convert_element_type.149, f32[256,5,512]{2,1,0:T(8,128)} %get-tuple-element.643, (s32[]{:T(128)}, s32[]{:T(128)}, f32[256,15,512]{2,1,0:T(8,128)}, s32[]{:T(128)}, f32[256,5,512]{2,0,1:T(8,128)}, /*index=5*/f32[256,5,512]{2,1,0:T(8,128)}) %tuple.113), branch_computations={%region_2.2_spmd, %region_3.3_spmd} | conditional | flops 3276809 | bytes 14680192 | solution.py:65
  117.4 4.3 %multiply_subtract_fusion = (f32[256,5,256]{2,1,0:T(8,128)S(1)}, f32[256,5,256]{2,1,0:T(8,128)S(1)}) fusion(f32[256,15,512]{2,1,0:T(8,128)} %get-tuple-element.428, s32[]{:T(128)S(6)} %select_n.55, s32[]{:T(128)S(6)} %add.215, f32[256,256]{1,0:T(8,128)S(1)} %get-tuple-element.532, f32[256,256]{1,0:T(8,128)S(1)} %get-tuple-element.531), kind=kLoop, calls=%fused_computation.2 | loop fusion | flops 1966080 | bytes 5767176 | tf_op jit(solution)/shard_map/while/body/eval_jaxpr/cond/branch_1_fun/sub | solution.py:38
  121.7 5.0 %maximum_add_fusion = f32[256,5,512]{2,1,0:T(8,128)} fusion(f32[256,5,512]{2,1,0:T(8,128)} %get-tuple-element.427, f32[256,5,256]{2,1,0:T(8,128)S(1)} %get-tuple-element.530, f32[256,5,256]{2,1,0:T(8,128)S(1)} %get-tuple-element.529), kind=kLoop, calls=%fused_computation | loop fusion | flops 1310720 | bytes 7864320 | tf_op jit(solution)/shard_map/while/body/eval_jaxpr/cond/branch_1_fun/add | solution.py:60
  126.7 10.4 %conditional.4 = (f32[256,5,512]{2,1,0:T(8,128)}) conditional(s32[]{:T(128)} %convert_element_type.149, f32[256,5,512]{2,1,0:T(8,128)} %get-tuple-element.643, (s32[]{:T(128)}, s32[]{:T(128)}, f32[256,15,512]{2,1,0:T(8,128)}, s32[]{:T(128)}, f32[256,5,512]{2,0,1:T(8,128)}, /*index=5*/f32[256,5,512]{2,1,0:T(8,128)}) %tuple.113), branch_computations={%region_2.2_spmd, %region_3.3_spmd} | conditional | flops 3276809 | bytes 14680192 | solution.py:65
  127.8 4.3 %multiply_subtract_fusion = (f32[256,5,256]{2,1,0:T(8,128)S(1)}, f32[256,5,256]{2,1,0:T(8,128)S(1)}) fusion(f32[256,15,512]{2,1,0:T(8,128)} %get-tuple-element.428, s32[]{:T(128)S(6)} %select_n.55, s32[]{:T(128)S(6)} %add.215, f32[256,256]{1,0:T(8,128)S(1)} %get-tuple-element.532, f32[256,256]{1,0:T(8,128)S(1)} %get-tuple-element.531), kind=kLoop, calls=%fused_computation.2 | loop fusion | flops 1966080 | bytes 5767176 | tf_op jit(solution)/shard_map/while/body/eval_jaxpr/cond/branch_1_fun/sub | solution.py:38
  132.1 5.0 %maximum_add_fusion = f32[256,5,512]{2,1,0:T(8,128)} fusion(f32[256,5,512]{2,1,0:T(8,128)} %get-tuple-element.427, f32[256,5,256]{2,1,0:T(8,128)S(1)} %get-tuple-element.530, f32[256,5,256]{2,1,0:T(8,128)S(1)} %get-tuple-element.529), kind=kLoop, calls=%fused_computation | loop fusion | flops 1310720 | bytes 7864320 | tf_op jit(solution)/shard_map/while/body/eval_jaxpr/cond/branch_1_fun/add | solution.py:60
  137.0 10.4 %conditional.4 = (f32[256,5,512]{2,1,0:T(8,128)}) conditional(s32[]{:T(128)} %convert_element_type.149, f32[256,5,512]{2,1,0:T(8,128)} %get-tuple-element.643, (s32[]{:T(128)}, s32[]{:T(128)}, f32[256,15,512]{2,1,0:T(8,128)}, s32[]{:T(128)}, f32[256,5,512]{2,0,1:T(8,128)}, /*index=5*/f32[256,5,512]{2,1,0:T(8,128)}) %tuple.113), branch_computations={%region_2.2_spmd, %region_3.3_spmd} | conditional | flops 3276809 | bytes 14680192 | solution.py:65
  138.1 4.3 %multiply_subtract_fusion = (f32[256,5,256]{2,1,0:T(8,128)S(1)}, f32[256,5,256]{2,1,0:T(8,128)S(1)}) fusion(f32[256,15,512]{2,1,0:T(8,128)} %get-tuple-element.428, s32[]{:T(128)S(6)} %select_n.55, s32[]{:T(128)S(6)} %add.215, f32[256,256]{1,0:T(8,128)S(1)} %get-tuple-element.532, f32[256,256]{1,0:T(8,128)S(1)} %get-tuple-element.531), kind=kLoop, calls=%fused_computation.2 | loop fusion | flops 1966080 | bytes 5767176 | tf_op jit(solution)/shard_map/while/body/eval_jaxpr/cond/branch_1_fun/sub | solution.py:38
  142.5 5.0 %maximum_add_fusion = f32[256,5,512]{2,1,0:T(8,128)} fusion(f32[256,5,512]{2,1,0:T(8,128)} %get-tuple-element.427, f32[256,5,256]{2,1,0:T(8,128)S(1)} %get-tuple-element.530, f32[256,5,256]{2,1,0:T(8,128)S(1)} %get-tuple-element.529), kind=kLoop, calls=%fused_computation | loop fusion | flops 1310720 | bytes 7864320 | tf_op jit(solution)/shard_map/while/body/eval_jaxpr/cond/branch_1_fun/add | solution.py:60
  147.4 10.4 %conditional.4 = (f32[256,5,512]{2,1,0:T(8,128)}) conditional(s32[]{:T(128)} %convert_element_type.149, f32[256,5,512]{2,1,0:T(8,128)} %get-tuple-element.643, (s32[]{:T(128)}, s32[]{:T(128)}, f32[256,15,512]{2,1,0:T(8,128)}, s32[]{:T(128)}, f32[256,5,512]{2,0,1:T(8,128)}, /*index=5*/f32[256,5,512]{2,1,0:T(8,128)}) %tuple.113), branch_computations={%region_2.2_spmd, %region_3.3_spmd} | conditional | flops 3276809 | bytes 14680192 | solution.py:65
  148.5 4.3 %multiply_subtract_fusion = (f32[256,5,256]{2,1,0:T(8,128)S(1)}, f32[256,5,256]{2,1,0:T(8,128)S(1)}) fusion(f32[256,15,512]{2,1,0:T(8,128)} %get-tuple-element.428, s32[]{:T(128)S(6)} %select_n.55, s32[]{:T(128)S(6)} %add.215, f32[256,256]{1,0:T(8,128)S(1)} %get-tuple-element.532, f32[256,256]{1,0:T(8,128)S(1)} %get-tuple-element.531), kind=kLoop, calls=%fused_computation.2 | loop fusion | flops 1966080 | bytes 5767176 | tf_op jit(solution)/shard_map/while/body/eval_jaxpr/cond/branch_1_fun/sub | solution.py:38
  152.8 5.0 %maximum_add_fusion = f32[256,5,512]{2,1,0:T(8,128)} fusion(f32[256,5,512]{2,1,0:T(8,128)} %get-tuple-element.427, f32[256,5,256]{2,1,0:T(8,128)S(1)} %get-tuple-element.530, f32[256,5,256]{2,1,0:T(8,128)S(1)} %get-tuple-element.529), kind=kLoop, calls=%fused_computation | loop fusion | flops 1310720 | bytes 7864320 | tf_op jit(solution)/shard_map/while/body/eval_jaxpr/cond/branch_1_fun/add | solution.py:60
  159.0 2.7 fusion.26
  162.7 6.3 %fusion.12 = f32[256,5,128]{0,2,1:T(8,128)S(1)} fusion(f32[256,5,512]{2,1,0:T(8,128)} %get-tuple-element.458, f32[256,128]{0,1:T(8,128)S(1)} %copy-done.6, f32[256,128]{0,1:T(8,128)S(1)} %copy-done.5), kind=kOutput, calls=%fused_computation.23 | convolution fusion | flops 1006764032 | bytes 3538944 | tf_op jit(solution)/shard_map/caf,fi->cai/dot_general | solution.py:129
  169.9 102.6 %all-gather.6.cloned.1.call-done = bf16[4096,640]{0,1:T(8,128)(2,1)} async-done(((bf16[256,640]{0,1:T(8,128)(2,1)}), bf16[4096,640]{0,1:T(8,128)(2,1)}) %all-gather.6.cloned.1.call-update) | async-done | bytes 5242896 | tf_op jit(solution)/shard_map/all_gather | solution.py:136
  272.5 4.0 %fusion.22 = bf16[256,640]{0,1:T(8,128)(2,1)S(1)} fusion(bf16[4096,640]{0,1:T(8,128)(2,1)} %all-gather.6.cloned.1.call-done, bf16[256,4096]{1,0:T(8,128)(2,1)S(1)} %copy-done), kind=kOutput, calls=%fused_computation.34 | convolution fusion | flops 1342341120 | bytes 7667712 | tf_op jit(solution)/shard_map/dot_general | solution.py:135
  (60 shorter events, 21.9 us)
Async XLA Ops:
  6.5 265.9 %copy-start = (bf16[256,4096]{1,0:T(8,128)(2,1)S(1)}, bf16[256,4096]{1,0:T(8,128)(2,1)}, u32[]{:S(2)}) copy-start(bf16[256,4096]{1,0:T(8,128)(2,1)} %param.21) | copy-start | bytes 6291460
  6.5 61.9 %all-gather.4.cloned.1.call-start = ((), (), s32[]{:S(2)}) async-start(), calls=%async_computation | async-start | bytes 5570560 | tf_op jit(solution)/shard_map/all_gather | solution.py:74
  7.3 265.2 %all-gather.6.cloned.1.call-start = ((), (), s32[]{:S(2)}) async-start(), calls=%async_computation.1 | async-start | bytes 5570560 | tf_op jit(solution)/shard_map/all_gather | solution.py:136
  36.8 2.6 copy-start.7
  68.4 4.0 %copy-start.3 = (bf16[4096,640]{1,0:T(8,128)(2,1)S(1)}, bf16[4096,640]{1,0:T(8,128)(2,1)}, u32[]{:S(2)}) copy-start(bf16[4096,640]{1,0:T(8,128)(2,1)} %all-gather.4.cloned.1.call-done) | copy-start | bytes 15728644
  80.4 1.0 copy-start.4
  81.3 14.2 %collective-permute-start = (bf16[3,256,2]{1,2,0:T(2,128)(2,1)S(1)}, bf16[3,256,2]{1,2,0:T(2,128)(2,1)S(1)}, u32[]{:S(2)}, u32[]{:S(2)}) collective-permute-start(bf16[3,256,2]{1,2,0:T(2,128)(2,1)S(1)} %slice.88), channel_id=1, source_target_pairs={{0,1},{2,3},{4,5},{6,7},{8,9},{10,11},{12,13},{14,15},{16,17},{18,... | collective-permute-start | bytes 9224 | tf_op jit(solution)/shard_map/ppermute | solution.py:15
  97.5 2.9 %copy-start.1 = (f32[3,256,640]{1,2,0:T(8,128)}, f32[3,256,640]{1,2,0:T(8,128)S(1)}, u32[]{:S(2)}) copy-start(f32[3,256,640]{1,2,0:T(8,128)S(1)} %fusion.14) | copy-start | bytes 5898244
  98.4 59.4 %collective-permute-start.1 = (bf16[256,640]{0,1:T(8,128)(2,1)}, bf16[256,640]{0,1:T(8,128)(2,1)}, u32[]{:S(2)}, u32[]{:S(2)}) collective-permute-start(bf16[256,640]{0,1:T(8,128)(2,1)} %fusion.61), channel_id=1, source_target_pairs={{0,1},{2,3},{4,5},{6,7},{8,9},{10,11},{12,13},{14,15},{16,17},{18,... | collective-permute-start | bytes 983048 | tf_op jit(solution)/shard_map/while/body/eval_jaxpr/ppermute | solution.py:15
  161.7 0.9 copy-start.5
  161.7 1.0 copy-start.6
  161.8 7.2 %copy-start.2 = (f32[3,256,640]{1,2,0:T(8,128)S(1)}, f32[3,256,640]{1,2,0:T(8,128)}, u32[]{:S(2)}) copy-start(f32[3,256,640]{1,2,0:T(8,128)} %copy-done.1) | copy-start | bytes 5898244
  161.8 7.2 %copy-start.8 = (f32[256]{0:T(256)S(1)}, f32[256]{0:T(256)}, u32[]{:S(2)}) copy-start(f32[256]{0:T(256)} %param.20) | copy-start | bytes 3076
Sparse Core Ops, SparseCore 0:
  9.6 58.7 all-gather.3
  170.0 102.4 all-gather.5
where the time goes:
time: 285 us; the launch traced here: 284 us
  waiting for transfers between devices  123 us (43%)
  other arithmetic  57.3 us (20%)
  matrix products  31.5 us (11%)
  local copies, waits for them, and re-layouts  29.9 us (10%)
  blocking collectives  23.1 us (8%)
  between operations  13.6 us (5%)
  starting transfers between devices  5.59 us (2%)
    all_gather x1, waiting for transfers between devices, shards(): lax.all_gather(mixed, 'fsdp', axis=0, tiled=True)  103 us
    add x5, other arithmetic, apply_block(): return inner + complex_product(chosen, spectrum[:, None, :])  24.8 us
    all_gather x1, blocking collectives, shards(): lax.all_gather(norm_gain.astype(jnp.bfloat16), 'fsdp', axis=0, tiled=True)  23.1 us
    sub x5, other arithmetic, complex_product(): left_re * right_re - left_im * right_im  21.7 us
    all_gather x1, waiting for transfers between devices, shards(): lax.all_gather(activations, 'fsdp', axis=0, tiled=True)  19.8 us
    unnamed x25, local copies, waits for them, and re-layouts  13.5 us
    dot_general x1, matrix products, shards(): jnp.einsum('sci,it->sct', w_in, normed, preferred_element_type=jnp.float32)  7.9 us
    dot_general x1, matrix products, shards(): jnp.einsum('ckn,nf->ckf', segments, forward_pass, precision=highest_preci...  7.83 us
  transfers between devices with their start and end apart: 4, of which 2 were waited for; matrix products, arithmetic and copies ran while one was open for 30% of the time, Pallas kernels for 0%

commit v1 on v0

v1 whole, which is shorter than its diff:
```python
import math

import jax
import jax.numpy as jnp
import numpy as np
from jax import lax
from jax.experimental import pallas as pl
from jax.experimental.pallas import tpu as pltpu
from jax.sharding import PartitionSpec as P

epsilon = 1e-05
block_len = 128
side_rows = 8
bf16 = jnp.bfloat16
f32 = jnp.float32


def split_table(table):
    high = table.astype(bf16)
    low = (table - high.astype(np.float64)).astype(bf16)
    return np.stack([high, low])


def dft_tables():
    size = 2 * block_len
    freq = np.arange(block_len) + 0.5
    angle = 2.0 * math.pi / size * np.arange(size)[:, None] * freq[None, :]
    forward = np.concatenate([np.cos(angle), -np.sin(angle)], axis=1)
    back = angle[block_len:].T
    inverse = np.concatenate([np.cos(back), -np.sin(back)], axis=0) * (2.0 / size)
    return split_table(forward), split_table(inverse)


def whole(shape):
    return pl.BlockSpec(shape, lambda *_: (0,) * len(shape))


def dot(left, right):
    return jnp.dot(left, right, preferred_element_type=f32)


def prepare_kernel(x_ref, gain_ref, first_ref, second_ref):
    rows = x_ref.shape[0]
    half = rows // 2
    wide = x_ref[...].astype(f32)
    gain = jnp.broadcast_to(gain_ref[...], (8, rows)).T[:, :1]
    scaled = (wide * gain).astype(bf16)
    squares = jnp.sum(wide * wide, axis=0, keepdims=True)
    high = squares.astype(bf16)
    low = (squares - high.astype(f32)).astype(bf16)
    first_ref[:half] = scaled[:half]
    row = lax.broadcasted_iota(jnp.int32, (side_rows, wide.shape[1]), 0)
    side = jnp.where(row == 0, high.astype(f32), jnp.where(row == 1, low.astype(f32), 0.0))
    first_ref[half:] = side.astype(bf16)
    second_ref[...] = scaled[half:]


def prepare(x, gain):
    rows, tokens = x.shape
    half = rows // 2
    return pl.pallas_call(
        prepare_kernel,
        out_shape=(
            jax.ShapeDtypeStruct((half + side_rows, tokens), bf16),
            jax.ShapeDtypeStruct((half, tokens), bf16),
        ),
        name="prepare",
    )(x, gain.reshape(1, rows))


def ring_places(count):
    evens = list(range(0, count, 2))
    odds = list(range(1, count, 2))
    return evens + odds[::-1]


def ring_maps():
    chips = lax.axis_size("fsdp") // 2
    order = ring_places(chips)
    ahead = [
        (order[i] * 2 + core, order[(i + 1) % chips] * 2 + core)
        for i in range(chips)
        for core in range(2)
    ]
    behind = [(b, a) for a, b in ahead]
    return ahead, behind, [(i, i ^ 1) for i in range(2 * chips)]


def ring_ids():
    chips = lax.axis_size("fsdp") // 2
    me = lax.axis_index("fsdp")
    chip, core = me // 2, me % 2
    place = jnp.where(chip % 2 == 0, chip // 2, chips - 1 - chip // 2)
    others = (place - jnp.arange(chips, dtype=jnp.int32) + chips) % chips
    ids = jnp.where(others < (chips + 1) // 2, 2 * others, 2 * (chips - 1 - others) + 1)
    return jnp.concatenate([ids, core[None]]).astype(jnp.int32)


def ring_steps(first, second):
    chips = lax.axis_size("fsdp") // 2
    ahead, behind, _ = ring_maps()
    fa, fb, ba, bb = first, second, first, second
    for step in range(1, chips // 2 + 1):
        fa = lax.ppermute(fa, "fsdp", ahead)
        bb = lax.ppermute(bb, "fsdp", behind)
        if step < chips // 2:
            fb = lax.ppermute(fb, "fsdp", ahead)
            ba = lax.ppermute(ba, "fsdp", behind)
            yield [(step, fa, fb), (chips - step, ba, bb)]
        else:
            yield [(step, fa, bb)]


def other_core(block):
    return lax.ppermute(block, "fsdp", ring_maps()[2])


def product_kernel(slots, parts, rows, first_group, side, finish, extra, *refs):
    ids_ref, refs = refs[0], list(refs[1:])
    mine = refs[: 2 * len(slots)]
    theirs = refs[2 * len(slots) : 4 * len(slots)]
    refs = refs[4 * len(slots) :]
    weights, refs = refs[: len(slots)], refs[len(slots) :]
    total = None
    side_in = None
    if not first_group:
        total, refs = refs[0], refs[1:]
        if side:
            side_in, refs = refs[0], refs[1:]
    extras, refs = refs[:extra], refs[extra:]
    *outs, gathered = refs if not (side and finish) else refs[:-1]
    if side and finish:
        outs, gathered, side_total = refs[:-2], refs[-2], refs[-1]
    half = rows // 2
    step = pl.program_id(0)

    @pl.when(step == 0)
    def _():
        core = ids_ref[ids_ref.shape[0] - 1]
        side_sum = None if side_in is None else side_in[...]
        for k in range(len(slots)):
            base = 2 * k * rows
            own = pl.multiple_of(base + core * rows, half)
            other = pl.multiple_of(base + (1 - core) * rows, half)
            for start, pair in ((own, mine[2 * k : 2 * k + 2]), (other, theirs[2 * k : 2 * k + 2])):
                gathered[pl.ds(start, half)] = pair[0][:half]
                gathered[pl.ds(pl.multiple_of(start + half, half), half)] = pair[1][...]
                if side:
                    more = pair[0][half:].astype(f32)
                    side_sum = more if side_sum is None else side_sum + more
        if side:
            if finish:
                side_total[...] = side_sum
            else:
                outs[1][...] = side_sum

    product = None if first_group else total[0]
    for k in range(len(slots)):
        term = dot(weights[k][0], gathered[2 * k * rows : 2 * (k + 1) * rows])
        product = term if product is None else product + term
    if finish:
        finish(step, product, side_total if side else None, extras, outs)
    else:
        outs[0][0] = product


def products(ids, slots, mine, theirs, weight, running, side, finish=None, extras=(), name="sum"):
    streams, out_rows, features = weight.shape
    rows = features // (2 * (ids.shape[0] - 1))
    tokens = mine[1].shape[1]
    first_group = running is None
    state = () if first_group else running

    def weight_spec(slot):
        return pl.BlockSpec((1, out_rows, 2 * rows), lambda s, ids: (s, 0, ids[slot]))

    in_specs = [whole(a.shape) for a in mine + theirs] + [weight_spec(slot) for slot in slots]
    total_spec = pl.BlockSpec((1, out_rows, tokens), lambda s, ids: (s, 0, 0))
    if not first_group:
        in_specs.append(total_spec)
        if side:
            in_specs.append(whole(state[1].shape))
    in_specs += [whole(a.shape) for a in extras]
    scratch = [pltpu.VMEM((2 * len(slots) * rows, tokens), bf16)]
    if finish is None:
        out_shape = [jax.ShapeDtypeStruct((streams, out_rows, tokens), f32)]
        out_specs = [total_spec]
        if side:
            out_shape.append(jax.ShapeDtypeStruct((side_rows, tokens), f32))
            out_specs.append(whole((side_rows, tokens)))
        body = None
    else:
        body, out_shape, out_specs, more_scratch = finish
        if side:
            scratch.append(pltpu.VMEM((side_rows, tokens), f32))
    kernel = lambda *refs: product_kernel(
        slots, None, rows, first_group, side, body, len(extras), *refs
    )
    return pl.pallas_call(
        kernel,
        grid_spec=pltpu.PrefetchScalarGridSpec(
            num_scalar_prefetch=1,
            grid=(streams,),
            in_specs=in_specs,
            out_specs=out_specs,
            scratch_shapes=scratch,
        ),
        out_shape=out_shape,
        compiler_params=pltpu.CompilerParams(vmem_limit_bytes=48 * 2**20),
        cost_estimate=pl.CostEstimate(
            flops=2 * streams * out_rows * tokens * 2 * rows * len(slots),
            bytes_accessed=streams * out_rows * (4 * rows * len(slots) + 8 * tokens),
            transcendentals=0,
        ),
        name=name,
    )(ids, *mine, *theirs, *[weight] * len(slots), *state, *extras)


def gather_products(ids, first, second, weight, side, finish, extras=(), name="sum"):
    chips = lax.axis_size("fsdp") // 2
    running = None
    pending = [(0, first, second)]
    groups = list(ring_steps(first, second))
    groups[0] = pending + groups[0]
    for number, group in enumerate(groups):
        slots = [g[0] for g in group]
        mine = [half for g in group for half in g[1:]]
        theirs = [other_core(half) for half in mine]
        last = number == len(groups) - 1
        running = products(
            ids,
            slots,
            mine,
            theirs,
            weight,
            running,
            side,
            finish if last else None,
            extras if last else (),
            name=f"{name}_{number}",
        )
    return running


def smooth(projected, taps, halo):
    tokens = projected.shape[1]
    lane = lax.broadcasted_iota(jnp.int32, projected.shape, 1)
    out = taps[:, :1] * projected
    count = taps.shape[1]
    for tap in range(1, count):
        moved = pltpu.roll(projected, tap, 1)
        for place in range(tap):
            if halo is None:
                edge = 0.0
            else:
                at = count - 1 - tap + place
                edge = halo[:, at : at + 1]
            moved = jnp.where(lane == place, edge, moved)
        out = out + taps[:, tap : tap + 1] * moved
    return out


def projection_finish(features):
    def body(step, product, side_total, extras, outs):
        projected_ref, gated_ref = outs
        taps_ref = extras[0]
        mean = jnp.sum(side_total[...], axis=0, keepdims=True) * (1.0 / features)
        factor = lax.rsqrt(mean + epsilon)
        projected_ref[pl.ds(step, 1)] = (product * factor).astype(bf16)[None]

        @pl.when(step == 2)
        def _():
            key = smooth(projected_ref[1].astype(f32), taps_ref[1], None)
            value = smooth(projected_ref[2].astype(f32), taps_ref[2], None)
            gated_ref[...] = (key * value).astype(bf16)

    return body


def spectra_kernel(filter_ref, table_ref, out_ref):
    blocks = filter_ref.shape[1] // block_len
    before = jnp.zeros((filter_ref.shape[0], block_len), bf16)
    for k in range(blocks):
        now = filter_ref[:, k * block_len : (k + 1) * block_len]
        segment = jnp.concatenate([before, now], axis=1)
        out_ref[:, 2 * k * block_len : 2 * (k + 1) * block_len] = dot(
            segment, table_ref[0]
        ) + dot(segment, table_ref[1])
        before = now


def filter_spectra(long_filter, table):
    channels, lags = long_filter.shape
    tile = min(channels, 64)
    return pl.pallas_call(
        spectra_kernel,
        grid=(channels // tile,),
        in_specs=[pl.BlockSpec((tile, lags), lambda i: (i, 0)), whole(table.shape)],
        out_specs=pl.BlockSpec((tile, 2 * lags), lambda i: (i, 0)),
        out_shape=jax.ShapeDtypeStruct((channels, 2 * lags), f32),
        name="filter_spectra",
    )(long_filter, table)


def block_spectra(gated, table, spec_ref):
    for b in range(gated.shape[1] // block_len):
        piece = gated[:, b * block_len : (b + 1) * block_len]
        spec_ref[:, 2 * b * block_len : 2 * (b + 1) * block_len] = dot(
            piece, table[0, :block_len]
        ) + dot(piece, table[1, :block_len])


def multiply_spectra(source, filters, pairs, total_ref, fresh):
    def rows_of(i, carry):
        rows = pl.ds(pl.multiple_of(i * 8, 8), 8)

        def part(ref, k, imaginary):
            start = (2 * k + imaginary) * block_len
            return ref[rows, start : start + block_len]

        for a, terms in enumerate(pairs):
            if fresh:
                real = jnp.zeros((8, block_len), f32)
                imag = jnp.zeros((8, block_len), f32)
            else:
                real, imag = part(total_ref, a, 0), part(total_ref, a, 1)
            for b, d in terms:
                gr, gi = part(source, b, 0), part(source, b, 1)
                hr, hi = part(filters, d, 0), part(filters, d, 1)
                real = real + gr * hr - gi * hi
                imag = imag + gr * hi + gi * hr
            total_ref[rows, 2 * a * block_len : (2 * a + 1) * block_len] = real
            total_ref[rows, (2 * a + 1) * block_len : (2 * a + 2) * block_len] = imag
        return carry

    lax.fori_loop(0, total_ref.shape[0] // 8, rows_of, 0)


def own_kernel(projected_ref, halo_ref, taps_ref, filters_ref, table_ref, *refs):
    query_ref, gated_ref, total_ref, spec_ref = refs
    smoothed = [
        smooth(projected_ref[s].astype(f32), taps_ref[s], halo_ref[s].astype(f32))
        for s in range(3)
    ]
    query_ref[...] = smoothed[0]
    gated_ref[...] = (smoothed[1] * smoothed[2]).astype(bf16)
    block_spectra(gated_ref, table_ref, spec_ref)
    blocks = gated_ref.shape[1] // block_len
    pairs = [[(b, a - b) for b in range(a + 1)] for a in range(blocks)]
    multiply_spectra(spec_ref, filters_ref, pairs, total_ref, True)


def own_part(projected, halo, taps, filters, table):
    _, channels, tokens = projected.shape
    tile = min(channels, 64)
    rows = lambda width: pl.BlockSpec((tile, width), lambda i: (i, 0))
    deep = lambda width: pl.BlockSpec((3, tile, width), lambda i: (0, i, 0))
    return pl.pallas_call(
        own_kernel,
        grid=(channels // tile,),
        in_specs=[
            deep(tokens),
            deep(halo.shape[2]),
            deep(taps.shape[2]),
            rows(2 * tokens),
            whole(table.shape),
        ],
        out_specs=[rows(tokens), rows(tokens), rows(2 * tokens)],
        out_shape=[
            jax.ShapeDtypeStruct((channels, tokens), f32),
            jax.ShapeDtypeStruct((channels, tokens), bf16),
            jax.ShapeDtypeStruct((channels, 2 * tokens), f32),
        ],
        scratch_shapes=[pltpu.VMEM((tile, 2 * tokens), f32)],
        compiler_params=pltpu.CompilerParams(vmem_limit_bytes=48 * 2**20),
        cost_estimate=pl.CostEstimate(flops=6 * 10**8, bytes_accessed=6 * 10**6, transcendentals=0),
        name="own_part",
    )(projected, halo, taps, filters, table)


def far_kernel(turn, last, *refs):
    moved_ref, total_ref, filters_ref, table_ref = refs[:4]
    blocks = moved_ref.shape[1] // block_len
    pairs = [
        [(b, turn * blocks + a - b) for b in range(blocks)] for a in range(blocks)
    ]
    if not last:
        out_ref, spec_ref = refs[4:]
        out_ref[...] = total_ref[...]
        block_spectra(moved_ref, table_ref, spec_ref)
        multiply_spectra(spec_ref, filters_ref, pairs, out_ref, False)
        return
    back_ref, query_ref, gated_ref, skip_ref, out_ref, spec_ref, sum_ref = refs[4:]
    sum_ref[...] = total_ref[...]
    block_spectra(moved_ref, table_ref, spec_ref)
    multiply_spectra(spec_ref, filters_ref, pairs, sum_ref, False)
    rows = out_ref.shape[0]
    skip = jnp.broadcast_to(skip_ref[0], (8, rows)).T[:, :1]
    for a in range(blocks):
        lanes = slice(a * block_len, (a + 1) * block_len)
        spectrum = sum_ref[:, 2 * a * block_len : 2 * (a + 1) * block_len]
        high = spectrum.astype(bf16)
        low = (spectrum - high.astype(f32)).astype(bf16)
        filtered = dot(high, back_ref[0]) + (dot(low, back_ref[0]) + dot(high, back_ref[1]))
        gated = gated_ref[:, lanes].astype(f32)
        out_ref[:, lanes] = (query_ref[:, lanes] * (filtered + skip * gated)).astype(bf16)


def far_part(turn, part, moved, total, filters, table, last):
    rows_n, tokens = moved.shape
    filters_n = filters.shape[1]
    at = lambda width: pl.BlockSpec((rows_n, width), lambda i: (part, 0))
    in_specs = [whole(moved.shape), at(2 * tokens) if total.shape[0] != rows_n else whole(total.shape)]
    in_specs += [at(filters_n), whole(table.shape)]
    scratch = [pltpu.VMEM((rows_n, 2 * tokens), f32)]
    if last is None:
        args = ()
        out_shape = jax.ShapeDtypeStruct((rows_n, 2 * tokens), f32)
    else:
        inverse, query, gated, skip = last
        args = (inverse, query, gated, skip.reshape(2, 1, rows_n))
        in_specs += [whole(inverse.shape), at(tokens), at(tokens)]
        in_specs += [pl.BlockSpec((1, 1, rows_n), lambda i: (part, 0, 0))]
        out_shape = jax.ShapeDtypeStruct((rows_n, tokens), bf16)
        scratch.append(pltpu.VMEM((rows_n, 2 * tokens), f32))
    return pl.pallas_call(
        lambda *refs: far_kernel(turn, last is not None, *refs),
        grid=(1,),
        in_specs=in_specs,
        out_specs=whole(out_shape.shape),
        out_shape=out_shape,
        scratch_shapes=scratch,
        compiler_params=pltpu.CompilerParams(vmem_limit_bytes=48 * 2**20),
        cost_estimate=pl.CostEstimate(flops=4 * 10**8, bytes_accessed=4 * 10**6, transcendentals=0),
        name=f"far_part_{turn}_{part}",
    )(moved, total, filters, table, *args)


def from_before(block):
    count = lax.axis_size("ctx")
    return lax.ppermute(block, "ctx", [(i - 1, i) for i in range(1, count)])


def output_finish(step, product, side_total, extras, outs):
    outs[0][...] = product.astype(bf16)


def shards(activations, norm_gain, w_in, w_short, long_filter, skip_gain, w_out):
    channels, tokens = activations.shape
    features = w_in.shape[2]
    turns = lax.axis_size("ctx")
    half = channels // 2
    forward, inverse = (jnp.asarray(t) for t in dft_tables())
    ids = ring_ids()
    first, second = prepare(activations, norm_gain)
    filters = filter_spectra(long_filter, forward)

    finish = (
        projection_finish(features),
        [
            jax.ShapeDtypeStruct((3, channels, tokens), bf16),
            jax.ShapeDtypeStruct((channels, tokens), bf16),
        ],
        [whole((3, channels, tokens)), whole((channels, tokens))],
        None,
    )
    projected, gated_alone = gather_products(
        ids, first, second, w_in, True, finish, (w_short,), "projection"
    )

    taps = w_short.shape[2]
    halo = from_before(projected[:, :, tokens - (taps - 1) :])
    moving = None
    if turns == 2:
        moving = [gated_alone[:half], gated_alone[half:]]
        moving = [from_before(m) for m in moving]
    query, gated, total = own_part(projected, halo, w_short, filters, forward)
    if moving is None:
        moving = [from_before(m) for m in (gated[:half], gated[half:])]
    totals = [total, total]
    mixed = [None, None]
    for turn in range(1, turns):
        for part in range(2):
            last = None
            if turn == turns - 1:
                last = (inverse, query, gated, skip_gain)
            totals[part] = far_part(turn, part, moving[part], totals[part], filters, forward, last)
            if last is None:
                moving[part] = from_before(moving[part])
    mixed = totals

    out_finish = (
        output_finish,
        [jax.ShapeDtypeStruct((channels, tokens), bf16)],
        [whole((channels, tokens))],
        None,
    )
    (result,) = gather_products(
        ids, mixed[0], mixed[1], w_out[None], False, out_finish, (), "output"
    )
    return result


def solution(mesh):
    placed = (
        P("fsdp", "ctx"),
        P("fsdp"),
        P(None, "fsdp", None),
        P(None, "fsdp", None),
        P("fsdp", None),
        P("fsdp"),
        P("fsdp", None),
    )
    return jax.shard_map(
        shards, mesh=mesh, in_specs=placed, out_specs=P("fsdp", "ctx"), check_vma=False
    )
```

time: 285 us -> 122 us (0.43)
  waiting for transfers between devices: 123 us -> 30.1 us
  other arithmetic: 57.3 us -> 0.09 us
  starting transfers between devices: 5.59 us -> 44.5 us
  Pallas kernels: 0 us -> 36.5 us
  matrix products: 31.5 us -> 0 us
  blocking collectives: 23.1 us -> 0 us
  local copies, waits for them, and re-layouts: 29.9 us -> 9.22 us
  between operations: 13.6 us -> 0.36 us
    all_gather x2 -> x0, waiting for transfers between devices: 122 us -> none  [the longest x1 103 us: shards(): lax.all_gather(mixed, 'fsdp', axis=0, tiled=True)]
    ppermute x2 -> x63, starting transfers between devices: 5.54 us -> 44.5 us  [the longest x6 9.7 us: ring_steps(): ba = lax.ppermute(ba, 'fsdp', behind)]
    pallas_call x0 -> x13, Pallas kernels: none -> 36.5 us  [the longest x8 22.5 us: products(): pl.pallas_call(kernel, grid_spec=pltpu.PrefetchScalarGridSpec(num_scalar_...]
    dot_general x6 -> x0, matrix products: 31.5 us -> none  [the longest x1 7.9 us: shards(): jnp.einsum('sci,it->sct', w_in, normed, preferred_element_type=jnp.float32)]
    ppermute x2 -> x63, waiting for transfers between devices: 0.01 us -> 30.1 us  [the longest x6 7.27 us: ring_steps(): fb = lax.ppermute(fb, 'fsdp', ahead)]
    add x7 -> x0, other arithmetic: 25.3 us -> none  [the longest x5 24.8 us: apply_block(): return inner + complex_product(chosen, spectrum[:, None, :])]
    all_gather x1 -> x0, blocking collectives: 23.1 us -> none  [shards(): lax.all_gather(norm_gain.astype(jnp.bfloat16), 'fsdp', axis=0, tiled=True)]
    sub x5 -> x0, other arithmetic: 21.7 us -> none  [complex_product(): left_re * right_re - left_im * right_im]
  transfers between devices with their start and end apart: 4 -> 63, of which waited for: 2 -> 21; matrix products, arithmetic and copies ran while one was open for 30% -> 1% of each run, Pallas kernels for 0% -> 24%
where the time goes in v1:
time: 122 us; the launch traced here: 121 us
  starting transfers between devices  44.5 us (36%)
  Pallas kernels  36.5 us (30%)
  waiting for transfers between devices  30.1 us (25%)
  local copies, waits for them, and re-layouts  9.22 us (8%)
    pallas_call x8, Pallas kernels, products(): pl.pallas_call(kernel, grid_spec=pltpu.PrefetchScalarGridSpec(num_scalar_...  22.5 us
    ppermute x6, starting transfers between devices, ring_steps(): ba = lax.ppermute(ba, 'fsdp', behind)  9.7 us
    ppermute x6, starting transfers between devices, ring_steps(): fb = lax.ppermute(fb, 'fsdp', ahead)  9.67 us
    unnamed x31, local copies, waits for them, and re-layouts  9.07 us
    ppermute x8, starting transfers between devices, ring_steps(): fa = lax.ppermute(fa, 'fsdp', ahead)  8.42 us
    ppermute x6, waiting for transfers between devices, ring_steps(): fb = lax.ppermute(fb, 'fsdp', ahead)  7.27 us
    ppermute x6, waiting for transfers between devices, ring_steps(): ba = lax.ppermute(ba, 'fsdp', behind)  7.19 us
    ppermute x8, starting transfers between devices, ring_steps(): bb = lax.ppermute(bb, 'fsdp', behind)  6.9 us
  transfers between devices with their start and end apart: 63, of which 21 were waited for; matrix products, arithmetic and copies ran while one was open for 1% of the time, Pallas kernels for 24%

profile of v1, /device:TPU:0, one launch (start us, length us, event | category | flops | bytes accessed | tf_op | source)
XLA Modules:
  0.0 120.7 jit_solution(7214464465733423581)
XLA Ops:
  0.0 1.9 %prepare.1 = (bf16[136,640]{1,0:T(8,128)(2,1)}, bf16[128,640]{1,0:T(8,128)(2,1)}) custom-call(bf16[256,640]{1,0:T(8,128)(2,1)} %x_ref.1, f32[1,256]{1,0:T(1,128)} %bitcast.14), custom_call_target="tpu_custom_call" | custom-call | tf_op jit(solution)/shard_map/prepare/pallas_call | solution.py:61
  2.4 2.6 %collective-permute-start.10 = (bf16[128,640]{1,0:T(8,128)(2,1)}, bf16[128,640]{1,0:T(8,128)(2,1)S(1)}, u32[]{:S(2)}, u32[]{:S(2)}) collective-permute-start(bf16[128,640]{1,0:T(8,128)(2,1)} %get-tuple-element.19.refs_2_), channel_id=1, source_target_pairs={{0,8},{2,10},{8,16},{10,18},{16,24},{18,26},{24,28},{26,30},{28,20... | collective-permute-start | bytes 491528 | tf_op jit(solution)/shard_map/ppermute | solution.py:107
  5.2 1.7 %collective-permute-start.13 = (bf16[136,640]{1,0:T(8,128)(2,1)}, bf16[136,640]{1,0:T(8,128)(2,1)S(1)}, u32[]{:S(2)}, u32[]{:S(2)}) collective-permute-start(bf16[136,640]{1,0:T(8,128)(2,1)} %get-tuple-element.18.refs_1_), channel_id=1, source_target_pairs={{8,0},{10,2},{16,8},{18,10},{24,16},{26,18},{28,24},{30,26},{20,28... | collective-permute-start | bytes 522248 | tf_op jit(solution)/shard_map/ppermute | solution.py:108
  7.2 2.8 %collective-permute-done.10.refs_4_ = bf16[128,640]{1,0:T(8,128)(2,1)S(1)} collective-permute-done((bf16[128,640]{1,0:T(8,128)(2,1)}, bf16[128,640]{1,0:T(8,128)(2,1)S(1)}, u32[]{:S(2)}, u32[]{:S(2)}) %collective-permute-start.10) | collective-permute-done | bytes 163872 | tf_op jit(solution)/shard_map/ppermute | solution.py:107
  10.0 2.2 %collective-permute-done.4.refs_6_ = bf16[128,640]{1,0:T(8,128)(2,1)S(1)} collective-permute-done((bf16[128,640]{1,0:T(8,128)(2,1)}, bf16[128,640]{1,0:T(8,128)(2,1)S(1)}, u32[]{:S(2)}, u32[]{:S(2)}) %collective-permute-start.4) | collective-permute-done | bytes 163872 | tf_op jit(solution)/shard_map/ppermute | solution.py:105
  12.2 1.6 %collective-permute-start.11 = (bf16[128,640]{1,0:T(8,128)(2,1)S(1)}, bf16[128,640]{1,0:T(8,128)(2,1)S(1)}, u32[]{:S(2)}, u32[]{:S(2)}) collective-permute-start(bf16[128,640]{1,0:T(8,128)(2,1)S(1)} %collective-permute-done.10.refs_4_), channel_id=1, source_target_pairs={{0,8},{2,10},{8,16},{10,18},{16,24},{18,26},{24,28},{26,30},{28,20... | collective-permute-start | bytes 491528 | tf_op jit(solution)/shard_map/ppermute | solution.py:107
  13.8 1.4 %collective-permute-done.13.refs_5_ = bf16[136,640]{1,0:T(8,128)(2,1)S(1)} collective-permute-done((bf16[136,640]{1,0:T(8,128)(2,1)}, bf16[136,640]{1,0:T(8,128)(2,1)S(1)}, u32[]{:S(2)}, u32[]{:S(2)}) %collective-permute-start.13) | collective-permute-done | bytes 174112 | tf_op jit(solution)/shard_map/ppermute | solution.py:108
  16.3 1.7 %collective-permute-start.14 = (bf16[136,640]{1,0:T(8,128)(2,1)S(1)}, bf16[136,640]{1,0:T(8,128)(2,1)S(1)}, u32[]{:S(2)}, u32[]{:S(2)}) collective-permute-start(bf16[136,640]{1,0:T(8,128)(2,1)S(1)} %collective-permute-done.13.refs_5_), channel_id=1, source_target_pairs={{8,0},{10,2},{16,8},{18,10},{24,16},{26,18},{28,24},{30,26},{20,28... | collective-permute-start | bytes 522248 | tf_op jit(solution)/shard_map/ppermute | solution.py:108
  19.8 2.4 %collective-permute-done.5.refs_4_ = bf16[128,640]{1,0:T(8,128)(2,1)S(1)} collective-permute-done((bf16[128,640]{1,0:T(8,128)(2,1)S(1)}, bf16[128,640]{1,0:T(8,128)(2,1)S(1)}, u32[]{:S(2)}, u32[]{:S(2)}) %collective-permute-start.5) | collective-permute-done | bytes 163872 | tf_op jit(solution)/shard_map/ppermute | solution.py:105
  22.2 1.4 %collective-permute-start.12 = (bf16[128,640]{1,0:T(8,128)(2,1)S(1)}, bf16[128,640]{1,0:T(8,128)(2,1)}, u32[]{:S(2)}, u32[]{:S(2)}) collective-permute-start(bf16[128,640]{1,0:T(8,128)(2,1)S(1)} %collective-permute-done.11.refs_2_), channel_id=1, source_target_pairs={{0,8},{2,10},{8,16},{10,18},{16,24},{18,26},{24,28},{26,30},{28,20... | collective-permute-start | bytes 491528 | tf_op jit(solution)/shard_map/ppermute | solution.py:107
  27.4 1.6 %collective-permute-done.12.refs_2_ = bf16[128,640]{1,0:T(8,128)(2,1)} collective-permute-done((bf16[128,640]{1,0:T(8,128)(2,1)S(1)}, bf16[128,640]{1,0:T(8,128)(2,1)}, u32[]{:S(2)}, u32[]{:S(2)}) %collective-permute-start.12) | collective-permute-done | bytes 163872 | tf_op jit(solution)/shard_map/ppermute | solution.py:107
  29.0 1.6 %collective-permute-start.15 = (bf16[136,640]{1,0:T(8,128)(2,1)S(1)}, bf16[136,640]{1,0:T(8,128)(2,1)S(1)}, u32[]{:S(2)}, u32[]{:S(2)}) collective-permute-start(bf16[136,640]{1,0:T(8,128)(2,1)S(1)} %collective-permute-done.14.refs_3_), channel_id=1, source_target_pairs={{8,0},{10,2},{16,8},{18,10},{24,16},{26,18},{28,24},{30,26},{20,28... | collective-permute-start | bytes 522248 | tf_op jit(solution)/shard_map/ppermute | solution.py:108
  31.8 1.6 %collective-permute-start.7 = (bf16[128,640]{1,0:T(8,128)(2,1)}, bf16[128,640]{1,0:T(8,128)(2,1)}, u32[]{:S(2)}, u32[]{:S(2)}) collective-permute-start(bf16[128,640]{1,0:T(8,128)(2,1)} %collective-permute-done.6.refs_4_), channel_id=1, source_target_pairs={{8,0},{10,2},{16,8},{18,10},{24,16},{26,18},{28,24},{30,26},{20,28... | collective-permute-start | bytes 491528 | tf_op jit(solution)/shard_map/ppermute | solution.py:105
  39.8 4.5 %projection_0.1 = (f32[3,256,640]{2,1,0:T(8,128)S(1)}, f32[8,640]{1,0:T(8,128)S(1)}) custom-call(s32[9]{0:T(128)S(1)} %pad_add_fusion.refs_0_, bf16[136,640]{1,0:T(8,128)(2,1)S(1)} %copy-done.4, bf16[128,640]{1,0:T(8,128)(2,1)S(1)} %copy-done.5, bf16[136,640]{1,0:T(8,128)(2,1)S(1)} %collective-permute-done.refs_3_, ...), custom_call_target="tpu_custom_call" | custom-call | flops 1509949440 | bytes 6291456 | tf_op jit(solution)/shard_map/projection_0/pallas_call | solution.py:199
  46.8 3.9 %projection_1.1 = (f32[3,256,640]{2,1,0:T(8,128)S(1)}, f32[8,640]{1,0:T(8,128)S(1)}) custom-call(s32[9]{0:T(128)S(1)} %pad_add_fusion.refs_0_, bf16[136,640]{1,0:T(8,128)(2,1)S(1)} %collective-permute-done.1.refs_1_, bf16[128,640]{1,0:T(8,128)(2,1)S(1)} %collective-permute-done.11.refs_2_, bf16[136,640]{1,0:T(8,128)(2,1)S(1)} %collective-permute-done.14.refs_3_, ...), custom_call_target="tpu_custom_call" | custom-call | flops 1006632960 | bytes 5505024 | tf_op jit(solution)/shard_map/projection_1/pallas_call | solution.py:199
  50.8 4.1 %projection_2.1 = (f32[3,256,640]{2,1,0:T(8,128)S(1)}, f32[8,640]{1,0:T(8,128)S(1)}) custom-call(s32[9]{0:T(128)S(1)} %pad_add_fusion.refs_0_, bf16[136,640]{1,0:T(8,128)(2,1)S(1)} %collective-permute-done.2.refs_1_, bf16[128,640]{1,0:T(8,128)(2,1)} %collective-permute-done.12.refs_2_, bf16[136,640]{1,0:T(8,128)(2,1)S(1)} %collective-permute-done.15.refs_3_, ...), custom_call_target="tpu_custom_call" | custom-call | flops 1006632960 | bytes 5505024 | tf_op jit(solution)/shard_map/projection_2/pallas_call | solution.py:199
  54.9 4.3 %projection_3.1 = (bf16[3,256,640]{2,1,0:T(8,128)(2,1)S(1)}, bf16[256,640]{1,0:T(8,128)(2,1)S(1)}) custom-call(s32[9]{0:T(128)S(1)} %pad_add_fusion.refs_0_, bf16[136,640]{1,0:T(8,128)(2,1)S(1)} %collective-permute-done.3.refs_1_, bf16[128,640]{1,0:T(8,128)(2,1)} %collective-permute-done.7.refs_2_, bf16[136,640]{1,0:T(8,128)(2,1)S(1)} %collective-permute-done.8.refs_3_, ...), custom_call_target="tpu_custom_call" | custom-call | flops 503316480 | bytes 4718592 | tf_op jit(solution)/shard_map/projection_3/pallas_call | solution.py:199
  59.2 3.6 %collective-permute-start.30 = (bf16[128,640]{1,0:T(8,128)(2,1)S(1)}, bf16[128,640]{1,0:T(8,128)(2,1)S(1)}, u32[]{:S(2)}, u32[]{:S(2)}) collective-permute-start(bf16[128,640]{1,0:T(8,128)(2,1)S(1)} %get-tuple-element.32), channel_id=1, source_target_pairs={{0,1},{2,3},{4,5},{6,7},{8,9},{10,11},{12,13},{14,15},{16,17},{18,... | collective-permute-start | bytes 491528 | tf_op jit(solution)/shard_map/ppermute | solution.py:441
  65.5 4.8 %filter_spectra.1.filters_ref.refs_2_ = f32[256,2560]{1,0:T(8,128)} custom-call(bf16[256,1280]{1,0:T(8,128)(2,1)} %filter_ref.1, bf16[2,256,256]{2,1,0:T(8,128)(2,1)} %constant.69.clone.table_ref.refs_3_), custom_call_target="tpu_custom_call" | custom-call | tf_op jit(solution)/shard_map/filter_spectra/pallas_call | solution.py:295
  70.3 4.2 %collective-permute-done.31.halo_ref = bf16[3,256,2]{2,1,0:T(8,128)(2,1)S(1)} collective-permute-done((bf16[3,256,2]{2,1,0:T(8,128)(2,1)S(1)}, bf16[3,256,2]{2,1,0:T(8,128)(2,1)S(1)}, u32[]{:S(2)}, u32[]{:S(2)}) %collective-permute-start.31) | collective-permute-done | bytes 3104 | tf_op jit(solution)/shard_map/ppermute | solution.py:441
  74.5 4.4 %own_part.1 = (f32[256,640]{1,0:T(8,128)S(1)}, bf16[256,640]{1,0:T(8,128)(2,1)S(1)}, f32[256,1280]{1,0:T(8,128)S(1)}) custom-call(bf16[3,256,640]{2,1,0:T(8,128)(2,1)S(1)} %get-tuple-element.27.projected_ref, bf16[3,256,2]{2,1,0:T(8,128)(2,1)S(1)} %collective-permute-done.31.halo_ref, f32[3,256,3]{2,1,0:T(8,128)S(1)} %copy.10.refs_8_.taps_ref, ...), custom_call_target="tpu_custom_call" | custom-call | flops 600000000 | bytes 6000000 | tf_op jit(solution)/shard_map/own_part/pallas_call | solution.py:358
  79.0 1.4 %far_part_1_0.1.refs_1_ = bf16[128,640]{1,0:T(8,128)(2,1)S(1)} custom-call(bf16[128,640]{1,0:T(8,128)(2,1)S(1)} %collective-permute-done.30.refs_0_, f32[256,1280]{1,0:T(8,128)S(1)} %get-tuple-element.28.refs_1_, f32[256,2560]{1,0:T(8,128)S(1)} %copy-done.1, bf16[2,256,256]{2,1,0:T(8,128)(2,1)S(1)} %copy-done.2, bf16[2,256,128]{2,1,0:T(8,128)(2,1)S(1)} %copy-done.3, ...), custom_call_target="tpu_custom_call" | custom-call | flops 400000000 | bytes 4000000 | tf_op jit(solution)/shard_map/far_part_1_0/pallas_call | solution.py:426
  88.0 2.0 %collective-permute-start.47 = (bf16[128,640]{1,0:T(8,128)(2,1)S(1)}, bf16[128,640]{1,0:T(8,128)(2,1)S(1)}, u32[]{:S(2)}, u32[]{:S(2)}) collective-permute-start(bf16[128,640]{1,0:T(8,128)(2,1)S(1)} %collective-permute-done.46.refs_5_), channel_id=1, source_target_pairs={{8,0},{10,2},{16,8},{18,10},{24,16},{26,18},{28,24},{30,26},{20,28... | collective-permute-start | bytes 491528 | tf_op jit(solution)/shard_map/ppermute | solution.py:108
  95.9 2.3 %collective-permute-done.33.refs_1_ = bf16[128,640]{1,0:T(8,128)(2,1)S(1)} collective-permute-done((bf16[128,640]{1,0:T(8,128)(2,1)S(1)}, bf16[128,640]{1,0:T(8,128)(2,1)S(1)}, u32[]{:S(2)}, u32[]{:S(2)}) %collective-permute-start.33) | collective-permute-done | bytes 163872 | tf_op jit(solution)/shard_map/ppermute | solution.py:104
  98.2 1.9 %collective-permute-start.48 = (bf16[128,640]{1,0:T(8,128)(2,1)S(1)}, bf16[128,640]{1,0:T(8,128)(2,1)S(1)}, u32[]{:S(2)}, u32[]{:S(2)}) collective-permute-start(bf16[128,640]{1,0:T(8,128)(2,1)S(1)} %collective-permute-done.47.refs_3_), channel_id=1, source_target_pairs={{8,0},{10,2},{16,8},{18,10},{24,16},{26,18},{28,24},{30,26},{20,28... | collective-permute-start | bytes 491528 | tf_op jit(solution)/shard_map/ppermute | solution.py:108
  102.8 2.3 %collective-permute-done.48.refs_3_ = bf16[128,640]{1,0:T(8,128)(2,1)S(1)} collective-permute-done((bf16[128,640]{1,0:T(8,128)(2,1)S(1)}, bf16[128,640]{1,0:T(8,128)(2,1)S(1)}, u32[]{:S(2)}, u32[]{:S(2)}) %collective-permute-start.48) | collective-permute-done | bytes 163872 | tf_op jit(solution)/shard_map/ppermute | solution.py:108
  105.1 1.7 %collective-permute-start.45 = (bf16[128,640]{1,0:T(8,128)(2,1)S(1)}, bf16[128,640]{1,0:T(8,128)(2,1)S(1)}, u32[]{:S(2)}, u32[]{:S(2)}) collective-permute-start(bf16[128,640]{1,0:T(8,128)(2,1)S(1)} %collective-permute-done.44.refs_2_), channel_id=1, source_target_pairs={{0,8},{2,10},{8,16},{10,18},{16,24},{18,26},{24,28},{26,30},{28,20... | collective-permute-start | bytes 491528 | tf_op jit(solution)/shard_map/ppermute | solution.py:107
  107.3 1.7 %collective-permute-start.35 = (bf16[128,640]{1,0:T(8,128)(2,1)S(1)}, bf16[128,640]{1,0:T(8,128)(2,1)S(1)}, u32[]{:S(2)}, u32[]{:S(2)}) collective-permute-start(bf16[128,640]{1,0:T(8,128)(2,1)S(1)} %collective-permute-done.34.refs_1_), channel_id=1, source_target_pairs={{0,8},{2,10},{8,16},{10,18},{16,24},{18,26},{24,28},{26,30},{28,20... | collective-permute-start | bytes 491528 | tf_op jit(solution)/shard_map/ppermute | solution.py:104
  110.2 1.4 %collective-permute-done.45.refs_2_ = bf16[128,640]{1,0:T(8,128)(2,1)S(1)} collective-permute-done((bf16[128,640]{1,0:T(8,128)(2,1)S(1)}, bf16[128,640]{1,0:T(8,128)(2,1)S(1)}, u32[]{:S(2)}, u32[]{:S(2)}) %collective-permute-start.45) | collective-permute-done | bytes 163872 | tf_op jit(solution)/shard_map/ppermute | solution.py:107
  112.2 2.2 %collective-permute-done.35.refs_1_ = bf16[128,640]{1,0:T(8,128)(2,1)S(1)} collective-permute-done((bf16[128,640]{1,0:T(8,128)(2,1)S(1)}, bf16[128,640]{1,0:T(8,128)(2,1)S(1)}, u32[]{:S(2)}, u32[]{:S(2)}) %collective-permute-start.35) | collective-permute-done | bytes 163872 | tf_op jit(solution)/shard_map/ppermute | solution.py:104
  115.0 1.5 %output_0.1.refs_11_ = f32[1,256,640]{2,1,0:T(8,128)S(1)} custom-call(s32[9]{0:T(128)S(1)} %pad_add_fusion.refs_0_, bf16[128,640]{1,0:T(8,128)(2,1)S(1)} %far_part_1_0.1.refs_1_, bf16[128,640]{1,0:T(8,128)(2,1)S(1)} %far_part_1_1.1.refs_2_, bf16[128,640]{1,0:T(8,128)(2,1)S(1)} %collective-permute-done.32.refs_3_, ...), custom_call_target="tpu_custom_call" | custom-call | flops 503316480 | bytes 2097152 | tf_op jit(solution)/shard_map/output_0/pallas_call | solution.py:199
  119.0 1.7 %output_3.1 = bf16[256,640]{1,0:T(8,128)(2,1)} custom-call(s32[9]{0:T(128)S(1)} %pad_add_fusion.refs_0_, bf16[128,640]{1,0:T(8,128)(2,1)S(1)} %collective-permute-done.35.refs_1_, bf16[128,640]{1,0:T(8,128)(2,1)S(1)} %collective-permute-done.40.refs_2_, bf16[128,640]{1,0:T(8,128)(2,1)S(1)} %collective-permute-done.41.refs_3_, ...), custom_call_target="tpu_custom_call" | custom-call | flops 167772160 | bytes 1572864 | tf_op jit(solution)/shard_map/output_3/pallas_call | solution.py:199
  (142 shorter events, 41.9 us)
Async XLA Ops:
  2.4 7.6 %collective-permute-start.10 = (bf16[128,640]{1,0:T(8,128)(2,1)}, bf16[128,640]{1,0:T(8,128)(2,1)S(1)}, u32[]{:S(2)}, u32[]{:S(2)}) collective-permute-start(bf16[128,640]{1,0:T(8,128)(2,1)} %get-tuple-element.19.refs_2_), channel_id=1, source_target_pairs={{0,8},{2,10},{8,16},{10,18},{16,24},{18,26},{24,28},{26,30},{28,20... | collective-permute-start | bytes 491528 | tf_op jit(solution)/shard_map/ppermute | solution.py:107
  5.0 7.2 %collective-permute-start.4 = (bf16[128,640]{1,0:T(8,128)(2,1)}, bf16[128,640]{1,0:T(8,128)(2,1)S(1)}, u32[]{:S(2)}, u32[]{:S(2)}) collective-permute-start(bf16[128,640]{1,0:T(8,128)(2,1)} %get-tuple-element.19.refs_2_), channel_id=1, source_target_pairs={{8,0},{10,2},{16,8},{18,10},{24,16},{26,18},{28,24},{30,26},{20,28... | collective-permute-start | bytes 491528 | tf_op jit(solution)/shard_map/ppermute | solution.py:105
  5.0 8.8 %collective-permute-start.24 = (bf16[136,640]{1,0:T(8,128)(2,1)}, bf16[136,640]{1,0:T(8,128)(2,1)S(1)}, u32[]{:S(2)}, u32[]{:S(2)}) collective-permute-start(bf16[136,640]{1,0:T(8,128)(2,1)} %get-tuple-element.18.refs_1_), channel_id=1, source_target_pairs={{0,2},{2,0},{4,6},{6,4},{8,10},{10,8},{12,14},{14,12},{16,18},{18,... | collective-permute-start | bytes 522248 | tf_op jit(solution)/shard_map/ppermute | solution.py:115
  5.2 10.0 %collective-permute-start.13 = (bf16[136,640]{1,0:T(8,128)(2,1)}, bf16[136,640]{1,0:T(8,128)(2,1)S(1)}, u32[]{:S(2)}, u32[]{:S(2)}) collective-permute-start(bf16[136,640]{1,0:T(8,128)(2,1)} %get-tuple-element.18.refs_1_), channel_id=1, source_target_pairs={{8,0},{10,2},{16,8},{18,10},{24,16},{26,18},{28,24},{30,26},{20,28... | collective-permute-start | bytes 522248 | tf_op jit(solution)/shard_map/ppermute | solution.py:108
  7.0 8.6 %collective-permute-start = (bf16[136,640]{1,0:T(8,128)(2,1)}, bf16[136,640]{1,0:T(8,128)(2,1)S(1)}, u32[]{:S(2)}, u32[]{:S(2)}) collective-permute-start(bf16[136,640]{1,0:T(8,128)(2,1)} %get-tuple-element.18.refs_1_), channel_id=1, source_target_pairs={{0,8},{2,10},{8,16},{10,18},{16,24},{18,26},{24,28},{26,30},{28,20... | collective-permute-start | bytes 522248 | tf_op jit(solution)/shard_map/ppermute | solution.py:104
  15.3 7.0 %collective-permute-start.5 = (bf16[128,640]{1,0:T(8,128)(2,1)S(1)}, bf16[128,640]{1,0:T(8,128)(2,1)S(1)}, u32[]{:S(2)}, u32[]{:S(2)}) collective-permute-start(bf16[128,640]{1,0:T(8,128)(2,1)S(1)} %collective-permute-done.4.refs_6_), channel_id=1, source_target_pairs={{8,0},{10,2},{16,8},{18,10},{24,16},{26,18},{28,24},{30,26},{20,28... | collective-permute-start | bytes 491528 | tf_op jit(solution)/shard_map/ppermute | solution.py:105
  15.6 6.7 %collective-permute-start.28 = (bf16[136,640]{1,0:T(8,128)(2,1)S(1)}, bf16[136,640]{1,0:T(8,128)(2,1)S(1)}, u32[]{:S(2)}, u32[]{:S(2)}) collective-permute-start(bf16[136,640]{1,0:T(8,128)(2,1)S(1)} %collective-permute-done.13.refs_5_), channel_id=1, source_target_pairs={{0,2},{2,0},{4,6},{6,4},{8,10},{10,8},{12,14},{14,12},{16,18},{18,... | collective-permute-start | bytes 522248 | tf_op jit(solution)/shard_map/ppermute | solution.py:115
  16.3 8.2 %collective-permute-start.14 = (bf16[136,640]{1,0:T(8,128)(2,1)S(1)}, bf16[136,640]{1,0:T(8,128)(2,1)S(1)}, u32[]{:S(2)}, u32[]{:S(2)}) collective-permute-start(bf16[136,640]{1,0:T(8,128)(2,1)S(1)} %collective-permute-done.13.refs_5_), channel_id=1, source_target_pairs={{8,0},{10,2},{16,8},{18,10},{24,16},{26,18},{28,24},{30,26},{20,28... | collective-permute-start | bytes 522248 | tf_op jit(solution)/shard_map/ppermute | solution.py:108
  22.2 6.8 %collective-permute-start.12 = (bf16[128,640]{1,0:T(8,128)(2,1)S(1)}, bf16[128,640]{1,0:T(8,128)(2,1)}, u32[]{:S(2)}, u32[]{:S(2)}) collective-permute-start(bf16[128,640]{1,0:T(8,128)(2,1)S(1)} %collective-permute-done.11.refs_2_), channel_id=1, source_target_pairs={{0,8},{2,10},{8,16},{10,18},{16,24},{18,26},{24,28},{26,30},{28,20... | collective-permute-start | bytes 491528 | tf_op jit(solution)/shard_map/ppermute | solution.py:107
  24.5 6.8 %collective-permute-start.6 = (bf16[128,640]{1,0:T(8,128)(2,1)S(1)}, bf16[128,640]{1,0:T(8,128)(2,1)}, u32[]{:S(2)}, u32[]{:S(2)}) collective-permute-start(bf16[128,640]{1,0:T(8,128)(2,1)S(1)} %collective-permute-done.5.refs_4_), channel_id=1, source_target_pairs={{8,0},{10,2},{16,8},{18,10},{24,16},{26,18},{28,24},{30,26},{20,28... | collective-permute-start | bytes 491528 | tf_op jit(solution)/shard_map/ppermute | solution.py:105
  26.1 7.4 %collective-permute-start.2 = (bf16[136,640]{1,0:T(8,128)(2,1)S(1)}, bf16[136,640]{1,0:T(8,128)(2,1)S(1)}, u32[]{:S(2)}, u32[]{:S(2)}) collective-permute-start(bf16[136,640]{1,0:T(8,128)(2,1)S(1)} %collective-permute-done.1.refs_1_), channel_id=1, source_target_pairs={{0,8},{2,10},{8,16},{10,18},{16,24},{18,26},{24,28},{26,30},{28,20... | collective-permute-start | bytes 522248 | tf_op jit(solution)/shard_map/ppermute | solution.py:104
  31.8 12.5 %collective-permute-start.7 = (bf16[128,640]{1,0:T(8,128)(2,1)}, bf16[128,640]{1,0:T(8,128)(2,1)}, u32[]{:S(2)}, u32[]{:S(2)}) collective-permute-start(bf16[128,640]{1,0:T(8,128)(2,1)} %collective-permute-done.6.refs_4_), channel_id=1, source_target_pairs={{8,0},{10,2},{16,8},{18,10},{24,16},{26,18},{28,24},{30,26},{20,28... | collective-permute-start | bytes 491528 | tf_op jit(solution)/shard_map/ppermute | solution.py:105
  33.5 11.4 %collective-permute-start.3 = (bf16[136,640]{1,0:T(8,128)(2,1)S(1)}, bf16[136,640]{1,0:T(8,128)(2,1)S(1)}, u32[]{:S(2)}, u32[]{:S(2)}) collective-permute-start(bf16[136,640]{1,0:T(8,128)(2,1)S(1)} %collective-permute-done.2.refs_1_), channel_id=1, source_target_pairs={{0,8},{2,10},{8,16},{10,18},{16,24},{18,26},{24,28},{26,30},{28,20... | collective-permute-start | bytes 522248 | tf_op jit(solution)/shard_map/ppermute | solution.py:104
  35.6 15.2 %collective-permute-start.19 = (bf16[128,640]{1,0:T(8,128)(2,1)}, bf16[128,640]{1,0:T(8,128)(2,1)S(1)}, u32[]{:S(2)}, u32[]{:S(2)}) collective-permute-start(bf16[128,640]{1,0:T(8,128)(2,1)} %collective-permute-done.6.refs_4_), channel_id=1, source_target_pairs={{0,2},{2,0},{4,6},{6,4},{8,10},{10,8},{12,14},{14,12},{16,18},{18,... | collective-permute-start | bytes 491528 | tf_op jit(solution)/shard_map/ppermute | solution.py:115
  35.6 15.2 %collective-permute-start.16 = (bf16[136,640]{1,0:T(8,128)(2,1)S(1)}, bf16[136,640]{1,0:T(8,128)(2,1)S(1)}, u32[]{:S(2)}, u32[]{:S(2)}) collective-permute-start(bf16[136,640]{1,0:T(8,128)(2,1)S(1)} %collective-permute-done.2.refs_1_), channel_id=1, source_target_pairs={{0,2},{2,0},{4,6},{6,4},{8,10},{10,8},{12,14},{14,12},{16,18},{18,... | collective-permute-start | bytes 522248 | tf_op jit(solution)/shard_map/ppermute | solution.py:115
  36.1 14.7 %collective-permute-start.18 = (bf16[136,640]{1,0:T(8,128)(2,1)S(1)}, bf16[136,640]{1,0:T(8,128)(2,1)S(1)}, u32[]{:S(2)}, u32[]{:S(2)}) collective-permute-start(bf16[136,640]{1,0:T(8,128)(2,1)S(1)} %collective-permute-done.15.refs_3_), channel_id=1, source_target_pairs={{0,2},{2,0},{4,6},{6,4},{8,10},{10,8},{12,14},{14,12},{16,18},{18,... | collective-permute-start | bytes 522248 | tf_op jit(solution)/shard_map/ppermute | solution.py:115
  44.4 10.5 %collective-permute-start.9 = (bf16[128,640]{1,0:T(8,128)(2,1)}, bf16[128,640]{1,0:T(8,128)(2,1)S(1)}, u32[]{:S(2)}, u32[]{:S(2)}) collective-permute-start(bf16[128,640]{1,0:T(8,128)(2,1)} %collective-permute-done.7.refs_2_), channel_id=1, source_target_pairs={{0,2},{2,0},{4,6},{6,4},{8,10},{10,8},{12,14},{14,12},{16,18},{18,... | collective-permute-start | bytes 491528 | tf_op jit(solution)/shard_map/ppermute | solution.py:115
  44.9 10.0 %collective-permute-start.8 = (bf16[136,640]{1,0:T(8,128)(2,1)S(1)}, bf16[136,640]{1,0:T(8,128)(2,1)S(1)}, u32[]{:S(2)}, u32[]{:S(2)}) collective-permute-start(bf16[136,640]{1,0:T(8,128)(2,1)S(1)} %collective-permute-done.3.refs_1_), channel_id=1, source_target_pairs={{0,2},{2,0},{4,6},{6,4},{8,10},{10,8},{12,14},{14,12},{16,18},{18,... | collective-permute-start | bytes 522248 | tf_op jit(solution)/shard_map/ppermute | solution.py:115
  59.2 19.7 %collective-permute-start.30 = (bf16[128,640]{1,0:T(8,128)(2,1)S(1)}, bf16[128,640]{1,0:T(8,128)(2,1)S(1)}, u32[]{:S(2)}, u32[]{:S(2)}) collective-permute-start(bf16[128,640]{1,0:T(8,128)(2,1)S(1)} %get-tuple-element.32), channel_id=1, source_target_pairs={{0,1},{2,3},{4,5},{6,7},{8,9},{10,11},{12,13},{14,15},{16,17},{18,... | collective-permute-start | bytes 491528 | tf_op jit(solution)/shard_map/ppermute | solution.py:441
  62.8 19.8 %collective-permute-start.36 = (bf16[128,640]{1,0:T(8,128)(2,1)S(1)}, bf16[128,640]{1,0:T(8,128)(2,1)S(1)}, u32[]{:S(2)}, u32[]{:S(2)}) collective-permute-start(bf16[128,640]{1,0:T(8,128)(2,1)S(1)} %get-tuple-element.31), channel_id=1, source_target_pairs={{0,1},{2,3},{4,5},{6,7},{8,9},{10,11},{12,13},{14,15},{16,17},{18,... | collective-permute-start | bytes 491528 | tf_op jit(solution)/shard_map/ppermute | solution.py:441
  64.2 10.3 %collective-permute-start.31 = (bf16[3,256,2]{2,1,0:T(8,128)(2,1)S(1)}, bf16[3,256,2]{2,1,0:T(8,128)(2,1)S(1)}, u32[]{:S(2)}, u32[]{:S(2)}) collective-permute-start(bf16[3,256,2]{2,1,0:T(8,128)(2,1)S(1)} %slice.10), channel_id=1, source_target_pairs={{0,1},{2,3},{4,5},{6,7},{8,9},{10,11},{12,13},{14,15},{16,17},{18,... | collective-permute-start | bytes 9224 | tf_op jit(solution)/shard_map/ppermute | solution.py:441
  81.3 6.7 %collective-permute-start.32 = (bf16[128,640]{1,0:T(8,128)(2,1)S(1)}, bf16[128,640]{1,0:T(8,128)(2,1)S(1)}, u32[]{:S(2)}, u32[]{:S(2)}) collective-permute-start(bf16[128,640]{1,0:T(8,128)(2,1)S(1)} %far_part_1_0.1.refs_1_), channel_id=1, source_target_pairs={{0,8},{2,10},{8,16},{10,18},{16,24},{18,26},{24,28},{26,30},{28,20... | collective-permute-start | bytes 491528 | tf_op jit(solution)/shard_map/ppermute | solution.py:104
  84.1 7.1 %collective-permute-start.43 = (bf16[128,640]{1,0:T(8,128)(2,1)S(1)}, bf16[128,640]{1,0:T(8,128)(2,1)S(1)}, u32[]{:S(2)}, u32[]{:S(2)}) collective-permute-start(bf16[128,640]{1,0:T(8,128)(2,1)S(1)} %far_part_1_1.1.refs_2_), channel_id=1, source_target_pairs={{0,8},{2,10},{8,16},{10,18},{16,24},{18,26},{24,28},{26,30},{28,20... | collective-permute-start | bytes 491528 | tf_op jit(solution)/shard_map/ppermute | solution.py:107
  85.1 7.2 %collective-permute-start.37 = (bf16[128,640]{1,0:T(8,128)(2,1)S(1)}, bf16[128,640]{1,0:T(8,128)(2,1)S(1)}, u32[]{:S(2)}, u32[]{:S(2)}) collective-permute-start(bf16[128,640]{1,0:T(8,128)(2,1)S(1)} %far_part_1_1.1.refs_2_), channel_id=1, source_target_pairs={{8,0},{10,2},{16,8},{18,10},{24,16},{26,18},{28,24},{30,26},{20,28... | collective-permute-start | bytes 491528 | tf_op jit(solution)/shard_map/ppermute | solution.py:105
  88.0 6.9 %collective-permute-start.47 = (bf16[128,640]{1,0:T(8,128)(2,1)S(1)}, bf16[128,640]{1,0:T(8,128)(2,1)S(1)}, u32[]{:S(2)}, u32[]{:S(2)}) collective-permute-start(bf16[128,640]{1,0:T(8,128)(2,1)S(1)} %collective-permute-done.46.refs_5_), channel_id=1, source_target_pairs={{8,0},{10,2},{16,8},{18,10},{24,16},{26,18},{28,24},{30,26},{20,28... | collective-permute-start | bytes 491528 | tf_op jit(solution)/shard_map/ppermute | solution.py:108
  91.1 7.1 %collective-permute-start.33 = (bf16[128,640]{1,0:T(8,128)(2,1)S(1)}, bf16[128,640]{1,0:T(8,128)(2,1)S(1)}, u32[]{:S(2)}, u32[]{:S(2)}) collective-permute-start(bf16[128,640]{1,0:T(8,128)(2,1)S(1)} %collective-permute-done.32.refs_3_), channel_id=1, source_target_pairs={{0,8},{2,10},{8,16},{10,18},{16,24},{18,26},{24,28},{26,30},{28,20... | collective-permute-start | bytes 491528 | tf_op jit(solution)/shard_map/ppermute | solution.py:104
  92.4 8.1 %collective-permute-start.44 = (bf16[128,640]{1,0:T(8,128)(2,1)S(1)}, bf16[128,640]{1,0:T(8,128)(2,1)S(1)}, u32[]{:S(2)}, u32[]{:S(2)}) collective-permute-start(bf16[128,640]{1,0:T(8,128)(2,1)S(1)} %collective-permute-done.43.refs_4_), channel_id=1, source_target_pairs={{0,8},{2,10},{8,16},{10,18},{16,24},{18,26},{24,28},{26,30},{28,20... | collective-permute-start | bytes 491528 | tf_op jit(solution)/shard_map/ppermute | solution.py:107
  94.9 6.7 %collective-permute-start.38 = (bf16[128,640]{1,0:T(8,128)(2,1)S(1)}, bf16[128,640]{1,0:T(8,128)(2,1)S(1)}, u32[]{:S(2)}, u32[]{:S(2)}) collective-permute-start(bf16[128,640]{1,0:T(8,128)(2,1)S(1)} %collective-permute-done.37.refs_6_), channel_id=1, source_target_pairs={{8,0},{10,2},{16,8},{18,10},{24,16},{26,18},{28,24},{30,26},{20,28... | collective-permute-start | bytes 491528 | tf_op jit(solution)/shard_map/ppermute | solution.py:105
  98.2 6.8 %collective-permute-start.48 = (bf16[128,640]{1,0:T(8,128)(2,1)S(1)}, bf16[128,640]{1,0:T(8,128)(2,1)S(1)}, u32[]{:S(2)}, u32[]{:S(2)}) collective-permute-start(bf16[128,640]{1,0:T(8,128)(2,1)S(1)} %collective-permute-done.47.refs_3_), channel_id=1, source_target_pairs={{8,0},{10,2},{16,8},{18,10},{24,16},{26,18},{28,24},{30,26},{20,28... | collective-permute-start | bytes 491528 | tf_op jit(solution)/shard_map/ppermute | solution.py:108
  100.5 6.6 %collective-permute-start.34 = (bf16[128,640]{1,0:T(8,128)(2,1)S(1)}, bf16[128,640]{1,0:T(8,128)(2,1)S(1)}, u32[]{:S(2)}, u32[]{:S(2)}) collective-permute-start(bf16[128,640]{1,0:T(8,128)(2,1)S(1)} %collective-permute-done.33.refs_1_), channel_id=1, source_target_pairs={{0,8},{2,10},{8,16},{10,18},{16,24},{18,26},{24,28},{26,30},{28,20... | collective-permute-start | bytes 491528 | tf_op jit(solution)/shard_map/ppermute | solution.py:104
  101.7 7.4 %collective-permute-start.39 = (bf16[128,640]{1,0:T(8,128)(2,1)S(1)}, bf16[128,640]{1,0:T(8,128)(2,1)S(1)}, u32[]{:S(2)}, u32[]{:S(2)}) collective-permute-start(bf16[128,640]{1,0:T(8,128)(2,1)S(1)} %collective-permute-done.38.refs_4_), channel_id=1, source_target_pairs={{8,0},{10,2},{16,8},{18,10},{24,16},{26,18},{28,24},{30,26},{20,28... | collective-permute-start | bytes 491528 | tf_op jit(solution)/shard_map/ppermute | solution.py:105
  107.3 7.2 %collective-permute-start.35 = (bf16[128,640]{1,0:T(8,128)(2,1)S(1)}, bf16[128,640]{1,0:T(8,128)(2,1)S(1)}, u32[]{:S(2)}, u32[]{:S(2)}) collective-permute-start(bf16[128,640]{1,0:T(8,128)(2,1)S(1)} %collective-permute-done.34.refs_1_), channel_id=1, source_target_pairs={{0,8},{2,10},{8,16},{10,18},{16,24},{18,26},{24,28},{26,30},{28,20... | collective-permute-start | bytes 491528 | tf_op jit(solution)/shard_map/ppermute | solution.py:104
  (46 other events, 247.5 us)

commit v2 on v0

v2 whole, which is shorter than its diff:
```python
import math

import jax
import jax.numpy as jnp
import numpy as np
from jax import lax
from jax.experimental import pallas as pl
from jax.experimental.pallas import tpu as pltpu
from jax.sharding import PartitionSpec as P

epsilon = 1e-05
block_len = 128
side_rows = 8
bf16 = jnp.bfloat16
f32 = jnp.float32
in_vmem = pl.BlockSpec(memory_space=pltpu.VMEM)
in_smem = pl.BlockSpec(memory_space=pltpu.SMEM)
params = pltpu.CompilerParams(vmem_limit_bytes=20 * 2**20)


def shape_of(shape, dtype):
    return jax.ShapeDtypeStruct(tuple(shape), dtype)


def dot(left, right):
    return jnp.dot(left, right, preferred_element_type=f32)


def column(row):
    return jnp.broadcast_to(row, (8, row.shape[1])).T[:, :1]


def tap_columns(taps):
    return jnp.concatenate([taps, jnp.zeros((8 - taps.shape[0], taps.shape[1]), f32)], axis=0).T


def estimate(flops, size):
    return pl.CostEstimate(flops=int(flops), bytes_accessed=int(size), transcendentals=0)


def prepare_kernel(x_ref, gain_ref, out_ref):
    rows = x_ref.shape[0]
    wide = x_ref[...].astype(f32)
    out_ref[:rows] = (wide * column(gain_ref[...])).astype(bf16)
    squares = jnp.sum(wide * wide, axis=0, keepdims=True)
    high = squares.astype(bf16).astype(f32)
    row = lax.broadcasted_iota(jnp.int32, (side_rows, wide.shape[1]), 0)
    side = jnp.where(row == 0, high, jnp.where(row == 1, squares - high, 0.0))
    out_ref[rows:] = side.astype(bf16)


def prepare(x, gain):
    rows, tokens = x.shape
    return pl.pallas_call(
        prepare_kernel,
        in_specs=[in_vmem, in_vmem],
        out_specs=in_vmem,
        out_shape=shape_of((rows + side_rows, tokens), bf16),
        compiler_params=params,
        name="prepare",
    )(x, gain.reshape(1, rows))


def chip_count():
    return lax.axis_size("fsdp") // 2


def ring_order(count):
    return list(range(0, count, 2)) + list(range(1, count, 2))[::-1]


def along_ring(block):
    chips = chip_count()
    order = ring_order(chips)
    pairs = []
    for i in range(chips):
        here, after = order[i], order[(i + 1) % chips]
        pairs += [(2 * here, 2 * after), (2 * after + 1, 2 * here + 1)]
    return lax.ppermute(block, "fsdp", pairs)


def other_core(block):
    return lax.ppermute(block, "fsdp", [(i, i ^ 1) for i in range(2 * chip_count())])


def ring_ids():
    chips = chip_count()
    me = lax.axis_index("fsdp")
    chip, core = me // 2, me % 2
    place = jnp.where(chip % 2 == 0, chip // 2, chips - 1 - chip // 2)
    steps = jnp.arange(chips, dtype=jnp.int32)
    places = (place + jnp.where(core == 0, chips - steps, steps)) % chips
    ids = jnp.where(places < (chips + 1) // 2, 2 * places, 2 * (chips - 1 - places) + 1)
    return jnp.concatenate([ids, core[None]]).astype(jnp.int32)


def gather_in_order(ids_ref, slots, shards, ordered):
    core = ids_ref[ids_ref.shape[0] - 1]
    rows = ordered.shape[0] // (2 * len(slots))
    for k in range(len(slots)):
        for index in range(2):
            place = core if index == 0 else 1 - core
            at = pl.multiple_of((2 * k + place) * rows, rows)
            ordered[pl.ds(at, rows)] = shards[2 * k + index][:rows]


def products(ids, slots, shards, weight, running, side, finish=None, name="sum"):
    streams, out_rows, features = weight.shape
    rows = features // (2 * (ids.shape[0] - 1))
    tokens = shards[0].shape[1]
    count = len(shards)
    first_group = running is None
    state = [] if first_group else list(running)
    body, extras, out_shape = finish if finish else (None, [], None)
    assembled = rows % 128 != 0
    width = 2 * rows if assembled else rows
    scratch_shapes = [pltpu.VMEM((count * rows, tokens), bf16)] if assembled else []

    def kernel(ids_ref, *refs):
        refs = list(refs)
        take = lambda n: [refs.pop(0) for _ in range(n)]
        shard_refs = take(count)
        (weight_ref,) = take(1)
        state_refs = take(len(state))
        extra_refs = take(len(extras))
        outs = take(len(out_shape))
        core = ids_ref[ids_ref.shape[0] - 1]
        if assembled:
            gather_in_order(ids_ref, slots, shard_refs, refs[0])
            right = refs[0][...]
        else:
            right = jnp.concatenate([ref[:rows] for ref in shard_refs], axis=0)
        side_sum = None
        if side:
            parts = [ref[rows:].astype(f32) for ref in shard_refs]
            parts += [] if first_group else [state_refs[1][...]]
            side_sum = sum(parts[1:], parts[0])

        def total(stream):
            left = []
            for k in range(count * rows // width):
                if assembled:
                    block = ids_ref[slots[k]]
                else:
                    block = 2 * ids_ref[slots[k // 2]] + (core if k % 2 == 0 else 1 - core)
                at = pl.ds(pl.multiple_of(block * width, width), width)
                left.append(weight_ref[stream, :, at])
            product = dot(jnp.concatenate(left, axis=1), right)
            return product if first_group else state_refs[0][stream] + product

        if body is not None:
            body(total, side_sum, extra_refs, outs)
            return
        for stream in range(streams):
            outs[0][stream] = total(stream)
        if side:
            outs[1][...] = side_sum

    aliases = {}
    if body is None:
        out_shape = [shape_of((streams, out_rows, tokens), f32)]
        if side:
            out_shape.append(shape_of((side_rows, tokens), f32))
        if not first_group:
            aliases = {1 + count + 1 + i: i for i in range(len(state))}
    return pl.pallas_call(
        kernel,
        in_specs=[in_smem] + [in_vmem] * (count + 1 + len(state) + len(extras)),
        out_specs=[in_vmem] * len(out_shape),
        out_shape=out_shape,
        scratch_shapes=scratch_shapes,
        input_output_aliases=aliases,
        compiler_params=params,
        cost_estimate=estimate(
            2 * streams * out_rows * tokens * rows * count, 2 * streams * out_rows * rows * count
        ),
        name=name,
    )(ids, *shards, weight, *state, *extras)


def gather_products(ids, own, weight, side, finish, name):
    chips = chip_count()
    last_step = chips // 2
    sibling = other_core(own)
    near, far = own, sibling
    running = None
    slots, group = [0], [own, sibling]
    for step in range(1, last_step + 1):
        near = along_ring(near)
        if step < last_step:
            if running is not None:
                far, *running = lax.optimization_barrier((far, *running))
            far = along_ring(far)
        if step > 1:
            running = products(ids, slots, group, weight, running, side, None, f"{name}_{step - 1}")
            slots, group = [], []
        if step < last_step:
            slots = slots + [step, chips - step]
            group = group + [near, far, other_core(far), other_core(near)]
        else:
            slots, group = [step], [near, other_core(near)]
    return products(ids, slots, group, weight, running, side, finish, f"{name}_{last_step}")


def smooth(projected, taps, count, halo):
    lane = lax.broadcasted_iota(jnp.int32, projected.shape, 1)
    out = taps[:, :1] * projected
    for tap in range(1, count):
        moved = pltpu.roll(projected, tap, 1)
        for place in range(tap):
            edge = 0.0
            if halo is not None:
                at = halo.shape[1] - tap + place
                edge = halo[:, at : at + 1]
            moved = jnp.where(lane == place, edge, moved)
        out = out + taps[:, tap : tap + 1] * moved
    return out


def projection_finish(features, w_short, tokens):
    streams, count, channels = w_short.shape

    def body(total, side_sum, extra_refs, outs):
        (taps_ref,) = extra_refs
        projected_ref, gated_ref, halo_ref = outs
        mean = jnp.sum(side_sum, axis=0, keepdims=True) * (1.0 / features)
        factor = lax.rsqrt(mean + epsilon)

        for stream in range(streams):
            projected = (total(stream) * factor).astype(bf16)
            projected_ref[stream] = projected
            tail = projected[:, tokens - block_len :].astype(f32).T
            halo_ref[stream] = tail[block_len - 8 :]

        taps = [tap_columns(taps_ref[stream]) for stream in (1, 2)]
        tile = min(channels, 64)
        for start in range(0, channels, tile):
            rows = slice(start, start + tile)
            key, value = (
                smooth(projected_ref[s, rows].astype(f32), taps[s - 1][rows], count, None)
                for s in (1, 2)
            )
            gated_ref[rows] = (key * value).astype(bf16)

    out_shape = [
        shape_of((streams, channels, tokens), bf16),
        shape_of((channels, tokens), bf16),
        shape_of((streams, 8, channels), f32),
    ]
    return body, [w_short], out_shape


def split_table(table):
    high = table.astype(bf16)
    low = (table - high.astype(np.float64)).astype(bf16)
    return np.stack([high, low])


def dft_tables():
    size = 2 * block_len
    freq = np.arange(block_len) + 0.5
    angle = 2.0 * math.pi / size * np.arange(size)[:, None] * freq[None, :]
    forward = np.concatenate([np.cos(angle), -np.sin(angle)], axis=1)
    back = angle[block_len:].T
    inverse = np.concatenate([np.cos(back), -np.sin(back)], axis=0) * (2.0 / size)
    return split_table(forward), split_table(inverse)


def spectrum_lanes(k):
    return slice(2 * k * block_len, 2 * (k + 1) * block_len)


def block_lanes(k):
    return slice(k * block_len, (k + 1) * block_len)


def spectra_kernel(filter_ref, table_ref, out_ref):
    blocks = filter_ref.shape[1] // block_len
    before = jnp.zeros((filter_ref.shape[0], block_len), bf16)
    for k in range(blocks):
        now = filter_ref[:, block_lanes(k)]
        segment = jnp.concatenate([before, now], axis=1)
        out_ref[:, spectrum_lanes(k)] = dot(segment, table_ref[0]) + dot(segment, table_ref[1])
        before = now


def filter_spectra(long_filter, table):
    channels, lags = long_filter.shape
    return pl.pallas_call(
        spectra_kernel,
        in_specs=[in_vmem, in_vmem],
        out_specs=in_vmem,
        out_shape=shape_of((channels, 2 * lags), f32),
        compiler_params=params,
        cost_estimate=estimate(8 * channels * lags * 2 * block_len, 10 * channels * lags),
        name="filter_spectra",
    )(long_filter, table)


def block_spectra(gated_ref, table_ref, spec_ref):
    for b in range(gated_ref.shape[1] // block_len):
        piece = gated_ref[:, block_lanes(b)]
        spec_ref[:, spectrum_lanes(b)] = dot(piece, table_ref[0, :block_len]) + dot(
            piece, table_ref[1, :block_len]
        )


def multiply_spectra(source_ref, filters_ref, filter_start, pairs, before_ref, total_ref):
    def one_tile(i, carry):
        here = pl.ds(pl.multiple_of(i * 8, 8), 8)
        there = pl.ds(pl.multiple_of(filter_start + i * 8, 8), 8)

        def part(ref, rows, k, imaginary):
            start = (2 * k + imaginary) * block_len
            return ref[rows, start : start + block_len]

        for a, terms in enumerate(pairs):
            real = imag = None
            if before_ref is not None:
                real, imag = part(before_ref, here, a, 0), part(before_ref, here, a, 1)
            for b, d in terms:
                gr, gi = part(source_ref, here, b, 0), part(source_ref, here, b, 1)
                hr, hi = part(filters_ref, there, d, 0), part(filters_ref, there, d, 1)
                more_real, more_imag = gr * hr - gi * hi, gr * hi + gi * hr
                real = more_real if real is None else real + more_real
                imag = more_imag if imag is None else imag + more_imag
            start = 2 * a * block_len
            total_ref[here, start : start + block_len] = real
            total_ref[here, start + block_len : start + 2 * block_len] = imag
        return carry

    lax.fori_loop(0, total_ref.shape[0] // 8, one_tile, 0)


def own_kernel(projected_ref, halo_ref, taps_ref, filters_ref, table_ref, *refs):
    query_ref, gated_ref, first_ref, second_ref, spec_ref, total_ref = refs
    channels, tokens = gated_ref.shape
    half = channels // 2
    count = taps_ref.shape[1]
    halo = [halo_ref[s].T for s in range(3)]
    taps = [tap_columns(taps_ref[s]) for s in range(3)]
    tile = min(channels, 64)
    for start in range(0, channels, tile):
        rows = slice(start, start + tile)
        query, key, value = (
            smooth(projected_ref[s, rows].astype(f32), taps[s][rows], count, halo[s][rows])
            for s in range(3)
        )
        query_ref[rows] = query
        gated_ref[rows] = (key * value).astype(bf16)
    block_spectra(gated_ref, table_ref, spec_ref)
    blocks = tokens // block_len
    pairs = [[(b, a - b) for b in range(a + 1)] for a in range(blocks)]
    multiply_spectra(spec_ref, filters_ref, 0, pairs, None, total_ref)
    first_ref[...] = total_ref[:half]
    second_ref[...] = total_ref[half:]


def own_part(projected, halo, taps, filters, table):
    _, channels, tokens = projected.shape
    return pl.pallas_call(
        own_kernel,
        in_specs=[in_vmem] * 5,
        out_specs=[in_vmem] * 4,
        out_shape=[
            shape_of((channels, tokens), f32),
            shape_of((channels, tokens), bf16),
            shape_of((channels // 2, 2 * tokens), f32),
            shape_of((channels // 2, 2 * tokens), f32),
        ],
        scratch_shapes=[pltpu.VMEM((channels, 2 * tokens), f32)] * 2,
        compiler_params=params,
        cost_estimate=estimate(6 * 10**8, 6 * 10**6),
        name="own_part",
    )(projected, halo, taps, filters, table)


def far_part(turn, part, moved, total, filters, table, last):
    rows, tokens = moved.shape
    blocks = tokens // block_len
    pairs = [[(b, turn * blocks + a - b) for b in range(blocks)] for a in range(blocks)]

    def kernel(moved_ref, total_ref, filters_ref, table_ref, *refs):
        *refs, spec_ref = refs
        block_spectra(moved_ref, table_ref, spec_ref)
        if last is None:
            multiply_spectra(spec_ref, filters_ref, part * rows, pairs, total_ref, refs[0])
            return
        *refs, sum_ref = refs
        back_ref, query_ref, gated_ref, skip_ref = refs[:4]
        out_ref = refs[-1]
        multiply_spectra(spec_ref, filters_ref, part * rows, pairs, total_ref, sum_ref)
        here = slice(part * rows, (part + 1) * rows)
        skip = column(skip_ref[...])[here]
        for a in range(blocks):
            lanes = block_lanes(a)
            spectrum = sum_ref[:, spectrum_lanes(a)]
            high = spectrum.astype(bf16)
            low = (spectrum - high.astype(f32)).astype(bf16)
            filtered = dot(high, back_ref[0]) + (dot(low, back_ref[0]) + dot(high, back_ref[1]))
            gated = gated_ref[here, lanes].astype(f32)
            out_ref[here, lanes] = (query_ref[here, lanes] * (filtered + skip * gated)).astype(bf16)

    args = [moved, total, filters, table]
    aliases = {}
    scratch = [pltpu.VMEM((rows, 2 * tokens), f32)]
    out_shape = shape_of((rows, 2 * tokens), f32)
    if last is not None:
        inverse, query, gated, skip, mixed = last
        args += [inverse, query, gated, skip.reshape(1, 2 * rows)]
        if mixed is not None:
            aliases = {len(args): 0}
            args.append(mixed)
        out_shape = shape_of((2 * rows, tokens), bf16)
        scratch.append(pltpu.VMEM((rows, 2 * tokens), f32))
    return pl.pallas_call(
        kernel,
        in_specs=[in_vmem] * len(args),
        out_specs=in_vmem,
        out_shape=out_shape,
        scratch_shapes=scratch[::-1],
        input_output_aliases=aliases,
        compiler_params=params,
        cost_estimate=estimate(4 * 10**8, 4 * 10**6),
        name=f"far_part_{turn}_{part}",
    )(*args)


def from_before(block):
    count = lax.axis_size("ctx")
    return lax.ppermute(block, "ctx", [(i - 1, i) for i in range(1, count)])


def output_finish(channels, tokens):
    def body(total, side_sum, extra_refs, outs):
        outs[0][...] = total(0).astype(bf16)

    return body, [], [shape_of((channels, tokens), bf16)]


def shards(activations, norm_gain, w_in, w_short, long_filter, skip_gain, w_out):
    channels, tokens = activations.shape
    features = w_in.shape[2]
    w_short = w_short.transpose(0, 2, 1)
    turns = lax.axis_size("ctx")
    half = channels // 2
    forward, inverse = (jnp.asarray(t) for t in dft_tables())
    ids = ring_ids()
    own = prepare(activations, norm_gain)
    filters = filter_spectra(long_filter, forward)

    finish = projection_finish(features, w_short, tokens)
    projected, gated_alone, tail = gather_products(ids, own, w_in, True, finish, "projection")

    halo = from_before(tail)
    moving = None
    if turns == 2:
        moving = [from_before(gated_alone[:half]), from_before(gated_alone[half:])]
    query, gated, *totals = own_part(projected, halo, w_short, filters, forward)
    if moving is None:
        moving = [from_before(gated[:half]), from_before(gated[half:])]
    mixed = None
    for turn in range(1, turns):
        for part in range(2):
            if turn < turns - 1:
                totals[part] = far_part(
                    turn, part, moving[part], totals[part], filters, forward, None
                )
                moving[part] = from_before(moving[part])
            else:
                last = (inverse, query, gated, skip_gain, mixed)
                mixed = far_part(turn, part, moving[part], totals[part], filters, forward, last)

    (result,) = gather_products(
        ids, mixed, w_out[None], False, output_finish(channels, tokens), "output"
    )
    return result


def solution(mesh):
    placed = (
        P("fsdp", "ctx"),
        P("fsdp"),
        P(None, "fsdp", None),
        P(None, "fsdp", None),
        P("fsdp", None),
        P("fsdp"),
        P("fsdp", None),
    )
    return jax.shard_map(
        shards, mesh=mesh, in_specs=placed, out_specs=P("fsdp", "ctx"), check_vma=False
    )
```

time: 285 us -> 92.3 us (0.32)
  waiting for transfers between devices: 123 us -> 33.8 us
  other arithmetic: 57.3 us -> 0.09 us
  matrix products: 31.5 us -> 0 us
  starting transfers between devices: 5.59 us -> 32.4 us
  local copies, waits for them, and re-layouts: 29.9 us -> 4.51 us
  blocking collectives: 23.1 us -> 0 us
  Pallas kernels: 0 us -> 20.8 us
  between operations: 13.6 us -> 0.32 us
    all_gather x2 -> x0, waiting for transfers between devices: 122 us -> none  [the longest x1 103 us: shards(): lax.all_gather(mixed, 'fsdp', axis=0, tiled=True)]
    ppermute x2 -> x33, waiting for transfers between devices: 0.01 us -> 33.8 us  [the longest x14 29.1 us: along_ring(): return lax.ppermute(block, 'fsdp', pairs)]
    dot_general x6 -> x0, matrix products: 31.5 us -> none  [the longest x1 7.9 us: shards(): jnp.einsum('sci,it->sct', w_in, normed, preferred_element_type=jnp.float32)]
    ppermute x2 -> x33, starting transfers between devices: 5.54 us -> 32.4 us  [the longest x14 24.8 us: along_ring(): return lax.ppermute(block, 'fsdp', pairs)]
    add x7 -> x0, other arithmetic: 25.3 us -> none  [the longest x5 24.8 us: apply_block(): return inner + complex_product(chosen, spectrum[:, None, :])]
    all_gather x1 -> x0, blocking collectives: 23.1 us -> none  [shards(): lax.all_gather(norm_gain.astype(jnp.bfloat16), 'fsdp', axis=0, tiled=True)]
    sub x5 -> x0, other arithmetic: 21.7 us -> none  [complex_product(): left_re * right_re - left_im * right_im]
    pallas_call x0 -> x13, Pallas kernels: none -> 20.8 us  [the longest x8 14 us: products(): pl.pallas_call(kernel, in_specs=[in_smem] + [in_vmem] * (count + 1 + len(...]
  transfers between devices with their start and end apart: 4 -> 33, of which waited for: 2 -> 13; matrix products, arithmetic and copies ran while one was open for 30% -> 0% of each run, Pallas kernels for 0% -> 17%
where the time goes in v2:
time: 92.3 us; the launch traced here: 91.9 us
  waiting for transfers between devices  33.8 us (37%)
  starting transfers between devices  32.4 us (35%)
  Pallas kernels  20.8 us (23%)
  local copies, waits for them, and re-layouts  4.51 us (5%)
    ppermute x14, waiting for transfers between devices, along_ring(): return lax.ppermute(block, 'fsdp', pairs)  29.1 us
    ppermute x14, starting transfers between devices, along_ring(): return lax.ppermute(block, 'fsdp', pairs)  24.8 us
    pallas_call x8, Pallas kernels, products(): pl.pallas_call(kernel, in_specs=[in_smem] + [in_vmem] * (count + 1 + len(...  14 us
    ppermute x3, starting transfers between devices, from_before(): return lax.ppermute(block, 'ctx', [(i - 1, i) for i in range(1, count)])  6 us
    ppermute x3, waiting for transfers between devices, from_before(): return lax.ppermute(block, 'ctx', [(i - 1, i) for i in range(1, count)])  4.66 us
    unnamed x20, local copies, waits for them, and re-layouts  4.48 us
    pallas_call x1, Pallas kernels, own_part(): pl.pallas_call(own_kernel, in_specs=[in_vmem] * 5, out_specs=[in_vmem] *...  2.95 us
    pallas_call x2, Pallas kernels, far_part(): pl.pallas_call(kernel, in_specs=[in_vmem] * len(args), out_specs=in_vmem,...  2.74 us
  transfers between devices with their start and end apart: 33, of which 13 were waited for; matrix products, arithmetic and copies ran while one was open for 0% of the time, Pallas kernels for 17%

profile of v2, /device:TPU:0, one launch (start us, length us, event | category | flops | bytes accessed | tf_op | source)
XLA Modules:
  0.0 91.9 jit_solution(3551055692215979483)
XLA Ops:
  2.4 2.6 %collective-permute-start = (bf16[264,640]{1,0:T(8,128)(2,1)S(1)}, bf16[264,640]{1,0:T(8,128)(2,1)S(1)}, u32[]{:S(2)}, u32[]{:S(2)}) collective-permute-start(bf16[264,640]{1,0:T(8,128)(2,1)S(1)} %prepare.1.refs_0_), channel_id=1, source_target_pairs={{0,8},{10,2},{8,16},{18,10},{16,24},{26,18},{24,28},{30,26},{28,20... | collective-permute-start | bytes 1013768 | tf_op jit(solution)/shard_map/ppermute | solution.py:79
  5.1 1.6 %collective-permute-start.6 = (bf16[264,640]{1,0:T(8,128)(2,1)S(1)}, bf16[264,640]{1,0:T(8,128)(2,1)S(1)}, u32[]{:S(2)}, u32[]{:S(2)}) collective-permute-start(bf16[264,640]{1,0:T(8,128)(2,1)S(1)} %collective-permute-done.5.refs_1_), channel_id=1, source_target_pairs={{0,8},{10,2},{8,16},{18,10},{16,24},{26,18},{24,28},{30,26},{28,20... | collective-permute-start | bytes 1013768 | tf_op jit(solution)/shard_map/ppermute | solution.py:79
  6.6 3.5 %collective-permute-done.refs_2_ = bf16[264,640]{1,0:T(8,128)(2,1)S(1)} collective-permute-done((bf16[264,640]{1,0:T(8,128)(2,1)S(1)}, bf16[264,640]{1,0:T(8,128)(2,1)S(1)}, u32[]{:S(2)}, u32[]{:S(2)}) %collective-permute-start) | collective-permute-done | bytes 337952 | tf_op jit(solution)/shard_map/ppermute | solution.py:79
  10.2 2.1 %collective-permute-start.1 = (bf16[264,640]{1,0:T(8,128)(2,1)S(1)}, bf16[264,640]{1,0:T(8,128)(2,1)S(1)}, u32[]{:S(2)}, u32[]{:S(2)}) collective-permute-start(bf16[264,640]{1,0:T(8,128)(2,1)S(1)} %collective-permute-done.refs_2_), channel_id=1, source_target_pairs={{0,8},{10,2},{8,16},{18,10},{16,24},{26,18},{24,28},{30,26},{28,20... | collective-permute-start | bytes 1013768 | tf_op jit(solution)/shard_map/ppermute | solution.py:79
  12.3 1.5 %collective-permute-done.6.refs_3_ = bf16[264,640]{1,0:T(8,128)(2,1)S(1)} collective-permute-done((bf16[264,640]{1,0:T(8,128)(2,1)S(1)}, bf16[264,640]{1,0:T(8,128)(2,1)S(1)}, u32[]{:S(2)}, u32[]{:S(2)}) %collective-permute-start.6) | collective-permute-done | bytes 337952 | tf_op jit(solution)/shard_map/ppermute | solution.py:79
  13.8 2.1 %collective-permute-start.7 = (bf16[264,640]{1,0:T(8,128)(2,1)S(1)}, bf16[264,640]{1,0:T(8,128)(2,1)S(1)}, u32[]{:S(2)}, u32[]{:S(2)}) collective-permute-start(bf16[264,640]{1,0:T(8,128)(2,1)S(1)} %collective-permute-done.6.refs_3_), channel_id=1, source_target_pairs={{0,8},{10,2},{8,16},{18,10},{16,24},{26,18},{24,28},{30,26},{28,20... | collective-permute-start | bytes 1013768 | tf_op jit(solution)/shard_map/ppermute | solution.py:79
  17.4 2.1 %collective-permute-start.2 = (bf16[264,640]{1,0:T(8,128)(2,1)S(1)}, bf16[264,640]{1,0:T(8,128)(2,1)S(1)}, u32[]{:S(2)}, u32[]{:S(2)}) collective-permute-start(bf16[264,640]{1,0:T(8,128)(2,1)S(1)} %collective-permute-done.1.refs_0_), channel_id=1, source_target_pairs={{0,8},{10,2},{8,16},{18,10},{16,24},{26,18},{24,28},{30,26},{28,20... | collective-permute-start | bytes 1013768 | tf_op jit(solution)/shard_map/ppermute | solution.py:79
  19.6 2.8 %copy-done = bf16[3,256,4096]{2,1,0:T(8,128)(2,1)S(1)} copy-done((bf16[3,256,4096]{2,1,0:T(8,128)(2,1)S(1)}, bf16[3,256,4096]{2,1,0:T(8,128)(2,1)}, u32[]{:S(2)}) %copy-start) | copy-done | bytes 6291480
  22.4 2.6 %projection_1.1 = (f32[3,256,640]{2,1,0:T(8,128)S(1)}, f32[8,640]{1,0:T(8,128)S(1)}) custom-call(s32[9]{0:T(128)S(1)} %pad_add_fusion.ids_ref, bf16[264,640]{1,0:T(8,128)(2,1)S(1)} %prepare.1.refs_0_, bf16[264,640]{1,0:T(8,128)(2,1)S(1)} %collective-permute-done.5.refs_1_, bf16[264,640]{1,0:T(8,128)(2,1)S(1)} %collective-permute-done.refs_2_, ...), custom_call_target="tpu_custom_call" | custom-call | flops 1509949440 | bytes 2359296 | tf_op jit(solution)/shard_map/projection_1/pallas_call | solution.py:166
  25.0 1.6 %collective-permute-start.10 = (bf16[264,640]{1,0:T(8,128)(2,1)S(1)}, bf16[264,640]{1,0:T(8,128)(2,1)S(1)}, u32[]{:S(2)}, u32[]{:S(2)}) collective-permute-start(bf16[264,640]{1,0:T(8,128)(2,1)S(1)} %collective-permute-done.7.refs_1_), channel_id=1, source_target_pairs={{0,8},{10,2},{8,16},{18,10},{16,24},{26,18},{24,28},{30,26},{28,20... | collective-permute-start | bytes 1013768 | tf_op jit(solution)/shard_map/ppermute | solution.py:79
  26.6 1.6 %collective-permute-start.3 = (bf16[264,640]{1,0:T(8,128)(2,1)S(1)}, bf16[264,640]{1,0:T(8,128)(2,1)S(1)}, u32[]{:S(2)}, u32[]{:S(2)}) collective-permute-start(bf16[264,640]{1,0:T(8,128)(2,1)S(1)} %collective-permute-done.2.refs_0_), channel_id=1, source_target_pairs={{0,8},{10,2},{8,16},{18,10},{16,24},{26,18},{24,28},{30,26},{28,20... | collective-permute-start | bytes 1013768 | tf_op jit(solution)/shard_map/ppermute | solution.py:79
  28.7 3.5 %collective-permute-done.10.refs_1_ = bf16[264,640]{1,0:T(8,128)(2,1)S(1)} collective-permute-done((bf16[264,640]{1,0:T(8,128)(2,1)S(1)}, bf16[264,640]{1,0:T(8,128)(2,1)S(1)}, u32[]{:S(2)}, u32[]{:S(2)}) %collective-permute-start.10) | collective-permute-done | bytes 337952 | tf_op jit(solution)/shard_map/ppermute | solution.py:79
  32.2 3.6 %collective-permute-done.3.refs_0_ = bf16[264,640]{1,0:T(8,128)(2,1)S(1)} collective-permute-done((bf16[264,640]{1,0:T(8,128)(2,1)S(1)}, bf16[264,640]{1,0:T(8,128)(2,1)S(1)}, u32[]{:S(2)}, u32[]{:S(2)}) %collective-permute-start.3) | collective-permute-done | bytes 337952 | tf_op jit(solution)/shard_map/ppermute | solution.py:79
  35.8 2.1 %projection_2.1 = (f32[3,256,640]{2,1,0:T(8,128)S(1)}, f32[8,640]{1,0:T(8,128)S(1)}) custom-call(s32[9]{0:T(128)S(1)} %pad_add_fusion.ids_ref, bf16[264,640]{1,0:T(8,128)(2,1)S(1)} %collective-permute-done.1.refs_0_, bf16[264,640]{1,0:T(8,128)(2,1)S(1)} %collective-permute-done.7.refs_1_, ...), custom_call_target="tpu_custom_call", output_to_operand_aliasing={{0}: (6, {}), {1}: (7, {})} | custom-call | flops 1006632960 | bytes 1572864 | tf_op jit(solution)/shard_map/projection_2/pallas_call | solution.py:166
  38.0 2.1 %projection_3.1 = (f32[3,256,640]{2,1,0:T(8,128)S(1)}, f32[8,640]{1,0:T(8,128)S(1)}) custom-call(s32[9]{0:T(128)S(1)} %pad_add_fusion.ids_ref, bf16[264,640]{1,0:T(8,128)(2,1)S(1)} %collective-permute-done.2.refs_0_, bf16[264,640]{1,0:T(8,128)(2,1)S(1)} %collective-permute-done.10.refs_1_, ...), custom_call_target="tpu_custom_call", output_to_operand_aliasing={{0}: (6, {}), {1}: (7, {})} | custom-call | flops 1006632960 | bytes 1572864 | tf_op jit(solution)/shard_map/projection_3/pallas_call | solution.py:166
  40.1 1.9 %projection_4.1 = (bf16[3,256,640]{2,1,0:T(8,128)(2,1)S(1)}, bf16[256,640]{1,0:T(8,128)(2,1)S(1)}, f32[3,8,256]{2,1,0:T(8,128)S(1)}) custom-call(s32[9]{0:T(128)S(1)} %pad_add_fusion.ids_ref, bf16[264,640]{1,0:T(8,128)(2,1)S(1)} %collective-permute-done.3.refs_0_, bf16[264,640]{1,0:T(8,128)(2,1)S(1)} %collective-permute-done.4.refs_1_, ...), custom_call_target="tpu_custom_call" | custom-call | flops 503316480 | bytes 786432 | tf_op jit(solution)/shard_map/projection_4/pallas_call | solution.py:166
  42.1 3.4 %collective-permute-start.17 = (bf16[128,640]{1,0:T(8,128)(2,1)S(1)}, bf16[128,640]{1,0:T(8,128)(2,1)S(1)}, u32[]{:S(2)}, u32[]{:S(2)}) collective-permute-start(bf16[128,640]{1,0:T(8,128)(2,1)S(1)} %get-tuple-element.41), channel_id=1, source_target_pairs={{0,1},{2,3},{4,5},{6,7},{8,9},{10,11},{12,13},{14,15},{16,17},{18,... | collective-permute-start | bytes 491528 | tf_op jit(solution)/shard_map/ppermute | solution.py:431
  49.0 4.7 %collective-permute-done.16.halo_ref = f32[3,8,256]{2,1,0:T(8,128)S(1)} collective-permute-done((f32[3,8,256]{2,1,0:T(8,128)S(1)}, f32[3,8,256]{2,1,0:T(8,128)S(1)}, u32[]{:S(2)}, u32[]{:S(2)}) %collective-permute-start.16) | collective-permute-done | bytes 24608 | tf_op jit(solution)/shard_map/ppermute | solution.py:431
  53.7 2.9 %own_part.1 = (f32[256,640]{1,0:T(8,128)S(1)}, bf16[256,640]{1,0:T(8,128)(2,1)S(1)}, f32[128,1280]{1,0:T(8,128)S(1)}, f32[128,1280]{1,0:T(8,128)S(1)}) custom-call(bf16[3,256,640]{2,1,0:T(8,128)(2,1)S(1)} %get-tuple-element.33.projected_ref, f32[3,8,256]{2,1,0:T(8,128)S(1)} %collective-permute-done.16.halo_ref, f32[3,3,256]{2,1,0:T(4,128)S(1)} %bitcast.10, ...), custom_call_target="tpu_custom_call" | custom-call | flops 600000000 | bytes 6000000 | tf_op jit(solution)/shard_map/own_part/pallas_call | solution.py:361
  59.5 1.6 %collective-permute-start.18 = (bf16[256,640]{1,0:T(8,128)(2,1)S(1)}, bf16[256,640]{1,0:T(8,128)(2,1)S(1)}, u32[]{:S(2)}, u32[]{:S(2)}) collective-permute-start(bf16[256,640]{1,0:T(8,128)(2,1)S(1)} %far_part_1_1.1.refs_0_), channel_id=1, source_target_pairs={{0,8},{10,2},{8,16},{18,10},{16,24},{26,18},{24,28},{30,26},{28,20... | collective-permute-start | bytes 983048 | tf_op jit(solution)/shard_map/ppermute | solution.py:79
  61.2 1.6 %collective-permute-start.24 = (bf16[256,640]{1,0:T(8,128)(2,1)S(1)}, bf16[256,640]{1,0:T(8,128)(2,1)S(1)}, u32[]{:S(2)}, u32[]{:S(2)}) collective-permute-start(bf16[256,640]{1,0:T(8,128)(2,1)S(1)} %collective-permute-done.23.refs_1_), channel_id=1, source_target_pairs={{0,8},{10,2},{8,16},{18,10},{16,24},{26,18},{24,28},{30,26},{28,20... | collective-permute-start | bytes 983048 | tf_op jit(solution)/shard_map/ppermute | solution.py:79
  62.7 3.9 %collective-permute-done.18.refs_2_ = bf16[256,640]{1,0:T(8,128)(2,1)S(1)} collective-permute-done((bf16[256,640]{1,0:T(8,128)(2,1)S(1)}, bf16[256,640]{1,0:T(8,128)(2,1)S(1)}, u32[]{:S(2)}, u32[]{:S(2)}) %collective-permute-start.18) | collective-permute-done | bytes 327712 | tf_op jit(solution)/shard_map/ppermute | solution.py:79
  66.7 1.6 %collective-permute-start.19 = (bf16[256,640]{1,0:T(8,128)(2,1)S(1)}, bf16[256,640]{1,0:T(8,128)(2,1)S(1)}, u32[]{:S(2)}, u32[]{:S(2)}) collective-permute-start(bf16[256,640]{1,0:T(8,128)(2,1)S(1)} %collective-permute-done.18.refs_2_), channel_id=1, source_target_pairs={{0,8},{10,2},{8,16},{18,10},{16,24},{26,18},{24,28},{30,26},{28,20... | collective-permute-start | bytes 983048 | tf_op jit(solution)/shard_map/ppermute | solution.py:79
  68.2 1.9 %collective-permute-done.24.refs_3_ = bf16[256,640]{1,0:T(8,128)(2,1)S(1)} collective-permute-done((bf16[256,640]{1,0:T(8,128)(2,1)S(1)}, bf16[256,640]{1,0:T(8,128)(2,1)S(1)}, u32[]{:S(2)}, u32[]{:S(2)}) %collective-permute-start.24) | collective-permute-done | bytes 327712 | tf_op jit(solution)/shard_map/ppermute | solution.py:79
  70.2 1.6 %collective-permute-start.25 = (bf16[256,640]{1,0:T(8,128)(2,1)S(1)}, bf16[256,640]{1,0:T(8,128)(2,1)S(1)}, u32[]{:S(2)}, u32[]{:S(2)}) collective-permute-start(bf16[256,640]{1,0:T(8,128)(2,1)S(1)} %collective-permute-done.24.refs_3_), channel_id=1, source_target_pairs={{0,8},{10,2},{8,16},{18,10},{16,24},{26,18},{24,28},{30,26},{28,20... | collective-permute-start | bytes 983048 | tf_op jit(solution)/shard_map/ppermute | solution.py:79
  71.7 2.0 %collective-permute-done.19.refs_0_ = bf16[256,640]{1,0:T(8,128)(2,1)S(1)} collective-permute-done((bf16[256,640]{1,0:T(8,128)(2,1)S(1)}, bf16[256,640]{1,0:T(8,128)(2,1)S(1)}, u32[]{:S(2)}, u32[]{:S(2)}) %collective-permute-start.19) | collective-permute-done | bytes 327712 | tf_op jit(solution)/shard_map/ppermute | solution.py:79
  73.7 1.6 %collective-permute-start.20 = (bf16[256,640]{1,0:T(8,128)(2,1)S(1)}, bf16[256,640]{1,0:T(8,128)(2,1)S(1)}, u32[]{:S(2)}, u32[]{:S(2)}) collective-permute-start(bf16[256,640]{1,0:T(8,128)(2,1)S(1)} %collective-permute-done.19.refs_0_), channel_id=1, source_target_pairs={{0,8},{10,2},{8,16},{18,10},{16,24},{26,18},{24,28},{30,26},{28,20... | collective-permute-start | bytes 983048 | tf_op jit(solution)/shard_map/ppermute | solution.py:79
  77.2 1.6 %collective-permute-start.28 = (bf16[256,640]{1,0:T(8,128)(2,1)S(1)}, bf16[256,640]{1,0:T(8,128)(2,1)S(1)}, u32[]{:S(2)}, u32[]{:S(2)}) collective-permute-start(bf16[256,640]{1,0:T(8,128)(2,1)S(1)} %collective-permute-done.25.refs_1_), channel_id=1, source_target_pairs={{0,8},{10,2},{8,16},{18,10},{16,24},{26,18},{24,28},{30,26},{28,20... | collective-permute-start | bytes 983048 | tf_op jit(solution)/shard_map/ppermute | solution.py:79
  78.8 2.0 %collective-permute-done.20.refs_0_ = bf16[256,640]{1,0:T(8,128)(2,1)S(1)} collective-permute-done((bf16[256,640]{1,0:T(8,128)(2,1)S(1)}, bf16[256,640]{1,0:T(8,128)(2,1)S(1)}, u32[]{:S(2)}, u32[]{:S(2)}) %collective-permute-start.20) | collective-permute-done | bytes 327712 | tf_op jit(solution)/shard_map/ppermute | solution.py:79
  80.8 1.6 %collective-permute-start.21 = (bf16[256,640]{1,0:T(8,128)(2,1)S(1)}, bf16[256,640]{1,0:T(8,128)(2,1)S(1)}, u32[]{:S(2)}, u32[]{:S(2)}) collective-permute-start(bf16[256,640]{1,0:T(8,128)(2,1)S(1)} %collective-permute-done.20.refs_0_), channel_id=1, source_target_pairs={{0,8},{10,2},{8,16},{18,10},{16,24},{26,18},{24,28},{30,26},{28,20... | collective-permute-start | bytes 983048 | tf_op jit(solution)/shard_map/ppermute | solution.py:79
  84.3 3.6 %collective-permute-done.21.refs_0_ = bf16[256,640]{1,0:T(8,128)(2,1)S(1)} collective-permute-done((bf16[256,640]{1,0:T(8,128)(2,1)S(1)}, bf16[256,640]{1,0:T(8,128)(2,1)S(1)}, u32[]{:S(2)}, u32[]{:S(2)}) %collective-permute-start.21) | collective-permute-done | bytes 327712 | tf_op jit(solution)/shard_map/ppermute | solution.py:79
  90.2 1.6 %output_4.1 = bf16[256,640]{1,0:T(8,128)(2,1)} custom-call(s32[9]{0:T(128)S(1)} %pad_add_fusion.ids_ref, bf16[256,640]{1,0:T(8,128)(2,1)S(1)} %collective-permute-done.21.refs_0_, bf16[256,640]{1,0:T(8,128)(2,1)S(1)} %collective-permute-done.22.refs_1_, bf16[1,256,4096]{2,1,0:T(8,128)(2,1)S(1)} %bitcast.8, f32[1,256,640]{2,1,0:T(8,128)S(1)} %output_3.1.refs_3_), custom_call_target="tpu_custom_call" | custom-call | flops 167772160 | bytes 262144 | tf_op jit(solution)/shard_map/output_4/pallas_call | solution.py:166
  (70 shorter events, 17.1 us)
Async XLA Ops:
  1.9 3.2 %collective-permute-start.5 = (bf16[264,640]{1,0:T(8,128)(2,1)S(1)}, bf16[264,640]{1,0:T(8,128)(2,1)S(1)}, u32[]{:S(2)}, u32[]{:S(2)}) collective-permute-start(bf16[264,640]{1,0:T(8,128)(2,1)S(1)} %prepare.1.refs_0_), channel_id=1, source_target_pairs={{0,2},{2,0},{4,6},{6,4},{8,10},{10,8},{12,14},{14,12},{16,18},{18,... | collective-permute-start | bytes 1013768 | tf_op jit(solution)/shard_map/ppermute | solution.py:83
  2.4 7.7 %collective-permute-start = (bf16[264,640]{1,0:T(8,128)(2,1)S(1)}, bf16[264,640]{1,0:T(8,128)(2,1)S(1)}, u32[]{:S(2)}, u32[]{:S(2)}) collective-permute-start(bf16[264,640]{1,0:T(8,128)(2,1)S(1)} %prepare.1.refs_0_), channel_id=1, source_target_pairs={{0,8},{10,2},{8,16},{18,10},{16,24},{26,18},{24,28},{30,26},{28,20... | collective-permute-start | bytes 1013768 | tf_op jit(solution)/shard_map/ppermute | solution.py:79
  5.1 8.7 %collective-permute-start.6 = (bf16[264,640]{1,0:T(8,128)(2,1)S(1)}, bf16[264,640]{1,0:T(8,128)(2,1)S(1)}, u32[]{:S(2)}, u32[]{:S(2)}) collective-permute-start(bf16[264,640]{1,0:T(8,128)(2,1)S(1)} %collective-permute-done.5.refs_1_), channel_id=1, source_target_pairs={{0,8},{10,2},{8,16},{18,10},{16,24},{26,18},{24,28},{30,26},{28,20... | collective-permute-start | bytes 1013768 | tf_op jit(solution)/shard_map/ppermute | solution.py:79
  10.2 7.2 %collective-permute-start.1 = (bf16[264,640]{1,0:T(8,128)(2,1)S(1)}, bf16[264,640]{1,0:T(8,128)(2,1)S(1)}, u32[]{:S(2)}, u32[]{:S(2)}) collective-permute-start(bf16[264,640]{1,0:T(8,128)(2,1)S(1)} %collective-permute-done.refs_2_), channel_id=1, source_target_pairs={{0,8},{10,2},{8,16},{18,10},{16,24},{26,18},{24,28},{30,26},{28,20... | collective-permute-start | bytes 1013768 | tf_op jit(solution)/shard_map/ppermute | solution.py:79
  12.3 7.3 %collective-permute-start.9 = (bf16[264,640]{1,0:T(8,128)(2,1)S(1)}, bf16[264,640]{1,0:T(8,128)(2,1)S(1)}, u32[]{:S(2)}, u32[]{:S(2)}) collective-permute-start(bf16[264,640]{1,0:T(8,128)(2,1)S(1)} %collective-permute-done.refs_2_), channel_id=1, source_target_pairs={{0,2},{2,0},{4,6},{6,4},{8,10},{10,8},{12,14},{14,12},{16,18},{18,... | collective-permute-start | bytes 1013768 | tf_op jit(solution)/shard_map/ppermute | solution.py:83
  13.8 5.8 %collective-permute-start.8 = (bf16[264,640]{1,0:T(8,128)(2,1)S(1)}, bf16[264,640]{1,0:T(8,128)(2,1)S(1)}, u32[]{:S(2)}, u32[]{:S(2)}) collective-permute-start(bf16[264,640]{1,0:T(8,128)(2,1)S(1)} %collective-permute-done.6.refs_3_), channel_id=1, source_target_pairs={{0,2},{2,0},{4,6},{6,4},{8,10},{10,8},{12,14},{14,12},{16,18},{18,... | collective-permute-start | bytes 1013768 | tf_op jit(solution)/shard_map/ppermute | solution.py:83
  13.8 11.2 %collective-permute-start.7 = (bf16[264,640]{1,0:T(8,128)(2,1)S(1)}, bf16[264,640]{1,0:T(8,128)(2,1)S(1)}, u32[]{:S(2)}, u32[]{:S(2)}) collective-permute-start(bf16[264,640]{1,0:T(8,128)(2,1)S(1)} %collective-permute-done.6.refs_3_), channel_id=1, source_target_pairs={{0,8},{10,2},{8,16},{18,10},{16,24},{26,18},{24,28},{30,26},{28,20... | collective-permute-start | bytes 1013768 | tf_op jit(solution)/shard_map/ppermute | solution.py:79
  17.4 9.2 %collective-permute-start.2 = (bf16[264,640]{1,0:T(8,128)(2,1)S(1)}, bf16[264,640]{1,0:T(8,128)(2,1)S(1)}, u32[]{:S(2)}, u32[]{:S(2)}) collective-permute-start(bf16[264,640]{1,0:T(8,128)(2,1)S(1)} %collective-permute-done.1.refs_0_), channel_id=1, source_target_pairs={{0,8},{10,2},{8,16},{18,10},{16,24},{26,18},{24,28},{30,26},{28,20... | collective-permute-start | bytes 1013768 | tf_op jit(solution)/shard_map/ppermute | solution.py:79
  25.0 7.2 %collective-permute-start.10 = (bf16[264,640]{1,0:T(8,128)(2,1)S(1)}, bf16[264,640]{1,0:T(8,128)(2,1)S(1)}, u32[]{:S(2)}, u32[]{:S(2)}) collective-permute-start(bf16[264,640]{1,0:T(8,128)(2,1)S(1)} %collective-permute-done.7.refs_1_), channel_id=1, source_target_pairs={{0,8},{10,2},{8,16},{18,10},{16,24},{26,18},{24,28},{30,26},{28,20... | collective-permute-start | bytes 1013768 | tf_op jit(solution)/shard_map/ppermute | solution.py:79
  26.6 9.2 %collective-permute-start.3 = (bf16[264,640]{1,0:T(8,128)(2,1)S(1)}, bf16[264,640]{1,0:T(8,128)(2,1)S(1)}, u32[]{:S(2)}, u32[]{:S(2)}) collective-permute-start(bf16[264,640]{1,0:T(8,128)(2,1)S(1)} %collective-permute-done.2.refs_0_), channel_id=1, source_target_pairs={{0,8},{10,2},{8,16},{18,10},{16,24},{26,18},{24,28},{30,26},{28,20... | collective-permute-start | bytes 1013768 | tf_op jit(solution)/shard_map/ppermute | solution.py:79
  28.2 7.6 %collective-permute-start.14 = (bf16[264,640]{1,0:T(8,128)(2,1)S(1)}, bf16[264,640]{1,0:T(8,128)(2,1)S(1)}, u32[]{:S(2)}, u32[]{:S(2)}) collective-permute-start(bf16[264,640]{1,0:T(8,128)(2,1)S(1)} %collective-permute-done.1.refs_0_), channel_id=1, source_target_pairs={{0,2},{2,0},{4,6},{6,4},{8,10},{10,8},{12,14},{14,12},{16,18},{18,... | collective-permute-start | bytes 1013768 | tf_op jit(solution)/shard_map/ppermute | solution.py:83
  28.2 7.6 %collective-permute-start.13 = (bf16[264,640]{1,0:T(8,128)(2,1)S(1)}, bf16[264,640]{1,0:T(8,128)(2,1)S(1)}, u32[]{:S(2)}, u32[]{:S(2)}) collective-permute-start(bf16[264,640]{1,0:T(8,128)(2,1)S(1)} %collective-permute-done.7.refs_1_), channel_id=1, source_target_pairs={{0,2},{2,0},{4,6},{6,4},{8,10},{10,8},{12,14},{14,12},{16,18},{18,... | collective-permute-start | bytes 1013768 | tf_op jit(solution)/shard_map/ppermute | solution.py:83
  28.7 9.3 %collective-permute-start.12 = (bf16[264,640]{1,0:T(8,128)(2,1)S(1)}, bf16[264,640]{1,0:T(8,128)(2,1)S(1)}, u32[]{:S(2)}, u32[]{:S(2)}) collective-permute-start(bf16[264,640]{1,0:T(8,128)(2,1)S(1)} %collective-permute-done.2.refs_0_), channel_id=1, source_target_pairs={{0,2},{2,0},{4,6},{6,4},{8,10},{10,8},{12,14},{14,12},{16,18},{18,... | collective-permute-start | bytes 1013768 | tf_op jit(solution)/shard_map/ppermute | solution.py:83
  32.2 5.8 %collective-permute-start.11 = (bf16[264,640]{1,0:T(8,128)(2,1)S(1)}, bf16[264,640]{1,0:T(8,128)(2,1)S(1)}, u32[]{:S(2)}, u32[]{:S(2)}) collective-permute-start(bf16[264,640]{1,0:T(8,128)(2,1)S(1)} %collective-permute-done.10.refs_1_), channel_id=1, source_target_pairs={{0,2},{2,0},{4,6},{6,4},{8,10},{10,8},{12,14},{14,12},{16,18},{18,... | collective-permute-start | bytes 1013768 | tf_op jit(solution)/shard_map/ppermute | solution.py:83
  35.8 4.3 %collective-permute-start.4 = (bf16[264,640]{1,0:T(8,128)(2,1)S(1)}, bf16[264,640]{1,0:T(8,128)(2,1)S(1)}, u32[]{:S(2)}, u32[]{:S(2)}) collective-permute-start(bf16[264,640]{1,0:T(8,128)(2,1)S(1)} %collective-permute-done.3.refs_0_), channel_id=1, source_target_pairs={{0,2},{2,0},{4,6},{6,4},{8,10},{10,8},{12,14},{14,12},{16,18},{18,... | collective-permute-start | bytes 1013768 | tf_op jit(solution)/shard_map/ppermute | solution.py:83
  42.1 14.5 %collective-permute-start.17 = (bf16[128,640]{1,0:T(8,128)(2,1)S(1)}, bf16[128,640]{1,0:T(8,128)(2,1)S(1)}, u32[]{:S(2)}, u32[]{:S(2)}) collective-permute-start(bf16[128,640]{1,0:T(8,128)(2,1)S(1)} %get-tuple-element.41), channel_id=1, source_target_pairs={{0,1},{2,3},{4,5},{6,7},{8,9},{10,11},{12,13},{14,15},{16,17},{18,... | collective-permute-start | bytes 491528 | tf_op jit(solution)/shard_map/ppermute | solution.py:431
  45.5 12.5 %collective-permute-start.15 = (bf16[128,640]{1,0:T(8,128)(2,1)S(1)}, bf16[128,640]{1,0:T(8,128)(2,1)S(1)}, u32[]{:S(2)}, u32[]{:S(2)}) collective-permute-start(bf16[128,640]{1,0:T(8,128)(2,1)S(1)} %get-tuple-element.42), channel_id=1, source_target_pairs={{0,1},{2,3},{4,5},{6,7},{8,9},{10,11},{12,13},{14,15},{16,17},{18,... | collective-permute-start | bytes 491528 | tf_op jit(solution)/shard_map/ppermute | solution.py:431
  46.9 6.8 %collective-permute-start.16 = (f32[3,8,256]{2,1,0:T(8,128)S(1)}, f32[3,8,256]{2,1,0:T(8,128)S(1)}, u32[]{:S(2)}, u32[]{:S(2)}) collective-permute-start(f32[3,8,256]{2,1,0:T(8,128)S(1)} %get-tuple-element.34), channel_id=1, source_target_pairs={{0,1},{2,3},{4,5},{6,7},{8,9},{10,11},{12,13},{14,15},{16,17},{18,... | collective-permute-start | bytes 73736 | tf_op jit(solution)/shard_map/ppermute | solution.py:431
  59.5 7.1 %collective-permute-start.18 = (bf16[256,640]{1,0:T(8,128)(2,1)S(1)}, bf16[256,640]{1,0:T(8,128)(2,1)S(1)}, u32[]{:S(2)}, u32[]{:S(2)}) collective-permute-start(bf16[256,640]{1,0:T(8,128)(2,1)S(1)} %far_part_1_1.1.refs_0_), channel_id=1, source_target_pairs={{0,8},{10,2},{8,16},{18,10},{16,24},{26,18},{24,28},{30,26},{28,20... | collective-permute-start | bytes 983048 | tf_op jit(solution)/shard_map/ppermute | solution.py:79
  61.2 9.0 %collective-permute-start.24 = (bf16[256,640]{1,0:T(8,128)(2,1)S(1)}, bf16[256,640]{1,0:T(8,128)(2,1)S(1)}, u32[]{:S(2)}, u32[]{:S(2)}) collective-permute-start(bf16[256,640]{1,0:T(8,128)(2,1)S(1)} %collective-permute-done.23.refs_1_), channel_id=1, source_target_pairs={{0,8},{10,2},{8,16},{18,10},{16,24},{26,18},{24,28},{30,26},{28,20... | collective-permute-start | bytes 983048 | tf_op jit(solution)/shard_map/ppermute | solution.py:79
  66.7 7.1 %collective-permute-start.19 = (bf16[256,640]{1,0:T(8,128)(2,1)S(1)}, bf16[256,640]{1,0:T(8,128)(2,1)S(1)}, u32[]{:S(2)}, u32[]{:S(2)}) collective-permute-start(bf16[256,640]{1,0:T(8,128)(2,1)S(1)} %collective-permute-done.18.refs_2_), channel_id=1, source_target_pairs={{0,8},{10,2},{8,16},{18,10},{16,24},{26,18},{24,28},{30,26},{28,20... | collective-permute-start | bytes 983048 | tf_op jit(solution)/shard_map/ppermute | solution.py:79
  68.2 7.1 %collective-permute-start.27 = (bf16[256,640]{1,0:T(8,128)(2,1)S(1)}, bf16[256,640]{1,0:T(8,128)(2,1)S(1)}, u32[]{:S(2)}, u32[]{:S(2)}) collective-permute-start(bf16[256,640]{1,0:T(8,128)(2,1)S(1)} %collective-permute-done.18.refs_2_), channel_id=1, source_target_pairs={{0,2},{2,0},{4,6},{6,4},{8,10},{10,8},{12,14},{14,12},{16,18},{18,... | collective-permute-start | bytes 983048 | tf_op jit(solution)/shard_map/ppermute | solution.py:83
  70.2 5.2 %collective-permute-start.26 = (bf16[256,640]{1,0:T(8,128)(2,1)S(1)}, bf16[256,640]{1,0:T(8,128)(2,1)S(1)}, u32[]{:S(2)}, u32[]{:S(2)}) collective-permute-start(bf16[256,640]{1,0:T(8,128)(2,1)S(1)} %collective-permute-done.24.refs_3_), channel_id=1, source_target_pairs={{0,2},{2,0},{4,6},{6,4},{8,10},{10,8},{12,14},{14,12},{16,18},{18,... | collective-permute-start | bytes 983048 | tf_op jit(solution)/shard_map/ppermute | solution.py:83
  70.2 7.1 %collective-permute-start.25 = (bf16[256,640]{1,0:T(8,128)(2,1)S(1)}, bf16[256,640]{1,0:T(8,128)(2,1)S(1)}, u32[]{:S(2)}, u32[]{:S(2)}) collective-permute-start(bf16[256,640]{1,0:T(8,128)(2,1)S(1)} %collective-permute-done.24.refs_3_), channel_id=1, source_target_pairs={{0,8},{10,2},{8,16},{18,10},{16,24},{26,18},{24,28},{30,26},{28,20... | collective-permute-start | bytes 983048 | tf_op jit(solution)/shard_map/ppermute | solution.py:79
  73.7 7.1 %collective-permute-start.20 = (bf16[256,640]{1,0:T(8,128)(2,1)S(1)}, bf16[256,640]{1,0:T(8,128)(2,1)S(1)}, u32[]{:S(2)}, u32[]{:S(2)}) collective-permute-start(bf16[256,640]{1,0:T(8,128)(2,1)S(1)} %collective-permute-done.19.refs_0_), channel_id=1, source_target_pairs={{0,8},{10,2},{8,16},{18,10},{16,24},{26,18},{24,28},{30,26},{28,20... | collective-permute-start | bytes 983048 | tf_op jit(solution)/shard_map/ppermute | solution.py:79
  77.2 7.1 %collective-permute-start.28 = (bf16[256,640]{1,0:T(8,128)(2,1)S(1)}, bf16[256,640]{1,0:T(8,128)(2,1)S(1)}, u32[]{:S(2)}, u32[]{:S(2)}) collective-permute-start(bf16[256,640]{1,0:T(8,128)(2,1)S(1)} %collective-permute-done.25.refs_1_), channel_id=1, source_target_pairs={{0,8},{10,2},{8,16},{18,10},{16,24},{26,18},{24,28},{30,26},{28,20... | collective-permute-start | bytes 983048 | tf_op jit(solution)/shard_map/ppermute | solution.py:79
  80.8 7.1 %collective-permute-start.21 = (bf16[256,640]{1,0:T(8,128)(2,1)S(1)}, bf16[256,640]{1,0:T(8,128)(2,1)S(1)}, u32[]{:S(2)}, u32[]{:S(2)}) collective-permute-start(bf16[256,640]{1,0:T(8,128)(2,1)S(1)} %collective-permute-done.20.refs_0_), channel_id=1, source_target_pairs={{0,8},{10,2},{8,16},{18,10},{16,24},{26,18},{24,28},{30,26},{28,20... | collective-permute-start | bytes 983048 | tf_op jit(solution)/shard_map/ppermute | solution.py:79
  82.4 5.5 %collective-permute-start.32 = (bf16[256,640]{1,0:T(8,128)(2,1)S(1)}, bf16[256,640]{1,0:T(8,128)(2,1)S(1)}, u32[]{:S(2)}, u32[]{:S(2)}) collective-permute-start(bf16[256,640]{1,0:T(8,128)(2,1)S(1)} %collective-permute-done.19.refs_0_), channel_id=1, source_target_pairs={{0,2},{2,0},{4,6},{6,4},{8,10},{10,8},{12,14},{14,12},{16,18},{18,... | collective-permute-start | bytes 983048 | tf_op jit(solution)/shard_map/ppermute | solution.py:83
  82.4 5.5 %collective-permute-start.31 = (bf16[256,640]{1,0:T(8,128)(2,1)S(1)}, bf16[256,640]{1,0:T(8,128)(2,1)S(1)}, u32[]{:S(2)}, u32[]{:S(2)}) collective-permute-start(bf16[256,640]{1,0:T(8,128)(2,1)S(1)} %collective-permute-done.25.refs_1_), channel_id=1, source_target_pairs={{0,2},{2,0},{4,6},{6,4},{8,10},{10,8},{12,14},{14,12},{16,18},{18,... | collective-permute-start | bytes 983048 | tf_op jit(solution)/shard_map/ppermute | solution.py:83
  82.9 6.2 %collective-permute-start.30 = (bf16[256,640]{1,0:T(8,128)(2,1)S(1)}, bf16[256,640]{1,0:T(8,128)(2,1)S(1)}, u32[]{:S(2)}, u32[]{:S(2)}) collective-permute-start(bf16[256,640]{1,0:T(8,128)(2,1)S(1)} %collective-permute-done.20.refs_0_), channel_id=1, source_target_pairs={{0,2},{2,0},{4,6},{6,4},{8,10},{10,8},{12,14},{14,12},{16,18},{18,... | collective-permute-start | bytes 983048 | tf_op jit(solution)/shard_map/ppermute | solution.py:83
  84.3 4.7 %collective-permute-start.29 = (bf16[256,640]{1,0:T(8,128)(2,1)S(1)}, bf16[256,640]{1,0:T(8,128)(2,1)S(1)}, u32[]{:S(2)}, u32[]{:S(2)}) collective-permute-start(bf16[256,640]{1,0:T(8,128)(2,1)S(1)} %collective-permute-done.28.refs_1_), channel_id=1, source_target_pairs={{0,2},{2,0},{4,6},{6,4},{8,10},{10,8},{12,14},{14,12},{16,18},{18,... | collective-permute-start | bytes 983048 | tf_op jit(solution)/shard_map/ppermute | solution.py:83
  87.9 2.4 %collective-permute-start.22 = (bf16[256,640]{1,0:T(8,128)(2,1)S(1)}, bf16[256,640]{1,0:T(8,128)(2,1)S(1)}, u32[]{:S(2)}, u32[]{:S(2)}) collective-permute-start(bf16[256,640]{1,0:T(8,128)(2,1)S(1)} %collective-permute-done.21.refs_0_), channel_id=1, source_target_pairs={{0,2},{2,0},{4,6},{6,4},{8,10},{10,8},{12,14},{14,12},{16,18},{18,... | collective-permute-start | bytes 983048 | tf_op jit(solution)/shard_map/ppermute | solution.py:83
  (11 other events, 70.3 us)

commit v3 on v2

v3 whole, which is shorter than its diff:
```python
import math

import jax
import jax.numpy as jnp
import numpy as np
from jax import lax
from jax.experimental import pallas as pl
from jax.experimental.pallas import tpu as pltpu
from jax.sharding import PartitionSpec as P

epsilon = 1e-05
block_len = 128
STAGGER = 2e9
side_rows = 8
bf16 = jnp.bfloat16
f32 = jnp.float32
in_vmem = pl.BlockSpec(memory_space=pltpu.VMEM)
in_smem = pl.BlockSpec(memory_space=pltpu.SMEM)
params = pltpu.CompilerParams(vmem_limit_bytes=20 * 2**20)


def shape_of(shape, dtype):
    return jax.ShapeDtypeStruct(tuple(shape), dtype)


def dot(left, right):
    return jnp.dot(left, right, preferred_element_type=f32)


def column(row):
    return jnp.broadcast_to(row, (8, row.shape[1])).T[:, :1]


def tap_columns(taps):
    return jnp.concatenate([taps, jnp.zeros((8 - taps.shape[0], taps.shape[1]), f32)], axis=0).T


def estimate(flops, size):
    return pl.CostEstimate(flops=int(flops), bytes_accessed=int(size), transcendentals=0)


def prepare_kernel(ids_ref, x_ref, gain_ref, out_ref):
    rows = x_ref.shape[0]
    wide = x_ref[...].astype(f32)
    out_ref[:rows] = (wide * column(gain_ref[...])).astype(bf16)
    squares = jnp.sum(wide * wide, axis=0, keepdims=True)
    high = squares.astype(bf16).astype(f32)
    row = lax.broadcasted_iota(jnp.int32, (side_rows, wide.shape[1]), 0)
    side = jnp.where(row == 0, high, jnp.where(row == 1, squares - high, 0.0))
    out_ref[rows:] = side.astype(bf16)


def prepare(ids, x, gain):
    rows, tokens = x.shape
    return pl.pallas_call(
        prepare_kernel,
        in_specs=[in_smem, in_vmem, in_vmem],
        out_specs=in_vmem,
        out_shape=shape_of((rows + side_rows, tokens), bf16),
        compiler_params=params,
        name="prepare",
    )(ids, x, gain.reshape(1, rows))


def chip_count():
    return lax.axis_size("fsdp") // 2


def ring_order(count):
    return list(range(0, count, 2)) + list(range(1, count, 2))[::-1]


def along_ring(block):
    chips = chip_count()
    order = ring_order(chips)
    pairs = []
    for i in range(chips):
        here, after = order[i], order[(i + 1) % chips]
        pairs += [(2 * here, 2 * after), (2 * after + 1, 2 * here + 1)]
    return lax.ppermute(block, "fsdp", pairs)


def other_core(block):
    return lax.ppermute(block, "fsdp", [(i, i ^ 1) for i in range(2 * chip_count())])


def ring_ids():
    chips = chip_count()
    me = lax.axis_index("fsdp")
    chip, core = me // 2, me % 2
    place = jnp.where(chip % 2 == 0, chip // 2, chips - 1 - chip // 2)
    steps = jnp.arange(chips, dtype=jnp.int32)
    places = (place + jnp.where(core == 0, chips - steps, steps)) % chips
    ids = jnp.where(places < (chips + 1) // 2, 2 * places, 2 * (chips - 1 - places) + 1)
    return jnp.concatenate([ids, core[None]]).astype(jnp.int32)


def products(ids, items, weight, running, side, finish, cost, name):
    streams, out_rows, features = weight.shape
    rows = features // (2 * (ids.shape[0] - 1))
    shards = [shard for _, _, shard in items]
    tokens = shards[0].shape[1]
    count = len(shards)
    first_group = running is None
    state = [] if first_group else list(running)
    body, extras, out_shape = finish if finish else (None, [], None)
    padded = rows % 128 != 0
    width = 2 * rows if padded else rows
    scratch_shapes = [pltpu.VMEM((count * width, tokens), bf16)] if padded else []

    def kernel(ids_ref, *refs):
        refs = list(refs)
        take = lambda n: [refs.pop(0) for _ in range(n)]
        shard_refs = take(count)
        (weight_ref,) = take(1)
        state_refs = take(len(state))
        extra_refs = take(len(extras))
        outs = take(len(out_shape))
        core = ids_ref[ids_ref.shape[0] - 1]
        if padded:
            (beside_ref,) = refs
            beside_ref[...] = jnp.zeros(beside_ref.shape, bf16)
            for k, (_, other, _) in enumerate(items):
                at = k * width + jnp.where(core == other, 0, rows)
                beside_ref[pl.ds(pl.multiple_of(at, rows), rows)] = shard_refs[k][:rows]
            right = beside_ref[...]
        else:
            right = jnp.concatenate([ref[:rows] for ref in shard_refs], axis=0)
        side_sum = None
        if side:
            parts = [ref[rows:].astype(f32) for ref in shard_refs]
            parts += [] if first_group else [state_refs[1][...]]
            side_sum = sum(parts[1:], parts[0])

        def total(stream):
            left = []
            for slot, other, _ in items:
                block = ids_ref[slot]
                if not padded:
                    block = 2 * block + (1 - core if other else core)
                at = pl.ds(pl.multiple_of(block * width, width), width)
                left.append(weight_ref[stream, :, at])
            product = dot(jnp.concatenate(left, axis=1), right)
            return product if first_group else state_refs[0][stream] + product

        if body is not None:
            body(total, side_sum, extra_refs, outs)
            return
        for stream in range(streams):
            outs[0][stream] = total(stream)
        if side:
            outs[1][...] = side_sum

    aliases = {}
    if body is None:
        out_shape = [shape_of((streams, out_rows, tokens), f32)]
        if side:
            out_shape.append(shape_of((side_rows, tokens), f32))
        if not first_group:
            aliases = {1 + count + 1 + i: i for i in range(len(state))}
    return pl.pallas_call(
        kernel,
        in_specs=[in_smem] + [in_vmem] * (count + 1 + len(state) + len(extras)),
        out_specs=[in_vmem] * len(out_shape),
        out_shape=out_shape,
        scratch_shapes=scratch_shapes,
        input_output_aliases=aliases,
        compiler_params=params,
        cost_estimate=estimate(cost, 0),
        name=name,
    )(ids, *shards, weight, *state, *extras)


def gather_products(ids, own, weight, beside, side, finish, name):
    chips = chip_count()
    last_step = chips // 2

    def send(way, block, scope):
        with jax.named_scope(f"{name}_{scope}"):
            return way(block)

    near, far = own, send(other_core, own, "core_own")
    items = [(0, 0, near), (0, 1, far)]
    running = None
    for step in range(1, last_step + 1):
        near = send(along_ring, near, f"near_{step}")
        arrived = near
        if running is not None:
            arrived, *running = lax.optimization_barrier((near, *running))
        elif beside:
            arrived, *beside = lax.optimization_barrier((near, *beside))
        theirs = send(other_core, arrived, f"core_near_{step}")
        pair = [(step, 0, arrived), (chips - step, 1, theirs)]
        if step < last_step:
            running = products(ids, items + pair, weight, running, side, None, 0, f"{name}_{step}")
            far = send(along_ring, far, f"far_{step}")
            theirs = send(other_core, far, f"core_far_{step}")
            items = [(step, 1, far), (chips - step, 0, theirs)]
        else:
            running = products(ids, items, weight, running, side, None, STAGGER, f"{name}_{step}")
            items = pair
    result = products(ids, items, weight, running, side, finish, 0, f"{name}_last")
    return result, beside


def smooth(projected, taps, count, halo):
    lane = lax.broadcasted_iota(jnp.int32, projected.shape, 1)
    out = taps[:, :1] * projected
    for tap in range(1, count):
        moved = pltpu.roll(projected, tap, 1)
        for place in range(tap):
            edge = 0.0
            if halo is not None:
                at = halo.shape[1] - tap + place
                edge = halo[:, at : at + 1]
            moved = jnp.where(lane == place, edge, moved)
        out = out + taps[:, tap : tap + 1] * moved
    return out


def projection_finish(features, w_short, tokens):
    streams, count, channels = w_short.shape
    half = channels // 2

    def body(total, side_sum, extra_refs, outs):
        (taps_ref,) = extra_refs
        projected_ref, *message_refs = outs
        mean = jnp.sum(side_sum, axis=0, keepdims=True) * (1.0 / features)
        factor = lax.rsqrt(mean + epsilon)
        tails = []
        for stream in range(streams):
            projected = (total(stream) * factor).astype(bf16)
            projected_ref[stream] = projected
            tail = projected[:, tokens - block_len :].astype(f32).T
            tails.append(tail[block_len - count + 1 :])
        taps = [tap_columns(taps_ref[stream]) for stream in (1, 2)]
        tile = min(half, 64)
        for part, message_ref in enumerate(message_refs):
            for start in range(0, half, tile):
                rows = slice(part * half + start, part * half + start + tile)
                key, value = (
                    smooth(projected_ref[s, rows].astype(f32), taps[s - 1][rows], count, None)
                    for s in (1, 2)
                )
                message_ref[start : start + tile] = (key * value).astype(bf16)
            rows = tails + [jnp.zeros((side_rows - streams * (count - 1), channels), f32)]
            side = jnp.concatenate(rows, axis=0)[:, part * half : (part + 1) * half]
            width = min(half, tokens)
            message_ref[half:] = jnp.zeros((side_rows, tokens), bf16)
            message_ref[half:, :width] = side.astype(bf16)

    message = shape_of((half + side_rows, tokens), bf16)
    return body, [w_short], [shape_of((streams, channels, tokens), bf16), message, message]


def halo_columns(message_ref, streams, count):
    half = message_ref.shape[0] - side_rows
    side = message_ref[half:, :half].astype(f32).T
    return [side[:, s * (count - 1) : (s + 1) * (count - 1)] for s in range(streams)]


def split_table(table):
    high = table.astype(bf16)
    low = (table - high.astype(np.float64)).astype(bf16)
    return np.stack([high, low])


def dft_tables():
    size = 2 * block_len
    freq = np.arange(block_len) + 0.5
    angle = 2.0 * math.pi / size * np.arange(size)[:, None] * freq[None, :]
    forward = np.concatenate([np.cos(angle), -np.sin(angle)], axis=1)
    back = angle[block_len:].T
    inverse = np.concatenate([np.cos(back), -np.sin(back)], axis=0) * (2.0 / size)
    return split_table(forward), split_table(inverse)


def spectrum_lanes(k):
    return slice(2 * k * block_len, 2 * (k + 1) * block_len)


def block_lanes(k):
    return slice(k * block_len, (k + 1) * block_len)


def filter_spectra(long_filter, table):
    channels, lags = long_filter.shape

    def kernel(filter_ref, table_ref, spectra_ref):
        before = jnp.zeros((channels, block_len), bf16)
        for k in range(lags // block_len):
            now = filter_ref[:, block_lanes(k)]
            segment = jnp.concatenate([before, now], axis=1)
            spectrum = dot(segment, table_ref[0]) + dot(segment, table_ref[1])
            spectra_ref[:, spectrum_lanes(k)] = spectrum
            before = now

    return pl.pallas_call(
        kernel,
        in_specs=[in_vmem, in_vmem],
        out_specs=in_vmem,
        out_shape=shape_of((channels, 2 * lags), f32),
        compiler_params=params,
        cost_estimate=estimate(8 * channels * lags * 2 * block_len, 10 * channels * lags),
        name="filter_spectra",
    )(long_filter, table)


def block_spectrum(block, table_ref):
    return dot(block, table_ref[0, :block_len]) + dot(block, table_ref[1, :block_len])


def block_spectra(gated_ref, rows, table_ref, spec_ref, first):
    for b in range(first, gated_ref.shape[1] // block_len):
        spec_ref[:, spectrum_lanes(b)] = block_spectrum(gated_ref[:rows, block_lanes(b)], table_ref)


def multiply_spectra(source_ref, filters_ref, filter_start, pairs, before_ref, total_ref):
    def one_tile(i, carry):
        here = pl.ds(pl.multiple_of(i * 8, 8), 8)
        there = pl.ds(pl.multiple_of(filter_start + i * 8, 8), 8)

        def part(ref, rows, k, imaginary):
            start = (2 * k + imaginary) * block_len
            return ref[rows, start : start + block_len]

        for a, terms in enumerate(pairs):
            real = imag = None
            if before_ref is not None:
                real, imag = part(before_ref, here, a, 0), part(before_ref, here, a, 1)
            for b, d in terms:
                gr, gi = part(source_ref, here, b, 0), part(source_ref, here, b, 1)
                hr, hi = part(filters_ref, there, d, 0), part(filters_ref, there, d, 1)
                more_real, more_imag = gr * hr - gi * hi, gr * hi + gi * hr
                real = more_real if real is None else real + more_real
                imag = more_imag if imag is None else imag + more_imag
            if real is None:
                real = imag = jnp.zeros((8, block_len), f32)
            start = 2 * a * block_len
            total_ref[here, start : start + block_len] = real
            total_ref[here, start + block_len : start + 2 * block_len] = imag
        return carry

    lax.fori_loop(0, total_ref.shape[0] // 8, one_tile, 0)


def own_part(projected, messages, moved, taps, filters, table):
    streams, channels, tokens = projected.shape
    half = channels // 2
    count = taps.shape[1]
    blocks = tokens // block_len
    first = 0 if moved else 1
    pairs = [[(b, a - b) for b in range(first, a + 1)] for a in range(blocks)]
    inputs = list(moved or messages)

    def kernel(projected_ref, one_ref, two_ref, taps_ref, filters_ref, table_ref, *refs):
        *refs, spec_ref = refs
        query_refs, total_refs, gated_refs = refs[:2], refs[2:4], refs[4:]
        columns = [tap_columns(taps_ref[s]) for s in range(streams)]
        tile = min(half, 64)
        for part, message_ref in enumerate((one_ref, two_ref)):
            halo = [None] * streams
            if moved:
                halo = halo_columns(message_ref, streams, count)
            for start in range(0, half, tile):
                here = slice(start, start + tile)
                rows = slice(part * half + start, part * half + start + tile)

                def smoothed(s):
                    edge = halo[s][here] if moved else None
                    wide = projected_ref[s, rows].astype(f32)
                    return smooth(wide, columns[s][rows], count, edge)

                query_refs[part][here] = smoothed(0)
                if moved:
                    gated_refs[part][here] = (smoothed(1) * smoothed(2)).astype(bf16)
            source_ref = gated_refs[part] if moved else message_ref
            block_spectra(source_ref, half, table_ref, spec_ref, first)
            multiply_spectra(spec_ref, filters_ref, part * half, pairs, None, total_refs[part])

    out_shape = [shape_of((half, tokens), f32)] * 2 + [shape_of((half, 2 * tokens), f32)] * 2
    if moved:
        out_shape += [shape_of((half, tokens), bf16)] * 2
    outs = pl.pallas_call(
        kernel,
        in_specs=[in_vmem] * 6,
        out_specs=[in_vmem] * len(out_shape),
        out_shape=out_shape,
        scratch_shapes=[pltpu.VMEM((half, 2 * tokens), f32)],
        compiler_params=params,
        cost_estimate=estimate(6 * 10**8, 6 * 10**6),
        name="own_part",
    )(projected, *inputs, taps, filters, table)
    return list(outs[:2]), list(outs[2:4]), list(outs[4:]) if moved else messages


def far_part(turn, part, moved, total, filters, table, last, own):
    rows, tokens = total.shape[0], moved.shape[1]
    blocks = tokens // block_len
    pairs = [[(b, turn * blocks + a - b) for b in range(blocks)] for a in range(blocks)]
    if own:
        pairs = [terms + [(blocks, a)] for a, terms in enumerate(pairs)]
    channels_here = slice(part * rows, (part + 1) * rows)

    def kernel(*refs):
        refs = list(refs)
        take = lambda n: [refs.pop(0) for _ in range(n)]
        moved_ref, total_ref, filters_ref, table_ref = take(4)
        own_refs = take(2) if own else None
        spec_ref = refs.pop()
        if last is None:
            block_spectra(moved_ref, rows, table_ref, spec_ref, 0)
            multiply_spectra(spec_ref, filters_ref, part * rows, pairs, total_ref, refs[0])
            return
        sum_ref = refs.pop()
        back_ref, query_ref, gated_ref, skip_ref = take(4)
        out_ref = refs[-1]
        query, gated = (
            [ref[:rows, block_lanes(a)] for a in range(blocks)] for ref in (query_ref, gated_ref)
        )
        if own:
            projected_ref, taps_ref = own_refs
            streams, count, _ = taps_ref.shape
            halo = halo_columns(moved_ref, streams, count)
            smoothed = []
            for s in range(streams):
                columns = tap_columns(taps_ref[s, :, channels_here])
                wide = projected_ref[s, channels_here, :block_len].astype(f32)
                smoothed.append(smooth(wide, columns, count, halo[s]))
            query[0] = smoothed[0]
            gated[0] = (smoothed[1] * smoothed[2]).astype(bf16)
            spec_ref[:, spectrum_lanes(blocks)] = block_spectrum(gated[0], table_ref)
        block_spectra(moved_ref, rows, table_ref, spec_ref, 0)
        multiply_spectra(spec_ref, filters_ref, part * rows, pairs, total_ref, sum_ref)
        skip = column(skip_ref[...])[channels_here]
        for a in range(blocks):
            spectrum = sum_ref[:, spectrum_lanes(a)]
            high = spectrum.astype(bf16)
            low = (spectrum - high.astype(f32)).astype(bf16)
            filtered = dot(high, back_ref[0]) + (dot(low, back_ref[0]) + dot(high, back_ref[1]))
            mixed = query[a] * (filtered + skip * gated[a].astype(f32))
            out_ref[channels_here, block_lanes(a)] = mixed.astype(bf16)

    args = [moved, total, filters, table]
    if own:
        args += list(own)
    aliases = {}
    scratch = [pltpu.VMEM((rows, 2 * (blocks + 1) * block_len), f32)]
    out_shape = shape_of((rows, 2 * tokens), f32)
    if last is not None:
        inverse, query, gated, skip, mixed = last
        args += [inverse, query, gated, skip.reshape(1, 2 * rows)]
        if mixed is not None:
            aliases = {len(args): 0}
            args.append(mixed)
        out_shape = shape_of((2 * rows, tokens), bf16)
        scratch.append(pltpu.VMEM((rows, 2 * tokens), f32))
    return pl.pallas_call(
        kernel,
        in_specs=[in_vmem] * len(args),
        out_specs=in_vmem,
        out_shape=out_shape,
        scratch_shapes=scratch[::-1],
        input_output_aliases=aliases,
        compiler_params=params,
        cost_estimate=estimate(4 * 10**8, 4 * 10**6),
        name=f"far_part_{turn}_{part}",
    )(*args)


def from_before(block):
    count = lax.axis_size("ctx")
    return lax.ppermute(block, "ctx", [(i - 1, i) for i in range(1, count)])


def output_finish(channels, tokens):
    def body(total, side_sum, extra_refs, outs):
        outs[0][...] = total(0).astype(bf16)

    return body, [], [shape_of((channels, tokens), bf16)]


def shards(activations, norm_gain, w_in, w_short, long_filter, skip_gain, w_out):
    channels, tokens = activations.shape
    features = w_in.shape[2]
    w_short = w_short.transpose(0, 2, 1)
    turns = lax.axis_size("ctx")
    forward, inverse = (jnp.asarray(t) for t in dft_tables())
    ids = ring_ids()
    own = prepare(ids, activations, norm_gain)

    finish = projection_finish(features, w_short, tokens)
    beside = [filter_spectra(long_filter, forward)]
    (projected, *messages), (filters,) = gather_products(
        ids, own, w_in, beside, True, finish, "projection"
    )
    moving = [from_before(message) for message in messages]
    exact = turns > 2
    query, totals, gated = own_part(
        projected, messages, moving if exact else None, w_short, filters, forward
    )
    if exact:
        moving = [from_before(part) for part in gated]
    mixed = None
    for turn in range(1, turns):
        for part in range(2):
            if turn < turns - 1:
                totals[part] = far_part(
                    turn, part, moving[part], totals[part], filters, forward, None, None
                )
                moving[part] = from_before(moving[part])
            else:
                last = (inverse, query[part], gated[part], skip_gain, mixed)
                first_block = None if exact else (projected, w_short)
                mixed = far_part(
                    turn, part, moving[part], totals[part], filters, forward, last, first_block
                )

    finish = output_finish(channels, tokens)
    (result,), _ = gather_products(ids, mixed, w_out[None], [], False, finish, "output")
    return result


def solution(mesh):
    placed = (
        P("fsdp", "ctx"),
        P("fsdp"),
        P(None, "fsdp", None),
        P(None, "fsdp", None),
        P("fsdp", None),
        P("fsdp"),
        P("fsdp", None),
    )
    return jax.shard_map(
        shards, mesh=mesh, in_specs=placed, out_specs=P("fsdp", "ctx"), check_vma=False
    )
```

time: 92.3 us -> 86.7 us (0.939)
  waiting for transfers between devices: 33.8 us -> 25.4 us
  local copies, waits for them, and re-layouts: 4.51 us -> 6.5 us
  Pallas kernels: 20.8 us -> 22.4 us
    ppermute x14, waiting for transfers between devices: 29.1 us -> 21.2 us  [along_ring(): return lax.ppermute(block, 'fsdp', pairs)]
    unnamed x20 -> x22, local copies, waits for them, and re-layouts: 4.48 us -> 6.5 us
    pallas_call x8 -> x10, Pallas kernels: 14 us -> 15.6 us  [products(): pl.pallas_call(kernel, in_specs=[in_smem] + [in_vmem] * (count + 1 + len(...]
    ppermute x3 -> x2, waiting for transfers between devices: 4.66 us -> 3.3 us  [from_before(): return lax.ppermute(block, 'ctx', [(i - 1, i) for i in range(1, count)])]
    ppermute x3 -> x2, starting transfers between devices: 6 us -> 4.73 us  [from_before(): return lax.ppermute(block, 'ctx', [(i - 1, i) for i in range(1, count)])]
    pallas_call x2, Pallas kernels: 2.74 us -> 3.96 us  [far_part(): pl.pallas_call(kernel, in_specs=[in_vmem] * len(args), out_specs=in_vmem,...]
    pallas_call x3, Pallas kernels: 4.03 us -> 2.88 us  [the longest x1 1.25 us: own_part(): pl.pallas_call(kernel, in_specs=[in_vmem] * 6, out_specs=[in_vmem] * len(...]
    ppermute x16, starting transfers between devices: 1.64 us -> 2.7 us  [other_core(): lax.ppermute(block, 'fsdp', [(i, i ^ 1) for i in range(2 * chip_count())])]
  transfers between devices with their start and end apart: 33 -> 32, of which waited for: 13 -> 16; matrix products, arithmetic and copies ran while one was open for 0% -> 0% of each run, Pallas kernels for 17% -> 19%
where the time goes in v3:
time: 86.7 us; the launch traced here: 86.4 us
  starting transfers between devices  31.7 us (37%)
  waiting for transfers between devices  25.4 us (29%)
  Pallas kernels  22.4 us (26%)
  local copies, waits for them, and re-layouts  6.5 us (7%)
    ppermute x14, starting transfers between devices, along_ring(): return lax.ppermute(block, 'fsdp', pairs)  24.3 us
    ppermute x14, waiting for transfers between devices, along_ring(): return lax.ppermute(block, 'fsdp', pairs)  21.2 us
    pallas_call x10, Pallas kernels, products(): pl.pallas_call(kernel, in_specs=[in_smem] + [in_vmem] * (count + 1 + len(...  15.6 us
    unnamed x22, local copies, waits for them, and re-layouts  6.5 us
    ppermute x2, starting transfers between devices, from_before(): return lax.ppermute(block, 'ctx', [(i - 1, i) for i in range(1, count)])  4.73 us
    pallas_call x2, Pallas kernels, far_part(): pl.pallas_call(kernel, in_specs=[in_vmem] * len(args), out_specs=in_vmem,...  3.96 us
    ppermute x2, waiting for transfers between devices, from_before(): return lax.ppermute(block, 'ctx', [(i - 1, i) for i in range(1, count)])  3.3 us
    ppermute x16, starting transfers between devices, other_core(): lax.ppermute(block, 'fsdp', [(i, i ^ 1) for i in range(2 * chip_count())])  2.7 us
  transfers between devices with their start and end apart: 32, of which 16 were waited for; matrix products, arithmetic and copies ran while one was open for 0% of the time, Pallas kernels for 19%

profile of v3, /device:TPU:0, one launch (start us, length us, event | category | flops | bytes accessed | tf_op | source)
XLA Modules:
  0.0 86.4 jit_solution(2346027228721121889)
XLA Ops:
  3.1 2.6 %collective-permute-start = (bf16[264,640]{1,0:T(8,128)(2,1)S(1)}, bf16[264,640]{1,0:T(8,128)(2,1)S(1)}, u32[]{:S(2)}, u32[]{:S(2)}) collective-permute-start(bf16[264,640]{1,0:T(8,128)(2,1)S(1)} %prepare.1.refs_0_), channel_id=1, source_target_pairs={{0,8},{10,2},{8,16},{18,10},{16,24},{26,18},{24,28},{30,26},{28,20... | collective-permute-start | bytes 1013768 | tf_op jit(solution)/shard_map/projection_near_1/ppermute | solution.py:80
  5.7 1.6 %collective-permute-start.5 = (bf16[264,640]{1,0:T(8,128)(2,1)S(1)}, bf16[264,640]{1,0:T(8,128)(2,1)S(1)}, u32[]{:S(2)}, u32[]{:S(2)}) collective-permute-start(bf16[264,640]{1,0:T(8,128)(2,1)S(1)} %collective-permute-done.4.refs_1_), channel_id=1, source_target_pairs={{0,8},{10,2},{8,16},{18,10},{16,24},{26,18},{24,28},{30,26},{28,20... | collective-permute-start | bytes 1013768 | tf_op jit(solution)/shard_map/projection_far_1/ppermute | solution.py:80
  10.8 2.1 %collective-permute-start.1 = (bf16[264,640]{1,0:T(8,128)(2,1)S(1)}, bf16[264,640]{1,0:T(8,128)(2,1)S(1)}, u32[]{:S(2)}, u32[]{:S(2)}) collective-permute-start(bf16[264,640]{1,0:T(8,128)(2,1)S(1)} %collective-permute-done.refs_2_), channel_id=1, source_target_pairs={{0,8},{10,2},{8,16},{18,10},{16,24},{26,18},{24,28},{30,26},{28,20... | collective-permute-start | bytes 1013768 | tf_op jit(solution)/shard_map/projection_near_2/ppermute | solution.py:80
  12.9 1.5 %collective-permute-done.5.refs_0_ = bf16[264,640]{1,0:T(8,128)(2,1)S(1)} collective-permute-done((bf16[264,640]{1,0:T(8,128)(2,1)S(1)}, bf16[264,640]{1,0:T(8,128)(2,1)S(1)}, u32[]{:S(2)}, u32[]{:S(2)}) %collective-permute-start.5) | collective-permute-done | bytes 337952 | tf_op jit(solution)/shard_map/projection_far_1/ppermute | solution.py:80
  14.4 2.1 %collective-permute-start.6 = (bf16[264,640]{1,0:T(8,128)(2,1)S(1)}, bf16[264,640]{1,0:T(8,128)(2,1)S(1)}, u32[]{:S(2)}, u32[]{:S(2)}) collective-permute-start(bf16[264,640]{1,0:T(8,128)(2,1)S(1)} %collective-permute-done.5.refs_0_), channel_id=1, source_target_pairs={{0,8},{10,2},{8,16},{18,10},{16,24},{26,18},{24,28},{30,26},{28,20... | collective-permute-start | bytes 1013768 | tf_op jit(solution)/shard_map/projection_far_2/ppermute | solution.py:80
  16.5 2.8 %copy-done = bf16[3,256,4096]{2,1,0:T(8,128)(2,1)S(1)} copy-done((bf16[3,256,4096]{2,1,0:T(8,128)(2,1)S(1)}, bf16[3,256,4096]{2,1,0:T(8,128)(2,1)}, u32[]{:S(2)}) %copy-start) | copy-done | bytes 6291480
  19.3 1.9 %projection_1.1 = (f32[3,256,640]{2,1,0:T(8,128)S(1)}, f32[8,640]{1,0:T(8,128)S(1)}) custom-call(s32[9]{0:T(128)S(1)} %pad_add_fusion.ids_ref, bf16[264,640]{1,0:T(8,128)(2,1)S(1)} %prepare.1.refs_0_, bf16[264,640]{1,0:T(8,128)(2,1)S(1)} %collective-permute-done.4.refs_1_, bf16[264,640]{1,0:T(8,128)(2,1)S(1)} %collective-permute-done.refs_2_, ...), custom_call_target="tpu_custom_call" | custom-call | tf_op jit(solution)/shard_map/projection_1/pallas_call | solution.py:161
  21.8 1.6 %collective-permute-start.2 = (bf16[264,640]{1,0:T(8,128)(2,1)S(1)}, bf16[264,640]{1,0:T(8,128)(2,1)S(1)}, u32[]{:S(2)}, u32[]{:S(2)}) collective-permute-start(bf16[264,640]{1,0:T(8,128)(2,1)S(1)} %collective-permute-done.1.refs_2_), channel_id=1, source_target_pairs={{0,8},{10,2},{8,16},{18,10},{16,24},{26,18},{24,28},{30,26},{28,20... | collective-permute-start | bytes 1013768 | tf_op jit(solution)/shard_map/projection_near_3/ppermute | solution.py:80
  23.4 1.6 %collective-permute-start.13 = (bf16[264,640]{1,0:T(8,128)(2,1)S(1)}, bf16[264,640]{1,0:T(8,128)(2,1)S(1)}, u32[]{:S(2)}, u32[]{:S(2)}) collective-permute-start(bf16[264,640]{1,0:T(8,128)(2,1)S(1)} %collective-permute-done.6.refs_0_), channel_id=1, source_target_pairs={{0,8},{10,2},{8,16},{18,10},{16,24},{26,18},{24,28},{30,26},{28,20... | collective-permute-start | bytes 1013768 | tf_op jit(solution)/shard_map/projection_far_3/ppermute | solution.py:80
  25.0 2.1 %projection_2.1 = (f32[3,256,640]{2,1,0:T(8,128)S(1)}, f32[8,640]{1,0:T(8,128)S(1)}) custom-call(s32[9]{0:T(128)S(1)} %pad_add_fusion.ids_ref, bf16[264,640]{1,0:T(8,128)(2,1)S(1)} %collective-permute-done.5.refs_0_, bf16[264,640]{1,0:T(8,128)(2,1)S(1)} %collective-permute-done.8.refs_1_, ...), custom_call_target="tpu_custom_call", output_to_operand_aliasing={{0}: (6, {}), {1}: (7, {})} | custom-call | tf_op jit(solution)/shard_map/projection_2/pallas_call | solution.py:161
  27.1 1.9 %collective-permute-done.2.refs_2_ = bf16[264,640]{1,0:T(8,128)(2,1)S(1)} collective-permute-done((bf16[264,640]{1,0:T(8,128)(2,1)S(1)}, bf16[264,640]{1,0:T(8,128)(2,1)S(1)}, u32[]{:S(2)}, u32[]{:S(2)}) %collective-permute-start.2) | collective-permute-done | bytes 337952 | tf_op jit(solution)/shard_map/projection_near_3/ppermute | solution.py:80
  29.5 1.6 %collective-permute-start.3 = (bf16[264,640]{1,0:T(8,128)(2,1)S(1)}, bf16[264,640]{1,0:T(8,128)(2,1)S(1)}, u32[]{:S(2)}, u32[]{:S(2)}) collective-permute-start(bf16[264,640]{1,0:T(8,128)(2,1)S(1)} %collective-permute-done.2.refs_2_), channel_id=1, source_target_pairs={{0,8},{10,2},{8,16},{18,10},{16,24},{26,18},{24,28},{30,26},{28,20... | collective-permute-start | bytes 1013768 | tf_op jit(solution)/shard_map/projection_near_4/ppermute | solution.py:80
  31.1 1.5 %collective-permute-done.13.refs_0_ = bf16[264,640]{1,0:T(8,128)(2,1)S(1)} collective-permute-done((bf16[264,640]{1,0:T(8,128)(2,1)S(1)}, bf16[264,640]{1,0:T(8,128)(2,1)S(1)}, u32[]{:S(2)}, u32[]{:S(2)}) %collective-permute-start.13) | collective-permute-done | bytes 337952 | tf_op jit(solution)/shard_map/projection_far_3/ppermute | solution.py:80
  32.7 2.1 %projection_3.1 = (f32[3,256,640]{2,1,0:T(8,128)S(1)}, f32[8,640]{1,0:T(8,128)S(1)}) custom-call(s32[9]{0:T(128)S(1)} %pad_add_fusion.ids_ref, bf16[264,640]{1,0:T(8,128)(2,1)S(1)} %collective-permute-done.6.refs_0_, bf16[264,640]{1,0:T(8,128)(2,1)S(1)} %collective-permute-done.7.refs_1_, ...), custom_call_target="tpu_custom_call", output_to_operand_aliasing={{0}: (6, {}), {1}: (7, {})} | custom-call | tf_op jit(solution)/shard_map/projection_3/pallas_call | solution.py:161
  34.8 1.9 %collective-permute-done.3.refs_0_ = bf16[264,640]{1,0:T(8,128)(2,1)S(1)} collective-permute-done((bf16[264,640]{1,0:T(8,128)(2,1)S(1)}, bf16[264,640]{1,0:T(8,128)(2,1)S(1)}, u32[]{:S(2)}, u32[]{:S(2)}) %collective-permute-start.3) | collective-permute-done | bytes 337952 | tf_op jit(solution)/shard_map/projection_near_4/ppermute | solution.py:80
  36.7 1.5 %projection_4.1 = (f32[3,256,640]{2,1,0:T(8,128)S(1)}, f32[8,640]{1,0:T(8,128)S(1)}) custom-call(s32[9]{0:T(128)S(1)} %pad_add_fusion.ids_ref, bf16[264,640]{1,0:T(8,128)(2,1)S(1)} %collective-permute-done.13.refs_0_, bf16[264,640]{1,0:T(8,128)(2,1)S(1)} %collective-permute-done.14.refs_1_, ...), custom_call_target="tpu_custom_call", output_to_operand_aliasing={{0}: (4, {}), {1}: (5, {})} | custom-call | flops 2000000000 | tf_op jit(solution)/shard_map/projection_4/pallas_call | solution.py:161
  38.4 1.9 %projection_last.1 = (bf16[3,256,640]{2,1,0:T(8,128)(2,1)S(1)}, bf16[136,640]{1,0:T(8,128)(2,1)S(1)}, bf16[136,640]{1,0:T(8,128)(2,1)S(1)}) custom-call(s32[9]{0:T(128)S(1)} %pad_add_fusion.ids_ref, bf16[264,640]{1,0:T(8,128)(2,1)S(1)} %collective-permute-done.3.refs_0_, bf16[264,640]{1,0:T(8,128)(2,1)S(1)} %collective-permute-done.12.refs_1_, ...), custom_call_target="tpu_custom_call" | custom-call | tf_op jit(solution)/shard_map/projection_last/pallas_call | solution.py:161
  40.3 3.4 %collective-permute-start.16 = (bf16[136,640]{1,0:T(8,128)(2,1)S(1)}, bf16[136,640]{1,0:T(8,128)(2,1)S(1)}, u32[]{:S(2)}, u32[]{:S(2)}) collective-permute-start(bf16[136,640]{1,0:T(8,128)(2,1)S(1)} %get-tuple-element.57.one_ref.refs_8_), channel_id=1, source_target_pairs={{0,1},{2,3},{4,5},{6,7},{8,9},{10,11},{12,13},{14,15},{16,17},{18,... | collective-permute-start | bytes 522248 | tf_op jit(solution)/shard_map/ppermute | solution.py:473
  46.4 2.1 %collective-permute-done.16.refs_0_ = bf16[136,640]{1,0:T(8,128)(2,1)S(1)} collective-permute-done((bf16[136,640]{1,0:T(8,128)(2,1)S(1)}, bf16[136,640]{1,0:T(8,128)(2,1)S(1)}, u32[]{:S(2)}, u32[]{:S(2)}) %collective-permute-start.16) | collective-permute-done | bytes 174112 | tf_op jit(solution)/shard_map/ppermute | solution.py:473
  48.5 2.0 %far_part_1_0.1.refs_10_ = bf16[256,640]{1,0:T(8,128)(2,1)S(1)} custom-call(bf16[136,640]{1,0:T(8,128)(2,1)S(1)} %collective-permute-done.16.refs_0_, f32[128,1280]{1,0:T(8,128)S(1)} %get-tuple-element.61.refs_1_, f32[256,2560]{1,0:T(8,128)S(1)} %filter_spectra.1.filters_ref.refs_2_, bf16[2,256,256]{2,1,0:T(8,128)(2,1)S(1)} %copy-done.4, ...), custom_call_target="tpu_custom_call" | custom-call | flops 400000000 | bytes 4000000 | tf_op jit(solution)/shard_map/far_part_1_0/pallas_call | solution.py:458
  51.6 2.0 %far_part_1_1.1.refs_0_ = bf16[256,640]{1,0:T(8,128)(2,1)S(1)} custom-call(bf16[136,640]{1,0:T(8,128)(2,1)S(1)} %collective-permute-done.15.refs_0_, f32[128,1280]{1,0:T(8,128)S(1)} %get-tuple-element.59.refs_1_, f32[256,2560]{1,0:T(8,128)S(1)} %filter_spectra.1.filters_ref.refs_2_, ...), custom_call_target="tpu_custom_call", output_to_operand_aliasing={{}: (10, {})} | custom-call | flops 400000000 | bytes 4000000 | tf_op jit(solution)/shard_map/far_part_1_1/pallas_call | solution.py:458
  53.7 1.6 %collective-permute-start.17 = (bf16[256,640]{1,0:T(8,128)(2,1)S(1)}, bf16[256,640]{1,0:T(8,128)(2,1)S(1)}, u32[]{:S(2)}, u32[]{:S(2)}) collective-permute-start(bf16[256,640]{1,0:T(8,128)(2,1)S(1)} %far_part_1_1.1.refs_0_), channel_id=1, source_target_pairs={{0,8},{10,2},{8,16},{18,10},{16,24},{26,18},{24,28},{30,26},{28,20... | collective-permute-start | bytes 983048 | tf_op jit(solution)/shard_map/output_near_1/ppermute | solution.py:80
  55.4 1.6 %collective-permute-start.22 = (bf16[256,640]{1,0:T(8,128)(2,1)S(1)}, bf16[256,640]{1,0:T(8,128)(2,1)S(1)}, u32[]{:S(2)}, u32[]{:S(2)}) collective-permute-start(bf16[256,640]{1,0:T(8,128)(2,1)S(1)} %collective-permute-done.21.refs_1_), channel_id=1, source_target_pairs={{0,8},{10,2},{8,16},{18,10},{16,24},{26,18},{24,28},{30,26},{28,20... | collective-permute-start | bytes 983048 | tf_op jit(solution)/shard_map/output_far_1/ppermute | solution.py:80
  56.9 3.9 %collective-permute-done.17.refs_2_ = bf16[256,640]{1,0:T(8,128)(2,1)S(1)} collective-permute-done((bf16[256,640]{1,0:T(8,128)(2,1)S(1)}, bf16[256,640]{1,0:T(8,128)(2,1)S(1)}, u32[]{:S(2)}, u32[]{:S(2)}) %collective-permute-start.17) | collective-permute-done | bytes 327712 | tf_op jit(solution)/shard_map/output_near_1/ppermute | solution.py:80
  60.8 1.6 %collective-permute-start.18 = (bf16[256,640]{1,0:T(8,128)(2,1)S(1)}, bf16[256,640]{1,0:T(8,128)(2,1)S(1)}, u32[]{:S(2)}, u32[]{:S(2)}) collective-permute-start(bf16[256,640]{1,0:T(8,128)(2,1)S(1)} %collective-permute-done.17.refs_2_), channel_id=1, source_target_pairs={{0,8},{10,2},{8,16},{18,10},{16,24},{26,18},{24,28},{30,26},{28,20... | collective-permute-start | bytes 983048 | tf_op jit(solution)/shard_map/output_near_2/ppermute | solution.py:80
  62.4 1.9 %collective-permute-done.22.refs_0_ = bf16[256,640]{1,0:T(8,128)(2,1)S(1)} collective-permute-done((bf16[256,640]{1,0:T(8,128)(2,1)S(1)}, bf16[256,640]{1,0:T(8,128)(2,1)S(1)}, u32[]{:S(2)}, u32[]{:S(2)}) %collective-permute-start.22) | collective-permute-done | bytes 327712 | tf_op jit(solution)/shard_map/output_far_1/ppermute | solution.py:80
  64.4 1.6 %collective-permute-start.23 = (bf16[256,640]{1,0:T(8,128)(2,1)S(1)}, bf16[256,640]{1,0:T(8,128)(2,1)S(1)}, u32[]{:S(2)}, u32[]{:S(2)}) collective-permute-start(bf16[256,640]{1,0:T(8,128)(2,1)S(1)} %collective-permute-done.22.refs_0_), channel_id=1, source_target_pairs={{0,8},{10,2},{8,16},{18,10},{16,24},{26,18},{24,28},{30,26},{28,20... | collective-permute-start | bytes 983048 | tf_op jit(solution)/shard_map/output_far_2/ppermute | solution.py:80
  68.4 1.6 %collective-permute-start.19 = (bf16[256,640]{1,0:T(8,128)(2,1)S(1)}, bf16[256,640]{1,0:T(8,128)(2,1)S(1)}, u32[]{:S(2)}, u32[]{:S(2)}) collective-permute-start(bf16[256,640]{1,0:T(8,128)(2,1)S(1)} %collective-permute-done.18.refs_2_), channel_id=1, source_target_pairs={{0,8},{10,2},{8,16},{18,10},{16,24},{26,18},{24,28},{30,26},{28,20... | collective-permute-start | bytes 983048 | tf_op jit(solution)/shard_map/output_near_3/ppermute | solution.py:80
  71.4 1.6 %collective-permute-start.30 = (bf16[256,640]{1,0:T(8,128)(2,1)S(1)}, bf16[256,640]{1,0:T(8,128)(2,1)S(1)}, u32[]{:S(2)}, u32[]{:S(2)}) collective-permute-start(bf16[256,640]{1,0:T(8,128)(2,1)S(1)} %collective-permute-done.23.refs_0_), channel_id=1, source_target_pairs={{0,8},{10,2},{8,16},{18,10},{16,24},{26,18},{24,28},{30,26},{28,20... | collective-permute-start | bytes 983048 | tf_op jit(solution)/shard_map/output_far_3/ppermute | solution.py:80
  76.0 1.6 %collective-permute-start.20 = (bf16[256,640]{1,0:T(8,128)(2,1)S(1)}, bf16[256,640]{1,0:T(8,128)(2,1)S(1)}, u32[]{:S(2)}, u32[]{:S(2)}) collective-permute-start(bf16[256,640]{1,0:T(8,128)(2,1)S(1)} %collective-permute-done.19.refs_2_), channel_id=1, source_target_pairs={{0,8},{10,2},{8,16},{18,10},{16,24},{26,18},{24,28},{30,26},{28,20... | collective-permute-start | bytes 983048 | tf_op jit(solution)/shard_map/output_near_4/ppermute | solution.py:80
  80.2 2.9 %collective-permute-done.20.refs_0_ = bf16[256,640]{1,0:T(8,128)(2,1)S(1)} collective-permute-done((bf16[256,640]{1,0:T(8,128)(2,1)S(1)}, bf16[256,640]{1,0:T(8,128)(2,1)S(1)}, u32[]{:S(2)}, u32[]{:S(2)}) %collective-permute-start.20) | collective-permute-done | bytes 327712 | tf_op jit(solution)/shard_map/output_near_4/ppermute | solution.py:80
  84.7 1.6 %output_last.1 = bf16[256,640]{1,0:T(8,128)(2,1)} custom-call(s32[9]{0:T(128)S(1)} %pad_add_fusion.ids_ref, bf16[256,640]{1,0:T(8,128)(2,1)S(1)} %collective-permute-done.20.refs_0_, bf16[256,640]{1,0:T(8,128)(2,1)S(1)} %collective-permute-done.29.refs_1_, bf16[1,256,4096]{2,1,0:T(8,128)(2,1)S(1)} %bitcast.9, f32[1,256,640]{2,1,0:T(8,128)S(1)} %output_4.1.refs_3_), custom_call_target="tpu_custom_call" | custom-call | tf_op jit(solution)/shard_map/output_last/pallas_call | solution.py:161
  (71 shorter events, 22.7 us)
Async XLA Ops:
  2.5 3.2 %collective-permute-start.4 = (bf16[264,640]{1,0:T(8,128)(2,1)S(1)}, bf16[264,640]{1,0:T(8,128)(2,1)S(1)}, u32[]{:S(2)}, u32[]{:S(2)}) collective-permute-start(bf16[264,640]{1,0:T(8,128)(2,1)S(1)} %prepare.1.refs_0_), channel_id=1, source_target_pairs={{0,2},{2,0},{4,6},{6,4},{8,10},{10,8},{12,14},{14,12},{16,18},{18,... | collective-permute-start | bytes 1013768 | tf_op jit(solution)/shard_map/projection_core_own/ppermute | solution.py:84
  3.1 7.7 %collective-permute-start = (bf16[264,640]{1,0:T(8,128)(2,1)S(1)}, bf16[264,640]{1,0:T(8,128)(2,1)S(1)}, u32[]{:S(2)}, u32[]{:S(2)}) collective-permute-start(bf16[264,640]{1,0:T(8,128)(2,1)S(1)} %prepare.1.refs_0_), channel_id=1, source_target_pairs={{0,8},{10,2},{8,16},{18,10},{16,24},{26,18},{24,28},{30,26},{28,20... | collective-permute-start | bytes 1013768 | tf_op jit(solution)/shard_map/projection_near_1/ppermute | solution.py:80
  5.7 8.7 %collective-permute-start.5 = (bf16[264,640]{1,0:T(8,128)(2,1)S(1)}, bf16[264,640]{1,0:T(8,128)(2,1)S(1)}, u32[]{:S(2)}, u32[]{:S(2)}) collective-permute-start(bf16[264,640]{1,0:T(8,128)(2,1)S(1)} %collective-permute-done.4.refs_1_), channel_id=1, source_target_pairs={{0,8},{10,2},{8,16},{18,10},{16,24},{26,18},{24,28},{30,26},{28,20... | collective-permute-start | bytes 1013768 | tf_op jit(solution)/shard_map/projection_far_1/ppermute | solution.py:80
  10.8 5.7 %collective-permute-start.9 = (bf16[264,640]{1,0:T(8,128)(2,1)S(1)}, bf16[264,640]{1,0:T(8,128)(2,1)S(1)}, u32[]{:S(2)}, u32[]{:S(2)}) collective-permute-start(bf16[264,640]{1,0:T(8,128)(2,1)S(1)} %collective-permute-done.refs_2_), channel_id=1, source_target_pairs={{0,2},{2,0},{4,6},{6,4},{8,10},{10,8},{12,14},{14,12},{16,18},{18,... | collective-permute-start | bytes 1013768 | tf_op jit(solution)/shard_map/projection_core_near_1/ppermute | solution.py:84
  10.8 10.4 %collective-permute-start.1 = (bf16[264,640]{1,0:T(8,128)(2,1)S(1)}, bf16[264,640]{1,0:T(8,128)(2,1)S(1)}, u32[]{:S(2)}, u32[]{:S(2)}) collective-permute-start(bf16[264,640]{1,0:T(8,128)(2,1)S(1)} %collective-permute-done.refs_2_), channel_id=1, source_target_pairs={{0,8},{10,2},{8,16},{18,10},{16,24},{26,18},{24,28},{30,26},{28,20... | collective-permute-start | bytes 1013768 | tf_op jit(solution)/shard_map/projection_near_2/ppermute | solution.py:80
  14.4 9.0 %collective-permute-start.6 = (bf16[264,640]{1,0:T(8,128)(2,1)S(1)}, bf16[264,640]{1,0:T(8,128)(2,1)S(1)}, u32[]{:S(2)}, u32[]{:S(2)}) collective-permute-start(bf16[264,640]{1,0:T(8,128)(2,1)S(1)} %collective-permute-done.5.refs_0_), channel_id=1, source_target_pairs={{0,8},{10,2},{8,16},{18,10},{16,24},{26,18},{24,28},{30,26},{28,20... | collective-permute-start | bytes 1013768 | tf_op jit(solution)/shard_map/projection_far_2/ppermute | solution.py:80
  21.3 3.7 %collective-permute-start.10 = (bf16[264,640]{1,0:T(8,128)(2,1)S(1)}, bf16[264,640]{1,0:T(8,128)(2,1)S(1)}, u32[]{:S(2)}, u32[]{:S(2)}) collective-permute-start(bf16[264,640]{1,0:T(8,128)(2,1)S(1)} %collective-permute-done.1.refs_2_), channel_id=1, source_target_pairs={{0,2},{2,0},{4,6},{6,4},{8,10},{10,8},{12,14},{14,12},{16,18},{18,... | collective-permute-start | bytes 1013768 | tf_op jit(solution)/shard_map/projection_core_near_2/ppermute | solution.py:84
  21.3 3.7 %collective-permute-start.8 = (bf16[264,640]{1,0:T(8,128)(2,1)S(1)}, bf16[264,640]{1,0:T(8,128)(2,1)S(1)}, u32[]{:S(2)}, u32[]{:S(2)}) collective-permute-start(bf16[264,640]{1,0:T(8,128)(2,1)S(1)} %collective-permute-done.5.refs_0_), channel_id=1, source_target_pairs={{0,2},{2,0},{4,6},{6,4},{8,10},{10,8},{12,14},{14,12},{16,18},{18,... | collective-permute-start | bytes 1013768 | tf_op jit(solution)/shard_map/projection_core_far_1/ppermute | solution.py:84
  21.8 7.2 %collective-permute-start.2 = (bf16[264,640]{1,0:T(8,128)(2,1)S(1)}, bf16[264,640]{1,0:T(8,128)(2,1)S(1)}, u32[]{:S(2)}, u32[]{:S(2)}) collective-permute-start(bf16[264,640]{1,0:T(8,128)(2,1)S(1)} %collective-permute-done.1.refs_2_), channel_id=1, source_target_pairs={{0,8},{10,2},{8,16},{18,10},{16,24},{26,18},{24,28},{30,26},{28,20... | collective-permute-start | bytes 1013768 | tf_op jit(solution)/shard_map/projection_near_3/ppermute | solution.py:80
  23.4 9.2 %collective-permute-start.13 = (bf16[264,640]{1,0:T(8,128)(2,1)S(1)}, bf16[264,640]{1,0:T(8,128)(2,1)S(1)}, u32[]{:S(2)}, u32[]{:S(2)}) collective-permute-start(bf16[264,640]{1,0:T(8,128)(2,1)S(1)} %collective-permute-done.6.refs_0_), channel_id=1, source_target_pairs={{0,8},{10,2},{8,16},{18,10},{16,24},{26,18},{24,28},{30,26},{28,20... | collective-permute-start | bytes 1013768 | tf_op jit(solution)/shard_map/projection_far_3/ppermute | solution.py:80
  29.0 3.6 %collective-permute-start.11 = (bf16[264,640]{1,0:T(8,128)(2,1)S(1)}, bf16[264,640]{1,0:T(8,128)(2,1)S(1)}, u32[]{:S(2)}, u32[]{:S(2)}) collective-permute-start(bf16[264,640]{1,0:T(8,128)(2,1)S(1)} %collective-permute-done.2.refs_2_), channel_id=1, source_target_pairs={{0,2},{2,0},{4,6},{6,4},{8,10},{10,8},{12,14},{14,12},{16,18},{18,... | collective-permute-start | bytes 1013768 | tf_op jit(solution)/shard_map/projection_core_near_3/ppermute | solution.py:84
  29.0 3.6 %collective-permute-start.7 = (bf16[264,640]{1,0:T(8,128)(2,1)S(1)}, bf16[264,640]{1,0:T(8,128)(2,1)S(1)}, u32[]{:S(2)}, u32[]{:S(2)}) collective-permute-start(bf16[264,640]{1,0:T(8,128)(2,1)S(1)} %collective-permute-done.6.refs_0_), channel_id=1, source_target_pairs={{0,2},{2,0},{4,6},{6,4},{8,10},{10,8},{12,14},{14,12},{16,18},{18,... | collective-permute-start | bytes 1013768 | tf_op jit(solution)/shard_map/projection_core_far_2/ppermute | solution.py:84
  29.5 7.2 %collective-permute-start.3 = (bf16[264,640]{1,0:T(8,128)(2,1)S(1)}, bf16[264,640]{1,0:T(8,128)(2,1)S(1)}, u32[]{:S(2)}, u32[]{:S(2)}) collective-permute-start(bf16[264,640]{1,0:T(8,128)(2,1)S(1)} %collective-permute-done.2.refs_2_), channel_id=1, source_target_pairs={{0,8},{10,2},{8,16},{18,10},{16,24},{26,18},{24,28},{30,26},{28,20... | collective-permute-start | bytes 1013768 | tf_op jit(solution)/shard_map/projection_near_4/ppermute | solution.py:80
  32.6 4.1 %collective-permute-start.14 = (bf16[264,640]{1,0:T(8,128)(2,1)S(1)}, bf16[264,640]{1,0:T(8,128)(2,1)S(1)}, u32[]{:S(2)}, u32[]{:S(2)}) collective-permute-start(bf16[264,640]{1,0:T(8,128)(2,1)S(1)} %collective-permute-done.13.refs_0_), channel_id=1, source_target_pairs={{0,2},{2,0},{4,6},{6,4},{8,10},{10,8},{12,14},{14,12},{16,18},{18,... | collective-permute-start | bytes 1013768 | tf_op jit(solution)/shard_map/projection_core_far_3/ppermute | solution.py:84
  36.7 1.6 %collective-permute-start.12 = (bf16[264,640]{1,0:T(8,128)(2,1)S(1)}, bf16[264,640]{1,0:T(8,128)(2,1)S(1)}, u32[]{:S(2)}, u32[]{:S(2)}) collective-permute-start(bf16[264,640]{1,0:T(8,128)(2,1)S(1)} %collective-permute-done.3.refs_0_), channel_id=1, source_target_pairs={{0,2},{2,0},{4,6},{6,4},{8,10},{10,8},{12,14},{14,12},{16,18},{18,... | collective-permute-start | bytes 1013768 | tf_op jit(solution)/shard_map/projection_core_near_4/ppermute | solution.py:84
  40.3 8.2 %collective-permute-start.16 = (bf16[136,640]{1,0:T(8,128)(2,1)S(1)}, bf16[136,640]{1,0:T(8,128)(2,1)S(1)}, u32[]{:S(2)}, u32[]{:S(2)}) collective-permute-start(bf16[136,640]{1,0:T(8,128)(2,1)S(1)} %get-tuple-element.57.one_ref.refs_8_), channel_id=1, source_target_pairs={{0,1},{2,3},{4,5},{6,7},{8,9},{10,11},{12,13},{14,15},{16,17},{18,... | collective-permute-start | bytes 522248 | tf_op jit(solution)/shard_map/ppermute | solution.py:473
  43.8 7.9 %collective-permute-start.15 = (bf16[136,640]{1,0:T(8,128)(2,1)S(1)}, bf16[136,640]{1,0:T(8,128)(2,1)S(1)}, u32[]{:S(2)}, u32[]{:S(2)}) collective-permute-start(bf16[136,640]{1,0:T(8,128)(2,1)S(1)} %get-tuple-element.55.two_ref.refs_8_), channel_id=1, source_target_pairs={{0,1},{2,3},{4,5},{6,7},{8,9},{10,11},{12,13},{14,15},{16,17},{18,... | collective-permute-start | bytes 522248 | tf_op jit(solution)/shard_map/ppermute | solution.py:473
  53.6 1.7 %collective-permute-start.21 = (bf16[256,640]{1,0:T(8,128)(2,1)S(1)}, bf16[256,640]{1,0:T(8,128)(2,1)S(1)}, u32[]{:S(2)}, u32[]{:S(2)}) collective-permute-start(bf16[256,640]{1,0:T(8,128)(2,1)S(1)} %far_part_1_1.1.refs_0_), channel_id=1, source_target_pairs={{0,2},{2,0},{4,6},{6,4},{8,10},{10,8},{12,14},{14,12},{16,18},{18,... | collective-permute-start | bytes 983048 | tf_op jit(solution)/shard_map/output_core_own/ppermute | solution.py:84
  53.7 7.1 %collective-permute-start.17 = (bf16[256,640]{1,0:T(8,128)(2,1)S(1)}, bf16[256,640]{1,0:T(8,128)(2,1)S(1)}, u32[]{:S(2)}, u32[]{:S(2)}) collective-permute-start(bf16[256,640]{1,0:T(8,128)(2,1)S(1)} %far_part_1_1.1.refs_0_), channel_id=1, source_target_pairs={{0,8},{10,2},{8,16},{18,10},{16,24},{26,18},{24,28},{30,26},{28,20... | collective-permute-start | bytes 983048 | tf_op jit(solution)/shard_map/output_near_1/ppermute | solution.py:80
  55.4 9.0 %collective-permute-start.22 = (bf16[256,640]{1,0:T(8,128)(2,1)S(1)}, bf16[256,640]{1,0:T(8,128)(2,1)S(1)}, u32[]{:S(2)}, u32[]{:S(2)}) collective-permute-start(bf16[256,640]{1,0:T(8,128)(2,1)S(1)} %collective-permute-done.21.refs_1_), channel_id=1, source_target_pairs={{0,8},{10,2},{8,16},{18,10},{16,24},{26,18},{24,28},{30,26},{28,20... | collective-permute-start | bytes 983048 | tf_op jit(solution)/shard_map/output_far_1/ppermute | solution.py:80
  60.8 5.1 %collective-permute-start.26 = (bf16[256,640]{1,0:T(8,128)(2,1)S(1)}, bf16[256,640]{1,0:T(8,128)(2,1)S(1)}, u32[]{:S(2)}, u32[]{:S(2)}) collective-permute-start(bf16[256,640]{1,0:T(8,128)(2,1)S(1)} %collective-permute-done.17.refs_2_), channel_id=1, source_target_pairs={{0,2},{2,0},{4,6},{6,4},{8,10},{10,8},{12,14},{14,12},{16,18},{18,... | collective-permute-start | bytes 983048 | tf_op jit(solution)/shard_map/output_core_near_1/ppermute | solution.py:84
  60.8 7.1 %collective-permute-start.18 = (bf16[256,640]{1,0:T(8,128)(2,1)S(1)}, bf16[256,640]{1,0:T(8,128)(2,1)S(1)}, u32[]{:S(2)}, u32[]{:S(2)}) collective-permute-start(bf16[256,640]{1,0:T(8,128)(2,1)S(1)} %collective-permute-done.17.refs_2_), channel_id=1, source_target_pairs={{0,8},{10,2},{8,16},{18,10},{16,24},{26,18},{24,28},{30,26},{28,20... | collective-permute-start | bytes 983048 | tf_op jit(solution)/shard_map/output_near_2/ppermute | solution.py:80
  64.4 7.1 %collective-permute-start.23 = (bf16[256,640]{1,0:T(8,128)(2,1)S(1)}, bf16[256,640]{1,0:T(8,128)(2,1)S(1)}, u32[]{:S(2)}, u32[]{:S(2)}) collective-permute-start(bf16[256,640]{1,0:T(8,128)(2,1)S(1)} %collective-permute-done.22.refs_0_), channel_id=1, source_target_pairs={{0,8},{10,2},{8,16},{18,10},{16,24},{26,18},{24,28},{30,26},{28,20... | collective-permute-start | bytes 983048 | tf_op jit(solution)/shard_map/output_far_2/ppermute | solution.py:80
  67.9 5.1 %collective-permute-start.27 = (bf16[256,640]{1,0:T(8,128)(2,1)S(1)}, bf16[256,640]{1,0:T(8,128)(2,1)S(1)}, u32[]{:S(2)}, u32[]{:S(2)}) collective-permute-start(bf16[256,640]{1,0:T(8,128)(2,1)S(1)} %collective-permute-done.18.refs_2_), channel_id=1, source_target_pairs={{0,2},{2,0},{4,6},{6,4},{8,10},{10,8},{12,14},{14,12},{16,18},{18,... | collective-permute-start | bytes 983048 | tf_op jit(solution)/shard_map/output_core_near_2/ppermute | solution.py:84
  67.9 5.1 %collective-permute-start.25 = (bf16[256,640]{1,0:T(8,128)(2,1)S(1)}, bf16[256,640]{1,0:T(8,128)(2,1)S(1)}, u32[]{:S(2)}, u32[]{:S(2)}) collective-permute-start(bf16[256,640]{1,0:T(8,128)(2,1)S(1)} %collective-permute-done.22.refs_0_), channel_id=1, source_target_pairs={{0,2},{2,0},{4,6},{6,4},{8,10},{10,8},{12,14},{14,12},{16,18},{18,... | collective-permute-start | bytes 983048 | tf_op jit(solution)/shard_map/output_core_far_1/ppermute | solution.py:84
  68.4 7.1 %collective-permute-start.19 = (bf16[256,640]{1,0:T(8,128)(2,1)S(1)}, bf16[256,640]{1,0:T(8,128)(2,1)S(1)}, u32[]{:S(2)}, u32[]{:S(2)}) collective-permute-start(bf16[256,640]{1,0:T(8,128)(2,1)S(1)} %collective-permute-done.18.refs_2_), channel_id=1, source_target_pairs={{0,8},{10,2},{8,16},{18,10},{16,24},{26,18},{24,28},{30,26},{28,20... | collective-permute-start | bytes 983048 | tf_op jit(solution)/shard_map/output_near_3/ppermute | solution.py:80
  71.4 7.6 %collective-permute-start.30 = (bf16[256,640]{1,0:T(8,128)(2,1)S(1)}, bf16[256,640]{1,0:T(8,128)(2,1)S(1)}, u32[]{:S(2)}, u32[]{:S(2)}) collective-permute-start(bf16[256,640]{1,0:T(8,128)(2,1)S(1)} %collective-permute-done.23.refs_0_), channel_id=1, source_target_pairs={{0,8},{10,2},{8,16},{18,10},{16,24},{26,18},{24,28},{30,26},{28,20... | collective-permute-start | bytes 983048 | tf_op jit(solution)/shard_map/output_far_3/ppermute | solution.py:80
  75.5 3.5 %collective-permute-start.28 = (bf16[256,640]{1,0:T(8,128)(2,1)S(1)}, bf16[256,640]{1,0:T(8,128)(2,1)S(1)}, u32[]{:S(2)}, u32[]{:S(2)}) collective-permute-start(bf16[256,640]{1,0:T(8,128)(2,1)S(1)} %collective-permute-done.19.refs_2_), channel_id=1, source_target_pairs={{0,2},{2,0},{4,6},{6,4},{8,10},{10,8},{12,14},{14,12},{16,18},{18,... | collective-permute-start | bytes 983048 | tf_op jit(solution)/shard_map/output_core_near_3/ppermute | solution.py:84
  75.5 3.5 %collective-permute-start.24 = (bf16[256,640]{1,0:T(8,128)(2,1)S(1)}, bf16[256,640]{1,0:T(8,128)(2,1)S(1)}, u32[]{:S(2)}, u32[]{:S(2)}) collective-permute-start(bf16[256,640]{1,0:T(8,128)(2,1)S(1)} %collective-permute-done.23.refs_0_), channel_id=1, source_target_pairs={{0,2},{2,0},{4,6},{6,4},{8,10},{10,8},{12,14},{14,12},{16,18},{18,... | collective-permute-start | bytes 983048 | tf_op jit(solution)/shard_map/output_core_far_2/ppermute | solution.py:84
  76.0 7.1 %collective-permute-start.20 = (bf16[256,640]{1,0:T(8,128)(2,1)S(1)}, bf16[256,640]{1,0:T(8,128)(2,1)S(1)}, u32[]{:S(2)}, u32[]{:S(2)}) collective-permute-start(bf16[256,640]{1,0:T(8,128)(2,1)S(1)} %collective-permute-done.19.refs_2_), channel_id=1, source_target_pairs={{0,8},{10,2},{8,16},{18,10},{16,24},{26,18},{24,28},{30,26},{28,20... | collective-permute-start | bytes 983048 | tf_op jit(solution)/shard_map/output_near_4/ppermute | solution.py:80
  79.0 4.1 %collective-permute-start.31 = (bf16[256,640]{1,0:T(8,128)(2,1)S(1)}, bf16[256,640]{1,0:T(8,128)(2,1)S(1)}, u32[]{:S(2)}, u32[]{:S(2)}) collective-permute-start(bf16[256,640]{1,0:T(8,128)(2,1)S(1)} %collective-permute-done.30.refs_0_), channel_id=1, source_target_pairs={{0,2},{2,0},{4,6},{6,4},{8,10},{10,8},{12,14},{14,12},{16,18},{18,... | collective-permute-start | bytes 983048 | tf_op jit(solution)/shard_map/output_core_far_3/ppermute | solution.py:84
  83.1 1.6 %collective-permute-start.29 = (bf16[256,640]{1,0:T(8,128)(2,1)S(1)}, bf16[256,640]{1,0:T(8,128)(2,1)S(1)}, u32[]{:S(2)}, u32[]{:S(2)}) collective-permute-start(bf16[256,640]{1,0:T(8,128)(2,1)S(1)} %collective-permute-done.20.refs_0_), channel_id=1, source_target_pairs={{0,2},{2,0},{4,6},{6,4},{8,10},{10,8},{12,14},{14,12},{16,18},{18,... | collective-permute-start | bytes 983048 | tf_op jit(solution)/shard_map/output_core_near_4/ppermute | solution.py:84
  (11 other events, 41.7 us)

commit v4 on v3

v4 whole, which is shorter than its diff:
```python
import math

import jax
import jax.numpy as jnp
import numpy as np
from jax import lax
from jax.experimental import pallas as pl
from jax.experimental.pallas import tpu as pltpu
from jax.sharding import PartitionSpec as P

epsilon = 1e-05
block_len = 128
STAGGER = 2e9
side_rows = 8
bf16 = jnp.bfloat16
f32 = jnp.float32
in_vmem = pl.BlockSpec(memory_space=pltpu.VMEM)
in_smem = pl.BlockSpec(memory_space=pltpu.SMEM)
params = pltpu.CompilerParams(vmem_limit_bytes=12 * 2**20)


def shape_of(shape, dtype):
    return jax.ShapeDtypeStruct(tuple(shape), dtype)


def dot(left, right):
    return jnp.dot(left, right, preferred_element_type=f32)


def column(row):
    return jnp.broadcast_to(row, (8, row.shape[1])).T[:, :1]


def tap_columns(taps):
    return jnp.concatenate([taps, jnp.zeros((8 - taps.shape[0], taps.shape[1]), f32)], axis=0).T


def estimate(flops, size):
    return pl.CostEstimate(flops=int(flops), bytes_accessed=int(size), transcendentals=0)


def prepare_kernel(ids_ref, x_ref, gain_ref, out_ref):
    rows = x_ref.shape[0]
    wide = x_ref[...].astype(f32)
    out_ref[:rows] = (wide * column(gain_ref[...])).astype(bf16)
    squares = jnp.sum(wide * wide, axis=0, keepdims=True)
    high = squares.astype(bf16).astype(f32)
    row = lax.broadcasted_iota(jnp.int32, (side_rows, wide.shape[1]), 0)
    side = jnp.where(row == 0, high, jnp.where(row == 1, squares - high, 0.0))
    out_ref[rows:] = side.astype(bf16)


def prepare(ids, x, gain):
    rows, tokens = x.shape
    return pl.pallas_call(
        prepare_kernel,
        in_specs=[in_smem, in_vmem, in_vmem],
        out_specs=in_vmem,
        out_shape=shape_of((rows + side_rows, tokens), bf16),
        compiler_params=params,
        cost_estimate=estimate(3e9, 0),
        name="prepare",
    )(ids, x, gain.reshape(1, rows))


def chip_count():
    return lax.axis_size("fsdp") // 2


def ring_order(count):
    return list(range(0, count, 2)) + list(range(1, count, 2))[::-1]


def along_ring(block):
    chips = chip_count()
    order = ring_order(chips)
    pairs = []
    for i in range(chips):
        here, after = order[i], order[(i + 1) % chips]
        pairs += [(2 * here, 2 * after), (2 * after + 1, 2 * here + 1)]
    return lax.ppermute(block, "fsdp", pairs)


def other_core(block):
    return lax.ppermute(block, "fsdp", [(i, i ^ 1) for i in range(2 * chip_count())])


def ring_ids():
    chips = chip_count()
    me = lax.axis_index("fsdp")
    chip, core = me // 2, me % 2
    place = jnp.where(chip % 2 == 0, chip // 2, chips - 1 - chip // 2)
    steps = jnp.arange(chips, dtype=jnp.int32)
    places = (place + jnp.where(core == 0, chips - steps, steps)) % chips
    ids = jnp.where(places < (chips + 1) // 2, 2 * places, 2 * (chips - 1 - places) + 1)
    mine = jnp.stack([core, lax.axis_index("ctx")])
    return jnp.concatenate([ids, mine]).astype(jnp.int32)


def core_of(ids_ref):
    return ids_ref[ids_ref.shape[0] - 2]


def turn_of(ids_ref):
    return ids_ref[ids_ref.shape[0] - 1]


def products(ids, items, weight, running, side, finish, cost, name, cut=(0, 1)):
    streams, out_rows, features = weight.shape
    out_rows //= cut[1]
    out_here = slice(cut[0] * out_rows, (cut[0] + 1) * out_rows)
    rows = features // lax.axis_size("fsdp")
    shards = [shard for _, _, shard in items]
    tokens = shards[0].shape[1]
    count = len(shards)
    first_group = running is None
    state = [] if first_group else list(running)
    body, extras, out_shape = finish if finish else (None, [], None)
    padded = rows % 128 != 0
    width = 2 * rows if padded else rows
    scratch_shapes = [pltpu.VMEM((count * width, tokens), bf16)] if padded else []

    def kernel(ids_ref, *refs):
        refs = list(refs)
        take = lambda n: [refs.pop(0) for _ in range(n)]
        shard_refs = take(count)
        (weight_ref,) = take(1)
        state_refs = take(len(state))
        extra_refs = take(len(extras))
        outs = take(len(out_shape))
        core = core_of(ids_ref)
        if padded:
            (beside_ref,) = refs
            beside_ref[...] = jnp.zeros(beside_ref.shape, bf16)
            for k, (_, other, _) in enumerate(items):
                at = k * width + jnp.where(core == other, 0, rows)
                beside_ref[pl.ds(pl.multiple_of(at, rows), rows)] = shard_refs[k][:rows]
            right = beside_ref[...]
        else:
            right = jnp.concatenate([ref[:rows] for ref in shard_refs], axis=0)
        side_sum = None
        if side:
            parts = [ref[rows:].astype(f32) for ref in shard_refs]
            parts += [] if first_group else [state_refs[1][...]]
            side_sum = sum(parts[1:], parts[0])

        def total(stream):
            left = []
            for slot, other, _ in items:
                block = ids_ref[slot]
                if not padded:
                    block = 2 * block + (1 - core if other else core)
                at = pl.ds(pl.multiple_of(block * width, width), width)
                left.append(weight_ref[stream, out_here, at])
            product = dot(jnp.concatenate(left, axis=1), right)
            return product if first_group else state_refs[0][stream, out_here] + product

        if body is not None:
            body(total, side_sum, extra_refs, outs)
            return
        for stream in range(streams):
            outs[0][stream] = total(stream)
        if side:
            outs[1][...] = side_sum

    aliases = {}
    if body is None:
        out_shape = [shape_of((streams, out_rows, tokens), f32)]
        if side:
            out_shape.append(shape_of((side_rows, tokens), f32))
        if not first_group:
            aliases = {1 + count + 1 + i: i for i in range(len(state))}
    return pl.pallas_call(
        kernel,
        in_specs=[in_smem] + [in_vmem] * (count + 1 + len(state) + len(extras)),
        out_specs=[in_vmem] * len(out_shape),
        out_shape=out_shape,
        scratch_shapes=scratch_shapes,
        input_output_aliases=aliases,
        compiler_params=params,
        cost_estimate=estimate(cost, 0),
        name=name,
    )(ids, *shards, weight, *state, *extras)


def gather_products(ids, own, weight, beside, side, finish, name):
    chips = chip_count()
    last_step = chips // 2

    def send(way, block, scope):
        with jax.named_scope(f"{name}_{scope}"):
            return way(block)

    near, far = own, send(other_core, own, "core_own")
    items = [(0, 0, near), (0, 1, far)]
    running = None
    for step in range(1, last_step + 1):
        near = send(along_ring, near, f"near_{step}")
        arrived = near
        if running is not None:
            arrived, *running = lax.optimization_barrier((near, *running))
        elif beside:
            arrived, *beside = lax.optimization_barrier((near, *beside))
        theirs = send(other_core, arrived, f"core_near_{step}")
        pair = [(step, 0, arrived), (chips - step, 1, theirs)]
        if step < last_step:
            running = products(ids, items + pair, weight, running, side, None, 0, f"{name}_{step}")
            far = send(along_ring, far, f"far_{step}")
            theirs = send(other_core, far, f"core_far_{step}")
            items = [(step, 1, far), (chips - step, 0, theirs)]
        else:
            running = products(ids, items, weight, running, side, None, STAGGER, f"{name}_{step}")
            items = pair
    results = [
        products(ids, items, weight, running, side, end, 0, f"{name}_last_{k}", (k, len(finish)))
        for k, end in enumerate(finish)
    ]
    return results, beside


def smooth(projected, taps, count, halo):
    lane = lax.broadcasted_iota(jnp.int32, projected.shape, 1)
    out = taps[:, :1] * projected
    for tap in range(1, count):
        moved = pltpu.roll(projected, tap, 1)
        for place in range(tap):
            edge = 0.0
            if halo is not None:
                at = halo.shape[1] - tap + place
                edge = halo[:, at : at + 1]
            moved = jnp.where(lane == place, edge, moved)
        out = out + taps[:, tap : tap + 1] * moved
    return out


def channel_parts(channels):
    return [(0, channels // 2), (channels // 2, channels // 2)]


def projection_finish(features, w_short, tokens, half_index):
    streams, count, channels = w_short.shape
    half = channels // 2
    begin = half_index * half
    parts = [part for part in channel_parts(channels) if begin <= part[0] < begin + half]

    def body(total, side_sum, extra_refs, outs):
        (taps_ref,) = extra_refs
        projected_ref, *message_refs = outs
        mean = jnp.sum(side_sum, axis=0, keepdims=True) * (1.0 / features)
        factor = lax.rsqrt(mean + epsilon)
        tails = []
        for stream in range(streams):
            projected = (total(stream) * factor).astype(bf16)
            projected_ref[stream] = projected
            tail = projected[:, tokens - block_len :].astype(f32).T
            tails.append(tail[block_len - count + 1 :])
        tails.append(jnp.zeros((side_rows - streams * (count - 1), half), f32))
        side = jnp.concatenate(tails, axis=0)
        taps = [tap_columns(taps_ref[stream]) for stream in (1, 2)]
        for (first, rows), message_ref in zip(parts, message_refs):
            tile = min(rows, 64)
            for start in range(first, first + rows, tile):
                here = slice(start - begin, start - begin + tile)
                key, value = (
                    smooth(
                        projected_ref[s, here].astype(f32),
                        taps[s - 1][start : start + tile],
                        count,
                        None,
                    )
                    for s in (1, 2)
                )
                message_ref[start - first : start - first + tile] = (key * value).astype(bf16)
            message_ref[rows:] = jnp.zeros((side_rows, tokens), bf16)
            here = side[:, first - begin : first - begin + rows]
            message_ref[rows:, :rows] = here.astype(bf16)

    out_shape = [shape_of((streams, half, tokens), bf16)]
    out_shape += [shape_of((rows + side_rows, tokens), bf16) for _, rows in parts]
    return body, [w_short], out_shape


def halo_columns(message_ref, streams, count, inside):
    rows = message_ref.shape[0] - side_rows
    side = jnp.where(inside, message_ref[rows:, :rows].astype(f32), 0.0).T
    return [side[:, s * (count - 1) : (s + 1) * (count - 1)] for s in range(streams)]


def split_table(table):
    high = table.astype(bf16)
    return high, (table - high.astype(np.float64)).astype(bf16)


def dft_tables():
    size = 2 * block_len
    freq = np.arange(block_len) + 0.5
    angle = 2.0 * math.pi / size * np.arange(size)[:, None] * freq[None, :]
    high, low = split_table(np.concatenate([np.cos(angle), -np.sin(angle)], axis=1))
    block = np.concatenate([high[:block_len], low[:block_len]])
    segment = np.concatenate([high, low])
    back = angle[block_len:].T
    inverse = np.concatenate([np.cos(back), -np.sin(back)], axis=0) * (2.0 / size)
    high, low = split_table(inverse)
    return block, segment, np.concatenate([high, low], axis=1)


def spectrum_lanes(k):
    return slice(2 * k * block_len, 2 * (k + 1) * block_len)


def block_lanes(k):
    return slice(k * block_len, (k + 1) * block_len)


def filter_spectra(long_filter, table):
    channels, lags = long_filter.shape

    def kernel(filter_ref, table_ref, spectra_ref):
        before = jnp.zeros((channels, block_len), bf16)
        for k in range(lags // block_len):
            now = filter_ref[:, block_lanes(k)]
            segment = jnp.concatenate([before, now, before, now], axis=1)
            spectra_ref[:, spectrum_lanes(k)] = dot(segment, table_ref[...])
            before = now

    return pl.pallas_call(
        kernel,
        in_specs=[in_vmem, in_vmem],
        out_specs=in_vmem,
        out_shape=shape_of((channels, 2 * lags), f32),
        compiler_params=params,
        cost_estimate=estimate(6e9, 0),
        name="filter_spectra",
    )(long_filter, table)


def block_spectra(pieces, table_ref, spec_ref, first):
    rows = pieces[0].shape[0]
    stacked = jnp.concatenate(pieces, axis=0)
    spectra = dot(jnp.concatenate([stacked, stacked], axis=1), table_ref[...])
    for k in range(len(pieces)):
        spec_ref[:rows, spectrum_lanes(first + k)] = spectra[k * rows : (k + 1) * rows]


def multiply_spectra(source_ref, filters_ref, filter_start, pairs, before_ref, total_ref):
    def one_tile(i, carry):
        here = pl.ds(pl.multiple_of(i * 8, 8), 8)
        there = pl.ds(pl.multiple_of(filter_start + i * 8, 8), 8)

        def parts(ref, rows, k):
            start = 2 * k * block_len
            return (
                ref[rows, start : start + block_len],
                ref[rows, start + block_len : start + 2 * block_len],
            )

        used = [term for terms in pairs for term in terms]
        sources = {b: parts(source_ref, here, b) for b in sorted({b for b, _ in used})}
        filters = {d: parts(filters_ref, there, d) for d in sorted({d for _, d in used})}
        for a, terms in enumerate(pairs):
            real = imag = None
            if before_ref is not None:
                real, imag = parts(before_ref, here, a)
            for b, d in terms:
                gr, gi = sources[b]
                hr, hi = filters[d]
                more_real, more_imag = gr * hr - gi * hi, gr * hi + gi * hr
                real = more_real if real is None else real + more_real
                imag = more_imag if imag is None else imag + more_imag
            if real is None:
                real = imag = jnp.zeros((8, block_len), f32)
            start = 2 * a * block_len
            total_ref[here, start : start + block_len] = real
            total_ref[here, start + block_len : start + 2 * block_len] = imag
        return carry

    lax.fori_loop(0, total_ref.shape[0] // 8, one_tile, 0)


def own_part(ids, projected, messages, moved, taps, filters, table):
    streams, half, tokens = projected[0].shape
    parts = channel_parts(2 * half)
    number = len(parts)
    count = taps.shape[1]
    blocks = tokens // block_len
    first = 0 if moved else 1
    pairs = [[(b, a - b) for b in range(first, a + 1)] for a in range(blocks)]

    def kernel(ids_ref, *refs):
        refs = list(refs)
        take = lambda n: [refs.pop(0) for _ in range(n)]
        projected_refs, message_refs = take(2), take(number)
        taps_ref, filters_ref, table_ref = take(3)
        query_refs, total_refs = take(number), take(number)
        gated_refs = take(number) if moved else None
        (spec_ref,) = refs
        columns = [tap_columns(taps_ref[s]) for s in range(streams)]
        for part, (begin, rows) in enumerate(parts):
            if moved:
                inside = turn_of(ids_ref) > 0
                halo = halo_columns(message_refs[part], streams, count, inside)
            tile = min(rows, 64)
            for start in range(0, rows, tile):
                here = slice(start, start + tile)
                there = slice(begin + start, begin + start + tile)
                in_half = (begin + start) % half
                projected_ref = projected_refs[begin // half]

                def smoothed(s):
                    edge = halo[s][here] if moved else None
                    wide = projected_ref[s, in_half : in_half + tile].astype(f32)
                    return smooth(wide, columns[s][there], count, edge)

                query_refs[part][here] = smoothed(0)
                if moved:
                    gated_refs[part][here] = (smoothed(1) * smoothed(2)).astype(bf16)
            source_ref = gated_refs[part] if moved else message_refs[part]
            pieces = [source_ref[:rows, block_lanes(b)] for b in range(first, blocks)]
            block_spectra(pieces, table_ref, spec_ref, first)
            multiply_spectra(spec_ref, filters_ref, begin, pairs, None, total_refs[part])

    out_shape = [shape_of((rows, tokens), f32) for _, rows in parts]
    out_shape += [shape_of((rows, 2 * tokens), f32) for _, rows in parts]
    if moved:
        out_shape += [shape_of((rows, tokens), bf16) for _, rows in parts]
    inputs = [*projected, *(moved or messages), taps, filters, table]
    outs = pl.pallas_call(
        kernel,
        in_specs=[in_smem] + [in_vmem] * len(inputs),
        out_specs=[in_vmem] * len(out_shape),
        out_shape=out_shape,
        scratch_shapes=[pltpu.VMEM((half, 2 * tokens), f32)],
        compiler_params=params,
        cost_estimate=estimate(0, 0),
        name="own_part",
    )(ids, *inputs)
    gated = list(outs[2 * number :]) if moved else messages
    return list(outs[:number]), list(outs[number : 2 * number]), gated


def far_part(ids, turn, begin, moved, total, filters, table, last, own):
    rows, tokens = total.shape[0], moved.shape[1]
    blocks = tokens // block_len
    pairs = [[(b, turn * blocks + a - b) for b in range(blocks)] for a in range(blocks)]
    if own:
        pairs = [terms + [(blocks, a)] for a, terms in enumerate(pairs)]
    channels_here = slice(begin, begin + rows)

    def kernel(ids_ref, *refs):
        refs = list(refs)
        take = lambda n: [refs.pop(0) for _ in range(n)]
        moved_ref, total_ref, filters_ref, table_ref = take(4)
        own_refs = take(2) if own else None
        spec_ref = refs.pop()
        inside = turn_of(ids_ref) >= turn
        pieces = [
            jnp.where(inside, moved_ref[:rows, block_lanes(b)], jnp.zeros((), bf16))
            for b in range(blocks)
        ]
        if last is None:
            block_spectra(pieces, table_ref, spec_ref, 0)
            multiply_spectra(spec_ref, filters_ref, begin, pairs, total_ref, refs[0])
            return
        sum_ref = refs.pop()
        back_ref, query_ref, gated_ref, skip_ref = take(4)
        out_ref = refs[-1]
        query, gated = (
            [ref[:rows, block_lanes(a)] for a in range(blocks)] for ref in (query_ref, gated_ref)
        )
        if own:
            projected_ref, taps_ref = own_refs
            streams, count, _ = taps_ref.shape
            halo = halo_columns(moved_ref, streams, count, inside)
            in_half = begin % projected_ref.shape[1]
            smoothed = []
            for s in range(streams):
                columns = tap_columns(taps_ref[s])[channels_here]
                wide = projected_ref[s, in_half : in_half + rows, :block_len].astype(f32)
                smoothed.append(smooth(wide, columns, count, halo[s]))
            query[0] = smoothed[0]
            gated[0] = (smoothed[1] * smoothed[2]).astype(bf16)
            pieces.append(gated[0])
        block_spectra(pieces, table_ref, spec_ref, 0)
        multiply_spectra(spec_ref, filters_ref, begin, pairs, total_ref, sum_ref)
        skip = column(skip_ref[...])[channels_here]
        spectra = [sum_ref[:, spectrum_lanes(a)] for a in range(blocks)]
        highs = [spectrum.astype(bf16) for spectrum in spectra]
        lows = [(s - high.astype(f32)).astype(bf16) for s, high in zip(spectra, highs)]
        both = dot(jnp.concatenate(highs, axis=0), back_ref[...])
        small = dot(jnp.concatenate(lows, axis=0), back_ref[:, :block_len])
        filtered = both[:, :block_len] + (both[:, block_len:] + small)
        for a in range(blocks):
            here = filtered[a * rows : (a + 1) * rows]
            mixed = query[a] * (here + skip * gated[a].astype(f32))
            out_ref[channels_here, block_lanes(a)] = mixed.astype(bf16)

    args = [moved, total, filters, table]
    if own:
        args += list(own)
    aliases = {}
    scratch = [pltpu.VMEM((rows, 2 * (blocks + 1) * block_len), f32)]
    out_shape = shape_of((rows, 2 * tokens), f32)
    if last is not None:
        inverse, query, gated, skip, mixed = last
        channels = skip.shape[0]
        args += [inverse, query, gated, skip.reshape(1, channels)]
        if mixed is not None:
            aliases = {1 + len(args): 0}
            args.append(mixed)
        out_shape = shape_of((channels, tokens), bf16)
        scratch.append(pltpu.VMEM((rows, 2 * tokens), f32))
    return pl.pallas_call(
        kernel,
        in_specs=[in_smem] + [in_vmem] * len(args),
        out_specs=in_vmem,
        out_shape=out_shape,
        scratch_shapes=scratch[::-1],
        input_output_aliases=aliases,
        compiler_params=params,
        cost_estimate=estimate(0, 0),
        name=f"far_part_{turn}_{begin}",
    )(ids, *args)


def from_before(block):
    count = lax.axis_size("ctx")
    return lax.ppermute(block, "ctx", [(i, (i + 1) % count) for i in range(count)])


def output_finish(channels, tokens):
    def body(total, side_sum, extra_refs, outs):
        outs[0][...] = total(0).astype(bf16)

    return body, [], [shape_of((channels, tokens), bf16)]


def shards(activations, norm_gain, w_in, w_short, long_filter, skip_gain, w_out):
    channels, tokens = activations.shape
    features = w_in.shape[2]
    w_short = w_short.transpose(0, 2, 1)
    turns = lax.axis_size("ctx")
    parts = channel_parts(channels)
    forward, segments, inverse = (jnp.asarray(t) for t in dft_tables())
    ids = ring_ids()
    own = prepare(ids, activations, norm_gain)

    filters = filter_spectra(long_filter, segments)
    finish = [projection_finish(features, w_short, tokens, k) for k in range(2)]
    results, (filters,) = gather_products(ids, own, w_in, [filters], True, finish, "projection")
    projected = [result[0] for result in results]
    messages = [message for result in results for message in result[1:]]
    moving = [from_before(message) for message in messages]
    exact = turns > 2
    query, totals, gated = own_part(
        ids, projected, messages, moving if exact else None, w_short, filters, forward
    )
    if exact:
        moving = [from_before(part) for part in gated]
    mixed = None
    for turn in range(1, turns):
        for k, (begin, _) in enumerate(parts):
            last = own_block = None
            if turn == turns - 1:
                last = (inverse, query[k], gated[k], skip_gain, mixed)
                if not exact:
                    own_block = (projected[2 * begin // channels], w_short)
            done = far_part(
                ids, turn, begin, moving[k], totals[k], filters, forward, last, own_block
            )
            if last is None:
                totals[k] = done
                moving[k] = from_before(moving[k])
            else:
                mixed = done

    finish = [output_finish(channels, tokens)]
    ((result,),), _ = gather_products(ids, mixed, w_out[None], [], False, finish, "output")
    return result


def solution(mesh):
    placed = (
        P("fsdp", "ctx"),
        P("fsdp"),
        P(None, "fsdp", None),
        P(None, "fsdp", None),
        P("fsdp", None),
        P("fsdp"),
        P("fsdp", None),
    )
    return jax.shard_map(
        shards, mesh=mesh, in_specs=placed, out_specs=P("fsdp", "ctx"), check_vma=False
    )
```

time: 86.7 us -> 82.8 us (0.955)
  local copies, waits for them, and re-layouts: 6.5 us -> 1.69 us
  starting transfers between devices: 31.7 us -> 29.5 us
  Pallas kernels: 22.4 us -> 24.5 us
  waiting for transfers between devices: 25.4 us -> 26.6 us
    unnamed x22, local copies, waits for them, and re-layouts: 6.5 us -> 1.69 us
    ppermute x2, starting transfers between devices: 4.73 us -> 2.16 us  [from_before(): lax.ppermute(block, 'ctx', [(i, (i + 1) % count) for i in range(count)])]
    ppermute x14, waiting for transfers between devices: 21.2 us -> 22.9 us  [along_ring(): return lax.ppermute(block, 'fsdp', pairs)]
    pallas_call x3, Pallas kernels: 5.21 us -> 6.57 us  [the longest x2 4.85 us: far_part(): pl.pallas_call(kernel, in_specs=[in_smem] + [in_vmem] * len(args), out_sp...]
    pallas_call x10 -> x11, Pallas kernels: 15.6 us -> 16.3 us  [products(): pl.pallas_call(kernel, in_specs=[in_smem] + [in_vmem] * (count + 1 + len(...]
  transfers between devices with their start and end apart: 32 -> 32, of which waited for: 16 -> 17; matrix products, arithmetic and copies ran while one was open for 0% -> 0% of each run, Pallas kernels for 19% -> 22%
where the time goes in v4:
time: 82.8 us; the launch traced here: 82.6 us
  starting transfers between devices  29.5 us (36%)
  waiting for transfers between devices  26.6 us (32%)
  Pallas kernels  24.5 us (30%)
  local copies, waits for them, and re-layouts  1.69 us (2%)
    ppermute x14, starting transfers between devices, along_ring(): return lax.ppermute(block, 'fsdp', pairs)  24.7 us
    ppermute x14, waiting for transfers between devices, along_ring(): return lax.ppermute(block, 'fsdp', pairs)  22.9 us
    pallas_call x11, Pallas kernels, products(): pl.pallas_call(kernel, in_specs=[in_smem] + [in_vmem] * (count + 1 + len(...  16.3 us
    pallas_call x2, Pallas kernels, far_part(): pl.pallas_call(kernel, in_specs=[in_smem] + [in_vmem] * len(args), out_sp...  4.85 us
    ppermute x2, waiting for transfers between devices, from_before(): lax.ppermute(block, 'ctx', [(i, (i + 1) % count) for i in range(count)])  2.81 us
    ppermute x16, starting transfers between devices, other_core(): lax.ppermute(block, 'fsdp', [(i, i ^ 1) for i in range(2 * chip_count())])  2.7 us
    ppermute x2, starting transfers between devices, from_before(): lax.ppermute(block, 'ctx', [(i, (i + 1) % count) for i in range(count)])  2.16 us
    pallas_call x1, Pallas kernels, own_part(): pl.pallas_call(kernel, in_specs=[in_smem] + [in_vmem] * len(inputs), out_...  1.71 us
  transfers between devices with their start and end apart: 32, of which 17 were waited for; matrix products, arithmetic and copies ran while one was open for 0% of the time, Pallas kernels for 22%

profile of v4, /device:TPU:0, one launch (start us, length us, event | category | flops | bytes accessed | tf_op | source)
XLA Modules:
  0.0 82.6 jit_solution(10269731143379140924)
XLA Ops:
  3.1 2.6 %collective-permute-start = (bf16[264,640]{1,0:T(8,128)(2,1)S(1)}, bf16[264,640]{1,0:T(8,128)(2,1)S(1)}, u32[]{:S(2)}, u32[]{:S(2)}) collective-permute-start(bf16[264,640]{1,0:T(8,128)(2,1)S(1)} %prepare.1.refs_0_), channel_id=1, source_target_pairs={{0,8},{10,2},{8,16},{18,10},{16,24},{26,18},{24,28},{30,26},{28,20... | collective-permute-start | bytes 1013768 | tf_op jit(solution)/shard_map/projection_near_1/ppermute | solution.py:81
  5.7 1.6 %collective-permute-start.5 = (bf16[264,640]{1,0:T(8,128)(2,1)S(1)}, bf16[264,640]{1,0:T(8,128)(2,1)S(1)}, u32[]{:S(2)}, u32[]{:S(2)}) collective-permute-start(bf16[264,640]{1,0:T(8,128)(2,1)S(1)} %collective-permute-done.4.refs_1_), channel_id=1, source_target_pairs={{0,8},{10,2},{8,16},{18,10},{16,24},{26,18},{24,28},{30,26},{28,20... | collective-permute-start | bytes 1013768 | tf_op jit(solution)/shard_map/projection_far_1/ppermute | solution.py:81
  8.2 2.7 %collective-permute-done.refs_2_ = bf16[264,640]{1,0:T(8,128)(2,1)S(1)} collective-permute-done((bf16[264,640]{1,0:T(8,128)(2,1)S(1)}, bf16[264,640]{1,0:T(8,128)(2,1)S(1)}, u32[]{:S(2)}, u32[]{:S(2)}) %collective-permute-start) | collective-permute-done | bytes 337952 | tf_op jit(solution)/shard_map/projection_near_1/ppermute | solution.py:81
  10.8 2.1 %collective-permute-start.1 = (bf16[264,640]{1,0:T(8,128)(2,1)S(1)}, bf16[264,640]{1,0:T(8,128)(2,1)S(1)}, u32[]{:S(2)}, u32[]{:S(2)}) collective-permute-start(bf16[264,640]{1,0:T(8,128)(2,1)S(1)} %collective-permute-done.refs_2_), channel_id=1, source_target_pairs={{0,8},{10,2},{8,16},{18,10},{16,24},{26,18},{24,28},{30,26},{28,20... | collective-permute-start | bytes 1013768 | tf_op jit(solution)/shard_map/projection_near_2/ppermute | solution.py:81
  12.9 1.5 %collective-permute-done.5.refs_0_ = bf16[264,640]{1,0:T(8,128)(2,1)S(1)} collective-permute-done((bf16[264,640]{1,0:T(8,128)(2,1)S(1)}, bf16[264,640]{1,0:T(8,128)(2,1)S(1)}, u32[]{:S(2)}, u32[]{:S(2)}) %collective-permute-start.5) | collective-permute-done | bytes 337952 | tf_op jit(solution)/shard_map/projection_far_1/ppermute | solution.py:81
  14.4 2.1 %collective-permute-start.6 = (bf16[264,640]{1,0:T(8,128)(2,1)S(1)}, bf16[264,640]{1,0:T(8,128)(2,1)S(1)}, u32[]{:S(2)}, u32[]{:S(2)}) collective-permute-start(bf16[264,640]{1,0:T(8,128)(2,1)S(1)} %collective-permute-done.5.refs_0_), channel_id=1, source_target_pairs={{0,8},{10,2},{8,16},{18,10},{16,24},{26,18},{24,28},{30,26},{28,20... | collective-permute-start | bytes 1013768 | tf_op jit(solution)/shard_map/projection_far_2/ppermute | solution.py:81
  16.5 2.0 %projection_1.1 = (f32[3,256,640]{2,1,0:T(8,128)S(1)}, f32[8,640]{1,0:T(8,128)S(1)}) custom-call(s32[10]{0:T(128)S(1)} %pad_add_fusion.ids_ref, bf16[264,640]{1,0:T(8,128)(2,1)S(1)} %prepare.1.refs_0_, bf16[264,640]{1,0:T(8,128)(2,1)S(1)} %collective-permute-done.4.refs_1_, bf16[264,640]{1,0:T(8,128)(2,1)S(1)} %collective-permute-done.refs_2_, ...), custom_call_target="tpu_custom_call" | custom-call | tf_op jit(solution)/shard_map/projection_1/pallas_call | solution.py:173
  19.1 1.6 %collective-permute-start.2 = (bf16[264,640]{1,0:T(8,128)(2,1)S(1)}, bf16[264,640]{1,0:T(8,128)(2,1)S(1)}, u32[]{:S(2)}, u32[]{:S(2)}) collective-permute-start(bf16[264,640]{1,0:T(8,128)(2,1)S(1)} %collective-permute-done.1.refs_2_), channel_id=1, source_target_pairs={{0,8},{10,2},{8,16},{18,10},{16,24},{26,18},{24,28},{30,26},{28,20... | collective-permute-start | bytes 1013768 | tf_op jit(solution)/shard_map/projection_near_3/ppermute | solution.py:81
  21.7 2.1 %collective-permute-start.13 = (bf16[264,640]{1,0:T(8,128)(2,1)S(1)}, bf16[264,640]{1,0:T(8,128)(2,1)S(1)}, u32[]{:S(2)}, u32[]{:S(2)}) collective-permute-start(bf16[264,640]{1,0:T(8,128)(2,1)S(1)} %collective-permute-done.6.refs_0_), channel_id=1, source_target_pairs={{0,8},{10,2},{8,16},{18,10},{16,24},{26,18},{24,28},{30,26},{28,20... | collective-permute-start | bytes 1013768 | tf_op jit(solution)/shard_map/projection_far_3/ppermute | solution.py:81
  23.8 2.1 %projection_2.1 = (f32[3,256,640]{2,1,0:T(8,128)S(1)}, f32[8,640]{1,0:T(8,128)S(1)}) custom-call(s32[10]{0:T(128)S(1)} %pad_add_fusion.ids_ref, bf16[264,640]{1,0:T(8,128)(2,1)S(1)} %collective-permute-done.5.refs_0_, bf16[264,640]{1,0:T(8,128)(2,1)S(1)} %collective-permute-done.8.refs_1_, ...), custom_call_target="tpu_custom_call", output_to_operand_aliasing={{0}: (6, {}), {1}: (7, {})} | custom-call | tf_op jit(solution)/shard_map/projection_2/pallas_call | solution.py:173
  26.8 1.6 %collective-permute-start.3 = (bf16[264,640]{1,0:T(8,128)(2,1)S(1)}, bf16[264,640]{1,0:T(8,128)(2,1)S(1)}, u32[]{:S(2)}, u32[]{:S(2)}) collective-permute-start(bf16[264,640]{1,0:T(8,128)(2,1)S(1)} %collective-permute-done.2.refs_2_), channel_id=1, source_target_pairs={{0,8},{10,2},{8,16},{18,10},{16,24},{26,18},{24,28},{30,26},{28,20... | collective-permute-start | bytes 1013768 | tf_op jit(solution)/shard_map/projection_near_4/ppermute | solution.py:81
  28.4 1.5 %collective-permute-done.13.refs_0_ = bf16[264,640]{1,0:T(8,128)(2,1)S(1)} collective-permute-done((bf16[264,640]{1,0:T(8,128)(2,1)S(1)}, bf16[264,640]{1,0:T(8,128)(2,1)S(1)}, u32[]{:S(2)}, u32[]{:S(2)}) %collective-permute-start.13) | collective-permute-done | bytes 337952 | tf_op jit(solution)/shard_map/projection_far_3/ppermute | solution.py:81
  29.9 2.1 %projection_3.1 = (f32[3,256,640]{2,1,0:T(8,128)S(1)}, f32[8,640]{1,0:T(8,128)S(1)}) custom-call(s32[10]{0:T(128)S(1)} %pad_add_fusion.ids_ref, bf16[264,640]{1,0:T(8,128)(2,1)S(1)} %collective-permute-done.6.refs_0_, bf16[264,640]{1,0:T(8,128)(2,1)S(1)} %collective-permute-done.7.refs_1_, ...), custom_call_target="tpu_custom_call", output_to_operand_aliasing={{0}: (6, {}), {1}: (7, {})} | custom-call | tf_op jit(solution)/shard_map/projection_3/pallas_call | solution.py:173
  32.0 1.9 %collective-permute-done.3.refs_0_ = bf16[264,640]{1,0:T(8,128)(2,1)S(1)} collective-permute-done((bf16[264,640]{1,0:T(8,128)(2,1)S(1)}, bf16[264,640]{1,0:T(8,128)(2,1)S(1)}, u32[]{:S(2)}, u32[]{:S(2)}) %collective-permute-start.3) | collective-permute-done | bytes 337952 | tf_op jit(solution)/shard_map/projection_near_4/ppermute | solution.py:81
  34.0 1.5 %projection_4.1 = (f32[3,256,640]{2,1,0:T(8,128)S(1)}, f32[8,640]{1,0:T(8,128)S(1)}) custom-call(s32[10]{0:T(128)S(1)} %pad_add_fusion.ids_ref, bf16[264,640]{1,0:T(8,128)(2,1)S(1)} %collective-permute-done.13.refs_0_, bf16[264,640]{1,0:T(8,128)(2,1)S(1)} %collective-permute-done.14.refs_1_, ...), custom_call_target="tpu_custom_call", output_to_operand_aliasing={{0}: (4, {}), {1}: (5, {})} | custom-call | flops 2000000000 | tf_op jit(solution)/shard_map/projection_4/pallas_call | solution.py:173
  37.0 1.6 %collective-permute-start.16 = (bf16[136,640]{1,0:T(8,128)(2,1)S(1)}, bf16[136,640]{1,0:T(8,128)(2,1)S(1)}, u32[]{:S(2)}, u32[]{:S(2)}) collective-permute-start(bf16[136,640]{1,0:T(8,128)(2,1)S(1)} %get-tuple-element.59.refs_2_.refs_8_), channel_id=1, source_target_pairs={{0,1},{1,0},{2,3},{3,2},{4,5},{5,4},{6,7},{7,6},{8,9},{9,8},{10,11... | collective-permute-start | bytes 522248 | tf_op jit(solution)/shard_map/ppermute | solution.py:527
  40.5 1.7 %own_part.1 = (f32[128,640]{1,0:T(8,128)S(1)}, f32[128,640]{1,0:T(8,128)S(1)}, f32[128,1280]{1,0:T(8,128)S(1)}, f32[128,1280]{1,0:T(8,128)S(1)}) custom-call(s32[10]{0:T(128)S(1)} %pad_add_fusion.ids_ref, bf16[3,128,640]{2,1,0:T(8,128)(2,1)S(1)} %get-tuple-element.57.refs_0_.refs_4_, bf16[3,128,640]{2,1,0:T(8,128)(2,1)S(1)} %get-tuple-element.58.refs_1_.refs_4_, ...), custom_call_target="tpu_custom_call" | custom-call | tf_op jit(solution)/shard_map/own_part/pallas_call | solution.py:427
  42.2 2.1 %collective-permute-done.16.refs_0_ = bf16[136,640]{1,0:T(8,128)(2,1)S(1)} collective-permute-done((bf16[136,640]{1,0:T(8,128)(2,1)S(1)}, bf16[136,640]{1,0:T(8,128)(2,1)S(1)}, u32[]{:S(2)}, u32[]{:S(2)}) %collective-permute-start.16) | collective-permute-done | bytes 174112 | tf_op jit(solution)/shard_map/ppermute | solution.py:527
  44.3 2.4 %far_part_1_0.1.refs_10_ = bf16[256,640]{1,0:T(8,128)(2,1)S(1)} custom-call(s32[10]{0:T(128)S(1)} %pad_add_fusion.ids_ref, bf16[136,640]{1,0:T(8,128)(2,1)S(1)} %collective-permute-done.16.refs_0_, f32[128,1280]{1,0:T(8,128)S(1)} %get-tuple-element.63.refs_1_, f32[256,2560]{1,0:T(8,128)S(1)} %filter_spectra.1.refs_5_.refs_2_, ...), custom_call_target="tpu_custom_call" | custom-call | tf_op jit(solution)/shard_map/far_part_1_0/pallas_call | solution.py:512
  47.5 2.4 %far_part_1_128.1.refs_0_ = bf16[256,640]{1,0:T(8,128)(2,1)S(1)} custom-call(s32[10]{0:T(128)S(1)} %pad_add_fusion.ids_ref, bf16[136,640]{1,0:T(8,128)(2,1)S(1)} %collective-permute-done.15.refs_0_, f32[128,1280]{1,0:T(8,128)S(1)} %get-tuple-element.61.refs_1_, f32[256,2560]{1,0:T(8,128)S(1)} %filter_spectra.1.refs_5_.refs_2_, ...), custom_call_target="tpu_custom_call", output_to_operand_aliasing={{}: (11, {})} | custom-call | tf_op jit(solution)/shard_map/far_part_1_128/pallas_call | solution.py:512
  50.0 1.6 %collective-permute-start.17 = (bf16[256,640]{1,0:T(8,128)(2,1)S(1)}, bf16[256,640]{1,0:T(8,128)(2,1)S(1)}, u32[]{:S(2)}, u32[]{:S(2)}) collective-permute-start(bf16[256,640]{1,0:T(8,128)(2,1)S(1)} %far_part_1_128.1.refs_0_), channel_id=1, source_target_pairs={{0,8},{10,2},{8,16},{18,10},{16,24},{26,18},{24,28},{30,26},{28,20... | collective-permute-start | bytes 983048 | tf_op jit(solution)/shard_map/output_near_1/ppermute | solution.py:81
  51.6 1.6 %collective-permute-start.22 = (bf16[256,640]{1,0:T(8,128)(2,1)S(1)}, bf16[256,640]{1,0:T(8,128)(2,1)S(1)}, u32[]{:S(2)}, u32[]{:S(2)}) collective-permute-start(bf16[256,640]{1,0:T(8,128)(2,1)S(1)} %collective-permute-done.21.refs_1_), channel_id=1, source_target_pairs={{0,8},{10,2},{8,16},{18,10},{16,24},{26,18},{24,28},{30,26},{28,20... | collective-permute-start | bytes 983048 | tf_op jit(solution)/shard_map/output_far_1/ppermute | solution.py:81
  53.2 3.9 %collective-permute-done.17.refs_2_ = bf16[256,640]{1,0:T(8,128)(2,1)S(1)} collective-permute-done((bf16[256,640]{1,0:T(8,128)(2,1)S(1)}, bf16[256,640]{1,0:T(8,128)(2,1)S(1)}, u32[]{:S(2)}, u32[]{:S(2)}) %collective-permute-start.17) | collective-permute-done | bytes 327712 | tf_op jit(solution)/shard_map/output_near_1/ppermute | solution.py:81
  57.1 1.6 %collective-permute-start.18 = (bf16[256,640]{1,0:T(8,128)(2,1)S(1)}, bf16[256,640]{1,0:T(8,128)(2,1)S(1)}, u32[]{:S(2)}, u32[]{:S(2)}) collective-permute-start(bf16[256,640]{1,0:T(8,128)(2,1)S(1)} %collective-permute-done.17.refs_2_), channel_id=1, source_target_pairs={{0,8},{10,2},{8,16},{18,10},{16,24},{26,18},{24,28},{30,26},{28,20... | collective-permute-start | bytes 983048 | tf_op jit(solution)/shard_map/output_near_2/ppermute | solution.py:81
  58.7 1.9 %collective-permute-done.22.refs_0_ = bf16[256,640]{1,0:T(8,128)(2,1)S(1)} collective-permute-done((bf16[256,640]{1,0:T(8,128)(2,1)S(1)}, bf16[256,640]{1,0:T(8,128)(2,1)S(1)}, u32[]{:S(2)}, u32[]{:S(2)}) %collective-permute-start.22) | collective-permute-done | bytes 327712 | tf_op jit(solution)/shard_map/output_far_1/ppermute | solution.py:81
  60.6 1.6 %collective-permute-start.23 = (bf16[256,640]{1,0:T(8,128)(2,1)S(1)}, bf16[256,640]{1,0:T(8,128)(2,1)S(1)}, u32[]{:S(2)}, u32[]{:S(2)}) collective-permute-start(bf16[256,640]{1,0:T(8,128)(2,1)S(1)} %collective-permute-done.22.refs_0_), channel_id=1, source_target_pairs={{0,8},{10,2},{8,16},{18,10},{16,24},{26,18},{24,28},{30,26},{28,20... | collective-permute-start | bytes 983048 | tf_op jit(solution)/shard_map/output_far_2/ppermute | solution.py:81
  64.7 1.6 %collective-permute-start.19 = (bf16[256,640]{1,0:T(8,128)(2,1)S(1)}, bf16[256,640]{1,0:T(8,128)(2,1)S(1)}, u32[]{:S(2)}, u32[]{:S(2)}) collective-permute-start(bf16[256,640]{1,0:T(8,128)(2,1)S(1)} %collective-permute-done.18.refs_2_), channel_id=1, source_target_pairs={{0,8},{10,2},{8,16},{18,10},{16,24},{26,18},{24,28},{30,26},{28,20... | collective-permute-start | bytes 983048 | tf_op jit(solution)/shard_map/output_near_3/ppermute | solution.py:81
  66.3 1.4 %collective-permute-done.23.refs_0_ = bf16[256,640]{1,0:T(8,128)(2,1)S(1)} collective-permute-done((bf16[256,640]{1,0:T(8,128)(2,1)S(1)}, bf16[256,640]{1,0:T(8,128)(2,1)S(1)}, u32[]{:S(2)}, u32[]{:S(2)}) %collective-permute-start.23) | collective-permute-done | bytes 327712 | tf_op jit(solution)/shard_map/output_far_2/ppermute | solution.py:81
  67.7 1.6 %collective-permute-start.30 = (bf16[256,640]{1,0:T(8,128)(2,1)S(1)}, bf16[256,640]{1,0:T(8,128)(2,1)S(1)}, u32[]{:S(2)}, u32[]{:S(2)}) collective-permute-start(bf16[256,640]{1,0:T(8,128)(2,1)S(1)} %collective-permute-done.23.refs_0_), channel_id=1, source_target_pairs={{0,8},{10,2},{8,16},{18,10},{16,24},{26,18},{24,28},{30,26},{28,20... | collective-permute-start | bytes 983048 | tf_op jit(solution)/shard_map/output_far_3/ppermute | solution.py:81
  72.3 1.6 %collective-permute-start.20 = (bf16[256,640]{1,0:T(8,128)(2,1)S(1)}, bf16[256,640]{1,0:T(8,128)(2,1)S(1)}, u32[]{:S(2)}, u32[]{:S(2)}) collective-permute-start(bf16[256,640]{1,0:T(8,128)(2,1)S(1)} %collective-permute-done.19.refs_2_), channel_id=1, source_target_pairs={{0,8},{10,2},{8,16},{18,10},{16,24},{26,18},{24,28},{30,26},{28,20... | collective-permute-start | bytes 983048 | tf_op jit(solution)/shard_map/output_near_4/ppermute | solution.py:81
  76.4 2.9 %collective-permute-done.20.refs_0_ = bf16[256,640]{1,0:T(8,128)(2,1)S(1)} collective-permute-done((bf16[256,640]{1,0:T(8,128)(2,1)S(1)}, bf16[256,640]{1,0:T(8,128)(2,1)S(1)}, u32[]{:S(2)}, u32[]{:S(2)}) %collective-permute-start.20) | collective-permute-done | bytes 327712 | tf_op jit(solution)/shard_map/output_near_4/ppermute | solution.py:81
  81.0 1.6 %output_last_0.1 = bf16[256,640]{1,0:T(8,128)(2,1)} custom-call(s32[10]{0:T(128)S(1)} %pad_add_fusion.ids_ref, bf16[256,640]{1,0:T(8,128)(2,1)S(1)} %collective-permute-done.20.refs_0_, bf16[256,640]{1,0:T(8,128)(2,1)S(1)} %collective-permute-done.29.refs_1_, bf16[1,256,4096]{2,1,0:T(8,128)(2,1)S(1)} %bitcast.12, f32[1,256,640]{2,1,0:T(8,128)S(1)} %output_4.1.refs_3_), custom_call_target="tpu_custom_call" | custom-call | tf_op jit(solution)/shard_map/output_last_0/pallas_call | solution.py:173
  (73 shorter events, 20.4 us)
Async XLA Ops:
  2.6 3.2 %collective-permute-start.4 = (bf16[264,640]{1,0:T(8,128)(2,1)S(1)}, bf16[264,640]{1,0:T(8,128)(2,1)S(1)}, u32[]{:S(2)}, u32[]{:S(2)}) collective-permute-start(bf16[264,640]{1,0:T(8,128)(2,1)S(1)} %prepare.1.refs_0_), channel_id=1, source_target_pairs={{0,2},{2,0},{4,6},{6,4},{8,10},{10,8},{12,14},{14,12},{16,18},{18,... | collective-permute-start | bytes 1013768 | tf_op jit(solution)/shard_map/projection_core_own/ppermute | solution.py:85
  3.1 7.7 %collective-permute-start = (bf16[264,640]{1,0:T(8,128)(2,1)S(1)}, bf16[264,640]{1,0:T(8,128)(2,1)S(1)}, u32[]{:S(2)}, u32[]{:S(2)}) collective-permute-start(bf16[264,640]{1,0:T(8,128)(2,1)S(1)} %prepare.1.refs_0_), channel_id=1, source_target_pairs={{0,8},{10,2},{8,16},{18,10},{16,24},{26,18},{24,28},{30,26},{28,20... | collective-permute-start | bytes 1013768 | tf_op jit(solution)/shard_map/projection_near_1/ppermute | solution.py:81
  5.7 8.7 %collective-permute-start.5 = (bf16[264,640]{1,0:T(8,128)(2,1)S(1)}, bf16[264,640]{1,0:T(8,128)(2,1)S(1)}, u32[]{:S(2)}, u32[]{:S(2)}) collective-permute-start(bf16[264,640]{1,0:T(8,128)(2,1)S(1)} %collective-permute-done.4.refs_1_), channel_id=1, source_target_pairs={{0,8},{10,2},{8,16},{18,10},{16,24},{26,18},{24,28},{30,26},{28,20... | collective-permute-start | bytes 1013768 | tf_op jit(solution)/shard_map/projection_far_1/ppermute | solution.py:81
  10.8 5.7 %collective-permute-start.9 = (bf16[264,640]{1,0:T(8,128)(2,1)S(1)}, bf16[264,640]{1,0:T(8,128)(2,1)S(1)}, u32[]{:S(2)}, u32[]{:S(2)}) collective-permute-start(bf16[264,640]{1,0:T(8,128)(2,1)S(1)} %collective-permute-done.refs_2_), channel_id=1, source_target_pairs={{0,2},{2,0},{4,6},{6,4},{8,10},{10,8},{12,14},{14,12},{16,18},{18,... | collective-permute-start | bytes 1013768 | tf_op jit(solution)/shard_map/projection_core_near_1/ppermute | solution.py:85
  10.8 7.7 %collective-permute-start.1 = (bf16[264,640]{1,0:T(8,128)(2,1)S(1)}, bf16[264,640]{1,0:T(8,128)(2,1)S(1)}, u32[]{:S(2)}, u32[]{:S(2)}) collective-permute-start(bf16[264,640]{1,0:T(8,128)(2,1)S(1)} %collective-permute-done.refs_2_), channel_id=1, source_target_pairs={{0,8},{10,2},{8,16},{18,10},{16,24},{26,18},{24,28},{30,26},{28,20... | collective-permute-start | bytes 1013768 | tf_op jit(solution)/shard_map/projection_near_2/ppermute | solution.py:81
  14.4 7.2 %collective-permute-start.6 = (bf16[264,640]{1,0:T(8,128)(2,1)S(1)}, bf16[264,640]{1,0:T(8,128)(2,1)S(1)}, u32[]{:S(2)}, u32[]{:S(2)}) collective-permute-start(bf16[264,640]{1,0:T(8,128)(2,1)S(1)} %collective-permute-done.5.refs_0_), channel_id=1, source_target_pairs={{0,8},{10,2},{8,16},{18,10},{16,24},{26,18},{24,28},{30,26},{28,20... | collective-permute-start | bytes 1013768 | tf_op jit(solution)/shard_map/projection_far_2/ppermute | solution.py:81
  18.5 5.3 %collective-permute-start.10 = (bf16[264,640]{1,0:T(8,128)(2,1)S(1)}, bf16[264,640]{1,0:T(8,128)(2,1)S(1)}, u32[]{:S(2)}, u32[]{:S(2)}) collective-permute-start(bf16[264,640]{1,0:T(8,128)(2,1)S(1)} %collective-permute-done.1.refs_2_), channel_id=1, source_target_pairs={{0,2},{2,0},{4,6},{6,4},{8,10},{10,8},{12,14},{14,12},{16,18},{18,... | collective-permute-start | bytes 1013768 | tf_op jit(solution)/shard_map/projection_core_near_2/ppermute | solution.py:85
  18.6 5.2 %collective-permute-start.8 = (bf16[264,640]{1,0:T(8,128)(2,1)S(1)}, bf16[264,640]{1,0:T(8,128)(2,1)S(1)}, u32[]{:S(2)}, u32[]{:S(2)}) collective-permute-start(bf16[264,640]{1,0:T(8,128)(2,1)S(1)} %collective-permute-done.5.refs_0_), channel_id=1, source_target_pairs={{0,2},{2,0},{4,6},{6,4},{8,10},{10,8},{12,14},{14,12},{16,18},{18,... | collective-permute-start | bytes 1013768 | tf_op jit(solution)/shard_map/projection_core_far_1/ppermute | solution.py:85
  19.1 7.2 %collective-permute-start.2 = (bf16[264,640]{1,0:T(8,128)(2,1)S(1)}, bf16[264,640]{1,0:T(8,128)(2,1)S(1)}, u32[]{:S(2)}, u32[]{:S(2)}) collective-permute-start(bf16[264,640]{1,0:T(8,128)(2,1)S(1)} %collective-permute-done.1.refs_2_), channel_id=1, source_target_pairs={{0,8},{10,2},{8,16},{18,10},{16,24},{26,18},{24,28},{30,26},{28,20... | collective-permute-start | bytes 1013768 | tf_op jit(solution)/shard_map/projection_near_3/ppermute | solution.py:81
  21.7 8.2 %collective-permute-start.13 = (bf16[264,640]{1,0:T(8,128)(2,1)S(1)}, bf16[264,640]{1,0:T(8,128)(2,1)S(1)}, u32[]{:S(2)}, u32[]{:S(2)}) collective-permute-start(bf16[264,640]{1,0:T(8,128)(2,1)S(1)} %collective-permute-done.6.refs_0_), channel_id=1, source_target_pairs={{0,8},{10,2},{8,16},{18,10},{16,24},{26,18},{24,28},{30,26},{28,20... | collective-permute-start | bytes 1013768 | tf_op jit(solution)/shard_map/projection_far_3/ppermute | solution.py:81
  26.3 3.6 %collective-permute-start.11 = (bf16[264,640]{1,0:T(8,128)(2,1)S(1)}, bf16[264,640]{1,0:T(8,128)(2,1)S(1)}, u32[]{:S(2)}, u32[]{:S(2)}) collective-permute-start(bf16[264,640]{1,0:T(8,128)(2,1)S(1)} %collective-permute-done.2.refs_2_), channel_id=1, source_target_pairs={{0,2},{2,0},{4,6},{6,4},{8,10},{10,8},{12,14},{14,12},{16,18},{18,... | collective-permute-start | bytes 1013768 | tf_op jit(solution)/shard_map/projection_core_near_3/ppermute | solution.py:85
  26.3 3.6 %collective-permute-start.7 = (bf16[264,640]{1,0:T(8,128)(2,1)S(1)}, bf16[264,640]{1,0:T(8,128)(2,1)S(1)}, u32[]{:S(2)}, u32[]{:S(2)}) collective-permute-start(bf16[264,640]{1,0:T(8,128)(2,1)S(1)} %collective-permute-done.6.refs_0_), channel_id=1, source_target_pairs={{0,2},{2,0},{4,6},{6,4},{8,10},{10,8},{12,14},{14,12},{16,18},{18,... | collective-permute-start | bytes 1013768 | tf_op jit(solution)/shard_map/projection_core_far_2/ppermute | solution.py:85
  26.8 7.2 %collective-permute-start.3 = (bf16[264,640]{1,0:T(8,128)(2,1)S(1)}, bf16[264,640]{1,0:T(8,128)(2,1)S(1)}, u32[]{:S(2)}, u32[]{:S(2)}) collective-permute-start(bf16[264,640]{1,0:T(8,128)(2,1)S(1)} %collective-permute-done.2.refs_2_), channel_id=1, source_target_pairs={{0,8},{10,2},{8,16},{18,10},{16,24},{26,18},{24,28},{30,26},{28,20... | collective-permute-start | bytes 1013768 | tf_op jit(solution)/shard_map/projection_near_4/ppermute | solution.py:81
  29.9 4.1 %collective-permute-start.14 = (bf16[264,640]{1,0:T(8,128)(2,1)S(1)}, bf16[264,640]{1,0:T(8,128)(2,1)S(1)}, u32[]{:S(2)}, u32[]{:S(2)}) collective-permute-start(bf16[264,640]{1,0:T(8,128)(2,1)S(1)} %collective-permute-done.13.refs_0_), channel_id=1, source_target_pairs={{0,2},{2,0},{4,6},{6,4},{8,10},{10,8},{12,14},{14,12},{16,18},{18,... | collective-permute-start | bytes 1013768 | tf_op jit(solution)/shard_map/projection_core_far_3/ppermute | solution.py:85
  34.0 1.6 %collective-permute-start.12 = (bf16[264,640]{1,0:T(8,128)(2,1)S(1)}, bf16[264,640]{1,0:T(8,128)(2,1)S(1)}, u32[]{:S(2)}, u32[]{:S(2)}) collective-permute-start(bf16[264,640]{1,0:T(8,128)(2,1)S(1)} %collective-permute-done.3.refs_0_), channel_id=1, source_target_pairs={{0,2},{2,0},{4,6},{6,4},{8,10},{10,8},{12,14},{14,12},{16,18},{18,... | collective-permute-start | bytes 1013768 | tf_op jit(solution)/shard_map/projection_core_near_4/ppermute | solution.py:85
  37.0 7.3 %collective-permute-start.16 = (bf16[136,640]{1,0:T(8,128)(2,1)S(1)}, bf16[136,640]{1,0:T(8,128)(2,1)S(1)}, u32[]{:S(2)}, u32[]{:S(2)}) collective-permute-start(bf16[136,640]{1,0:T(8,128)(2,1)S(1)} %get-tuple-element.59.refs_2_.refs_8_), channel_id=1, source_target_pairs={{0,1},{1,0},{2,3},{3,2},{4,5},{5,4},{6,7},{7,6},{8,9},{9,8},{10,11... | collective-permute-start | bytes 522248 | tf_op jit(solution)/shard_map/ppermute | solution.py:527
  39.9 7.6 %collective-permute-start.15 = (bf16[136,640]{1,0:T(8,128)(2,1)S(1)}, bf16[136,640]{1,0:T(8,128)(2,1)S(1)}, u32[]{:S(2)}, u32[]{:S(2)}) collective-permute-start(bf16[136,640]{1,0:T(8,128)(2,1)S(1)} %get-tuple-element.56.refs_3_.refs_8_), channel_id=1, source_target_pairs={{0,1},{1,0},{2,3},{3,2},{4,5},{5,4},{6,7},{7,6},{8,9},{9,8},{10,11... | collective-permute-start | bytes 522248 | tf_op jit(solution)/shard_map/ppermute | solution.py:527
  49.9 1.7 %collective-permute-start.21 = (bf16[256,640]{1,0:T(8,128)(2,1)S(1)}, bf16[256,640]{1,0:T(8,128)(2,1)S(1)}, u32[]{:S(2)}, u32[]{:S(2)}) collective-permute-start(bf16[256,640]{1,0:T(8,128)(2,1)S(1)} %far_part_1_128.1.refs_0_), channel_id=1, source_target_pairs={{0,2},{2,0},{4,6},{6,4},{8,10},{10,8},{12,14},{14,12},{16,18},{18,... | collective-permute-start | bytes 983048 | tf_op jit(solution)/shard_map/output_core_own/ppermute | solution.py:85
  50.0 7.1 %collective-permute-start.17 = (bf16[256,640]{1,0:T(8,128)(2,1)S(1)}, bf16[256,640]{1,0:T(8,128)(2,1)S(1)}, u32[]{:S(2)}, u32[]{:S(2)}) collective-permute-start(bf16[256,640]{1,0:T(8,128)(2,1)S(1)} %far_part_1_128.1.refs_0_), channel_id=1, source_target_pairs={{0,8},{10,2},{8,16},{18,10},{16,24},{26,18},{24,28},{30,26},{28,20... | collective-permute-start | bytes 983048 | tf_op jit(solution)/shard_map/output_near_1/ppermute | solution.py:81
  51.6 9.0 %collective-permute-start.22 = (bf16[256,640]{1,0:T(8,128)(2,1)S(1)}, bf16[256,640]{1,0:T(8,128)(2,1)S(1)}, u32[]{:S(2)}, u32[]{:S(2)}) collective-permute-start(bf16[256,640]{1,0:T(8,128)(2,1)S(1)} %collective-permute-done.21.refs_1_), channel_id=1, source_target_pairs={{0,8},{10,2},{8,16},{18,10},{16,24},{26,18},{24,28},{30,26},{28,20... | collective-permute-start | bytes 983048 | tf_op jit(solution)/shard_map/output_far_1/ppermute | solution.py:81
  57.1 5.1 %collective-permute-start.26 = (bf16[256,640]{1,0:T(8,128)(2,1)S(1)}, bf16[256,640]{1,0:T(8,128)(2,1)S(1)}, u32[]{:S(2)}, u32[]{:S(2)}) collective-permute-start(bf16[256,640]{1,0:T(8,128)(2,1)S(1)} %collective-permute-done.17.refs_2_), channel_id=1, source_target_pairs={{0,2},{2,0},{4,6},{6,4},{8,10},{10,8},{12,14},{14,12},{16,18},{18,... | collective-permute-start | bytes 983048 | tf_op jit(solution)/shard_map/output_core_near_1/ppermute | solution.py:85
  57.1 7.1 %collective-permute-start.18 = (bf16[256,640]{1,0:T(8,128)(2,1)S(1)}, bf16[256,640]{1,0:T(8,128)(2,1)S(1)}, u32[]{:S(2)}, u32[]{:S(2)}) collective-permute-start(bf16[256,640]{1,0:T(8,128)(2,1)S(1)} %collective-permute-done.17.refs_2_), channel_id=1, source_target_pairs={{0,8},{10,2},{8,16},{18,10},{16,24},{26,18},{24,28},{30,26},{28,20... | collective-permute-start | bytes 983048 | tf_op jit(solution)/shard_map/output_near_2/ppermute | solution.py:81
  60.6 7.1 %collective-permute-start.23 = (bf16[256,640]{1,0:T(8,128)(2,1)S(1)}, bf16[256,640]{1,0:T(8,128)(2,1)S(1)}, u32[]{:S(2)}, u32[]{:S(2)}) collective-permute-start(bf16[256,640]{1,0:T(8,128)(2,1)S(1)} %collective-permute-done.22.refs_0_), channel_id=1, source_target_pairs={{0,8},{10,2},{8,16},{18,10},{16,24},{26,18},{24,28},{30,26},{28,20... | collective-permute-start | bytes 983048 | tf_op jit(solution)/shard_map/output_far_2/ppermute | solution.py:81
  64.2 5.1 %collective-permute-start.27 = (bf16[256,640]{1,0:T(8,128)(2,1)S(1)}, bf16[256,640]{1,0:T(8,128)(2,1)S(1)}, u32[]{:S(2)}, u32[]{:S(2)}) collective-permute-start(bf16[256,640]{1,0:T(8,128)(2,1)S(1)} %collective-permute-done.18.refs_2_), channel_id=1, source_target_pairs={{0,2},{2,0},{4,6},{6,4},{8,10},{10,8},{12,14},{14,12},{16,18},{18,... | collective-permute-start | bytes 983048 | tf_op jit(solution)/shard_map/output_core_near_2/ppermute | solution.py:85
  64.2 5.1 %collective-permute-start.25 = (bf16[256,640]{1,0:T(8,128)(2,1)S(1)}, bf16[256,640]{1,0:T(8,128)(2,1)S(1)}, u32[]{:S(2)}, u32[]{:S(2)}) collective-permute-start(bf16[256,640]{1,0:T(8,128)(2,1)S(1)} %collective-permute-done.22.refs_0_), channel_id=1, source_target_pairs={{0,2},{2,0},{4,6},{6,4},{8,10},{10,8},{12,14},{14,12},{16,18},{18,... | collective-permute-start | bytes 983048 | tf_op jit(solution)/shard_map/output_core_far_1/ppermute | solution.py:85
  64.7 7.1 %collective-permute-start.19 = (bf16[256,640]{1,0:T(8,128)(2,1)S(1)}, bf16[256,640]{1,0:T(8,128)(2,1)S(1)}, u32[]{:S(2)}, u32[]{:S(2)}) collective-permute-start(bf16[256,640]{1,0:T(8,128)(2,1)S(1)} %collective-permute-done.18.refs_2_), channel_id=1, source_target_pairs={{0,8},{10,2},{8,16},{18,10},{16,24},{26,18},{24,28},{30,26},{28,20... | collective-permute-start | bytes 983048 | tf_op jit(solution)/shard_map/output_near_3/ppermute | solution.py:81
  67.7 7.6 %collective-permute-start.30 = (bf16[256,640]{1,0:T(8,128)(2,1)S(1)}, bf16[256,640]{1,0:T(8,128)(2,1)S(1)}, u32[]{:S(2)}, u32[]{:S(2)}) collective-permute-start(bf16[256,640]{1,0:T(8,128)(2,1)S(1)} %collective-permute-done.23.refs_0_), channel_id=1, source_target_pairs={{0,8},{10,2},{8,16},{18,10},{16,24},{26,18},{24,28},{30,26},{28,20... | collective-permute-start | bytes 983048 | tf_op jit(solution)/shard_map/output_far_3/ppermute | solution.py:81
  71.8 3.5 %collective-permute-start.28 = (bf16[256,640]{1,0:T(8,128)(2,1)S(1)}, bf16[256,640]{1,0:T(8,128)(2,1)S(1)}, u32[]{:S(2)}, u32[]{:S(2)}) collective-permute-start(bf16[256,640]{1,0:T(8,128)(2,1)S(1)} %collective-permute-done.19.refs_2_), channel_id=1, source_target_pairs={{0,2},{2,0},{4,6},{6,4},{8,10},{10,8},{12,14},{14,12},{16,18},{18,... | collective-permute-start | bytes 983048 | tf_op jit(solution)/shard_map/output_core_near_3/ppermute | solution.py:85
  71.8 3.5 %collective-permute-start.24 = (bf16[256,640]{1,0:T(8,128)(2,1)S(1)}, bf16[256,640]{1,0:T(8,128)(2,1)S(1)}, u32[]{:S(2)}, u32[]{:S(2)}) collective-permute-start(bf16[256,640]{1,0:T(8,128)(2,1)S(1)} %collective-permute-done.23.refs_0_), channel_id=1, source_target_pairs={{0,2},{2,0},{4,6},{6,4},{8,10},{10,8},{12,14},{14,12},{16,18},{18,... | collective-permute-start | bytes 983048 | tf_op jit(solution)/shard_map/output_core_far_2/ppermute | solution.py:85
  72.3 7.1 %collective-permute-start.20 = (bf16[256,640]{1,0:T(8,128)(2,1)S(1)}, bf16[256,640]{1,0:T(8,128)(2,1)S(1)}, u32[]{:S(2)}, u32[]{:S(2)}) collective-permute-start(bf16[256,640]{1,0:T(8,128)(2,1)S(1)} %collective-permute-done.19.refs_2_), channel_id=1, source_target_pairs={{0,8},{10,2},{8,16},{18,10},{16,24},{26,18},{24,28},{30,26},{28,20... | collective-permute-start | bytes 983048 | tf_op jit(solution)/shard_map/output_near_4/ppermute | solution.py:81
  75.3 4.1 %collective-permute-start.31 = (bf16[256,640]{1,0:T(8,128)(2,1)S(1)}, bf16[256,640]{1,0:T(8,128)(2,1)S(1)}, u32[]{:S(2)}, u32[]{:S(2)}) collective-permute-start(bf16[256,640]{1,0:T(8,128)(2,1)S(1)} %collective-permute-done.30.refs_0_), channel_id=1, source_target_pairs={{0,2},{2,0},{4,6},{6,4},{8,10},{10,8},{12,14},{14,12},{16,18},{18,... | collective-permute-start | bytes 983048 | tf_op jit(solution)/shard_map/output_core_far_3/ppermute | solution.py:85
  79.3 1.6 %collective-permute-start.29 = (bf16[256,640]{1,0:T(8,128)(2,1)S(1)}, bf16[256,640]{1,0:T(8,128)(2,1)S(1)}, u32[]{:S(2)}, u32[]{:S(2)}) collective-permute-start(bf16[256,640]{1,0:T(8,128)(2,1)S(1)} %collective-permute-done.20.refs_0_), channel_id=1, source_target_pairs={{0,2},{2,0},{4,6},{6,4},{8,10},{10,8},{12,14},{14,12},{16,18},{18,... | collective-permute-start | bytes 983048 | tf_op jit(solution)/shard_map/output_core_near_4/ppermute | solution.py:85
  (11 other events, 69.0 us)

commit v5 on v4

--- a/solution.py
+++ b/solution.py
@@ -105,12 +105,16 @@
     return ids_ref[ids_ref.shape[0] - 1]
 
 
+def take_from(refs, number):
+    return [refs.pop(0) for _ in range(number)]
+
+
 def products(ids, items, weight, running, side, finish, cost, name, cut=(0, 1)):
     streams, out_rows, features = weight.shape
     out_rows //= cut[1]
     out_here = slice(cut[0] * out_rows, (cut[0] + 1) * out_rows)
     rows = features // lax.axis_size("fsdp")
-    shards = [shard for _, _, shard in items]
+    shards = [piece for _, _, pieces in items for piece in pieces]
     tokens = shards[0].shape[1]
     count = len(shards)
     first_group = running is None
@@ -118,7 +122,7 @@
     body, extras, out_shape = finish if finish else (None, [], None)
     padded = rows % 128 != 0
     width = 2 * rows if padded else rows
-    scratch_shapes = [pltpu.VMEM((count * width, tokens), bf16)] if padded else []
+    scratch_shapes = [pltpu.VMEM((len(items) * width, tokens), bf16)] if padded else []
 
     def kernel(ids_ref, *refs):
         refs = list(refs)
@@ -132,16 +136,24 @@
         if padded:
             (beside_ref,) = refs
             beside_ref[...] = jnp.zeros(beside_ref.shape, bf16)
-            for k, (_, other, _) in enumerate(items):
-                at = k * width + jnp.where(core == other, 0, rows)
-                beside_ref[pl.ds(pl.multiple_of(at, rows), rows)] = shard_refs[k][:rows]
-            right = beside_ref[...]
-        else:
-            right = jnp.concatenate([ref[:rows] for ref in shard_refs], axis=0)
+        sides, right = [], []
+        for k, (_, other, pieces) in enumerate(items):
+            done = 0
+            for piece_ref in take_from(shard_refs, len(pieces)):
+                more = min(piece_ref.shape[0], rows - done)
+                if padded:
+                    at = k * width + jnp.where(core == other, 0, rows) + done
+                    at = pl.multiple_of(at, math.gcd(rows, done or rows))
+                    beside_ref[pl.ds(at, more)] = piece_ref[:more]
+                else:
+                    right.append(piece_ref[:more])
+                if more < piece_ref.shape[0]:
+                    sides.append(piece_ref[more:].astype(f32))
+                done += more
+        right = beside_ref[...] if padded else jnp.concatenate(right, axis=0)
         side_sum = None
         if side:
-            parts = [ref[rows:].astype(f32) for ref in shard_refs]
-            parts += [] if first_group else [state_refs[1][...]]
+            parts = sides + ([] if first_group else [state_refs[1][...]])
             side_sum = sum(parts[1:], parts[0])
 
         def total(stream):
@@ -187,25 +199,31 @@
     chips = chip_count()
     last_step = chips // 2
 
-    def send(way, block, scope):
-        with jax.named_scope(f"{name}_{scope}"):
-            return way(block)
+    def send(way, pieces, scope):
+        sent = []
+        for k, piece in enumerate(pieces):
+            with jax.named_scope(f"{name}_{scope}_{k}"):
+                sent.append(way(piece))
+        return sent
+
+    def joined(pieces):
+        return [jnp.concatenate(pieces, axis=0)] if len(pieces) > 1 else pieces
 
     near, far = own, send(other_core, own, "core_own")
     items = [(0, 0, near), (0, 1, far)]
     running = None
     for step in range(1, last_step + 1):
-        near = send(along_ring, near, f"near_{step}")
+        near = joined(send(along_ring, near, f"near_{step}"))
         arrived = near
         if running is not None:
-            arrived, *running = lax.optimization_barrier((near, *running))
+            arrived, running = lax.optimization_barrier((near, running))
         elif beside:
-            arrived, *beside = lax.optimization_barrier((near, *beside))
+            arrived, beside = lax.optimization_barrier((near, beside))
         theirs = send(other_core, arrived, f"core_near_{step}")
         pair = [(step, 0, arrived), (chips - step, 1, theirs)]
         if step < last_step:
             running = products(ids, items + pair, weight, running, side, None, 0, f"{name}_{step}")
-            far = send(along_ring, far, f"far_{step}")
+            far = joined(send(along_ring, far, f"far_{step}"))
             theirs = send(other_core, far, f"core_far_{step}")
             items = [(step, 1, far), (chips - step, 0, theirs)]
         else:
@@ -245,7 +263,7 @@
 
     def body(total, side_sum, extra_refs, outs):
         (taps_ref,) = extra_refs
-        projected_ref, *message_refs = outs
+        projected_ref, first_ref, *message_refs = outs
         mean = jnp.sum(side_sum, axis=0, keepdims=True) * (1.0 / features)
         factor = lax.rsqrt(mean + epsilon)
         tails = []
@@ -270,12 +288,14 @@
                     )
                     for s in (1, 2)
                 )
+                first_ref[0, here] = key[:, :block_len]
+                first_ref[1, here] = value[:, :block_len]
                 message_ref[start - first : start - first + tile] = (key * value).astype(bf16)
             message_ref[rows:] = jnp.zeros((side_rows, tokens), bf16)
             here = side[:, first - begin : first - begin + rows]
             message_ref[rows:, :rows] = here.astype(bf16)
 
-    out_shape = [shape_of((streams, half, tokens), bf16)]
+    out_shape = [shape_of((streams, half, tokens), bf16), shape_of((2, half, block_len), f32)]
     out_shape += [shape_of((rows + side_rows, tokens), bf16) for _, rows in parts]
     return body, [w_short], out_shape
 
@@ -284,6 +304,30 @@
     rows = message_ref.shape[0] - side_rows
     side = jnp.where(inside, message_ref[rows:, :rows].astype(f32), 0.0).T
     return [side[:, s * (count - 1) : (s + 1) * (count - 1)] for s in range(streams)]
+
+
+def halo_edges(message_ref, taps, inside):
+    streams, count, rows = taps.shape
+    side = jnp.where(inside, message_ref[rows:, :rows].astype(f32), 0.0)
+    lines = []
+    for s in range(streams):
+        for token in range(count - 1):
+            line = jnp.zeros((1, rows), f32)
+            for tap in range(token + 1, count):
+                at = s * (count - 1) + count - 1 + token - tap
+                line = line + taps[s, tap : tap + 1] * side[at : at + 1]
+            lines.append(line)
+    lines.append(jnp.zeros((-len(lines) % 8, rows), f32))
+    columns = jnp.concatenate(lines, axis=0).T
+    lane = lax.broadcasted_iota(jnp.int32, (rows, block_len), 1)
+    edges = []
+    for s in range(streams):
+        edge = jnp.zeros((rows, block_len), f32)
+        for token in range(count - 1):
+            at = s * (count - 1) + token
+            edge = jnp.where(lane == token, columns[:, at : at + 1], edge)
+        edges.append(edge)
+    return edges
 
 
 def split_table(table):
@@ -343,18 +387,14 @@
 
 
 def multiply_spectra(source_ref, filters_ref, filter_start, pairs, before_ref, total_ref):
-    def one_tile(i, carry):
-        here = pl.ds(pl.multiple_of(i * 8, 8), 8)
-        there = pl.ds(pl.multiple_of(filter_start + i * 8, 8), 8)
+    used = [term for terms in pairs for term in terms]
+    for start in range(0, total_ref.shape[0], 8):
+        here = slice(start, start + 8)
+        there = slice(filter_start + start, filter_start + start + 8)
 
         def parts(ref, rows, k):
-            start = 2 * k * block_len
-            return (
-                ref[rows, start : start + block_len],
-                ref[rows, start + block_len : start + 2 * block_len],
-            )
-
-        used = [term for terms in pairs for term in terms]
+            return ref[rows, block_lanes(2 * k)], ref[rows, block_lanes(2 * k + 1)]
+
         sources = {b: parts(source_ref, here, b) for b in sorted({b for b, _ in used})}
         filters = {d: parts(filters_ref, there, d) for d in sorted({d for _, d in used})}
         for a, terms in enumerate(pairs):
@@ -369,12 +409,8 @@
                 imag = more_imag if imag is None else imag + more_imag
             if real is None:
                 real = imag = jnp.zeros((8, block_len), f32)
-            start = 2 * a * block_len
-            total_ref[here, start : start + block_len] = real
-            total_ref[here, start + block_len : start + 2 * block_len] = imag
-        return carry
-
-    lax.fori_loop(0, total_ref.shape[0] // 8, one_tile, 0)
+            total_ref[here, block_lanes(2 * a)] = real
+            total_ref[here, block_lanes(2 * a + 1)] = imag
 
 
 def own_part(ids, projected, messages, moved, taps, filters, table):
@@ -468,17 +504,12 @@
             [ref[:rows, block_lanes(a)] for a in range(blocks)] for ref in (query_ref, gated_ref)
         )
         if own:
-            projected_ref, taps_ref = own_refs
-            streams, count, _ = taps_ref.shape
-            halo = halo_columns(moved_ref, streams, count, inside)
-            in_half = begin % projected_ref.shape[1]
-            smoothed = []
-            for s in range(streams):
-                columns = tap_columns(taps_ref[s])[channels_here]
-                wide = projected_ref[s, in_half : in_half + rows, :block_len].astype(f32)
-                smoothed.append(smooth(wide, columns, count, halo[s]))
-            query[0] = smoothed[0]
-            gated[0] = (smoothed[1] * smoothed[2]).astype(bf16)
+            first_ref, taps_ref = own_refs
+            in_half = slice(begin % first_ref.shape[1], begin % first_ref.shape[1] + rows)
+            edges = halo_edges(moved_ref, taps_ref[:, :, channels_here], inside)
+            query[0] = query[0] + edges[0]
+            key, value = first_ref[0, in_half] + edges[1], first_ref[1, in_half] + edges[2]
+            gated[0] = (key * value).astype(bf16)
             pieces.append(gated[0])
         block_spectra(pieces, table_ref, spec_ref, 0)
         multiply_spectra(spec_ref, filters_ref, begin, pairs, total_ref, sum_ref)
@@ -491,23 +522,18 @@
         filtered = both[:, :block_len] + (both[:, block_len:] + small)
         for a in range(blocks):
             here = filtered[a * rows : (a + 1) * rows]
-            mixed = query[a] * (here + skip * gated[a].astype(f32))
-            out_ref[channels_here, block_lanes(a)] = mixed.astype(bf16)
+            mixed = (query[a] * (here + skip * gated[a].astype(f32))).astype(bf16)
+            out_ref[:, block_lanes(a)] = mixed
 
     args = [moved, total, filters, table]
     if own:
         args += list(own)
-    aliases = {}
     scratch = [pltpu.VMEM((rows, 2 * (blocks + 1) * block_len), f32)]
     out_shape = shape_of((rows, 2 * tokens), f32)
     if last is not None:
-        inverse, query, gated, skip, mixed = last
-        channels = skip.shape[0]
-        args += [inverse, query, gated, skip.reshape(1, channels)]
-        if mixed is not None:
-            aliases = {1 + len(args): 0}
-            args.append(mixed)
-        out_shape = shape_of((channels, tokens), bf16)
+        inverse, query, gated, skip = last
+        args += [inverse, query, gated, skip.reshape(1, -1)]
+        out_shape = shape_of((rows, tokens), bf16)
         scratch.append(pltpu.VMEM((rows, 2 * tokens), f32))
     return pl.pallas_call(
         kernel,
@@ -515,7 +541,6 @@
         out_specs=in_vmem,
         out_shape=out_shape,
         scratch_shapes=scratch[::-1],
-        input_output_aliases=aliases,
         compiler_params=params,
         cost_estimate=estimate(0, 0),
         name=f"far_part_{turn}_{begin}",
@@ -546,9 +571,12 @@
 
     filters = filter_spectra(long_filter, segments)
     finish = [projection_finish(features, w_short, tokens, k) for k in range(2)]
-    results, (filters,) = gather_products(ids, own, w_in, [filters], True, finish, "projection")
+    results, (filters,) = gather_products(
+        ids, [own], w_in, [filters], True, finish, "projection"
+    )
     projected = [result[0] for result in results]
-    messages = [message for result in results for message in result[1:]]
+    first_blocks = [result[1] for result in results]
+    messages = [message for result in results for message in result[2:]]
     moving = [from_before(message) for message in messages]
     exact = turns > 2
     query, totals, gated = own_part(
@@ -556,14 +584,14 @@
     )
     if exact:
         moving = [from_before(part) for part in gated]
-    mixed = None
+    mixed = []
     for turn in range(1, turns):
         for k, (begin, _) in enumerate(parts):
             last = own_block = None
             if turn == turns - 1:
-                last = (inverse, query[k], gated[k], skip_gain, mixed)
+                last = (inverse, query[k], gated[k], skip_gain)
                 if not exact:
-                    own_block = (projected[2 * begin // channels], w_short)
+                    own_block = (first_blocks[2 * begin // channels], w_short)
             done = far_part(
                 ids, turn, begin, moving[k], totals[k], filters, forward, last, own_block
             )
@@ -571,10 +599,12 @@
                 totals[k] = done
                 moving[k] = from_before(moving[k])
             else:
-                mixed = done
+                mixed.append(done)
 
     finish = [output_finish(channels, tokens)]
-    ((result,),), _ = gather_products(ids, mixed, w_out[None], [], False, finish, "output")
+    ((result,),), _ = gather_products(
+        ids, mixed, w_out[None], [], False, finish, "output"
+    )
     return result
 
 

time: 82.8 us -> 79.9 us (0.965)
  waiting for transfers between devices: 26.6 us -> 22.6 us
  starting transfers between devices: 29.5 us -> 32.1 us
  Pallas kernels: 24.5 us -> 22.9 us
    ppermute x14 -> x16, waiting for transfers between devices: 22.9 us -> 19.4 us  [along_ring(): return lax.ppermute(block, 'fsdp', pairs)]
    ppermute x14 -> x16, starting transfers between devices: 24.7 us -> 28 us  [along_ring(): return lax.ppermute(block, 'fsdp', pairs)]
    pallas_call x2, Pallas kernels: 4.85 us -> 3.53 us  [far_part(): pl.pallas_call(kernel, in_specs=[in_smem] + [in_vmem] * len(args), out_sp...]
    ppermute x16 -> x17, starting transfers between devices: 2.7 us -> 1.91 us  [other_core(): lax.ppermute(block, 'fsdp', [(i, i ^ 1) for i in range(2 * chip_count())])]
    unnamed x22 -> x24, local copies, waits for them, and re-layouts: 1.69 us -> 1.72 us
  transfers between devices with their start and end apart: 32 -> 35, of which waited for: 17 -> 16; matrix products, arithmetic and copies ran while one was open for 0% -> 0% of each run, Pallas kernels for 22% -> 24%
where the time goes in v5:
time: 79.9 us; the launch traced here: 79.7 us
  starting transfers between devices  32.1 us (40%)
  Pallas kernels  22.9 us (29%)
  waiting for transfers between devices  22.6 us (28%)
  local copies, waits for them, and re-layouts  1.77 us (2%)
    ppermute x16, starting transfers between devices, along_ring(): return lax.ppermute(block, 'fsdp', pairs)  28 us
    ppermute x16, waiting for transfers between devices, along_ring(): return lax.ppermute(block, 'fsdp', pairs)  19.4 us
    pallas_call x11, Pallas kernels, products(): pl.pallas_call(kernel, in_specs=[in_smem] + [in_vmem] * (count + 1 + len(...  16.3 us
    pallas_call x2, Pallas kernels, far_part(): pl.pallas_call(kernel, in_specs=[in_smem] + [in_vmem] * len(args), out_sp...  3.53 us
    ppermute x2, waiting for transfers between devices, from_before(): lax.ppermute(block, 'ctx', [(i, (i + 1) % count) for i in range(count)])  2.33 us
    ppermute x2, starting transfers between devices, from_before(): lax.ppermute(block, 'ctx', [(i, (i + 1) % count) for i in range(count)])  2.16 us
    ppermute x17, starting transfers between devices, other_core(): lax.ppermute(block, 'fsdp', [(i, i ^ 1) for i in range(2 * chip_count())])  1.91 us
    unnamed x24, local copies, waits for them, and re-layouts  1.72 us
  transfers between devices with their start and end apart: 35, of which 16 were waited for; matrix products, arithmetic and copies ran while one was open for 0% of the time, Pallas kernels for 24%

profile of v5, /device:TPU:0, one launch (start us, length us, event | category | flops | bytes accessed | tf_op | source)
XLA Modules:
  0.0 79.7 jit_solution(15140815268289510818)
XLA Ops:
  3.1 2.6 %collective-permute-start = (bf16[264,640]{1,0:T(8,128)(2,1)S(1)}, bf16[264,640]{1,0:T(8,128)(2,1)S(1)}, u32[]{:S(2)}, u32[]{:S(2)}) collective-permute-start(bf16[264,640]{1,0:T(8,128)(2,1)S(1)} %prepare.1.refs_0_), channel_id=1, source_target_pairs={{0,8},{10,2},{8,16},{18,10},{16,24},{26,18},{24,28},{30,26},{28,20... | collective-permute-start | bytes 1013768 | tf_op jit(solution)/shard_map/projection_near_1_0/ppermute | solution.py:81
  5.7 1.6 %collective-permute-start.5 = (bf16[264,640]{1,0:T(8,128)(2,1)S(1)}, bf16[264,640]{1,0:T(8,128)(2,1)S(1)}, u32[]{:S(2)}, u32[]{:S(2)}) collective-permute-start(bf16[264,640]{1,0:T(8,128)(2,1)S(1)} %collective-permute-done.4.refs_1_), channel_id=1, source_target_pairs={{0,8},{10,2},{8,16},{18,10},{16,24},{26,18},{24,28},{30,26},{28,20... | collective-permute-start | bytes 1013768 | tf_op jit(solution)/shard_map/projection_far_1_0/ppermute | solution.py:81
  8.2 2.7 %collective-permute-done.refs_2_ = bf16[264,640]{1,0:T(8,128)(2,1)S(1)} collective-permute-done((bf16[264,640]{1,0:T(8,128)(2,1)S(1)}, bf16[264,640]{1,0:T(8,128)(2,1)S(1)}, u32[]{:S(2)}, u32[]{:S(2)}) %collective-permute-start) | collective-permute-done | bytes 337952 | tf_op jit(solution)/shard_map/projection_near_1_0/ppermute | solution.py:81
  10.8 2.1 %collective-permute-start.1 = (bf16[264,640]{1,0:T(8,128)(2,1)S(1)}, bf16[264,640]{1,0:T(8,128)(2,1)S(1)}, u32[]{:S(2)}, u32[]{:S(2)}) collective-permute-start(bf16[264,640]{1,0:T(8,128)(2,1)S(1)} %collective-permute-done.refs_2_), channel_id=1, source_target_pairs={{0,8},{10,2},{8,16},{18,10},{16,24},{26,18},{24,28},{30,26},{28,20... | collective-permute-start | bytes 1013768 | tf_op jit(solution)/shard_map/projection_near_2_0/ppermute | solution.py:81
  12.9 1.5 %collective-permute-done.5.refs_0_ = bf16[264,640]{1,0:T(8,128)(2,1)S(1)} collective-permute-done((bf16[264,640]{1,0:T(8,128)(2,1)S(1)}, bf16[264,640]{1,0:T(8,128)(2,1)S(1)}, u32[]{:S(2)}, u32[]{:S(2)}) %collective-permute-start.5) | collective-permute-done | bytes 337952 | tf_op jit(solution)/shard_map/projection_far_1_0/ppermute | solution.py:81
  14.4 2.1 %collective-permute-start.6 = (bf16[264,640]{1,0:T(8,128)(2,1)S(1)}, bf16[264,640]{1,0:T(8,128)(2,1)S(1)}, u32[]{:S(2)}, u32[]{:S(2)}) collective-permute-start(bf16[264,640]{1,0:T(8,128)(2,1)S(1)} %collective-permute-done.5.refs_0_), channel_id=1, source_target_pairs={{0,8},{10,2},{8,16},{18,10},{16,24},{26,18},{24,28},{30,26},{28,20... | collective-permute-start | bytes 1013768 | tf_op jit(solution)/shard_map/projection_far_2_0/ppermute | solution.py:81
  16.5 2.0 %projection_1.1 = (f32[3,256,640]{2,1,0:T(8,128)S(1)}, f32[8,640]{1,0:T(8,128)S(1)}) custom-call(s32[10]{0:T(128)S(1)} %pad_add_fusion.ids_ref, bf16[264,640]{1,0:T(8,128)(2,1)S(1)} %prepare.1.refs_0_, bf16[264,640]{1,0:T(8,128)(2,1)S(1)} %collective-permute-done.4.refs_1_, bf16[264,640]{1,0:T(8,128)(2,1)S(1)} %collective-permute-done.refs_2_, ...), custom_call_target="tpu_custom_call" | custom-call | tf_op jit(solution)/shard_map/projection_1/pallas_call | solution.py:185
  19.1 1.6 %collective-permute-start.2 = (bf16[264,640]{1,0:T(8,128)(2,1)S(1)}, bf16[264,640]{1,0:T(8,128)(2,1)S(1)}, u32[]{:S(2)}, u32[]{:S(2)}) collective-permute-start(bf16[264,640]{1,0:T(8,128)(2,1)S(1)} %collective-permute-done.1.refs_2_), channel_id=1, source_target_pairs={{0,8},{10,2},{8,16},{18,10},{16,24},{26,18},{24,28},{30,26},{28,20... | collective-permute-start | bytes 1013768 | tf_op jit(solution)/shard_map/projection_near_3_0/ppermute | solution.py:81
  21.7 2.1 %collective-permute-start.13 = (bf16[264,640]{1,0:T(8,128)(2,1)S(1)}, bf16[264,640]{1,0:T(8,128)(2,1)S(1)}, u32[]{:S(2)}, u32[]{:S(2)}) collective-permute-start(bf16[264,640]{1,0:T(8,128)(2,1)S(1)} %collective-permute-done.6.refs_0_), channel_id=1, source_target_pairs={{0,8},{10,2},{8,16},{18,10},{16,24},{26,18},{24,28},{30,26},{28,20... | collective-permute-start | bytes 1013768 | tf_op jit(solution)/shard_map/projection_far_3_0/ppermute | solution.py:81
  23.8 2.1 %projection_2.1 = (f32[3,256,640]{2,1,0:T(8,128)S(1)}, f32[8,640]{1,0:T(8,128)S(1)}) custom-call(s32[10]{0:T(128)S(1)} %pad_add_fusion.ids_ref, bf16[264,640]{1,0:T(8,128)(2,1)S(1)} %collective-permute-done.5.refs_0_, bf16[264,640]{1,0:T(8,128)(2,1)S(1)} %collective-permute-done.8.refs_1_, ...), custom_call_target="tpu_custom_call", output_to_operand_aliasing={{0}: (6, {}), {1}: (7, {})} | custom-call | tf_op jit(solution)/shard_map/projection_2/pallas_call | solution.py:185
  26.8 1.6 %collective-permute-start.3 = (bf16[264,640]{1,0:T(8,128)(2,1)S(1)}, bf16[264,640]{1,0:T(8,128)(2,1)S(1)}, u32[]{:S(2)}, u32[]{:S(2)}) collective-permute-start(bf16[264,640]{1,0:T(8,128)(2,1)S(1)} %collective-permute-done.2.refs_2_), channel_id=1, source_target_pairs={{0,8},{10,2},{8,16},{18,10},{16,24},{26,18},{24,28},{30,26},{28,20... | collective-permute-start | bytes 1013768 | tf_op jit(solution)/shard_map/projection_near_4_0/ppermute | solution.py:81
  28.4 1.5 %collective-permute-done.13.refs_0_ = bf16[264,640]{1,0:T(8,128)(2,1)S(1)} collective-permute-done((bf16[264,640]{1,0:T(8,128)(2,1)S(1)}, bf16[264,640]{1,0:T(8,128)(2,1)S(1)}, u32[]{:S(2)}, u32[]{:S(2)}) %collective-permute-start.13) | collective-permute-done | bytes 337952 | tf_op jit(solution)/shard_map/projection_far_3_0/ppermute | solution.py:81
  29.9 2.1 %projection_3.1 = (f32[3,256,640]{2,1,0:T(8,128)S(1)}, f32[8,640]{1,0:T(8,128)S(1)}) custom-call(s32[10]{0:T(128)S(1)} %pad_add_fusion.ids_ref, bf16[264,640]{1,0:T(8,128)(2,1)S(1)} %collective-permute-done.6.refs_0_, bf16[264,640]{1,0:T(8,128)(2,1)S(1)} %collective-permute-done.7.refs_1_, ...), custom_call_target="tpu_custom_call", output_to_operand_aliasing={{0}: (6, {}), {1}: (7, {})} | custom-call | tf_op jit(solution)/shard_map/projection_3/pallas_call | solution.py:185
  32.0 1.9 %collective-permute-done.3.refs_0_ = bf16[264,640]{1,0:T(8,128)(2,1)S(1)} collective-permute-done((bf16[264,640]{1,0:T(8,128)(2,1)S(1)}, bf16[264,640]{1,0:T(8,128)(2,1)S(1)}, u32[]{:S(2)}, u32[]{:S(2)}) %collective-permute-start.3) | collective-permute-done | bytes 337952 | tf_op jit(solution)/shard_map/projection_near_4_0/ppermute | solution.py:81
  37.0 1.6 %collective-permute-start.15 = (bf16[136,640]{1,0:T(8,128)(2,1)S(1)}, bf16[136,640]{1,0:T(8,128)(2,1)S(1)}, u32[]{:S(2)}, u32[]{:S(2)}) collective-permute-start(bf16[136,640]{1,0:T(8,128)(2,1)S(1)} %get-tuple-element.58.refs_2_.refs_8_), channel_id=1, source_target_pairs={{0,1},{1,0},{2,3},{3,2},{4,5},{5,4},{6,7},{7,6},{8,9},{9,8},{10,11... | collective-permute-start | bytes 522248 | tf_op jit(solution)/shard_map/ppermute | solution.py:552
  42.0 2.3 %collective-permute-done.15.refs_0_ = bf16[136,640]{1,0:T(8,128)(2,1)S(1)} collective-permute-done((bf16[136,640]{1,0:T(8,128)(2,1)S(1)}, bf16[136,640]{1,0:T(8,128)(2,1)S(1)}, u32[]{:S(2)}, u32[]{:S(2)}) %collective-permute-start.15) | collective-permute-done | bytes 174112 | tf_op jit(solution)/shard_map/ppermute | solution.py:552
  44.3 1.8 %far_part_1_0.1.refs_0_ = bf16[128,640]{1,0:T(8,128)(2,1)S(1)} custom-call(s32[10]{0:T(128)S(1)} %pad_add_fusion.ids_ref, bf16[136,640]{1,0:T(8,128)(2,1)S(1)} %collective-permute-done.15.refs_0_, f32[128,1280]{1,0:T(8,128)S(1)} %get-tuple-element.63.refs_1_, f32[256,2560]{1,0:T(8,128)S(1)} %filter_spectra.1.refs_5_.refs_2_, bf16[256,256]{1,0:T(8,128)(2,1)S(1)} %copy-done.1, ...), custom_call_target="tpu_custom_call" | custom-call | tf_op jit(solution)/shard_map/far_part_1_0/pallas_call | solution.py:538
  46.1 1.6 %collective-permute-start.16 = (bf16[128,640]{1,0:T(8,128)(2,1)S(1)}, bf16[128,640]{1,0:T(8,128)(2,1)S(1)}, u32[]{:S(2)}, u32[]{:S(2)}) collective-permute-start(bf16[128,640]{1,0:T(8,128)(2,1)S(1)} %far_part_1_0.1.refs_0_), channel_id=1, source_target_pairs={{0,8},{10,2},{8,16},{18,10},{16,24},{26,18},{24,28},{30,26},{28,20... | collective-permute-start | bytes 491528 | tf_op jit(solution)/shard_map/output_near_1_0/ppermute | solution.py:81
  47.8 1.8 %far_part_1_128.1.refs_1_ = bf16[128,640]{1,0:T(8,128)(2,1)S(1)} custom-call(s32[10]{0:T(128)S(1)} %pad_add_fusion.ids_ref, bf16[136,640]{1,0:T(8,128)(2,1)S(1)} %collective-permute-done.17.refs_0_, f32[128,1280]{1,0:T(8,128)S(1)} %get-tuple-element.66.refs_1_, f32[256,2560]{1,0:T(8,128)S(1)} %filter_spectra.1.refs_5_.refs_2_, ...), custom_call_target="tpu_custom_call" | custom-call | tf_op jit(solution)/shard_map/far_part_1_128/pallas_call | solution.py:538
  49.7 1.6 %collective-permute-start.18 = (bf16[128,640]{1,0:T(8,128)(2,1)S(1)}, bf16[128,640]{1,0:T(8,128)(2,1)S(1)}, u32[]{:S(2)}, u32[]{:S(2)}) collective-permute-start(bf16[128,640]{1,0:T(8,128)(2,1)S(1)} %far_part_1_128.1.refs_1_), channel_id=1, source_target_pairs={{0,8},{10,2},{8,16},{18,10},{16,24},{26,18},{24,28},{30,26},{28,20... | collective-permute-start | bytes 491528 | tf_op jit(solution)/shard_map/output_near_1_1/ppermute | solution.py:81
  51.3 1.5 %collective-permute-start.23 = (bf16[128,640]{1,0:T(8,128)(2,1)S(1)}, bf16[128,640]{1,0:T(8,128)(2,1)S(1)}, u32[]{:S(2)}, u32[]{:S(2)}) collective-permute-start(bf16[128,640]{1,0:T(8,128)(2,1)S(1)} %collective-permute-done.22.refs_2_), channel_id=1, source_target_pairs={{0,8},{10,2},{8,16},{18,10},{16,24},{26,18},{24,28},{30,26},{28,20... | collective-permute-start | bytes 491528 | tf_op jit(solution)/shard_map/output_far_1_0/ppermute | solution.py:81
  52.9 1.6 %collective-permute-start.25 = (bf16[128,640]{1,0:T(8,128)(2,1)S(1)}, bf16[128,640]{1,0:T(8,128)(2,1)S(1)}, u32[]{:S(2)}, u32[]{:S(2)}) collective-permute-start(bf16[128,640]{1,0:T(8,128)(2,1)S(1)} %collective-permute-done.24.refs_3_), channel_id=1, source_target_pairs={{0,8},{10,2},{8,16},{18,10},{16,24},{26,18},{24,28},{30,26},{28,20... | collective-permute-start | bytes 491528 | tf_op jit(solution)/shard_map/output_far_1_1/ppermute | solution.py:81
  55.1 1.6 %collective-permute-start.19 = (bf16[256,640]{1,0:T(8,128)(2,1)S(1)}, bf16[256,640]{1,0:T(8,128)(2,1)S(1)}, u32[]{:S(2)}, u32[]{:S(2)}) collective-permute-start(bf16[256,640]{1,0:T(8,128)(2,1)S(1)} %constant_dynamic-update-slice_fusion.refs_4_), channel_id=1, source_target_pairs={{0,8},{10,2},{8,16},{18,10},{16,24},{26,18},{24,28},{30,26},{28,20... | collective-permute-start | bytes 983048 | tf_op jit(solution)/shard_map/output_near_2_0/ppermute | solution.py:81
  56.8 1.7 %collective-permute-done.25 = bf16[128,640]{1,0:T(8,128)(2,1)S(1)} collective-permute-done((bf16[128,640]{1,0:T(8,128)(2,1)S(1)}, bf16[128,640]{1,0:T(8,128)(2,1)S(1)}, u32[]{:S(2)}, u32[]{:S(2)}) %collective-permute-start.25) | collective-permute-done | bytes 163872 | tf_op jit(solution)/shard_map/output_far_1_1/ppermute | solution.py:81
  58.6 1.8 %collective-permute-start.26 = (bf16[256,640]{1,0:T(8,128)(2,1)S(1)}, bf16[256,640]{1,0:T(8,128)(2,1)S(1)}, u32[]{:S(2)}, u32[]{:S(2)}) collective-permute-start(bf16[256,640]{1,0:T(8,128)(2,1)S(1)} %constant_dynamic-update-slice_fusion.2.refs_0_), channel_id=1, source_target_pairs={{0,8},{10,2},{8,16},{18,10},{16,24},{26,18},{24,28},{30,26},{28,20... | collective-permute-start | bytes 983048 | tf_op jit(solution)/shard_map/output_far_2_0/ppermute | solution.py:81
  62.3 1.6 %collective-permute-start.20 = (bf16[256,640]{1,0:T(8,128)(2,1)S(1)}, bf16[256,640]{1,0:T(8,128)(2,1)S(1)}, u32[]{:S(2)}, u32[]{:S(2)}) collective-permute-start(bf16[256,640]{1,0:T(8,128)(2,1)S(1)} %collective-permute-done.19.refs_2_), channel_id=1, source_target_pairs={{0,8},{10,2},{8,16},{18,10},{16,24},{26,18},{24,28},{30,26},{28,20... | collective-permute-start | bytes 983048 | tf_op jit(solution)/shard_map/output_near_3_0/ppermute | solution.py:81
  63.8 2.0 %collective-permute-done.26.refs_0_ = bf16[256,640]{1,0:T(8,128)(2,1)S(1)} collective-permute-done((bf16[256,640]{1,0:T(8,128)(2,1)S(1)}, bf16[256,640]{1,0:T(8,128)(2,1)S(1)}, u32[]{:S(2)}, u32[]{:S(2)}) %collective-permute-start.26) | collective-permute-done | bytes 327712 | tf_op jit(solution)/shard_map/output_far_2_0/ppermute | solution.py:81
  65.9 1.6 %collective-permute-start.33 = (bf16[256,640]{1,0:T(8,128)(2,1)S(1)}, bf16[256,640]{1,0:T(8,128)(2,1)S(1)}, u32[]{:S(2)}, u32[]{:S(2)}) collective-permute-start(bf16[256,640]{1,0:T(8,128)(2,1)S(1)} %collective-permute-done.26.refs_0_), channel_id=1, source_target_pairs={{0,8},{10,2},{8,16},{18,10},{16,24},{26,18},{24,28},{30,26},{28,20... | collective-permute-start | bytes 983048 | tf_op jit(solution)/shard_map/output_far_3_0/ppermute | solution.py:81
  69.4 1.6 %collective-permute-start.21 = (bf16[256,640]{1,0:T(8,128)(2,1)S(1)}, bf16[256,640]{1,0:T(8,128)(2,1)S(1)}, u32[]{:S(2)}, u32[]{:S(2)}) collective-permute-start(bf16[256,640]{1,0:T(8,128)(2,1)S(1)} %collective-permute-done.20.refs_2_), channel_id=1, source_target_pairs={{0,8},{10,2},{8,16},{18,10},{16,24},{26,18},{24,28},{30,26},{28,20... | collective-permute-start | bytes 983048 | tf_op jit(solution)/shard_map/output_near_4_0/ppermute | solution.py:81
  70.9 2.0 %collective-permute-done.33.refs_0_ = bf16[256,640]{1,0:T(8,128)(2,1)S(1)} collective-permute-done((bf16[256,640]{1,0:T(8,128)(2,1)S(1)}, bf16[256,640]{1,0:T(8,128)(2,1)S(1)}, u32[]{:S(2)}, u32[]{:S(2)}) %collective-permute-start.33) | collective-permute-done | bytes 327712 | tf_op jit(solution)/shard_map/output_far_3_0/ppermute | solution.py:81
  74.1 2.3 %collective-permute-done.21.refs_0_ = bf16[256,640]{1,0:T(8,128)(2,1)S(1)} collective-permute-done((bf16[256,640]{1,0:T(8,128)(2,1)S(1)}, bf16[256,640]{1,0:T(8,128)(2,1)S(1)}, u32[]{:S(2)}, u32[]{:S(2)}) %collective-permute-start.21) | collective-permute-done | bytes 327712 | tf_op jit(solution)/shard_map/output_near_4_0/ppermute | solution.py:81
  78.1 1.6 %output_last_0.1 = bf16[256,640]{1,0:T(8,128)(2,1)} custom-call(s32[10]{0:T(128)S(1)} %pad_add_fusion.ids_ref, bf16[256,640]{1,0:T(8,128)(2,1)S(1)} %collective-permute-done.21.refs_0_, bf16[256,640]{1,0:T(8,128)(2,1)S(1)} %collective-permute-done.32.refs_1_, bf16[1,256,4096]{2,1,0:T(8,128)(2,1)S(1)} %bitcast.12, f32[1,256,640]{2,1,0:T(8,128)S(1)} %output_4.1.refs_3_), custom_call_target="tpu_custom_call" | custom-call | tf_op jit(solution)/shard_map/output_last_0/pallas_call | solution.py:185
  (83 shorter events, 20.4 us)
Async XLA Ops:
  3.1 7.7 %collective-permute-start = (bf16[264,640]{1,0:T(8,128)(2,1)S(1)}, bf16[264,640]{1,0:T(8,128)(2,1)S(1)}, u32[]{:S(2)}, u32[]{:S(2)}) collective-permute-start(bf16[264,640]{1,0:T(8,128)(2,1)S(1)} %prepare.1.refs_0_), channel_id=1, source_target_pairs={{0,8},{10,2},{8,16},{18,10},{16,24},{26,18},{24,28},{30,26},{28,20... | collective-permute-start | bytes 1013768 | tf_op jit(solution)/shard_map/projection_near_1_0/ppermute | solution.py:81
  5.7 8.7 %collective-permute-start.5 = (bf16[264,640]{1,0:T(8,128)(2,1)S(1)}, bf16[264,640]{1,0:T(8,128)(2,1)S(1)}, u32[]{:S(2)}, u32[]{:S(2)}) collective-permute-start(bf16[264,640]{1,0:T(8,128)(2,1)S(1)} %collective-permute-done.4.refs_1_), channel_id=1, source_target_pairs={{0,8},{10,2},{8,16},{18,10},{16,24},{26,18},{24,28},{30,26},{28,20... | collective-permute-start | bytes 1013768 | tf_op jit(solution)/shard_map/projection_far_1_0/ppermute | solution.py:81
  10.8 5.7 %collective-permute-start.9 = (bf16[264,640]{1,0:T(8,128)(2,1)S(1)}, bf16[264,640]{1,0:T(8,128)(2,1)S(1)}, u32[]{:S(2)}, u32[]{:S(2)}) collective-permute-start(bf16[264,640]{1,0:T(8,128)(2,1)S(1)} %collective-permute-done.refs_2_), channel_id=1, source_target_pairs={{0,2},{2,0},{4,6},{6,4},{8,10},{10,8},{12,14},{14,12},{16,18},{18,... | collective-permute-start | bytes 1013768 | tf_op jit(solution)/shard_map/projection_core_near_1_0/ppermute | solution.py:85
  10.8 7.7 %collective-permute-start.1 = (bf16[264,640]{1,0:T(8,128)(2,1)S(1)}, bf16[264,640]{1,0:T(8,128)(2,1)S(1)}, u32[]{:S(2)}, u32[]{:S(2)}) collective-permute-start(bf16[264,640]{1,0:T(8,128)(2,1)S(1)} %collective-permute-done.refs_2_), channel_id=1, source_target_pairs={{0,8},{10,2},{8,16},{18,10},{16,24},{26,18},{24,28},{30,26},{28,20... | collective-permute-start | bytes 1013768 | tf_op jit(solution)/shard_map/projection_near_2_0/ppermute | solution.py:81
  14.4 7.2 %collective-permute-start.6 = (bf16[264,640]{1,0:T(8,128)(2,1)S(1)}, bf16[264,640]{1,0:T(8,128)(2,1)S(1)}, u32[]{:S(2)}, u32[]{:S(2)}) collective-permute-start(bf16[264,640]{1,0:T(8,128)(2,1)S(1)} %collective-permute-done.5.refs_0_), channel_id=1, source_target_pairs={{0,8},{10,2},{8,16},{18,10},{16,24},{26,18},{24,28},{30,26},{28,20... | collective-permute-start | bytes 1013768 | tf_op jit(solution)/shard_map/projection_far_2_0/ppermute | solution.py:81
  18.5 5.3 %collective-permute-start.10 = (bf16[264,640]{1,0:T(8,128)(2,1)S(1)}, bf16[264,640]{1,0:T(8,128)(2,1)S(1)}, u32[]{:S(2)}, u32[]{:S(2)}) collective-permute-start(bf16[264,640]{1,0:T(8,128)(2,1)S(1)} %collective-permute-done.1.refs_2_), channel_id=1, source_target_pairs={{0,2},{2,0},{4,6},{6,4},{8,10},{10,8},{12,14},{14,12},{16,18},{18,... | collective-permute-start | bytes 1013768 | tf_op jit(solution)/shard_map/projection_core_near_2_0/ppermute | solution.py:85
  18.6 5.2 %collective-permute-start.8 = (bf16[264,640]{1,0:T(8,128)(2,1)S(1)}, bf16[264,640]{1,0:T(8,128)(2,1)S(1)}, u32[]{:S(2)}, u32[]{:S(2)}) collective-permute-start(bf16[264,640]{1,0:T(8,128)(2,1)S(1)} %collective-permute-done.5.refs_0_), channel_id=1, source_target_pairs={{0,2},{2,0},{4,6},{6,4},{8,10},{10,8},{12,14},{14,12},{16,18},{18,... | collective-permute-start | bytes 1013768 | tf_op jit(solution)/shard_map/projection_core_far_1_0/ppermute | solution.py:85
  19.1 7.2 %collective-permute-start.2 = (bf16[264,640]{1,0:T(8,128)(2,1)S(1)}, bf16[264,640]{1,0:T(8,128)(2,1)S(1)}, u32[]{:S(2)}, u32[]{:S(2)}) collective-permute-start(bf16[264,640]{1,0:T(8,128)(2,1)S(1)} %collective-permute-done.1.refs_2_), channel_id=1, source_target_pairs={{0,8},{10,2},{8,16},{18,10},{16,24},{26,18},{24,28},{30,26},{28,20... | collective-permute-start | bytes 1013768 | tf_op jit(solution)/shard_map/projection_near_3_0/ppermute | solution.py:81
  21.7 8.2 %collective-permute-start.13 = (bf16[264,640]{1,0:T(8,128)(2,1)S(1)}, bf16[264,640]{1,0:T(8,128)(2,1)S(1)}, u32[]{:S(2)}, u32[]{:S(2)}) collective-permute-start(bf16[264,640]{1,0:T(8,128)(2,1)S(1)} %collective-permute-done.6.refs_0_), channel_id=1, source_target_pairs={{0,8},{10,2},{8,16},{18,10},{16,24},{26,18},{24,28},{30,26},{28,20... | collective-permute-start | bytes 1013768 | tf_op jit(solution)/shard_map/projection_far_3_0/ppermute | solution.py:81
  26.3 3.6 %collective-permute-start.11 = (bf16[264,640]{1,0:T(8,128)(2,1)S(1)}, bf16[264,640]{1,0:T(8,128)(2,1)S(1)}, u32[]{:S(2)}, u32[]{:S(2)}) collective-permute-start(bf16[264,640]{1,0:T(8,128)(2,1)S(1)} %collective-permute-done.2.refs_2_), channel_id=1, source_target_pairs={{0,2},{2,0},{4,6},{6,4},{8,10},{10,8},{12,14},{14,12},{16,18},{18,... | collective-permute-start | bytes 1013768 | tf_op jit(solution)/shard_map/projection_core_near_3_0/ppermute | solution.py:85
  26.3 3.6 %collective-permute-start.7 = (bf16[264,640]{1,0:T(8,128)(2,1)S(1)}, bf16[264,640]{1,0:T(8,128)(2,1)S(1)}, u32[]{:S(2)}, u32[]{:S(2)}) collective-permute-start(bf16[264,640]{1,0:T(8,128)(2,1)S(1)} %collective-permute-done.6.refs_0_), channel_id=1, source_target_pairs={{0,2},{2,0},{4,6},{6,4},{8,10},{10,8},{12,14},{14,12},{16,18},{18,... | collective-permute-start | bytes 1013768 | tf_op jit(solution)/shard_map/projection_core_far_2_0/ppermute | solution.py:85
  26.8 7.2 %collective-permute-start.3 = (bf16[264,640]{1,0:T(8,128)(2,1)S(1)}, bf16[264,640]{1,0:T(8,128)(2,1)S(1)}, u32[]{:S(2)}, u32[]{:S(2)}) collective-permute-start(bf16[264,640]{1,0:T(8,128)(2,1)S(1)} %collective-permute-done.2.refs_2_), channel_id=1, source_target_pairs={{0,8},{10,2},{8,16},{18,10},{16,24},{26,18},{24,28},{30,26},{28,20... | collective-permute-start | bytes 1013768 | tf_op jit(solution)/shard_map/projection_near_4_0/ppermute | solution.py:81
  29.9 4.1 %collective-permute-start.14 = (bf16[264,640]{1,0:T(8,128)(2,1)S(1)}, bf16[264,640]{1,0:T(8,128)(2,1)S(1)}, u32[]{:S(2)}, u32[]{:S(2)}) collective-permute-start(bf16[264,640]{1,0:T(8,128)(2,1)S(1)} %collective-permute-done.13.refs_0_), channel_id=1, source_target_pairs={{0,2},{2,0},{4,6},{6,4},{8,10},{10,8},{12,14},{14,12},{16,18},{18,... | collective-permute-start | bytes 1013768 | tf_op jit(solution)/shard_map/projection_core_far_3_0/ppermute | solution.py:85
  37.0 7.3 %collective-permute-start.15 = (bf16[136,640]{1,0:T(8,128)(2,1)S(1)}, bf16[136,640]{1,0:T(8,128)(2,1)S(1)}, u32[]{:S(2)}, u32[]{:S(2)}) collective-permute-start(bf16[136,640]{1,0:T(8,128)(2,1)S(1)} %get-tuple-element.58.refs_2_.refs_8_), channel_id=1, source_target_pairs={{0,1},{1,0},{2,3},{3,2},{4,5},{5,4},{6,7},{7,6},{8,9},{9,8},{10,11... | collective-permute-start | bytes 522248 | tf_op jit(solution)/shard_map/ppermute | solution.py:552
  39.9 7.9 %collective-permute-start.17 = (bf16[136,640]{1,0:T(8,128)(2,1)S(1)}, bf16[136,640]{1,0:T(8,128)(2,1)S(1)}, u32[]{:S(2)}, u32[]{:S(2)}) collective-permute-start(bf16[136,640]{1,0:T(8,128)(2,1)S(1)} %get-tuple-element.61.refs_3_.refs_8_), channel_id=1, source_target_pairs={{0,1},{1,0},{2,3},{3,2},{4,5},{5,4},{6,7},{7,6},{8,9},{9,8},{10,11... | collective-permute-start | bytes 522248 | tf_op jit(solution)/shard_map/ppermute | solution.py:552
  46.1 5.2 %collective-permute-start.22 = (bf16[128,640]{1,0:T(8,128)(2,1)S(1)}, bf16[128,640]{1,0:T(8,128)(2,1)S(1)}, u32[]{:S(2)}, u32[]{:S(2)}) collective-permute-start(bf16[128,640]{1,0:T(8,128)(2,1)S(1)} %far_part_1_0.1.refs_0_), channel_id=1, source_target_pairs={{0,2},{2,0},{4,6},{6,4},{8,10},{10,8},{12,14},{14,12},{16,18},{18,... | collective-permute-start | bytes 491528 | tf_op jit(solution)/shard_map/output_core_own_0/ppermute | solution.py:85
  46.1 6.7 %collective-permute-start.16 = (bf16[128,640]{1,0:T(8,128)(2,1)S(1)}, bf16[128,640]{1,0:T(8,128)(2,1)S(1)}, u32[]{:S(2)}, u32[]{:S(2)}) collective-permute-start(bf16[128,640]{1,0:T(8,128)(2,1)S(1)} %far_part_1_0.1.refs_0_), channel_id=1, source_target_pairs={{0,8},{10,2},{8,16},{18,10},{16,24},{26,18},{24,28},{30,26},{28,20... | collective-permute-start | bytes 491528 | tf_op jit(solution)/shard_map/output_near_1_0/ppermute | solution.py:81
  49.6 3.3 %collective-permute-start.24 = (bf16[128,640]{1,0:T(8,128)(2,1)S(1)}, bf16[128,640]{1,0:T(8,128)(2,1)S(1)}, u32[]{:S(2)}, u32[]{:S(2)}) collective-permute-start(bf16[128,640]{1,0:T(8,128)(2,1)S(1)} %far_part_1_128.1.refs_1_), channel_id=1, source_target_pairs={{0,2},{2,0},{4,6},{6,4},{8,10},{10,8},{12,14},{14,12},{16,18},{18,... | collective-permute-start | bytes 491528 | tf_op jit(solution)/shard_map/output_core_own_1/ppermute | solution.py:85
  49.7 5.3 %collective-permute-start.18 = (bf16[128,640]{1,0:T(8,128)(2,1)S(1)}, bf16[128,640]{1,0:T(8,128)(2,1)S(1)}, u32[]{:S(2)}, u32[]{:S(2)}) collective-permute-start(bf16[128,640]{1,0:T(8,128)(2,1)S(1)} %far_part_1_128.1.refs_1_), channel_id=1, source_target_pairs={{0,8},{10,2},{8,16},{18,10},{16,24},{26,18},{24,28},{30,26},{28,20... | collective-permute-start | bytes 491528 | tf_op jit(solution)/shard_map/output_near_1_1/ppermute | solution.py:81
  51.3 5.5 %collective-permute-start.23 = (bf16[128,640]{1,0:T(8,128)(2,1)S(1)}, bf16[128,640]{1,0:T(8,128)(2,1)S(1)}, u32[]{:S(2)}, u32[]{:S(2)}) collective-permute-start(bf16[128,640]{1,0:T(8,128)(2,1)S(1)} %collective-permute-done.22.refs_2_), channel_id=1, source_target_pairs={{0,8},{10,2},{8,16},{18,10},{16,24},{26,18},{24,28},{30,26},{28,20... | collective-permute-start | bytes 491528 | tf_op jit(solution)/shard_map/output_far_1_0/ppermute | solution.py:81
  52.9 5.7 %collective-permute-start.25 = (bf16[128,640]{1,0:T(8,128)(2,1)S(1)}, bf16[128,640]{1,0:T(8,128)(2,1)S(1)}, u32[]{:S(2)}, u32[]{:S(2)}) collective-permute-start(bf16[128,640]{1,0:T(8,128)(2,1)S(1)} %collective-permute-done.24.refs_3_), channel_id=1, source_target_pairs={{0,8},{10,2},{8,16},{18,10},{16,24},{26,18},{24,28},{30,26},{28,20... | collective-permute-start | bytes 491528 | tf_op jit(solution)/shard_map/output_far_1_1/ppermute | solution.py:81
  55.1 5.3 %collective-permute-start.29 = (bf16[256,640]{1,0:T(8,128)(2,1)S(1)}, bf16[256,640]{1,0:T(8,128)(2,1)S(1)}, u32[]{:S(2)}, u32[]{:S(2)}) collective-permute-start(bf16[256,640]{1,0:T(8,128)(2,1)S(1)} %constant_dynamic-update-slice_fusion.refs_4_), channel_id=1, source_target_pairs={{0,2},{2,0},{4,6},{6,4},{8,10},{10,8},{12,14},{14,12},{16,18},{18,... | collective-permute-start | bytes 983048 | tf_op jit(solution)/shard_map/output_core_near_1_0/ppermute | solution.py:85
  55.1 7.1 %collective-permute-start.19 = (bf16[256,640]{1,0:T(8,128)(2,1)S(1)}, bf16[256,640]{1,0:T(8,128)(2,1)S(1)}, u32[]{:S(2)}, u32[]{:S(2)}) collective-permute-start(bf16[256,640]{1,0:T(8,128)(2,1)S(1)} %constant_dynamic-update-slice_fusion.refs_4_), channel_id=1, source_target_pairs={{0,8},{10,2},{8,16},{18,10},{16,24},{26,18},{24,28},{30,26},{28,20... | collective-permute-start | bytes 983048 | tf_op jit(solution)/shard_map/output_near_2_0/ppermute | solution.py:81
  58.6 7.3 %collective-permute-start.26 = (bf16[256,640]{1,0:T(8,128)(2,1)S(1)}, bf16[256,640]{1,0:T(8,128)(2,1)S(1)}, u32[]{:S(2)}, u32[]{:S(2)}) collective-permute-start(bf16[256,640]{1,0:T(8,128)(2,1)S(1)} %constant_dynamic-update-slice_fusion.2.refs_0_), channel_id=1, source_target_pairs={{0,8},{10,2},{8,16},{18,10},{16,24},{26,18},{24,28},{30,26},{28,20... | collective-permute-start | bytes 983048 | tf_op jit(solution)/shard_map/output_far_2_0/ppermute | solution.py:81
  60.4 7.1 %collective-permute-start.28 = (bf16[256,640]{1,0:T(8,128)(2,1)S(1)}, bf16[256,640]{1,0:T(8,128)(2,1)S(1)}, u32[]{:S(2)}, u32[]{:S(2)}) collective-permute-start(bf16[256,640]{1,0:T(8,128)(2,1)S(1)} %constant_dynamic-update-slice_fusion.2.refs_0_), channel_id=1, source_target_pairs={{0,2},{2,0},{4,6},{6,4},{8,10},{10,8},{12,14},{14,12},{16,18},{18,... | collective-permute-start | bytes 983048 | tf_op jit(solution)/shard_map/output_core_far_1_0/ppermute | solution.py:85
  62.3 5.2 %collective-permute-start.30 = (bf16[256,640]{1,0:T(8,128)(2,1)S(1)}, bf16[256,640]{1,0:T(8,128)(2,1)S(1)}, u32[]{:S(2)}, u32[]{:S(2)}) collective-permute-start(bf16[256,640]{1,0:T(8,128)(2,1)S(1)} %collective-permute-done.19.refs_2_), channel_id=1, source_target_pairs={{0,2},{2,0},{4,6},{6,4},{8,10},{10,8},{12,14},{14,12},{16,18},{18,... | collective-permute-start | bytes 983048 | tf_op jit(solution)/shard_map/output_core_near_2_0/ppermute | solution.py:85
  62.3 7.1 %collective-permute-start.20 = (bf16[256,640]{1,0:T(8,128)(2,1)S(1)}, bf16[256,640]{1,0:T(8,128)(2,1)S(1)}, u32[]{:S(2)}, u32[]{:S(2)}) collective-permute-start(bf16[256,640]{1,0:T(8,128)(2,1)S(1)} %collective-permute-done.19.refs_2_), channel_id=1, source_target_pairs={{0,8},{10,2},{8,16},{18,10},{16,24},{26,18},{24,28},{30,26},{28,20... | collective-permute-start | bytes 983048 | tf_op jit(solution)/shard_map/output_near_3_0/ppermute | solution.py:81
  65.9 7.1 %collective-permute-start.33 = (bf16[256,640]{1,0:T(8,128)(2,1)S(1)}, bf16[256,640]{1,0:T(8,128)(2,1)S(1)}, u32[]{:S(2)}, u32[]{:S(2)}) collective-permute-start(bf16[256,640]{1,0:T(8,128)(2,1)S(1)} %collective-permute-done.26.refs_0_), channel_id=1, source_target_pairs={{0,8},{10,2},{8,16},{18,10},{16,24},{26,18},{24,28},{30,26},{28,20... | collective-permute-start | bytes 983048 | tf_op jit(solution)/shard_map/output_far_3_0/ppermute | solution.py:81
  67.4 5.5 %collective-permute-start.27 = (bf16[256,640]{1,0:T(8,128)(2,1)S(1)}, bf16[256,640]{1,0:T(8,128)(2,1)S(1)}, u32[]{:S(2)}, u32[]{:S(2)}) collective-permute-start(bf16[256,640]{1,0:T(8,128)(2,1)S(1)} %collective-permute-done.26.refs_0_), channel_id=1, source_target_pairs={{0,2},{2,0},{4,6},{6,4},{8,10},{10,8},{12,14},{14,12},{16,18},{18,... | collective-permute-start | bytes 983048 | tf_op jit(solution)/shard_map/output_core_far_2_0/ppermute | solution.py:85
  69.4 3.6 %collective-permute-start.31 = (bf16[256,640]{1,0:T(8,128)(2,1)S(1)}, bf16[256,640]{1,0:T(8,128)(2,1)S(1)}, u32[]{:S(2)}, u32[]{:S(2)}) collective-permute-start(bf16[256,640]{1,0:T(8,128)(2,1)S(1)} %collective-permute-done.20.refs_2_), channel_id=1, source_target_pairs={{0,2},{2,0},{4,6},{6,4},{8,10},{10,8},{12,14},{14,12},{16,18},{18,... | collective-permute-start | bytes 983048 | tf_op jit(solution)/shard_map/output_core_near_3_0/ppermute | solution.py:85
  69.4 7.1 %collective-permute-start.21 = (bf16[256,640]{1,0:T(8,128)(2,1)S(1)}, bf16[256,640]{1,0:T(8,128)(2,1)S(1)}, u32[]{:S(2)}, u32[]{:S(2)}) collective-permute-start(bf16[256,640]{1,0:T(8,128)(2,1)S(1)} %collective-permute-done.20.refs_2_), channel_id=1, source_target_pairs={{0,8},{10,2},{8,16},{18,10},{16,24},{26,18},{24,28},{30,26},{28,20... | collective-permute-start | bytes 983048 | tf_op jit(solution)/shard_map/output_near_4_0/ppermute | solution.py:81
  72.9 3.5 %collective-permute-start.34 = (bf16[256,640]{1,0:T(8,128)(2,1)S(1)}, bf16[256,640]{1,0:T(8,128)(2,1)S(1)}, u32[]{:S(2)}, u32[]{:S(2)}) collective-permute-start(bf16[256,640]{1,0:T(8,128)(2,1)S(1)} %collective-permute-done.33.refs_0_), channel_id=1, source_target_pairs={{0,2},{2,0},{4,6},{6,4},{8,10},{10,8},{12,14},{14,12},{16,18},{18,... | collective-permute-start | bytes 983048 | tf_op jit(solution)/shard_map/output_core_far_3_0/ppermute | solution.py:85
  (14 other events, 73.3 us)

commit v6 on v5

--- a/solution.py
+++ b/solution.py
@@ -15,7 +15,6 @@
 bf16 = jnp.bfloat16
 f32 = jnp.float32
 in_vmem = pl.BlockSpec(memory_space=pltpu.VMEM)
-in_smem = pl.BlockSpec(memory_space=pltpu.SMEM)
 params = pltpu.CompilerParams(vmem_limit_bytes=12 * 2**20)
 
 
@@ -39,7 +38,7 @@
     return pl.CostEstimate(flops=int(flops), bytes_accessed=int(size), transcendentals=0)
 
 
-def prepare_kernel(ids_ref, x_ref, gain_ref, out_ref):
+def prepare_kernel(x_ref, gain_ref, out_ref):
     rows = x_ref.shape[0]
     wide = x_ref[...].astype(f32)
     out_ref[:rows] = (wide * column(gain_ref[...])).astype(bf16)
@@ -50,17 +49,17 @@
     out_ref[rows:] = side.astype(bf16)
 
 
-def prepare(ids, x, gain):
+def prepare(x, gain):
     rows, tokens = x.shape
     return pl.pallas_call(
         prepare_kernel,
-        in_specs=[in_smem, in_vmem, in_vmem],
+        in_specs=[in_vmem, in_vmem],
         out_specs=in_vmem,
         out_shape=shape_of((rows + side_rows, tokens), bf16),
         compiler_params=params,
         cost_estimate=estimate(3e9, 0),
         name="prepare",
-    )(ids, x, gain.reshape(1, rows))
+    )(x, gain.reshape(1, rows))
 
 
 def chip_count():
@@ -85,31 +84,25 @@
     return lax.ppermute(block, "fsdp", [(i, i ^ 1) for i in range(2 * chip_count())])
 
 
-def ring_ids():
+def my_core():
+    return lax.axis_index("fsdp") & 1
+
+
+def source_chip(steps):
     chips = chip_count()
-    me = lax.axis_index("fsdp")
-    chip, core = me // 2, me % 2
-    place = jnp.where(chip % 2 == 0, chip // 2, chips - 1 - chip // 2)
-    steps = jnp.arange(chips, dtype=jnp.int32)
-    places = (place + jnp.where(core == 0, chips - steps, steps)) % chips
-    ids = jnp.where(places < (chips + 1) // 2, 2 * places, 2 * (chips - 1 - places) + 1)
-    mine = jnp.stack([core, lax.axis_index("ctx")])
-    return jnp.concatenate([ids, mine]).astype(jnp.int32)
-
-
-def core_of(ids_ref):
-    return ids_ref[ids_ref.shape[0] - 2]
-
-
-def turn_of(ids_ref):
-    return ids_ref[ids_ref.shape[0] - 1]
+    chip = lax.shift_right_logical(lax.axis_index("fsdp"), 1)
+    half = lax.shift_right_logical(chip, 1)
+    place = jnp.where(chip & 1 == 0, half, chips - 1 - half)
+    place = place + jnp.where(my_core() == 0, chips - steps, steps)
+    place = jnp.where(place >= chips, place - chips, place)
+    return jnp.where(place < (chips + 1) // 2, 2 * place, 2 * (chips - 1 - place) + 1)
 
 
 def take_from(refs, number):
     return [refs.pop(0) for _ in range(number)]
 
 
-def products(ids, items, weight, running, side, finish, cost, name, cut=(0, 1)):
+def products(items, weight, running, side, finish, cost, name, cut=(0, 1)):
     streams, out_rows, features = weight.shape
     out_rows //= cut[1]
     out_here = slice(cut[0] * out_rows, (cut[0] + 1) * out_rows)
@@ -124,15 +117,16 @@
     width = 2 * rows if padded else rows
     scratch_shapes = [pltpu.VMEM((len(items) * width, tokens), bf16)] if padded else []
 
-    def kernel(ids_ref, *refs):
+    def kernel(*refs):
         refs = list(refs)
-        take = lambda n: [refs.pop(0) for _ in range(n)]
+        take = lambda n: take_from(refs, n)
         shard_refs = take(count)
         (weight_ref,) = take(1)
         state_refs = take(len(state))
         extra_refs = take(len(extras))
         outs = take(len(out_shape))
-        core = core_of(ids_ref)
+        core = my_core()
+        chip_of = {steps: source_chip(steps) for steps in sorted({item[0] for item in items})}
         if padded:
             (beside_ref,) = refs
             beside_ref[...] = jnp.zeros(beside_ref.shape, bf16)
@@ -158,8 +152,8 @@
 
         def total(stream):
             left = []
-            for slot, other, _ in items:
-                block = ids_ref[slot]
+            for steps, other, _ in items:
+                block = chip_of[steps]
                 if not padded:
                     block = 2 * block + (1 - core if other else core)
                 at = pl.ds(pl.multiple_of(block * width, width), width)
@@ -181,10 +175,10 @@
         if side:
             out_shape.append(shape_of((side_rows, tokens), f32))
         if not first_group:
-            aliases = {1 + count + 1 + i: i for i in range(len(state))}
+            aliases = {count + 1 + i: i for i in range(len(state))}
     return pl.pallas_call(
         kernel,
-        in_specs=[in_smem] + [in_vmem] * (count + 1 + len(state) + len(extras)),
+        in_specs=[in_vmem] * (count + 1 + len(state) + len(extras)),
         out_specs=[in_vmem] * len(out_shape),
         out_shape=out_shape,
         scratch_shapes=scratch_shapes,
@@ -192,10 +186,10 @@
         compiler_params=params,
         cost_estimate=estimate(cost, 0),
         name=name,
-    )(ids, *shards, weight, *state, *extras)
-
-
-def gather_products(ids, own, weight, beside, side, finish, name):
+    )(*shards, weight, *state, *extras)
+
+
+def gather_products(own, weight, beside, side, finish, name):
     chips = chip_count()
     last_step = chips // 2
 
@@ -222,15 +216,15 @@
         theirs = send(other_core, arrived, f"core_near_{step}")
         pair = [(step, 0, arrived), (chips - step, 1, theirs)]
         if step < last_step:
-            running = products(ids, items + pair, weight, running, side, None, 0, f"{name}_{step}")
+            running = products(items + pair, weight, running, side, None, 0, f"{name}_{step}")
             far = joined(send(along_ring, far, f"far_{step}"))
             theirs = send(other_core, far, f"core_far_{step}")
             items = [(step, 1, far), (chips - step, 0, theirs)]
         else:
-            running = products(ids, items, weight, running, side, None, STAGGER, f"{name}_{step}")
+            running = products(items, weight, running, side, None, STAGGER, f"{name}_{step}")
             items = pair
     results = [
-        products(ids, items, weight, running, side, end, 0, f"{name}_last_{k}", (k, len(finish)))
+        products(items, weight, running, side, end, 0, f"{name}_last_{k}", (k, len(finish)))
         for k, end in enumerate(finish)
     ]
     return results, beside
@@ -413,7 +407,7 @@
             total_ref[here, block_lanes(2 * a + 1)] = imag
 
 
-def own_part(ids, projected, messages, moved, taps, filters, table):
+def own_part(projected, messages, moved, taps, filters, table):
     streams, half, tokens = projected[0].shape
     parts = channel_parts(2 * half)
     number = len(parts)
@@ -422,9 +416,9 @@
     first = 0 if moved else 1
     pairs = [[(b, a - b) for b in range(first, a + 1)] for a in range(blocks)]
 
-    def kernel(ids_ref, *refs):
+    def kernel(*refs):
         refs = list(refs)
-        take = lambda n: [refs.pop(0) for _ in range(n)]
+        take = lambda n: take_from(refs, n)
         projected_refs, message_refs = take(2), take(number)
         taps_ref, filters_ref, table_ref = take(3)
         query_refs, total_refs = take(number), take(number)
@@ -433,7 +427,7 @@
         columns = [tap_columns(taps_ref[s]) for s in range(streams)]
         for part, (begin, rows) in enumerate(parts):
             if moved:
-                inside = turn_of(ids_ref) > 0
+                inside = lax.axis_index("ctx") > 0
                 halo = halo_columns(message_refs[part], streams, count, inside)
             tile = min(rows, 64)
             for start in range(0, rows, tile):
@@ -462,19 +456,19 @@
     inputs = [*projected, *(moved or messages), taps, filters, table]
     outs = pl.pallas_call(
         kernel,
-        in_specs=[in_smem] + [in_vmem] * len(inputs),
+        in_specs=[in_vmem] * len(inputs),
         out_specs=[in_vmem] * len(out_shape),
         out_shape=out_shape,
         scratch_shapes=[pltpu.VMEM((half, 2 * tokens), f32)],
         compiler_params=params,
         cost_estimate=estimate(0, 0),
         name="own_part",
-    )(ids, *inputs)
+    )(*inputs)
     gated = list(outs[2 * number :]) if moved else messages
     return list(outs[:number]), list(outs[number : 2 * number]), gated
 
 
-def far_part(ids, turn, begin, moved, total, filters, table, last, own):
+def far_part(turn, begin, moved, total, filters, table, last, own):
     rows, tokens = total.shape[0], moved.shape[1]
     blocks = tokens // block_len
     pairs = [[(b, turn * blocks + a - b) for b in range(blocks)] for a in range(blocks)]
@@ -482,13 +476,13 @@
         pairs = [terms + [(blocks, a)] for a, terms in enumerate(pairs)]
     channels_here = slice(begin, begin + rows)
 
-    def kernel(ids_ref, *refs):
+    def kernel(*refs):
         refs = list(refs)
-        take = lambda n: [refs.pop(0) for _ in range(n)]
+        take = lambda n: take_from(refs, n)
         moved_ref, total_ref, filters_ref, table_ref = take(4)
         own_refs = take(2) if own else None
         spec_ref = refs.pop()
-        inside = turn_of(ids_ref) >= turn
+        inside = lax.axis_index("ctx") >= turn
         pieces = [
             jnp.where(inside, moved_ref[:rows, block_lanes(b)], jnp.zeros((), bf16))
             for b in range(blocks)
@@ -537,14 +531,14 @@
         scratch.append(pltpu.VMEM((rows, 2 * tokens), f32))
     return pl.pallas_call(
         kernel,
-        in_specs=[in_smem] + [in_vmem] * len(args),
+        in_specs=[in_vmem] * len(args),
         out_specs=in_vmem,
         out_shape=out_shape,
         scratch_shapes=scratch[::-1],
         compiler_params=params,
         cost_estimate=estimate(0, 0),
         name=f"far_part_{turn}_{begin}",
-    )(ids, *args)
+    )(*args)
 
 
 def from_before(block):
@@ -566,13 +560,12 @@
     turns = lax.axis_size("ctx")
     parts = channel_parts(channels)
     forward, segments, inverse = (jnp.asarray(t) for t in dft_tables())
-    ids = ring_ids()
-    own = prepare(ids, activations, norm_gain)
+    own = prepare(activations, norm_gain)
 
     filters = filter_spectra(long_filter, segments)
     finish = [projection_finish(features, w_short, tokens, k) for k in range(2)]
     results, (filters,) = gather_products(
-        ids, [own], w_in, [filters], True, finish, "projection"
+        [own], w_in, [filters], True, finish, "projection"
     )
     projected = [result[0] for result in results]
     first_blocks = [result[1] for result in results]
@@ -580,7 +573,7 @@
     moving = [from_before(message) for message in messages]
     exact = turns > 2
     query, totals, gated = own_part(
-        ids, projected, messages, moving if exact else None, w_short, filters, forward
+        projected, messages, moving if exact else None, w_short, filters, forward
     )
     if exact:
         moving = [from_before(part) for part in gated]
@@ -593,7 +586,7 @@
                 if not exact:
                     own_block = (first_blocks[2 * begin // channels], w_short)
             done = far_part(
-                ids, turn, begin, moving[k], totals[k], filters, forward, last, own_block
+                turn, begin, moving[k], totals[k], filters, forward, last, own_block
             )
             if last is None:
                 totals[k] = done
@@ -603,7 +596,7 @@
 
     finish = [output_finish(channels, tokens)]
     ((result,),), _ = gather_products(
-        ids, mixed, w_out[None], [], False, finish, "output"
+        mixed, w_out[None], [], False, finish, "output"
     )
     return result
 

time: 79.9 us -> 77.1 us (0.965)
  Pallas kernels: 22.9 us -> 14.9 us
  waiting for transfers between devices: 22.6 us -> 26.7 us
  starting transfers between devices: 32.1 us -> 33.5 us
    pallas_call x15, Pallas kernels: 22.1 us -> 14 us  [the longest x11 10.3 us: products(): pl.pallas_call(kernel, in_specs=[in_vmem] * (count + 1 + len(state) + len...]
    ppermute x16, waiting for transfers between devices: 19.4 us -> 21.3 us  [along_ring(): return lax.ppermute(block, 'fsdp', pairs)]
    ppermute x16, starting transfers between devices: 28 us -> 29.4 us  [along_ring(): return lax.ppermute(block, 'fsdp', pairs)]
    ppermute x17, waiting for transfers between devices: 0.91 us -> 1.98 us  [other_core(): lax.ppermute(block, 'fsdp', [(i, i ^ 1) for i in range(2 * chip_count())])]
    ppermute x2, waiting for transfers between devices: 2.33 us -> 3.39 us  [from_before(): lax.ppermute(block, 'ctx', [(i, (i + 1) % count) for i in range(count)])]
  transfers between devices with their start and end apart: 35 -> 35, of which waited for: 16 -> 18; matrix products, arithmetic and copies ran while one was open for 0% -> 0% of each run, Pallas kernels for 24% -> 17%
where the time goes in v6:
time: 77.1 us; the launch traced here: 77 us
  starting transfers between devices  33.5 us (43%)
  waiting for transfers between devices  26.7 us (35%)
  Pallas kernels  14.9 us (19%)
  local copies, waits for them, and re-layouts  1.76 us (2%)
    ppermute x16, starting transfers between devices, along_ring(): return lax.ppermute(block, 'fsdp', pairs)  29.4 us
    ppermute x16, waiting for transfers between devices, along_ring(): return lax.ppermute(block, 'fsdp', pairs)  21.3 us
    pallas_call x11, Pallas kernels, products(): pl.pallas_call(kernel, in_specs=[in_vmem] * (count + 1 + len(state) + len...  10.3 us
    ppermute x2, waiting for transfers between devices, from_before(): lax.ppermute(block, 'ctx', [(i, (i + 1) % count) for i in range(count)])  3.39 us
    pallas_call x2, Pallas kernels, far_part(): pl.pallas_call(kernel, in_specs=[in_vmem] * len(args), out_specs=in_vmem,...  2.47 us
    ppermute x2, starting transfers between devices, from_before(): lax.ppermute(block, 'ctx', [(i, (i + 1) % count) for i in range(count)])  2.16 us
    ppermute x17, waiting for transfers between devices, other_core(): lax.ppermute(block, 'fsdp', [(i, i ^ 1) for i in range(2 * chip_count())])  1.98 us
    ppermute x17, starting transfers between devices, other_core(): lax.ppermute(block, 'fsdp', [(i, i ^ 1) for i in range(2 * chip_count())])  1.88 us
  transfers between devices with their start and end apart: 35, of which 18 were waited for; matrix products, arithmetic and copies ran while one was open for 0% of the time, Pallas kernels for 17%

profile of v6, /device:TPU:0, one launch (start us, length us, event | category | flops | bytes accessed | tf_op | source)
XLA Modules:
  0.0 77.0 jit_solution(5639299497959020759)
XLA Ops:
  2.4 2.6 %collective-permute-start = (bf16[264,640]{1,0:T(8,128)(2,1)S(1)}, bf16[264,640]{1,0:T(8,128)(2,1)S(1)}, u32[]{:S(2)}, u32[]{:S(2)}) collective-permute-start(bf16[264,640]{1,0:T(8,128)(2,1)S(1)} %prepare.1.refs_0_), channel_id=1, source_target_pairs={{0,8},{10,2},{8,16},{18,10},{16,24},{26,18},{24,28},{30,26},{28,20... | collective-permute-start | bytes 1013768 | tf_op jit(solution)/shard_map/projection_near_1_0/ppermute | solution.py:80
  5.1 1.6 %collective-permute-start.5 = (bf16[264,640]{1,0:T(8,128)(2,1)S(1)}, bf16[264,640]{1,0:T(8,128)(2,1)S(1)}, u32[]{:S(2)}, u32[]{:S(2)}) collective-permute-start(bf16[264,640]{1,0:T(8,128)(2,1)S(1)} %collective-permute-done.4.refs_1_), channel_id=1, source_target_pairs={{0,8},{10,2},{8,16},{18,10},{16,24},{26,18},{24,28},{30,26},{28,20... | collective-permute-start | bytes 1013768 | tf_op jit(solution)/shard_map/projection_far_1_0/ppermute | solution.py:80
  7.5 2.7 %collective-permute-done.refs_2_ = bf16[264,640]{1,0:T(8,128)(2,1)S(1)} collective-permute-done((bf16[264,640]{1,0:T(8,128)(2,1)S(1)}, bf16[264,640]{1,0:T(8,128)(2,1)S(1)}, u32[]{:S(2)}, u32[]{:S(2)}) %collective-permute-start) | collective-permute-done | bytes 337952 | tf_op jit(solution)/shard_map/projection_near_1_0/ppermute | solution.py:80
  10.2 2.1 %collective-permute-start.1 = (bf16[264,640]{1,0:T(8,128)(2,1)S(1)}, bf16[264,640]{1,0:T(8,128)(2,1)S(1)}, u32[]{:S(2)}, u32[]{:S(2)}) collective-permute-start(bf16[264,640]{1,0:T(8,128)(2,1)S(1)} %collective-permute-done.refs_2_), channel_id=1, source_target_pairs={{0,8},{10,2},{8,16},{18,10},{16,24},{26,18},{24,28},{30,26},{28,20... | collective-permute-start | bytes 1013768 | tf_op jit(solution)/shard_map/projection_near_2_0/ppermute | solution.py:80
  12.3 1.5 %collective-permute-done.5.refs_0_ = bf16[264,640]{1,0:T(8,128)(2,1)S(1)} collective-permute-done((bf16[264,640]{1,0:T(8,128)(2,1)S(1)}, bf16[264,640]{1,0:T(8,128)(2,1)S(1)}, u32[]{:S(2)}, u32[]{:S(2)}) %collective-permute-start.5) | collective-permute-done | bytes 337952 | tf_op jit(solution)/shard_map/projection_far_1_0/ppermute | solution.py:80
  13.8 2.1 %collective-permute-start.6 = (bf16[264,640]{1,0:T(8,128)(2,1)S(1)}, bf16[264,640]{1,0:T(8,128)(2,1)S(1)}, u32[]{:S(2)}, u32[]{:S(2)}) collective-permute-start(bf16[264,640]{1,0:T(8,128)(2,1)S(1)} %collective-permute-done.5.refs_0_), channel_id=1, source_target_pairs={{0,8},{10,2},{8,16},{18,10},{16,24},{26,18},{24,28},{30,26},{28,20... | collective-permute-start | bytes 1013768 | tf_op jit(solution)/shard_map/projection_far_2_0/ppermute | solution.py:80
  15.9 1.4 %projection_1.1 = (f32[3,256,640]{2,1,0:T(8,128)S(1)}, f32[8,640]{1,0:T(8,128)S(1)}) custom-call(bf16[264,640]{1,0:T(8,128)(2,1)S(1)} %prepare.1.refs_0_, bf16[264,640]{1,0:T(8,128)(2,1)S(1)} %collective-permute-done.4.refs_1_, bf16[264,640]{1,0:T(8,128)(2,1)S(1)} %collective-permute-done.refs_2_, bf16[264,640]{1,0:T(8,128)(2,1)S(1)} %collective-permute-done.9.refs_3_, ...), custom_call_target="tpu_custom_call" | custom-call | tf_op jit(solution)/shard_map/projection_1/pallas_call | solution.py:179
  17.9 2.1 %collective-permute-start.2 = (bf16[264,640]{1,0:T(8,128)(2,1)S(1)}, bf16[264,640]{1,0:T(8,128)(2,1)S(1)}, u32[]{:S(2)}, u32[]{:S(2)}) collective-permute-start(bf16[264,640]{1,0:T(8,128)(2,1)S(1)} %collective-permute-done.1.refs_2_), channel_id=1, source_target_pairs={{0,8},{10,2},{8,16},{18,10},{16,24},{26,18},{24,28},{30,26},{28,20... | collective-permute-start | bytes 1013768 | tf_op jit(solution)/shard_map/projection_near_3_0/ppermute | solution.py:80
  21.1 2.1 %collective-permute-start.13 = (bf16[264,640]{1,0:T(8,128)(2,1)S(1)}, bf16[264,640]{1,0:T(8,128)(2,1)S(1)}, u32[]{:S(2)}, u32[]{:S(2)}) collective-permute-start(bf16[264,640]{1,0:T(8,128)(2,1)S(1)} %collective-permute-done.6.refs_0_), channel_id=1, source_target_pairs={{0,8},{10,2},{8,16},{18,10},{16,24},{26,18},{24,28},{30,26},{28,20... | collective-permute-start | bytes 1013768 | tf_op jit(solution)/shard_map/projection_far_3_0/ppermute | solution.py:80
  23.1 1.6 %projection_2.1 = (f32[3,256,640]{2,1,0:T(8,128)S(1)}, f32[8,640]{1,0:T(8,128)S(1)}) custom-call(bf16[264,640]{1,0:T(8,128)(2,1)S(1)} %collective-permute-done.5.refs_0_, bf16[264,640]{1,0:T(8,128)(2,1)S(1)} %collective-permute-done.8.refs_1_, bf16[264,640]{1,0:T(8,128)(2,1)S(1)} %collective-permute-done.1.refs_2_, ...), custom_call_target="tpu_custom_call", output_to_operand_aliasing={{0}: (5, {}), {1}: (6, {})} | custom-call | tf_op jit(solution)/shard_map/projection_2/pallas_call | solution.py:179
  25.6 2.1 %collective-permute-start.3 = (bf16[264,640]{1,0:T(8,128)(2,1)S(1)}, bf16[264,640]{1,0:T(8,128)(2,1)S(1)}, u32[]{:S(2)}, u32[]{:S(2)}) collective-permute-start(bf16[264,640]{1,0:T(8,128)(2,1)S(1)} %collective-permute-done.2.refs_2_), channel_id=1, source_target_pairs={{0,8},{10,2},{8,16},{18,10},{16,24},{26,18},{24,28},{30,26},{28,20... | collective-permute-start | bytes 1013768 | tf_op jit(solution)/shard_map/projection_near_4_0/ppermute | solution.py:80
  28.8 1.6 %projection_3.1 = (f32[3,256,640]{2,1,0:T(8,128)S(1)}, f32[8,640]{1,0:T(8,128)S(1)}) custom-call(bf16[264,640]{1,0:T(8,128)(2,1)S(1)} %collective-permute-done.6.refs_0_, bf16[264,640]{1,0:T(8,128)(2,1)S(1)} %collective-permute-done.7.refs_1_, bf16[264,640]{1,0:T(8,128)(2,1)S(1)} %collective-permute-done.2.refs_2_, ...), custom_call_target="tpu_custom_call", output_to_operand_aliasing={{0}: (5, {}), {1}: (6, {})} | custom-call | tf_op jit(solution)/shard_map/projection_3/pallas_call | solution.py:179
  30.3 2.5 %collective-permute-done.3.refs_0_ = bf16[264,640]{1,0:T(8,128)(2,1)S(1)} collective-permute-done((bf16[264,640]{1,0:T(8,128)(2,1)S(1)}, bf16[264,640]{1,0:T(8,128)(2,1)S(1)}, u32[]{:S(2)}, u32[]{:S(2)}) %collective-permute-start.3) | collective-permute-done | bytes 337952 | tf_op jit(solution)/shard_map/projection_near_4_0/ppermute | solution.py:80
  35.3 2.1 %collective-permute-start.15 = (bf16[136,640]{1,0:T(8,128)(2,1)S(1)}, bf16[136,640]{1,0:T(8,128)(2,1)S(1)}, u32[]{:S(2)}, u32[]{:S(2)}) collective-permute-start(bf16[136,640]{1,0:T(8,128)(2,1)S(1)} %get-tuple-element.58.refs_2_.refs_8_), channel_id=1, source_target_pairs={{0,1},{1,0},{2,3},{3,2},{4,5},{5,4},{6,7},{7,6},{8,9},{9,8},{10,11... | collective-permute-start | bytes 522248 | tf_op jit(solution)/shard_map/ppermute | solution.py:546
  39.2 3.4 %collective-permute-done.15.refs_0_ = bf16[136,640]{1,0:T(8,128)(2,1)S(1)} collective-permute-done((bf16[136,640]{1,0:T(8,128)(2,1)S(1)}, bf16[136,640]{1,0:T(8,128)(2,1)S(1)}, u32[]{:S(2)}, u32[]{:S(2)}) %collective-permute-start.15) | collective-permute-done | bytes 174112 | tf_op jit(solution)/shard_map/ppermute | solution.py:546
  42.6 1.2 %far_part_1_0.1.refs_0_ = bf16[128,640]{1,0:T(8,128)(2,1)S(1)} custom-call(bf16[136,640]{1,0:T(8,128)(2,1)S(1)} %collective-permute-done.15.refs_0_, f32[128,1280]{1,0:T(8,128)S(1)} %get-tuple-element.63.refs_1_, f32[256,2560]{1,0:T(8,128)S(1)} %filter_spectra.1.refs_5_.refs_2_, bf16[256,256]{1,0:T(8,128)(2,1)S(1)} %copy-done.1, ...), custom_call_target="tpu_custom_call" | custom-call | tf_op jit(solution)/shard_map/far_part_1_0/pallas_call | solution.py:532
  43.9 2.2 %collective-permute-start.16 = (bf16[128,640]{1,0:T(8,128)(2,1)S(1)}, bf16[128,640]{1,0:T(8,128)(2,1)S(1)}, u32[]{:S(2)}, u32[]{:S(2)}) collective-permute-start(bf16[128,640]{1,0:T(8,128)(2,1)S(1)} %far_part_1_0.1.refs_0_), channel_id=1, source_target_pairs={{0,8},{10,2},{8,16},{18,10},{16,24},{26,18},{24,28},{30,26},{28,20... | collective-permute-start | bytes 491528 | tf_op jit(solution)/shard_map/output_near_1_0/ppermute | solution.py:80
  47.5 1.5 %collective-permute-start.18 = (bf16[128,640]{1,0:T(8,128)(2,1)S(1)}, bf16[128,640]{1,0:T(8,128)(2,1)S(1)}, u32[]{:S(2)}, u32[]{:S(2)}) collective-permute-start(bf16[128,640]{1,0:T(8,128)(2,1)S(1)} %far_part_1_128.1.refs_1_), channel_id=1, source_target_pairs={{0,8},{10,2},{8,16},{18,10},{16,24},{26,18},{24,28},{30,26},{28,20... | collective-permute-start | bytes 491528 | tf_op jit(solution)/shard_map/output_near_1_1/ppermute | solution.py:80
  49.0 1.6 %collective-permute-start.23 = (bf16[128,640]{1,0:T(8,128)(2,1)S(1)}, bf16[128,640]{1,0:T(8,128)(2,1)S(1)}, u32[]{:S(2)}, u32[]{:S(2)}) collective-permute-start(bf16[128,640]{1,0:T(8,128)(2,1)S(1)} %collective-permute-done.22.refs_2_), channel_id=1, source_target_pairs={{0,8},{10,2},{8,16},{18,10},{16,24},{26,18},{24,28},{30,26},{28,20... | collective-permute-start | bytes 491528 | tf_op jit(solution)/shard_map/output_far_1_0/ppermute | solution.py:80
  50.6 1.6 %collective-permute-start.25 = (bf16[128,640]{1,0:T(8,128)(2,1)S(1)}, bf16[128,640]{1,0:T(8,128)(2,1)S(1)}, u32[]{:S(2)}, u32[]{:S(2)}) collective-permute-start(bf16[128,640]{1,0:T(8,128)(2,1)S(1)} %collective-permute-done.24.refs_3_), channel_id=1, source_target_pairs={{0,8},{10,2},{8,16},{18,10},{16,24},{26,18},{24,28},{30,26},{28,20... | collective-permute-start | bytes 491528 | tf_op jit(solution)/shard_map/output_far_1_1/ppermute | solution.py:80
  52.9 1.6 %collective-permute-start.19 = (bf16[256,640]{1,0:T(8,128)(2,1)S(1)}, bf16[256,640]{1,0:T(8,128)(2,1)S(1)}, u32[]{:S(2)}, u32[]{:S(2)}) collective-permute-start(bf16[256,640]{1,0:T(8,128)(2,1)S(1)} %constant_dynamic-update-slice_fusion.refs_4_), channel_id=1, source_target_pairs={{0,8},{10,2},{8,16},{18,10},{16,24},{26,18},{24,28},{30,26},{28,20... | collective-permute-start | bytes 983048 | tf_op jit(solution)/shard_map/output_near_2_0/ppermute | solution.py:80
  54.6 1.7 %collective-permute-done.25 = bf16[128,640]{1,0:T(8,128)(2,1)S(1)} collective-permute-done((bf16[128,640]{1,0:T(8,128)(2,1)S(1)}, bf16[128,640]{1,0:T(8,128)(2,1)S(1)}, u32[]{:S(2)}, u32[]{:S(2)}) %collective-permute-start.25) | collective-permute-done | bytes 163872 | tf_op jit(solution)/shard_map/output_far_1_1/ppermute | solution.py:80
  56.3 1.8 %collective-permute-start.26 = (bf16[256,640]{1,0:T(8,128)(2,1)S(1)}, bf16[256,640]{1,0:T(8,128)(2,1)S(1)}, u32[]{:S(2)}, u32[]{:S(2)}) collective-permute-start(bf16[256,640]{1,0:T(8,128)(2,1)S(1)} %constant_dynamic-update-slice_fusion.2.refs_0_), channel_id=1, source_target_pairs={{0,8},{10,2},{8,16},{18,10},{16,24},{26,18},{24,28},{30,26},{28,20... | collective-permute-start | bytes 983048 | tf_op jit(solution)/shard_map/output_far_2_0/ppermute | solution.py:80
  58.7 1.3 %collective-permute-done.19.refs_2_ = bf16[256,640]{1,0:T(8,128)(2,1)S(1)} collective-permute-done((bf16[256,640]{1,0:T(8,128)(2,1)S(1)}, bf16[256,640]{1,0:T(8,128)(2,1)S(1)}, u32[]{:S(2)}, u32[]{:S(2)}) %collective-permute-start.19) | collective-permute-done | bytes 327712 | tf_op jit(solution)/shard_map/output_near_2_0/ppermute | solution.py:80
  60.0 1.5 %collective-permute-start.20 = (bf16[256,640]{1,0:T(8,128)(2,1)S(1)}, bf16[256,640]{1,0:T(8,128)(2,1)S(1)}, u32[]{:S(2)}, u32[]{:S(2)}) collective-permute-start(bf16[256,640]{1,0:T(8,128)(2,1)S(1)} %collective-permute-done.19.refs_2_), channel_id=1, source_target_pairs={{0,8},{10,2},{8,16},{18,10},{16,24},{26,18},{24,28},{30,26},{28,20... | collective-permute-start | bytes 983048 | tf_op jit(solution)/shard_map/output_near_3_0/ppermute | solution.py:80
  61.6 2.1 %collective-permute-done.26.refs_0_ = bf16[256,640]{1,0:T(8,128)(2,1)S(1)} collective-permute-done((bf16[256,640]{1,0:T(8,128)(2,1)S(1)}, bf16[256,640]{1,0:T(8,128)(2,1)S(1)}, u32[]{:S(2)}, u32[]{:S(2)}) %collective-permute-start.26) | collective-permute-done | bytes 327712 | tf_op jit(solution)/shard_map/output_far_2_0/ppermute | solution.py:80
  63.7 1.5 %collective-permute-start.33 = (bf16[256,640]{1,0:T(8,128)(2,1)S(1)}, bf16[256,640]{1,0:T(8,128)(2,1)S(1)}, u32[]{:S(2)}, u32[]{:S(2)}) collective-permute-start(bf16[256,640]{1,0:T(8,128)(2,1)S(1)} %collective-permute-done.26.refs_0_), channel_id=1, source_target_pairs={{0,8},{10,2},{8,16},{18,10},{16,24},{26,18},{24,28},{30,26},{28,20... | collective-permute-start | bytes 983048 | tf_op jit(solution)/shard_map/output_far_3_0/ppermute | solution.py:80
  65.8 1.3 %collective-permute-done.20.refs_2_ = bf16[256,640]{1,0:T(8,128)(2,1)S(1)} collective-permute-done((bf16[256,640]{1,0:T(8,128)(2,1)S(1)}, bf16[256,640]{1,0:T(8,128)(2,1)S(1)}, u32[]{:S(2)}, u32[]{:S(2)}) %collective-permute-start.20) | collective-permute-done | bytes 327712 | tf_op jit(solution)/shard_map/output_near_3_0/ppermute | solution.py:80
  67.2 1.5 %collective-permute-start.21 = (bf16[256,640]{1,0:T(8,128)(2,1)S(1)}, bf16[256,640]{1,0:T(8,128)(2,1)S(1)}, u32[]{:S(2)}, u32[]{:S(2)}) collective-permute-start(bf16[256,640]{1,0:T(8,128)(2,1)S(1)} %collective-permute-done.20.refs_2_), channel_id=1, source_target_pairs={{0,8},{10,2},{8,16},{18,10},{16,24},{26,18},{24,28},{30,26},{28,20... | collective-permute-start | bytes 983048 | tf_op jit(solution)/shard_map/output_near_4_0/ppermute | solution.py:80
  68.7 2.0 %collective-permute-done.33.refs_0_ = bf16[256,640]{1,0:T(8,128)(2,1)S(1)} collective-permute-done((bf16[256,640]{1,0:T(8,128)(2,1)S(1)}, bf16[256,640]{1,0:T(8,128)(2,1)S(1)}, u32[]{:S(2)}, u32[]{:S(2)}) %collective-permute-start.33) | collective-permute-done | bytes 327712 | tf_op jit(solution)/shard_map/output_far_3_0/ppermute | solution.py:80
  71.4 2.9 %collective-permute-done.21.refs_0_ = bf16[256,640]{1,0:T(8,128)(2,1)S(1)} collective-permute-done((bf16[256,640]{1,0:T(8,128)(2,1)S(1)}, bf16[256,640]{1,0:T(8,128)(2,1)S(1)}, u32[]{:S(2)}, u32[]{:S(2)}) %collective-permute-start.21) | collective-permute-done | bytes 327712 | tf_op jit(solution)/shard_map/output_near_4_0/ppermute | solution.py:80
  74.6 1.2 %collective-permute-done.32.refs_1_ = bf16[256,640]{1,0:T(8,128)(2,1)S(1)} collective-permute-done((bf16[256,640]{1,0:T(8,128)(2,1)S(1)}, bf16[256,640]{1,0:T(8,128)(2,1)S(1)}, u32[]{:S(2)}, u32[]{:S(2)}) %collective-permute-start.32) | collective-permute-done | bytes 327712 | tf_op jit(solution)/shard_map/output_core_near_4_0/ppermute | solution.py:84
  (81 shorter events, 16.7 us)
Async XLA Ops:
  2.4 7.7 %collective-permute-start = (bf16[264,640]{1,0:T(8,128)(2,1)S(1)}, bf16[264,640]{1,0:T(8,128)(2,1)S(1)}, u32[]{:S(2)}, u32[]{:S(2)}) collective-permute-start(bf16[264,640]{1,0:T(8,128)(2,1)S(1)} %prepare.1.refs_0_), channel_id=1, source_target_pairs={{0,8},{10,2},{8,16},{18,10},{16,24},{26,18},{24,28},{30,26},{28,20... | collective-permute-start | bytes 1013768 | tf_op jit(solution)/shard_map/projection_near_1_0/ppermute | solution.py:80
  5.1 8.7 %collective-permute-start.5 = (bf16[264,640]{1,0:T(8,128)(2,1)S(1)}, bf16[264,640]{1,0:T(8,128)(2,1)S(1)}, u32[]{:S(2)}, u32[]{:S(2)}) collective-permute-start(bf16[264,640]{1,0:T(8,128)(2,1)S(1)} %collective-permute-done.4.refs_1_), channel_id=1, source_target_pairs={{0,8},{10,2},{8,16},{18,10},{16,24},{26,18},{24,28},{30,26},{28,20... | collective-permute-start | bytes 1013768 | tf_op jit(solution)/shard_map/projection_far_1_0/ppermute | solution.py:80
  10.2 5.7 %collective-permute-start.9 = (bf16[264,640]{1,0:T(8,128)(2,1)S(1)}, bf16[264,640]{1,0:T(8,128)(2,1)S(1)}, u32[]{:S(2)}, u32[]{:S(2)}) collective-permute-start(bf16[264,640]{1,0:T(8,128)(2,1)S(1)} %collective-permute-done.refs_2_), channel_id=1, source_target_pairs={{0,2},{2,0},{4,6},{6,4},{8,10},{10,8},{12,14},{14,12},{16,18},{18,... | collective-permute-start | bytes 1013768 | tf_op jit(solution)/shard_map/projection_core_near_1_0/ppermute | solution.py:84
  10.2 7.2 %collective-permute-start.1 = (bf16[264,640]{1,0:T(8,128)(2,1)S(1)}, bf16[264,640]{1,0:T(8,128)(2,1)S(1)}, u32[]{:S(2)}, u32[]{:S(2)}) collective-permute-start(bf16[264,640]{1,0:T(8,128)(2,1)S(1)} %collective-permute-done.refs_2_), channel_id=1, source_target_pairs={{0,8},{10,2},{8,16},{18,10},{16,24},{26,18},{24,28},{30,26},{28,20... | collective-permute-start | bytes 1013768 | tf_op jit(solution)/shard_map/projection_near_2_0/ppermute | solution.py:80
  13.8 7.2 %collective-permute-start.6 = (bf16[264,640]{1,0:T(8,128)(2,1)S(1)}, bf16[264,640]{1,0:T(8,128)(2,1)S(1)}, u32[]{:S(2)}, u32[]{:S(2)}) collective-permute-start(bf16[264,640]{1,0:T(8,128)(2,1)S(1)} %collective-permute-done.5.refs_0_), channel_id=1, source_target_pairs={{0,8},{10,2},{8,16},{18,10},{16,24},{26,18},{24,28},{30,26},{28,20... | collective-permute-start | bytes 1013768 | tf_op jit(solution)/shard_map/projection_far_2_0/ppermute | solution.py:80
  17.4 5.7 %collective-permute-start.10 = (bf16[264,640]{1,0:T(8,128)(2,1)S(1)}, bf16[264,640]{1,0:T(8,128)(2,1)S(1)}, u32[]{:S(2)}, u32[]{:S(2)}) collective-permute-start(bf16[264,640]{1,0:T(8,128)(2,1)S(1)} %collective-permute-done.1.refs_2_), channel_id=1, source_target_pairs={{0,2},{2,0},{4,6},{6,4},{8,10},{10,8},{12,14},{14,12},{16,18},{18,... | collective-permute-start | bytes 1013768 | tf_op jit(solution)/shard_map/projection_core_near_2_0/ppermute | solution.py:84
  17.4 5.7 %collective-permute-start.8 = (bf16[264,640]{1,0:T(8,128)(2,1)S(1)}, bf16[264,640]{1,0:T(8,128)(2,1)S(1)}, u32[]{:S(2)}, u32[]{:S(2)}) collective-permute-start(bf16[264,640]{1,0:T(8,128)(2,1)S(1)} %collective-permute-done.5.refs_0_), channel_id=1, source_target_pairs={{0,2},{2,0},{4,6},{6,4},{8,10},{10,8},{12,14},{14,12},{16,18},{18,... | collective-permute-start | bytes 1013768 | tf_op jit(solution)/shard_map/projection_core_far_1_0/ppermute | solution.py:84
  17.9 7.2 %collective-permute-start.2 = (bf16[264,640]{1,0:T(8,128)(2,1)S(1)}, bf16[264,640]{1,0:T(8,128)(2,1)S(1)}, u32[]{:S(2)}, u32[]{:S(2)}) collective-permute-start(bf16[264,640]{1,0:T(8,128)(2,1)S(1)} %collective-permute-done.1.refs_2_), channel_id=1, source_target_pairs={{0,8},{10,2},{8,16},{18,10},{16,24},{26,18},{24,28},{30,26},{28,20... | collective-permute-start | bytes 1013768 | tf_op jit(solution)/shard_map/projection_near_3_0/ppermute | solution.py:80
  21.1 7.7 %collective-permute-start.13 = (bf16[264,640]{1,0:T(8,128)(2,1)S(1)}, bf16[264,640]{1,0:T(8,128)(2,1)S(1)}, u32[]{:S(2)}, u32[]{:S(2)}) collective-permute-start(bf16[264,640]{1,0:T(8,128)(2,1)S(1)} %collective-permute-done.6.refs_0_), channel_id=1, source_target_pairs={{0,8},{10,2},{8,16},{18,10},{16,24},{26,18},{24,28},{30,26},{28,20... | collective-permute-start | bytes 1013768 | tf_op jit(solution)/shard_map/projection_far_3_0/ppermute | solution.py:80
  25.1 3.6 %collective-permute-start.11 = (bf16[264,640]{1,0:T(8,128)(2,1)S(1)}, bf16[264,640]{1,0:T(8,128)(2,1)S(1)}, u32[]{:S(2)}, u32[]{:S(2)}) collective-permute-start(bf16[264,640]{1,0:T(8,128)(2,1)S(1)} %collective-permute-done.2.refs_2_), channel_id=1, source_target_pairs={{0,2},{2,0},{4,6},{6,4},{8,10},{10,8},{12,14},{14,12},{16,18},{18,... | collective-permute-start | bytes 1013768 | tf_op jit(solution)/shard_map/projection_core_near_3_0/ppermute | solution.py:84
  25.1 3.6 %collective-permute-start.7 = (bf16[264,640]{1,0:T(8,128)(2,1)S(1)}, bf16[264,640]{1,0:T(8,128)(2,1)S(1)}, u32[]{:S(2)}, u32[]{:S(2)}) collective-permute-start(bf16[264,640]{1,0:T(8,128)(2,1)S(1)} %collective-permute-done.6.refs_0_), channel_id=1, source_target_pairs={{0,2},{2,0},{4,6},{6,4},{8,10},{10,8},{12,14},{14,12},{16,18},{18,... | collective-permute-start | bytes 1013768 | tf_op jit(solution)/shard_map/projection_core_far_2_0/ppermute | solution.py:84
  25.6 7.2 %collective-permute-start.3 = (bf16[264,640]{1,0:T(8,128)(2,1)S(1)}, bf16[264,640]{1,0:T(8,128)(2,1)S(1)}, u32[]{:S(2)}, u32[]{:S(2)}) collective-permute-start(bf16[264,640]{1,0:T(8,128)(2,1)S(1)} %collective-permute-done.2.refs_2_), channel_id=1, source_target_pairs={{0,8},{10,2},{8,16},{18,10},{16,24},{26,18},{24,28},{30,26},{28,20... | collective-permute-start | bytes 1013768 | tf_op jit(solution)/shard_map/projection_near_4_0/ppermute | solution.py:80
  28.8 4.1 %collective-permute-start.14 = (bf16[264,640]{1,0:T(8,128)(2,1)S(1)}, bf16[264,640]{1,0:T(8,128)(2,1)S(1)}, u32[]{:S(2)}, u32[]{:S(2)}) collective-permute-start(bf16[264,640]{1,0:T(8,128)(2,1)S(1)} %collective-permute-done.13.refs_0_), channel_id=1, source_target_pairs={{0,2},{2,0},{4,6},{6,4},{8,10},{10,8},{12,14},{14,12},{16,18},{18,... | collective-permute-start | bytes 1013768 | tf_op jit(solution)/shard_map/projection_core_far_3_0/ppermute | solution.py:84
  35.3 7.3 %collective-permute-start.15 = (bf16[136,640]{1,0:T(8,128)(2,1)S(1)}, bf16[136,640]{1,0:T(8,128)(2,1)S(1)}, u32[]{:S(2)}, u32[]{:S(2)}) collective-permute-start(bf16[136,640]{1,0:T(8,128)(2,1)S(1)} %get-tuple-element.58.refs_2_.refs_8_), channel_id=1, source_target_pairs={{0,1},{1,0},{2,3},{3,2},{4,5},{5,4},{6,7},{7,6},{8,9},{9,8},{10,11... | collective-permute-start | bytes 522248 | tf_op jit(solution)/shard_map/ppermute | solution.py:546
  38.1 7.9 %collective-permute-start.17 = (bf16[136,640]{1,0:T(8,128)(2,1)S(1)}, bf16[136,640]{1,0:T(8,128)(2,1)S(1)}, u32[]{:S(2)}, u32[]{:S(2)}) collective-permute-start(bf16[136,640]{1,0:T(8,128)(2,1)S(1)} %get-tuple-element.61.refs_3_.refs_8_), channel_id=1, source_target_pairs={{0,1},{1,0},{2,3},{3,2},{4,5},{5,4},{6,7},{7,6},{8,9},{9,8},{10,11... | collective-permute-start | bytes 522248 | tf_op jit(solution)/shard_map/ppermute | solution.py:546
  43.8 5.2 %collective-permute-start.22 = (bf16[128,640]{1,0:T(8,128)(2,1)S(1)}, bf16[128,640]{1,0:T(8,128)(2,1)S(1)}, u32[]{:S(2)}, u32[]{:S(2)}) collective-permute-start(bf16[128,640]{1,0:T(8,128)(2,1)S(1)} %far_part_1_0.1.refs_0_), channel_id=1, source_target_pairs={{0,2},{2,0},{4,6},{6,4},{8,10},{10,8},{12,14},{14,12},{16,18},{18,... | collective-permute-start | bytes 491528 | tf_op jit(solution)/shard_map/output_core_own_0/ppermute | solution.py:84
  43.9 6.7 %collective-permute-start.16 = (bf16[128,640]{1,0:T(8,128)(2,1)S(1)}, bf16[128,640]{1,0:T(8,128)(2,1)S(1)}, u32[]{:S(2)}, u32[]{:S(2)}) collective-permute-start(bf16[128,640]{1,0:T(8,128)(2,1)S(1)} %far_part_1_0.1.refs_0_), channel_id=1, source_target_pairs={{0,8},{10,2},{8,16},{18,10},{16,24},{26,18},{24,28},{30,26},{28,20... | collective-permute-start | bytes 491528 | tf_op jit(solution)/shard_map/output_near_1_0/ppermute | solution.py:80
  47.3 3.3 %collective-permute-start.24 = (bf16[128,640]{1,0:T(8,128)(2,1)S(1)}, bf16[128,640]{1,0:T(8,128)(2,1)S(1)}, u32[]{:S(2)}, u32[]{:S(2)}) collective-permute-start(bf16[128,640]{1,0:T(8,128)(2,1)S(1)} %far_part_1_128.1.refs_1_), channel_id=1, source_target_pairs={{0,2},{2,0},{4,6},{6,4},{8,10},{10,8},{12,14},{14,12},{16,18},{18,... | collective-permute-start | bytes 491528 | tf_op jit(solution)/shard_map/output_core_own_1/ppermute | solution.py:84
  47.5 5.3 %collective-permute-start.18 = (bf16[128,640]{1,0:T(8,128)(2,1)S(1)}, bf16[128,640]{1,0:T(8,128)(2,1)S(1)}, u32[]{:S(2)}, u32[]{:S(2)}) collective-permute-start(bf16[128,640]{1,0:T(8,128)(2,1)S(1)} %far_part_1_128.1.refs_1_), channel_id=1, source_target_pairs={{0,8},{10,2},{8,16},{18,10},{16,24},{26,18},{24,28},{30,26},{28,20... | collective-permute-start | bytes 491528 | tf_op jit(solution)/shard_map/output_near_1_1/ppermute | solution.py:80
  49.0 5.5 %collective-permute-start.23 = (bf16[128,640]{1,0:T(8,128)(2,1)S(1)}, bf16[128,640]{1,0:T(8,128)(2,1)S(1)}, u32[]{:S(2)}, u32[]{:S(2)}) collective-permute-start(bf16[128,640]{1,0:T(8,128)(2,1)S(1)} %collective-permute-done.22.refs_2_), channel_id=1, source_target_pairs={{0,8},{10,2},{8,16},{18,10},{16,24},{26,18},{24,28},{30,26},{28,20... | collective-permute-start | bytes 491528 | tf_op jit(solution)/shard_map/output_far_1_0/ppermute | solution.py:80
  50.6 5.7 %collective-permute-start.25 = (bf16[128,640]{1,0:T(8,128)(2,1)S(1)}, bf16[128,640]{1,0:T(8,128)(2,1)S(1)}, u32[]{:S(2)}, u32[]{:S(2)}) collective-permute-start(bf16[128,640]{1,0:T(8,128)(2,1)S(1)} %collective-permute-done.24.refs_3_), channel_id=1, source_target_pairs={{0,8},{10,2},{8,16},{18,10},{16,24},{26,18},{24,28},{30,26},{28,20... | collective-permute-start | bytes 491528 | tf_op jit(solution)/shard_map/output_far_1_1/ppermute | solution.py:80
  52.8 5.3 %collective-permute-start.29 = (bf16[256,640]{1,0:T(8,128)(2,1)S(1)}, bf16[256,640]{1,0:T(8,128)(2,1)S(1)}, u32[]{:S(2)}, u32[]{:S(2)}) collective-permute-start(bf16[256,640]{1,0:T(8,128)(2,1)S(1)} %constant_dynamic-update-slice_fusion.refs_4_), channel_id=1, source_target_pairs={{0,2},{2,0},{4,6},{6,4},{8,10},{10,8},{12,14},{14,12},{16,18},{18,... | collective-permute-start | bytes 983048 | tf_op jit(solution)/shard_map/output_core_near_1_0/ppermute | solution.py:84
  52.9 7.1 %collective-permute-start.19 = (bf16[256,640]{1,0:T(8,128)(2,1)S(1)}, bf16[256,640]{1,0:T(8,128)(2,1)S(1)}, u32[]{:S(2)}, u32[]{:S(2)}) collective-permute-start(bf16[256,640]{1,0:T(8,128)(2,1)S(1)} %constant_dynamic-update-slice_fusion.refs_4_), channel_id=1, source_target_pairs={{0,8},{10,2},{8,16},{18,10},{16,24},{26,18},{24,28},{30,26},{28,20... | collective-permute-start | bytes 983048 | tf_op jit(solution)/shard_map/output_near_2_0/ppermute | solution.py:80
  56.3 7.3 %collective-permute-start.26 = (bf16[256,640]{1,0:T(8,128)(2,1)S(1)}, bf16[256,640]{1,0:T(8,128)(2,1)S(1)}, u32[]{:S(2)}, u32[]{:S(2)}) collective-permute-start(bf16[256,640]{1,0:T(8,128)(2,1)S(1)} %constant_dynamic-update-slice_fusion.2.refs_0_), channel_id=1, source_target_pairs={{0,8},{10,2},{8,16},{18,10},{16,24},{26,18},{24,28},{30,26},{28,20... | collective-permute-start | bytes 983048 | tf_op jit(solution)/shard_map/output_far_2_0/ppermute | solution.py:80
  58.1 7.1 %collective-permute-start.28 = (bf16[256,640]{1,0:T(8,128)(2,1)S(1)}, bf16[256,640]{1,0:T(8,128)(2,1)S(1)}, u32[]{:S(2)}, u32[]{:S(2)}) collective-permute-start(bf16[256,640]{1,0:T(8,128)(2,1)S(1)} %constant_dynamic-update-slice_fusion.2.refs_0_), channel_id=1, source_target_pairs={{0,2},{2,0},{4,6},{6,4},{8,10},{10,8},{12,14},{14,12},{16,18},{18,... | collective-permute-start | bytes 983048 | tf_op jit(solution)/shard_map/output_core_far_1_0/ppermute | solution.py:84
  60.0 5.2 %collective-permute-start.30 = (bf16[256,640]{1,0:T(8,128)(2,1)S(1)}, bf16[256,640]{1,0:T(8,128)(2,1)S(1)}, u32[]{:S(2)}, u32[]{:S(2)}) collective-permute-start(bf16[256,640]{1,0:T(8,128)(2,1)S(1)} %collective-permute-done.19.refs_2_), channel_id=1, source_target_pairs={{0,2},{2,0},{4,6},{6,4},{8,10},{10,8},{12,14},{14,12},{16,18},{18,... | collective-permute-start | bytes 983048 | tf_op jit(solution)/shard_map/output_core_near_2_0/ppermute | solution.py:84
  60.0 7.1 %collective-permute-start.20 = (bf16[256,640]{1,0:T(8,128)(2,1)S(1)}, bf16[256,640]{1,0:T(8,128)(2,1)S(1)}, u32[]{:S(2)}, u32[]{:S(2)}) collective-permute-start(bf16[256,640]{1,0:T(8,128)(2,1)S(1)} %collective-permute-done.19.refs_2_), channel_id=1, source_target_pairs={{0,8},{10,2},{8,16},{18,10},{16,24},{26,18},{24,28},{30,26},{28,20... | collective-permute-start | bytes 983048 | tf_op jit(solution)/shard_map/output_near_3_0/ppermute | solution.py:80
  63.7 7.1 %collective-permute-start.33 = (bf16[256,640]{1,0:T(8,128)(2,1)S(1)}, bf16[256,640]{1,0:T(8,128)(2,1)S(1)}, u32[]{:S(2)}, u32[]{:S(2)}) collective-permute-start(bf16[256,640]{1,0:T(8,128)(2,1)S(1)} %collective-permute-done.26.refs_0_), channel_id=1, source_target_pairs={{0,8},{10,2},{8,16},{18,10},{16,24},{26,18},{24,28},{30,26},{28,20... | collective-permute-start | bytes 983048 | tf_op jit(solution)/shard_map/output_far_3_0/ppermute | solution.py:80
  65.2 5.5 %collective-permute-start.27 = (bf16[256,640]{1,0:T(8,128)(2,1)S(1)}, bf16[256,640]{1,0:T(8,128)(2,1)S(1)}, u32[]{:S(2)}, u32[]{:S(2)}) collective-permute-start(bf16[256,640]{1,0:T(8,128)(2,1)S(1)} %collective-permute-done.26.refs_0_), channel_id=1, source_target_pairs={{0,2},{2,0},{4,6},{6,4},{8,10},{10,8},{12,14},{14,12},{16,18},{18,... | collective-permute-start | bytes 983048 | tf_op jit(solution)/shard_map/output_core_far_2_0/ppermute | solution.py:84
  67.2 3.6 %collective-permute-start.31 = (bf16[256,640]{1,0:T(8,128)(2,1)S(1)}, bf16[256,640]{1,0:T(8,128)(2,1)S(1)}, u32[]{:S(2)}, u32[]{:S(2)}) collective-permute-start(bf16[256,640]{1,0:T(8,128)(2,1)S(1)} %collective-permute-done.20.refs_2_), channel_id=1, source_target_pairs={{0,2},{2,0},{4,6},{6,4},{8,10},{10,8},{12,14},{14,12},{16,18},{18,... | collective-permute-start | bytes 983048 | tf_op jit(solution)/shard_map/output_core_near_3_0/ppermute | solution.py:84
  67.2 7.1 %collective-permute-start.21 = (bf16[256,640]{1,0:T(8,128)(2,1)S(1)}, bf16[256,640]{1,0:T(8,128)(2,1)S(1)}, u32[]{:S(2)}, u32[]{:S(2)}) collective-permute-start(bf16[256,640]{1,0:T(8,128)(2,1)S(1)} %collective-permute-done.20.refs_2_), channel_id=1, source_target_pairs={{0,8},{10,2},{8,16},{18,10},{16,24},{26,18},{24,28},{30,26},{28,20... | collective-permute-start | bytes 983048 | tf_op jit(solution)/shard_map/output_near_4_0/ppermute | solution.py:80
  70.7 3.5 %collective-permute-start.34 = (bf16[256,640]{1,0:T(8,128)(2,1)S(1)}, bf16[256,640]{1,0:T(8,128)(2,1)S(1)}, u32[]{:S(2)}, u32[]{:S(2)}) collective-permute-start(bf16[256,640]{1,0:T(8,128)(2,1)S(1)} %collective-permute-done.33.refs_0_), channel_id=1, source_target_pairs={{0,2},{2,0},{4,6},{6,4},{8,10},{10,8},{12,14},{14,12},{16,18},{18,... | collective-permute-start | bytes 983048 | tf_op jit(solution)/shard_map/output_core_far_3_0/ppermute | solution.py:84
  (14 other events, 71.7 us)

commit v7 on v6

--- a/solution.py
+++ b/solution.py
@@ -38,7 +38,21 @@
     return pl.CostEstimate(flops=int(flops), bytes_accessed=int(size), transcendentals=0)
 
 
-def prepare_kernel(x_ref, gain_ref, out_ref):
+def begin():
+    def kernel(out_ref):
+        out_ref[...] = jnp.zeros(out_ref.shape, f32)
+
+    return pl.pallas_call(
+        kernel,
+        out_specs=in_vmem,
+        out_shape=shape_of((8, 128), f32),
+        compiler_params=params,
+        cost_estimate=estimate(3e9, 0),
+        name="begin",
+    )()
+
+
+def prepare_kernel(x_ref, gain_ref, begun_ref, out_ref):
     rows = x_ref.shape[0]
     wide = x_ref[...].astype(f32)
     out_ref[:rows] = (wide * column(gain_ref[...])).astype(bf16)
@@ -53,13 +67,13 @@
     rows, tokens = x.shape
     return pl.pallas_call(
         prepare_kernel,
-        in_specs=[in_vmem, in_vmem],
+        in_specs=[in_vmem, in_vmem, in_vmem],
         out_specs=in_vmem,
         out_shape=shape_of((rows + side_rows, tokens), bf16),
         compiler_params=params,
         cost_estimate=estimate(3e9, 0),
         name="prepare",
-    )(x, gain.reshape(1, rows))
+    )(x, gain.reshape(1, rows), begin())
 
 
 def chip_count():
@@ -221,8 +235,9 @@
             theirs = send(other_core, far, f"core_far_{step}")
             items = [(step, 1, far), (chips - step, 0, theirs)]
         else:
+            items.append(pair[0])
             running = products(items, weight, running, side, None, STAGGER, f"{name}_{step}")
-            items = pair
+            items = pair[1:]
     results = [
         products(items, weight, running, side, end, 0, f"{name}_last_{k}", (k, len(finish)))
         for k, end in enumerate(finish)

time: 77.1 us -> 76.3 us (0.990)
  no operation moved by 1% of the time
where the time goes in v7:
time: 76.3 us; the launch traced here: 76.1 us
  starting transfers between devices  33.5 us (44%)
  waiting for transfers between devices  26.3 us (34%)
  Pallas kernels  15 us (20%)
  local copies, waits for them, and re-layouts  1.1 us (1%)
    ppermute x16, starting transfers between devices, along_ring(): return lax.ppermute(block, 'fsdp', pairs)  29.4 us
    ppermute x16, waiting for transfers between devices, along_ring(): return lax.ppermute(block, 'fsdp', pairs)  21.3 us
    pallas_call x11, Pallas kernels, products(): pl.pallas_call(kernel, in_specs=[in_vmem] * (count + 1 + len(state) + len...  10.5 us
    ppermute x2, waiting for transfers between devices, from_before(): lax.ppermute(block, 'ctx', [(i, (i + 1) % count) for i in range(count)])  3.48 us
    pallas_call x2, Pallas kernels, far_part(): pl.pallas_call(kernel, in_specs=[in_vmem] * len(args), out_specs=in_vmem,...  2.47 us
    ppermute x2, starting transfers between devices, from_before(): lax.ppermute(block, 'ctx', [(i, (i + 1) % count) for i in range(count)])  2.16 us
    ppermute x17, starting transfers between devices, other_core(): lax.ppermute(block, 'fsdp', [(i, i ^ 1) for i in range(2 * chip_count())])  1.88 us
    ppermute x17, waiting for transfers between devices, other_core(): lax.ppermute(block, 'fsdp', [(i, i ^ 1) for i in range(2 * chip_count())])  1.55 us
  transfers between devices with their start and end apart: 35, of which 18 were waited for; matrix products, arithmetic and copies ran while one was open for 0% of the time, Pallas kernels for 17%

profile of v7, /device:TPU:0, one launch (start us, length us, event | category | flops | bytes accessed | tf_op | source)
XLA Modules:
  0.0 76.1 jit_solution(8900914213312762578)
XLA Ops:
  1.8 2.6 %collective-permute-start = (bf16[264,640]{1,0:T(8,128)(2,1)S(1)}, bf16[264,640]{1,0:T(8,128)(2,1)S(1)}, u32[]{:S(2)}, u32[]{:S(2)}) collective-permute-start(bf16[264,640]{1,0:T(8,128)(2,1)S(1)} %prepare.1.refs_0_), channel_id=1, source_target_pairs={{0,8},{10,2},{8,16},{18,10},{16,24},{26,18},{24,28},{30,26},{28,20... | collective-permute-start | bytes 1013768 | tf_op jit(solution)/shard_map/projection_near_1_0/ppermute | solution.py:94
  4.4 1.6 %collective-permute-start.5 = (bf16[264,640]{1,0:T(8,128)(2,1)S(1)}, bf16[264,640]{1,0:T(8,128)(2,1)S(1)}, u32[]{:S(2)}, u32[]{:S(2)}) collective-permute-start(bf16[264,640]{1,0:T(8,128)(2,1)S(1)} %collective-permute-done.4.refs_1_), channel_id=1, source_target_pairs={{0,8},{10,2},{8,16},{18,10},{16,24},{26,18},{24,28},{30,26},{28,20... | collective-permute-start | bytes 1013768 | tf_op jit(solution)/shard_map/projection_far_1_0/ppermute | solution.py:94
  6.9 2.7 %collective-permute-done.refs_2_ = bf16[264,640]{1,0:T(8,128)(2,1)S(1)} collective-permute-done((bf16[264,640]{1,0:T(8,128)(2,1)S(1)}, bf16[264,640]{1,0:T(8,128)(2,1)S(1)}, u32[]{:S(2)}, u32[]{:S(2)}) %collective-permute-start) | collective-permute-done | bytes 337952 | tf_op jit(solution)/shard_map/projection_near_1_0/ppermute | solution.py:94
  9.5 2.1 %collective-permute-start.1 = (bf16[264,640]{1,0:T(8,128)(2,1)S(1)}, bf16[264,640]{1,0:T(8,128)(2,1)S(1)}, u32[]{:S(2)}, u32[]{:S(2)}) collective-permute-start(bf16[264,640]{1,0:T(8,128)(2,1)S(1)} %collective-permute-done.refs_2_), channel_id=1, source_target_pairs={{0,8},{10,2},{8,16},{18,10},{16,24},{26,18},{24,28},{30,26},{28,20... | collective-permute-start | bytes 1013768 | tf_op jit(solution)/shard_map/projection_near_2_0/ppermute | solution.py:94
  11.6 1.5 %collective-permute-done.5.refs_0_ = bf16[264,640]{1,0:T(8,128)(2,1)S(1)} collective-permute-done((bf16[264,640]{1,0:T(8,128)(2,1)S(1)}, bf16[264,640]{1,0:T(8,128)(2,1)S(1)}, u32[]{:S(2)}, u32[]{:S(2)}) %collective-permute-start.5) | collective-permute-done | bytes 337952 | tf_op jit(solution)/shard_map/projection_far_1_0/ppermute | solution.py:94
  13.2 2.1 %collective-permute-start.6 = (bf16[264,640]{1,0:T(8,128)(2,1)S(1)}, bf16[264,640]{1,0:T(8,128)(2,1)S(1)}, u32[]{:S(2)}, u32[]{:S(2)}) collective-permute-start(bf16[264,640]{1,0:T(8,128)(2,1)S(1)} %collective-permute-done.5.refs_0_), channel_id=1, source_target_pairs={{0,8},{10,2},{8,16},{18,10},{16,24},{26,18},{24,28},{30,26},{28,20... | collective-permute-start | bytes 1013768 | tf_op jit(solution)/shard_map/projection_far_2_0/ppermute | solution.py:94
  15.2 1.4 %projection_1.1 = (f32[3,256,640]{2,1,0:T(8,128)S(1)}, f32[8,640]{1,0:T(8,128)S(1)}) custom-call(bf16[264,640]{1,0:T(8,128)(2,1)S(1)} %prepare.1.refs_0_, bf16[264,640]{1,0:T(8,128)(2,1)S(1)} %collective-permute-done.4.refs_1_, bf16[264,640]{1,0:T(8,128)(2,1)S(1)} %collective-permute-done.refs_2_, bf16[264,640]{1,0:T(8,128)(2,1)S(1)} %collective-permute-done.9.refs_3_, ...), custom_call_target="tpu_custom_call" | custom-call | tf_op jit(solution)/shard_map/projection_1/pallas_call | solution.py:193
  17.3 2.1 %collective-permute-start.2 = (bf16[264,640]{1,0:T(8,128)(2,1)S(1)}, bf16[264,640]{1,0:T(8,128)(2,1)S(1)}, u32[]{:S(2)}, u32[]{:S(2)}) collective-permute-start(bf16[264,640]{1,0:T(8,128)(2,1)S(1)} %collective-permute-done.1.refs_2_), channel_id=1, source_target_pairs={{0,8},{10,2},{8,16},{18,10},{16,24},{26,18},{24,28},{30,26},{28,20... | collective-permute-start | bytes 1013768 | tf_op jit(solution)/shard_map/projection_near_3_0/ppermute | solution.py:94
  20.4 2.1 %collective-permute-start.13 = (bf16[264,640]{1,0:T(8,128)(2,1)S(1)}, bf16[264,640]{1,0:T(8,128)(2,1)S(1)}, u32[]{:S(2)}, u32[]{:S(2)}) collective-permute-start(bf16[264,640]{1,0:T(8,128)(2,1)S(1)} %collective-permute-done.6.refs_0_), channel_id=1, source_target_pairs={{0,8},{10,2},{8,16},{18,10},{16,24},{26,18},{24,28},{30,26},{28,20... | collective-permute-start | bytes 1013768 | tf_op jit(solution)/shard_map/projection_far_3_0/ppermute | solution.py:94
  22.5 1.6 %projection_2.1 = (f32[3,256,640]{2,1,0:T(8,128)S(1)}, f32[8,640]{1,0:T(8,128)S(1)}) custom-call(bf16[264,640]{1,0:T(8,128)(2,1)S(1)} %collective-permute-done.5.refs_0_, bf16[264,640]{1,0:T(8,128)(2,1)S(1)} %collective-permute-done.8.refs_1_, bf16[264,640]{1,0:T(8,128)(2,1)S(1)} %collective-permute-done.1.refs_2_, ...), custom_call_target="tpu_custom_call", output_to_operand_aliasing={{0}: (5, {}), {1}: (6, {})} | custom-call | tf_op jit(solution)/shard_map/projection_2/pallas_call | solution.py:193
  25.0 2.1 %collective-permute-start.3 = (bf16[264,640]{1,0:T(8,128)(2,1)S(1)}, bf16[264,640]{1,0:T(8,128)(2,1)S(1)}, u32[]{:S(2)}, u32[]{:S(2)}) collective-permute-start(bf16[264,640]{1,0:T(8,128)(2,1)S(1)} %collective-permute-done.2.refs_2_), channel_id=1, source_target_pairs={{0,8},{10,2},{8,16},{18,10},{16,24},{26,18},{24,28},{30,26},{28,20... | collective-permute-start | bytes 1013768 | tf_op jit(solution)/shard_map/projection_near_4_0/ppermute | solution.py:94
  28.1 1.6 %projection_3.1 = (f32[3,256,640]{2,1,0:T(8,128)S(1)}, f32[8,640]{1,0:T(8,128)S(1)}) custom-call(bf16[264,640]{1,0:T(8,128)(2,1)S(1)} %collective-permute-done.6.refs_0_, bf16[264,640]{1,0:T(8,128)(2,1)S(1)} %collective-permute-done.7.refs_1_, bf16[264,640]{1,0:T(8,128)(2,1)S(1)} %collective-permute-done.2.refs_2_, ...), custom_call_target="tpu_custom_call", output_to_operand_aliasing={{0}: (5, {}), {1}: (6, {})} | custom-call | tf_op jit(solution)/shard_map/projection_3/pallas_call | solution.py:193
  29.7 2.5 %collective-permute-done.3.refs_2_ = bf16[264,640]{1,0:T(8,128)(2,1)S(1)} collective-permute-done((bf16[264,640]{1,0:T(8,128)(2,1)S(1)}, bf16[264,640]{1,0:T(8,128)(2,1)S(1)}, u32[]{:S(2)}, u32[]{:S(2)}) %collective-permute-start.3) | collective-permute-done | bytes 337952 | tf_op jit(solution)/shard_map/projection_near_4_0/ppermute | solution.py:94
  34.5 2.1 %collective-permute-start.15 = (bf16[136,640]{1,0:T(8,128)(2,1)S(1)}, bf16[136,640]{1,0:T(8,128)(2,1)S(1)}, u32[]{:S(2)}, u32[]{:S(2)}) collective-permute-start(bf16[136,640]{1,0:T(8,128)(2,1)S(1)} %get-tuple-element.58.refs_2_.refs_8_), channel_id=1, source_target_pairs={{0,1},{1,0},{2,3},{3,2},{4,5},{5,4},{6,7},{7,6},{8,9},{9,8},{10,11... | collective-permute-start | bytes 522248 | tf_op jit(solution)/shard_map/ppermute | solution.py:561
  38.3 3.5 %collective-permute-done.15.refs_0_ = bf16[136,640]{1,0:T(8,128)(2,1)S(1)} collective-permute-done((bf16[136,640]{1,0:T(8,128)(2,1)S(1)}, bf16[136,640]{1,0:T(8,128)(2,1)S(1)}, u32[]{:S(2)}, u32[]{:S(2)}) %collective-permute-start.15) | collective-permute-done | bytes 174112 | tf_op jit(solution)/shard_map/ppermute | solution.py:561
  41.8 1.2 %far_part_1_0.1.refs_0_ = bf16[128,640]{1,0:T(8,128)(2,1)S(1)} custom-call(bf16[136,640]{1,0:T(8,128)(2,1)S(1)} %collective-permute-done.15.refs_0_, f32[128,1280]{1,0:T(8,128)S(1)} %get-tuple-element.63.refs_1_, f32[256,2560]{1,0:T(8,128)S(1)} %filter_spectra.1.refs_5_.refs_2_, bf16[256,256]{1,0:T(8,128)(2,1)S(1)} %copy-done.1, ...), custom_call_target="tpu_custom_call" | custom-call | tf_op jit(solution)/shard_map/far_part_1_0/pallas_call | solution.py:547
  43.1 2.2 %collective-permute-start.16 = (bf16[128,640]{1,0:T(8,128)(2,1)S(1)}, bf16[128,640]{1,0:T(8,128)(2,1)S(1)}, u32[]{:S(2)}, u32[]{:S(2)}) collective-permute-start(bf16[128,640]{1,0:T(8,128)(2,1)S(1)} %far_part_1_0.1.refs_0_), channel_id=1, source_target_pairs={{0,8},{10,2},{8,16},{18,10},{16,24},{26,18},{24,28},{30,26},{28,20... | collective-permute-start | bytes 491528 | tf_op jit(solution)/shard_map/output_near_1_0/ppermute | solution.py:94
  45.3 1.2 %far_part_1_128.1.refs_1_ = bf16[128,640]{1,0:T(8,128)(2,1)S(1)} custom-call(bf16[136,640]{1,0:T(8,128)(2,1)S(1)} %collective-permute-done.17.refs_0_, f32[128,1280]{1,0:T(8,128)S(1)} %get-tuple-element.66.refs_1_, f32[256,2560]{1,0:T(8,128)S(1)} %filter_spectra.1.refs_5_.refs_2_, bf16[256,256]{1,0:T(8,128)(2,1)S(1)} %copy-done.1, ...), custom_call_target="tpu_custom_call" | custom-call | tf_op jit(solution)/shard_map/far_part_1_128/pallas_call | solution.py:547
  46.7 1.5 %collective-permute-start.18 = (bf16[128,640]{1,0:T(8,128)(2,1)S(1)}, bf16[128,640]{1,0:T(8,128)(2,1)S(1)}, u32[]{:S(2)}, u32[]{:S(2)}) collective-permute-start(bf16[128,640]{1,0:T(8,128)(2,1)S(1)} %far_part_1_128.1.refs_1_), channel_id=1, source_target_pairs={{0,8},{10,2},{8,16},{18,10},{16,24},{26,18},{24,28},{30,26},{28,20... | collective-permute-start | bytes 491528 | tf_op jit(solution)/shard_map/output_near_1_1/ppermute | solution.py:94
  48.3 1.6 %collective-permute-start.23 = (bf16[128,640]{1,0:T(8,128)(2,1)S(1)}, bf16[128,640]{1,0:T(8,128)(2,1)S(1)}, u32[]{:S(2)}, u32[]{:S(2)}) collective-permute-start(bf16[128,640]{1,0:T(8,128)(2,1)S(1)} %collective-permute-done.22.refs_2_), channel_id=1, source_target_pairs={{0,8},{10,2},{8,16},{18,10},{16,24},{26,18},{24,28},{30,26},{28,20... | collective-permute-start | bytes 491528 | tf_op jit(solution)/shard_map/output_far_1_0/ppermute | solution.py:94
  49.9 1.6 %collective-permute-start.25 = (bf16[128,640]{1,0:T(8,128)(2,1)S(1)}, bf16[128,640]{1,0:T(8,128)(2,1)S(1)}, u32[]{:S(2)}, u32[]{:S(2)}) collective-permute-start(bf16[128,640]{1,0:T(8,128)(2,1)S(1)} %collective-permute-done.24.refs_3_), channel_id=1, source_target_pairs={{0,8},{10,2},{8,16},{18,10},{16,24},{26,18},{24,28},{30,26},{28,20... | collective-permute-start | bytes 491528 | tf_op jit(solution)/shard_map/output_far_1_1/ppermute | solution.py:94
  52.1 1.6 %collective-permute-start.19 = (bf16[256,640]{1,0:T(8,128)(2,1)S(1)}, bf16[256,640]{1,0:T(8,128)(2,1)S(1)}, u32[]{:S(2)}, u32[]{:S(2)}) collective-permute-start(bf16[256,640]{1,0:T(8,128)(2,1)S(1)} %constant_dynamic-update-slice_fusion.refs_4_), channel_id=1, source_target_pairs={{0,8},{10,2},{8,16},{18,10},{16,24},{26,18},{24,28},{30,26},{28,20... | collective-permute-start | bytes 983048 | tf_op jit(solution)/shard_map/output_near_2_0/ppermute | solution.py:94
  53.8 1.7 %collective-permute-done.25 = bf16[128,640]{1,0:T(8,128)(2,1)S(1)} collective-permute-done((bf16[128,640]{1,0:T(8,128)(2,1)S(1)}, bf16[128,640]{1,0:T(8,128)(2,1)S(1)}, u32[]{:S(2)}, u32[]{:S(2)}) %collective-permute-start.25) | collective-permute-done | bytes 163872 | tf_op jit(solution)/shard_map/output_far_1_1/ppermute | solution.py:94
  55.6 1.8 %collective-permute-start.26 = (bf16[256,640]{1,0:T(8,128)(2,1)S(1)}, bf16[256,640]{1,0:T(8,128)(2,1)S(1)}, u32[]{:S(2)}, u32[]{:S(2)}) collective-permute-start(bf16[256,640]{1,0:T(8,128)(2,1)S(1)} %constant_dynamic-update-slice_fusion.2.refs_0_), channel_id=1, source_target_pairs={{0,8},{10,2},{8,16},{18,10},{16,24},{26,18},{24,28},{30,26},{28,20... | collective-permute-start | bytes 983048 | tf_op jit(solution)/shard_map/output_far_2_0/ppermute | solution.py:94
  57.9 1.3 %collective-permute-done.19.refs_2_ = bf16[256,640]{1,0:T(8,128)(2,1)S(1)} collective-permute-done((bf16[256,640]{1,0:T(8,128)(2,1)S(1)}, bf16[256,640]{1,0:T(8,128)(2,1)S(1)}, u32[]{:S(2)}, u32[]{:S(2)}) %collective-permute-start.19) | collective-permute-done | bytes 327712 | tf_op jit(solution)/shard_map/output_near_2_0/ppermute | solution.py:94
  59.3 1.5 %collective-permute-start.20 = (bf16[256,640]{1,0:T(8,128)(2,1)S(1)}, bf16[256,640]{1,0:T(8,128)(2,1)S(1)}, u32[]{:S(2)}, u32[]{:S(2)}) collective-permute-start(bf16[256,640]{1,0:T(8,128)(2,1)S(1)} %collective-permute-done.19.refs_2_), channel_id=1, source_target_pairs={{0,8},{10,2},{8,16},{18,10},{16,24},{26,18},{24,28},{30,26},{28,20... | collective-permute-start | bytes 983048 | tf_op jit(solution)/shard_map/output_near_3_0/ppermute | solution.py:94
  60.8 2.1 %collective-permute-done.26.refs_0_ = bf16[256,640]{1,0:T(8,128)(2,1)S(1)} collective-permute-done((bf16[256,640]{1,0:T(8,128)(2,1)S(1)}, bf16[256,640]{1,0:T(8,128)(2,1)S(1)}, u32[]{:S(2)}, u32[]{:S(2)}) %collective-permute-start.26) | collective-permute-done | bytes 327712 | tf_op jit(solution)/shard_map/output_far_2_0/ppermute | solution.py:94
  62.9 1.5 %collective-permute-start.33 = (bf16[256,640]{1,0:T(8,128)(2,1)S(1)}, bf16[256,640]{1,0:T(8,128)(2,1)S(1)}, u32[]{:S(2)}, u32[]{:S(2)}) collective-permute-start(bf16[256,640]{1,0:T(8,128)(2,1)S(1)} %collective-permute-done.26.refs_0_), channel_id=1, source_target_pairs={{0,8},{10,2},{8,16},{18,10},{16,24},{26,18},{24,28},{30,26},{28,20... | collective-permute-start | bytes 983048 | tf_op jit(solution)/shard_map/output_far_3_0/ppermute | solution.py:94
  65.0 1.4 %collective-permute-done.20.refs_2_ = bf16[256,640]{1,0:T(8,128)(2,1)S(1)} collective-permute-done((bf16[256,640]{1,0:T(8,128)(2,1)S(1)}, bf16[256,640]{1,0:T(8,128)(2,1)S(1)}, u32[]{:S(2)}, u32[]{:S(2)}) %collective-permute-start.20) | collective-permute-done | bytes 327712 | tf_op jit(solution)/shard_map/output_near_3_0/ppermute | solution.py:94
  66.4 1.5 %collective-permute-start.21 = (bf16[256,640]{1,0:T(8,128)(2,1)S(1)}, bf16[256,640]{1,0:T(8,128)(2,1)S(1)}, u32[]{:S(2)}, u32[]{:S(2)}) collective-permute-start(bf16[256,640]{1,0:T(8,128)(2,1)S(1)} %collective-permute-done.20.refs_2_), channel_id=1, source_target_pairs={{0,8},{10,2},{8,16},{18,10},{16,24},{26,18},{24,28},{30,26},{28,20... | collective-permute-start | bytes 983048 | tf_op jit(solution)/shard_map/output_near_4_0/ppermute | solution.py:94
  67.9 2.0 %collective-permute-done.33.refs_0_ = bf16[256,640]{1,0:T(8,128)(2,1)S(1)} collective-permute-done((bf16[256,640]{1,0:T(8,128)(2,1)S(1)}, bf16[256,640]{1,0:T(8,128)(2,1)S(1)}, u32[]{:S(2)}, u32[]{:S(2)}) %collective-permute-start.33) | collective-permute-done | bytes 327712 | tf_op jit(solution)/shard_map/output_far_3_0/ppermute | solution.py:94
  70.6 2.9 %collective-permute-done.21.refs_2_ = bf16[256,640]{1,0:T(8,128)(2,1)S(1)} collective-permute-done((bf16[256,640]{1,0:T(8,128)(2,1)S(1)}, bf16[256,640]{1,0:T(8,128)(2,1)S(1)}, u32[]{:S(2)}, u32[]{:S(2)}) %collective-permute-start.21) | collective-permute-done | bytes 327712 | tf_op jit(solution)/shard_map/output_near_4_0/ppermute | solution.py:94
  (82 shorter events, 15.8 us)
Async XLA Ops:
  1.8 7.7 %collective-permute-start = (bf16[264,640]{1,0:T(8,128)(2,1)S(1)}, bf16[264,640]{1,0:T(8,128)(2,1)S(1)}, u32[]{:S(2)}, u32[]{:S(2)}) collective-permute-start(bf16[264,640]{1,0:T(8,128)(2,1)S(1)} %prepare.1.refs_0_), channel_id=1, source_target_pairs={{0,8},{10,2},{8,16},{18,10},{16,24},{26,18},{24,28},{30,26},{28,20... | collective-permute-start | bytes 1013768 | tf_op jit(solution)/shard_map/projection_near_1_0/ppermute | solution.py:94
  4.4 8.7 %collective-permute-start.5 = (bf16[264,640]{1,0:T(8,128)(2,1)S(1)}, bf16[264,640]{1,0:T(8,128)(2,1)S(1)}, u32[]{:S(2)}, u32[]{:S(2)}) collective-permute-start(bf16[264,640]{1,0:T(8,128)(2,1)S(1)} %collective-permute-done.4.refs_1_), channel_id=1, source_target_pairs={{0,8},{10,2},{8,16},{18,10},{16,24},{26,18},{24,28},{30,26},{28,20... | collective-permute-start | bytes 1013768 | tf_op jit(solution)/shard_map/projection_far_1_0/ppermute | solution.py:94
  9.5 5.7 %collective-permute-start.9 = (bf16[264,640]{1,0:T(8,128)(2,1)S(1)}, bf16[264,640]{1,0:T(8,128)(2,1)S(1)}, u32[]{:S(2)}, u32[]{:S(2)}) collective-permute-start(bf16[264,640]{1,0:T(8,128)(2,1)S(1)} %collective-permute-done.refs_2_), channel_id=1, source_target_pairs={{0,2},{2,0},{4,6},{6,4},{8,10},{10,8},{12,14},{14,12},{16,18},{18,... | collective-permute-start | bytes 1013768 | tf_op jit(solution)/shard_map/projection_core_near_1_0/ppermute | solution.py:98
  9.5 7.2 %collective-permute-start.1 = (bf16[264,640]{1,0:T(8,128)(2,1)S(1)}, bf16[264,640]{1,0:T(8,128)(2,1)S(1)}, u32[]{:S(2)}, u32[]{:S(2)}) collective-permute-start(bf16[264,640]{1,0:T(8,128)(2,1)S(1)} %collective-permute-done.refs_2_), channel_id=1, source_target_pairs={{0,8},{10,2},{8,16},{18,10},{16,24},{26,18},{24,28},{30,26},{28,20... | collective-permute-start | bytes 1013768 | tf_op jit(solution)/shard_map/projection_near_2_0/ppermute | solution.py:94
  13.2 7.2 %collective-permute-start.6 = (bf16[264,640]{1,0:T(8,128)(2,1)S(1)}, bf16[264,640]{1,0:T(8,128)(2,1)S(1)}, u32[]{:S(2)}, u32[]{:S(2)}) collective-permute-start(bf16[264,640]{1,0:T(8,128)(2,1)S(1)} %collective-permute-done.5.refs_0_), channel_id=1, source_target_pairs={{0,8},{10,2},{8,16},{18,10},{16,24},{26,18},{24,28},{30,26},{28,20... | collective-permute-start | bytes 1013768 | tf_op jit(solution)/shard_map/projection_far_2_0/ppermute | solution.py:94
  16.8 5.7 %collective-permute-start.10 = (bf16[264,640]{1,0:T(8,128)(2,1)S(1)}, bf16[264,640]{1,0:T(8,128)(2,1)S(1)}, u32[]{:S(2)}, u32[]{:S(2)}) collective-permute-start(bf16[264,640]{1,0:T(8,128)(2,1)S(1)} %collective-permute-done.1.refs_2_), channel_id=1, source_target_pairs={{0,2},{2,0},{4,6},{6,4},{8,10},{10,8},{12,14},{14,12},{16,18},{18,... | collective-permute-start | bytes 1013768 | tf_op jit(solution)/shard_map/projection_core_near_2_0/ppermute | solution.py:98
  16.8 5.7 %collective-permute-start.8 = (bf16[264,640]{1,0:T(8,128)(2,1)S(1)}, bf16[264,640]{1,0:T(8,128)(2,1)S(1)}, u32[]{:S(2)}, u32[]{:S(2)}) collective-permute-start(bf16[264,640]{1,0:T(8,128)(2,1)S(1)} %collective-permute-done.5.refs_0_), channel_id=1, source_target_pairs={{0,2},{2,0},{4,6},{6,4},{8,10},{10,8},{12,14},{14,12},{16,18},{18,... | collective-permute-start | bytes 1013768 | tf_op jit(solution)/shard_map/projection_core_far_1_0/ppermute | solution.py:98
  17.3 7.2 %collective-permute-start.2 = (bf16[264,640]{1,0:T(8,128)(2,1)S(1)}, bf16[264,640]{1,0:T(8,128)(2,1)S(1)}, u32[]{:S(2)}, u32[]{:S(2)}) collective-permute-start(bf16[264,640]{1,0:T(8,128)(2,1)S(1)} %collective-permute-done.1.refs_2_), channel_id=1, source_target_pairs={{0,8},{10,2},{8,16},{18,10},{16,24},{26,18},{24,28},{30,26},{28,20... | collective-permute-start | bytes 1013768 | tf_op jit(solution)/shard_map/projection_near_3_0/ppermute | solution.py:94
  20.4 7.7 %collective-permute-start.13 = (bf16[264,640]{1,0:T(8,128)(2,1)S(1)}, bf16[264,640]{1,0:T(8,128)(2,1)S(1)}, u32[]{:S(2)}, u32[]{:S(2)}) collective-permute-start(bf16[264,640]{1,0:T(8,128)(2,1)S(1)} %collective-permute-done.6.refs_0_), channel_id=1, source_target_pairs={{0,8},{10,2},{8,16},{18,10},{16,24},{26,18},{24,28},{30,26},{28,20... | collective-permute-start | bytes 1013768 | tf_op jit(solution)/shard_map/projection_far_3_0/ppermute | solution.py:94
  24.5 3.6 %collective-permute-start.11 = (bf16[264,640]{1,0:T(8,128)(2,1)S(1)}, bf16[264,640]{1,0:T(8,128)(2,1)S(1)}, u32[]{:S(2)}, u32[]{:S(2)}) collective-permute-start(bf16[264,640]{1,0:T(8,128)(2,1)S(1)} %collective-permute-done.2.refs_2_), channel_id=1, source_target_pairs={{0,2},{2,0},{4,6},{6,4},{8,10},{10,8},{12,14},{14,12},{16,18},{18,... | collective-permute-start | bytes 1013768 | tf_op jit(solution)/shard_map/projection_core_near_3_0/ppermute | solution.py:98
  24.5 3.6 %collective-permute-start.7 = (bf16[264,640]{1,0:T(8,128)(2,1)S(1)}, bf16[264,640]{1,0:T(8,128)(2,1)S(1)}, u32[]{:S(2)}, u32[]{:S(2)}) collective-permute-start(bf16[264,640]{1,0:T(8,128)(2,1)S(1)} %collective-permute-done.6.refs_0_), channel_id=1, source_target_pairs={{0,2},{2,0},{4,6},{6,4},{8,10},{10,8},{12,14},{14,12},{16,18},{18,... | collective-permute-start | bytes 1013768 | tf_op jit(solution)/shard_map/projection_core_far_2_0/ppermute | solution.py:98
  25.0 7.2 %collective-permute-start.3 = (bf16[264,640]{1,0:T(8,128)(2,1)S(1)}, bf16[264,640]{1,0:T(8,128)(2,1)S(1)}, u32[]{:S(2)}, u32[]{:S(2)}) collective-permute-start(bf16[264,640]{1,0:T(8,128)(2,1)S(1)} %collective-permute-done.2.refs_2_), channel_id=1, source_target_pairs={{0,8},{10,2},{8,16},{18,10},{16,24},{26,18},{24,28},{30,26},{28,20... | collective-permute-start | bytes 1013768 | tf_op jit(solution)/shard_map/projection_near_4_0/ppermute | solution.py:94
  28.1 4.1 %collective-permute-start.14 = (bf16[264,640]{1,0:T(8,128)(2,1)S(1)}, bf16[264,640]{1,0:T(8,128)(2,1)S(1)}, u32[]{:S(2)}, u32[]{:S(2)}) collective-permute-start(bf16[264,640]{1,0:T(8,128)(2,1)S(1)} %collective-permute-done.13.refs_0_), channel_id=1, source_target_pairs={{0,2},{2,0},{4,6},{6,4},{8,10},{10,8},{12,14},{14,12},{16,18},{18,... | collective-permute-start | bytes 1013768 | tf_op jit(solution)/shard_map/projection_core_far_3_0/ppermute | solution.py:98
  34.5 7.3 %collective-permute-start.15 = (bf16[136,640]{1,0:T(8,128)(2,1)S(1)}, bf16[136,640]{1,0:T(8,128)(2,1)S(1)}, u32[]{:S(2)}, u32[]{:S(2)}) collective-permute-start(bf16[136,640]{1,0:T(8,128)(2,1)S(1)} %get-tuple-element.58.refs_2_.refs_8_), channel_id=1, source_target_pairs={{0,1},{1,0},{2,3},{3,2},{4,5},{5,4},{6,7},{7,6},{8,9},{9,8},{10,11... | collective-permute-start | bytes 522248 | tf_op jit(solution)/shard_map/ppermute | solution.py:561
  37.3 8.0 %collective-permute-start.17 = (bf16[136,640]{1,0:T(8,128)(2,1)S(1)}, bf16[136,640]{1,0:T(8,128)(2,1)S(1)}, u32[]{:S(2)}, u32[]{:S(2)}) collective-permute-start(bf16[136,640]{1,0:T(8,128)(2,1)S(1)} %get-tuple-element.61.refs_3_.refs_8_), channel_id=1, source_target_pairs={{0,1},{1,0},{2,3},{3,2},{4,5},{5,4},{6,7},{7,6},{8,9},{9,8},{10,11... | collective-permute-start | bytes 522248 | tf_op jit(solution)/shard_map/ppermute | solution.py:561
  43.1 5.2 %collective-permute-start.22 = (bf16[128,640]{1,0:T(8,128)(2,1)S(1)}, bf16[128,640]{1,0:T(8,128)(2,1)S(1)}, u32[]{:S(2)}, u32[]{:S(2)}) collective-permute-start(bf16[128,640]{1,0:T(8,128)(2,1)S(1)} %far_part_1_0.1.refs_0_), channel_id=1, source_target_pairs={{0,2},{2,0},{4,6},{6,4},{8,10},{10,8},{12,14},{14,12},{16,18},{18,... | collective-permute-start | bytes 491528 | tf_op jit(solution)/shard_map/output_core_own_0/ppermute | solution.py:98
  43.1 6.7 %collective-permute-start.16 = (bf16[128,640]{1,0:T(8,128)(2,1)S(1)}, bf16[128,640]{1,0:T(8,128)(2,1)S(1)}, u32[]{:S(2)}, u32[]{:S(2)}) collective-permute-start(bf16[128,640]{1,0:T(8,128)(2,1)S(1)} %far_part_1_0.1.refs_0_), channel_id=1, source_target_pairs={{0,8},{10,2},{8,16},{18,10},{16,24},{26,18},{24,28},{30,26},{28,20... | collective-permute-start | bytes 491528 | tf_op jit(solution)/shard_map/output_near_1_0/ppermute | solution.py:94
  46.5 3.3 %collective-permute-start.24 = (bf16[128,640]{1,0:T(8,128)(2,1)S(1)}, bf16[128,640]{1,0:T(8,128)(2,1)S(1)}, u32[]{:S(2)}, u32[]{:S(2)}) collective-permute-start(bf16[128,640]{1,0:T(8,128)(2,1)S(1)} %far_part_1_128.1.refs_1_), channel_id=1, source_target_pairs={{0,2},{2,0},{4,6},{6,4},{8,10},{10,8},{12,14},{14,12},{16,18},{18,... | collective-permute-start | bytes 491528 | tf_op jit(solution)/shard_map/output_core_own_1/ppermute | solution.py:98
  46.7 5.3 %collective-permute-start.18 = (bf16[128,640]{1,0:T(8,128)(2,1)S(1)}, bf16[128,640]{1,0:T(8,128)(2,1)S(1)}, u32[]{:S(2)}, u32[]{:S(2)}) collective-permute-start(bf16[128,640]{1,0:T(8,128)(2,1)S(1)} %far_part_1_128.1.refs_1_), channel_id=1, source_target_pairs={{0,8},{10,2},{8,16},{18,10},{16,24},{26,18},{24,28},{30,26},{28,20... | collective-permute-start | bytes 491528 | tf_op jit(solution)/shard_map/output_near_1_1/ppermute | solution.py:94
  48.3 5.5 %collective-permute-start.23 = (bf16[128,640]{1,0:T(8,128)(2,1)S(1)}, bf16[128,640]{1,0:T(8,128)(2,1)S(1)}, u32[]{:S(2)}, u32[]{:S(2)}) collective-permute-start(bf16[128,640]{1,0:T(8,128)(2,1)S(1)} %collective-permute-done.22.refs_2_), channel_id=1, source_target_pairs={{0,8},{10,2},{8,16},{18,10},{16,24},{26,18},{24,28},{30,26},{28,20... | collective-permute-start | bytes 491528 | tf_op jit(solution)/shard_map/output_far_1_0/ppermute | solution.py:94
  49.9 5.7 %collective-permute-start.25 = (bf16[128,640]{1,0:T(8,128)(2,1)S(1)}, bf16[128,640]{1,0:T(8,128)(2,1)S(1)}, u32[]{:S(2)}, u32[]{:S(2)}) collective-permute-start(bf16[128,640]{1,0:T(8,128)(2,1)S(1)} %collective-permute-done.24.refs_3_), channel_id=1, source_target_pairs={{0,8},{10,2},{8,16},{18,10},{16,24},{26,18},{24,28},{30,26},{28,20... | collective-permute-start | bytes 491528 | tf_op jit(solution)/shard_map/output_far_1_1/ppermute | solution.py:94
  52.1 5.3 %collective-permute-start.29 = (bf16[256,640]{1,0:T(8,128)(2,1)S(1)}, bf16[256,640]{1,0:T(8,128)(2,1)S(1)}, u32[]{:S(2)}, u32[]{:S(2)}) collective-permute-start(bf16[256,640]{1,0:T(8,128)(2,1)S(1)} %constant_dynamic-update-slice_fusion.refs_4_), channel_id=1, source_target_pairs={{0,2},{2,0},{4,6},{6,4},{8,10},{10,8},{12,14},{14,12},{16,18},{18,... | collective-permute-start | bytes 983048 | tf_op jit(solution)/shard_map/output_core_near_1_0/ppermute | solution.py:98
  52.1 7.1 %collective-permute-start.19 = (bf16[256,640]{1,0:T(8,128)(2,1)S(1)}, bf16[256,640]{1,0:T(8,128)(2,1)S(1)}, u32[]{:S(2)}, u32[]{:S(2)}) collective-permute-start(bf16[256,640]{1,0:T(8,128)(2,1)S(1)} %constant_dynamic-update-slice_fusion.refs_4_), channel_id=1, source_target_pairs={{0,8},{10,2},{8,16},{18,10},{16,24},{26,18},{24,28},{30,26},{28,20... | collective-permute-start | bytes 983048 | tf_op jit(solution)/shard_map/output_near_2_0/ppermute | solution.py:94
  55.6 7.3 %collective-permute-start.26 = (bf16[256,640]{1,0:T(8,128)(2,1)S(1)}, bf16[256,640]{1,0:T(8,128)(2,1)S(1)}, u32[]{:S(2)}, u32[]{:S(2)}) collective-permute-start(bf16[256,640]{1,0:T(8,128)(2,1)S(1)} %constant_dynamic-update-slice_fusion.2.refs_0_), channel_id=1, source_target_pairs={{0,8},{10,2},{8,16},{18,10},{16,24},{26,18},{24,28},{30,26},{28,20... | collective-permute-start | bytes 983048 | tf_op jit(solution)/shard_map/output_far_2_0/ppermute | solution.py:94
  57.3 7.1 %collective-permute-start.28 = (bf16[256,640]{1,0:T(8,128)(2,1)S(1)}, bf16[256,640]{1,0:T(8,128)(2,1)S(1)}, u32[]{:S(2)}, u32[]{:S(2)}) collective-permute-start(bf16[256,640]{1,0:T(8,128)(2,1)S(1)} %constant_dynamic-update-slice_fusion.2.refs_0_), channel_id=1, source_target_pairs={{0,2},{2,0},{4,6},{6,4},{8,10},{10,8},{12,14},{14,12},{16,18},{18,... | collective-permute-start | bytes 983048 | tf_op jit(solution)/shard_map/output_core_far_1_0/ppermute | solution.py:98
  59.3 5.2 %collective-permute-start.30 = (bf16[256,640]{1,0:T(8,128)(2,1)S(1)}, bf16[256,640]{1,0:T(8,128)(2,1)S(1)}, u32[]{:S(2)}, u32[]{:S(2)}) collective-permute-start(bf16[256,640]{1,0:T(8,128)(2,1)S(1)} %collective-permute-done.19.refs_2_), channel_id=1, source_target_pairs={{0,2},{2,0},{4,6},{6,4},{8,10},{10,8},{12,14},{14,12},{16,18},{18,... | collective-permute-start | bytes 983048 | tf_op jit(solution)/shard_map/output_core_near_2_0/ppermute | solution.py:98
  59.3 7.1 %collective-permute-start.20 = (bf16[256,640]{1,0:T(8,128)(2,1)S(1)}, bf16[256,640]{1,0:T(8,128)(2,1)S(1)}, u32[]{:S(2)}, u32[]{:S(2)}) collective-permute-start(bf16[256,640]{1,0:T(8,128)(2,1)S(1)} %collective-permute-done.19.refs_2_), channel_id=1, source_target_pairs={{0,8},{10,2},{8,16},{18,10},{16,24},{26,18},{24,28},{30,26},{28,20... | collective-permute-start | bytes 983048 | tf_op jit(solution)/shard_map/output_near_3_0/ppermute | solution.py:94
  62.9 7.1 %collective-permute-start.33 = (bf16[256,640]{1,0:T(8,128)(2,1)S(1)}, bf16[256,640]{1,0:T(8,128)(2,1)S(1)}, u32[]{:S(2)}, u32[]{:S(2)}) collective-permute-start(bf16[256,640]{1,0:T(8,128)(2,1)S(1)} %collective-permute-done.26.refs_0_), channel_id=1, source_target_pairs={{0,8},{10,2},{8,16},{18,10},{16,24},{26,18},{24,28},{30,26},{28,20... | collective-permute-start | bytes 983048 | tf_op jit(solution)/shard_map/output_far_3_0/ppermute | solution.py:94
  64.4 5.5 %collective-permute-start.27 = (bf16[256,640]{1,0:T(8,128)(2,1)S(1)}, bf16[256,640]{1,0:T(8,128)(2,1)S(1)}, u32[]{:S(2)}, u32[]{:S(2)}) collective-permute-start(bf16[256,640]{1,0:T(8,128)(2,1)S(1)} %collective-permute-done.26.refs_0_), channel_id=1, source_target_pairs={{0,2},{2,0},{4,6},{6,4},{8,10},{10,8},{12,14},{14,12},{16,18},{18,... | collective-permute-start | bytes 983048 | tf_op jit(solution)/shard_map/output_core_far_2_0/ppermute | solution.py:98
  66.4 3.6 %collective-permute-start.31 = (bf16[256,640]{1,0:T(8,128)(2,1)S(1)}, bf16[256,640]{1,0:T(8,128)(2,1)S(1)}, u32[]{:S(2)}, u32[]{:S(2)}) collective-permute-start(bf16[256,640]{1,0:T(8,128)(2,1)S(1)} %collective-permute-done.20.refs_2_), channel_id=1, source_target_pairs={{0,2},{2,0},{4,6},{6,4},{8,10},{10,8},{12,14},{14,12},{16,18},{18,... | collective-permute-start | bytes 983048 | tf_op jit(solution)/shard_map/output_core_near_3_0/ppermute | solution.py:98
  66.4 7.1 %collective-permute-start.21 = (bf16[256,640]{1,0:T(8,128)(2,1)S(1)}, bf16[256,640]{1,0:T(8,128)(2,1)S(1)}, u32[]{:S(2)}, u32[]{:S(2)}) collective-permute-start(bf16[256,640]{1,0:T(8,128)(2,1)S(1)} %collective-permute-done.20.refs_2_), channel_id=1, source_target_pairs={{0,8},{10,2},{8,16},{18,10},{16,24},{26,18},{24,28},{30,26},{28,20... | collective-permute-start | bytes 983048 | tf_op jit(solution)/shard_map/output_near_4_0/ppermute | solution.py:94
  70.0 3.5 %collective-permute-start.34 = (bf16[256,640]{1,0:T(8,128)(2,1)S(1)}, bf16[256,640]{1,0:T(8,128)(2,1)S(1)}, u32[]{:S(2)}, u32[]{:S(2)}) collective-permute-start(bf16[256,640]{1,0:T(8,128)(2,1)S(1)} %collective-permute-done.33.refs_0_), channel_id=1, source_target_pairs={{0,2},{2,0},{4,6},{6,4},{8,10},{10,8},{12,14},{14,12},{16,18},{18,... | collective-permute-start | bytes 983048 | tf_op jit(solution)/shard_map/output_core_far_3_0/ppermute | solution.py:98
  (14 other events, 71.8 us)

commit v8 on v7

--- a/solution.py
+++ b/solution.py
@@ -116,17 +116,17 @@
     return [refs.pop(0) for _ in range(number)]
 
 
-def products(items, weight, running, side, finish, cost, name, cut=(0, 1)):
+def products(items, weight, running, side, finish, cost, name):
+    body, extras, out_shape, cut, senders_only = finish or (None, [], None, None, False)
     streams, out_rows, features = weight.shape
-    out_rows //= cut[1]
-    out_here = slice(cut[0] * out_rows, (cut[0] + 1) * out_rows)
+    cut = cut or (0, out_rows)
+    out_here, out_rows = slice(cut[0], cut[0] + cut[1]), cut[1]
     rows = features // lax.axis_size("fsdp")
     shards = [piece for _, _, pieces in items for piece in pieces]
     tokens = shards[0].shape[1]
     count = len(shards)
     first_group = running is None
     state = [] if first_group else list(running)
-    body, extras, out_shape = finish if finish else (None, [], None)
     padded = rows % 128 != 0
     width = 2 * rows if padded else rows
     scratch_shapes = [pltpu.VMEM((len(items) * width, tokens), bf16)] if padded else []
@@ -139,49 +139,59 @@
         state_refs = take(len(state))
         extra_refs = take(len(extras))
         outs = take(len(out_shape))
-        core = my_core()
-        chip_of = {steps: source_chip(steps) for steps in sorted({item[0] for item in items})}
-        if padded:
-            (beside_ref,) = refs
-            beside_ref[...] = jnp.zeros(beside_ref.shape, bf16)
-        sides, right = [], []
-        for k, (_, other, pieces) in enumerate(items):
-            done = 0
-            for piece_ref in take_from(shard_refs, len(pieces)):
-                more = min(piece_ref.shape[0], rows - done)
-                if padded:
-                    at = k * width + jnp.where(core == other, 0, rows) + done
-                    at = pl.multiple_of(at, math.gcd(rows, done or rows))
-                    beside_ref[pl.ds(at, more)] = piece_ref[:more]
-                else:
-                    right.append(piece_ref[:more])
-                if more < piece_ref.shape[0]:
-                    sides.append(piece_ref[more:].astype(f32))
-                done += more
-        right = beside_ref[...] if padded else jnp.concatenate(right, axis=0)
-        side_sum = None
-        if side:
-            parts = sides + ([] if first_group else [state_refs[1][...]])
-            side_sum = sum(parts[1:], parts[0])
-
-        def total(stream):
-            left = []
-            for steps, other, _ in items:
-                block = chip_of[steps]
-                if not padded:
-                    block = 2 * block + (1 - core if other else core)
-                at = pl.ds(pl.multiple_of(block * width, width), width)
-                left.append(weight_ref[stream, out_here, at])
-            product = dot(jnp.concatenate(left, axis=1), right)
-            return product if first_group else state_refs[0][stream, out_here] + product
-
-        if body is not None:
-            body(total, side_sum, extra_refs, outs)
-            return
-        for stream in range(streams):
-            outs[0][stream] = total(stream)
-        if side:
-            outs[1][...] = side_sum
+
+        def work():
+            core = my_core()
+            chip_of = {steps: source_chip(steps) for steps in sorted({item[0] for item in items})}
+            if padded:
+                (beside_ref,) = refs
+                beside_ref[...] = jnp.zeros(beside_ref.shape, bf16)
+            sides, right = [], []
+            pieces_left = list(shard_refs)
+            for k, (_, other, pieces) in enumerate(items):
+                done = 0
+                for piece_ref in take_from(pieces_left, len(pieces)):
+                    more = min(piece_ref.shape[0], rows - done)
+                    if padded:
+                        at = k * width + jnp.where(core == other, 0, rows) + done
+                        at = pl.multiple_of(at, math.gcd(rows, done or rows))
+                        beside_ref[pl.ds(at, more)] = piece_ref[:more]
+                    else:
+                        right.append(piece_ref[:more])
+                    if more < piece_ref.shape[0]:
+                        sides.append(piece_ref[more:].astype(f32))
+                    done += more
+            right = beside_ref[...] if padded else jnp.concatenate(right, axis=0)
+            side_sum = None
+            if side:
+                parts = sides + ([] if first_group else [state_refs[1][...]])
+                side_sum = sum(parts[1:], parts[0])
+
+            def total(stream, lanes=slice(None)):
+                left = []
+                for steps, other, _ in items:
+                    block = chip_of[steps]
+                    if not padded:
+                        block = 2 * block + (1 - core if other else core)
+                    at = pl.ds(pl.multiple_of(block * width, width), width)
+                    left.append(weight_ref[stream, out_here, at])
+                product = dot(jnp.concatenate(left, axis=1), right[:, lanes])
+                if first_group:
+                    return product
+                return state_refs[0][stream, out_here, lanes] + product
+
+            if body is not None:
+                body(total, side_sum, extra_refs, outs)
+                return
+            for stream in range(streams):
+                outs[0][stream] = total(stream)
+            if side:
+                outs[1][...] = side_sum
+
+        if senders_only:
+            pl.when(lax.axis_index("ctx") < lax.axis_size("ctx") - 1)(work)
+        else:
+            work()
 
     aliases = {}
     if body is None:
@@ -203,7 +213,7 @@
     )(*shards, weight, *state, *extras)
 
 
-def gather_products(own, weight, beside, side, finish, name):
+def gather_products(own, weight, beside, side, name):
     chips = chip_count()
     last_step = chips // 2
 
@@ -238,11 +248,11 @@
             items.append(pair[0])
             running = products(items, weight, running, side, None, STAGGER, f"{name}_{step}")
             items = pair[1:]
-    results = [
-        products(items, weight, running, side, end, 0, f"{name}_last_{k}", (k, len(finish)))
-        for k, end in enumerate(finish)
-    ]
-    return results, beside
+
+    def last(finish, running):
+        return products(items, weight, running, side, finish, 0, f"{name}_last")
+
+    return last, running, beside
 
 
 def smooth(projected, taps, count, halo):
@@ -261,52 +271,81 @@
 
 
 def channel_parts(channels):
-    return [(0, channels // 2), (channels // 2, channels // 2)]
-
-
-def projection_finish(features, w_short, tokens, half_index):
+    first = channels * 4 // 8 // 16 * 16
+    return [(0, first), (first, channels - first)]
+
+
+def norm_factor(side_sum, features):
+    mean = jnp.sum(side_sum, axis=0, keepdims=True) * (1.0 / features)
+    return lax.rsqrt(mean + epsilon)
+
+
+def gate(projected, taps_ref, begin, write):
+    count = taps_ref.shape[1]
+    columns = [tap_columns(taps_ref[stream]) for stream in (1, 2)]
+    rows = projected[0].shape[0]
+    tile = math.gcd(rows, 64)
+    for start in range(0, rows, tile):
+        here = slice(start, start + tile)
+        there = slice(begin + start, begin + start + tile)
+        key, value = (
+            smooth(wide[here].astype(f32), column[there], count, None)
+            for wide, column in zip(projected, columns)
+        )
+        write(here, key, value)
+
+
+def message_finish(features, w_short, tokens, part):
     streams, count, channels = w_short.shape
-    half = channels // 2
-    begin = half_index * half
-    parts = [part for part in channel_parts(channels) if begin <= part[0] < begin + half]
+    parts = channel_parts(channels)
+    begin, rows = parts[part]
+    last = slice(tokens - block_len, tokens)
 
     def body(total, side_sum, extra_refs, outs):
-        (taps_ref,) = extra_refs
-        projected_ref, first_ref, *message_refs = outs
-        mean = jnp.sum(side_sum, axis=0, keepdims=True) * (1.0 / features)
-        factor = lax.rsqrt(mean + epsilon)
-        tails = []
+        (taps_ref,), (message_ref,) = extra_refs, outs
+        factor = norm_factor(side_sum, features)
+        projected = [(total(stream) * factor).astype(bf16) for stream in (1, 2)]
+        ends = [(total(0, last) * factor[:, last]).astype(bf16)]
+        ends += [wide[:, last] for wide in projected]
+        lines = [end.astype(f32).T[block_len - count + 1 :] for end in ends]
+        lines.append(jnp.zeros((side_rows - streams * (count - 1), rows), f32))
+
+        def write(here, key, value):
+            message_ref[here] = (key * value).astype(bf16)
+
+        gate(projected, taps_ref, begin, write)
+        message_ref[rows:] = jnp.zeros((side_rows, tokens), bf16)
+        message_ref[rows:, :rows] = jnp.concatenate(lines, axis=0).astype(bf16)
+
+    out_shape = [shape_of((rows + side_rows, tokens), bf16)]
+    return body, [w_short], out_shape, parts[part], True
+
+
+def projection_finish(features, w_short, tokens, part):
+    streams, _, channels = w_short.shape
+    parts = channel_parts(channels)
+    begin, rows = parts[part]
+
+    def body(total, side_sum, extra_refs, outs):
+        (taps_ref,), (projected_ref, first_ref, gated_ref) = extra_refs, outs
+        factor = norm_factor(side_sum, features)
+        projected = [(total(stream) * factor).astype(bf16) for stream in range(streams)]
         for stream in range(streams):
-            projected = (total(stream) * factor).astype(bf16)
-            projected_ref[stream] = projected
-            tail = projected[:, tokens - block_len :].astype(f32).T
-            tails.append(tail[block_len - count + 1 :])
-        tails.append(jnp.zeros((side_rows - streams * (count - 1), half), f32))
-        side = jnp.concatenate(tails, axis=0)
-        taps = [tap_columns(taps_ref[stream]) for stream in (1, 2)]
-        for (first, rows), message_ref in zip(parts, message_refs):
-            tile = min(rows, 64)
-            for start in range(first, first + rows, tile):
-                here = slice(start - begin, start - begin + tile)
-                key, value = (
-                    smooth(
-                        projected_ref[s, here].astype(f32),
-                        taps[s - 1][start : start + tile],
-                        count,
-                        None,
-                    )
-                    for s in (1, 2)
-                )
-                first_ref[0, here] = key[:, :block_len]
-                first_ref[1, here] = value[:, :block_len]
-                message_ref[start - first : start - first + tile] = (key * value).astype(bf16)
-            message_ref[rows:] = jnp.zeros((side_rows, tokens), bf16)
-            here = side[:, first - begin : first - begin + rows]
-            message_ref[rows:, :rows] = here.astype(bf16)
-
-    out_shape = [shape_of((streams, half, tokens), bf16), shape_of((2, half, block_len), f32)]
-    out_shape += [shape_of((rows + side_rows, tokens), bf16) for _, rows in parts]
-    return body, [w_short], out_shape
+            projected_ref[stream] = projected[stream]
+
+        def write(here, key, value):
+            first_ref[0, here] = key[:, :block_len]
+            first_ref[1, here] = value[:, :block_len]
+            gated_ref[here] = (key * value).astype(bf16)
+
+        gate(projected[1:], taps_ref, begin, write)
+
+    out_shape = [
+        shape_of((streams, rows, tokens), bf16),
+        shape_of((2, rows, block_len), f32),
+        shape_of((rows, tokens), bf16),
+    ]
+    return body, [w_short], out_shape, parts[part], False
 
 
 def halo_columns(message_ref, streams, count, inside):
@@ -315,9 +354,9 @@
     return [side[:, s * (count - 1) : (s + 1) * (count - 1)] for s in range(streams)]
 
 
-def halo_edges(message_ref, taps, inside):
+def halo_edges(message_ref, taps):
     streams, count, rows = taps.shape
-    side = jnp.where(inside, message_ref[rows:, :rows].astype(f32), 0.0)
+    side = message_ref[rows:, :rows].astype(f32)
     lines = []
     for s in range(streams):
         for token in range(count - 1):
@@ -422,9 +461,9 @@
             total_ref[here, block_lanes(2 * a + 1)] = imag
 
 
-def own_part(projected, messages, moved, taps, filters, table):
-    streams, half, tokens = projected[0].shape
-    parts = channel_parts(2 * half)
+def own_part(projected, alone, moved, taps, filters, table):
+    streams, _, tokens = projected[0].shape
+    parts = channel_parts(taps.shape[2])
     number = len(parts)
     count = taps.shape[1]
     blocks = tokens // block_len
@@ -434,7 +473,7 @@
     def kernel(*refs):
         refs = list(refs)
         take = lambda n: take_from(refs, n)
-        projected_refs, message_refs = take(2), take(number)
+        projected_refs, message_refs = take(number), take(number)
         taps_ref, filters_ref, table_ref = take(3)
         query_refs, total_refs = take(number), take(number)
         gated_refs = take(number) if moved else None
@@ -444,16 +483,15 @@
             if moved:
                 inside = lax.axis_index("ctx") > 0
                 halo = halo_columns(message_refs[part], streams, count, inside)
-            tile = min(rows, 64)
+            tile = math.gcd(rows, 64)
             for start in range(0, rows, tile):
                 here = slice(start, start + tile)
                 there = slice(begin + start, begin + start + tile)
-                in_half = (begin + start) % half
-                projected_ref = projected_refs[begin // half]
+                projected_ref = projected_refs[part]
 
                 def smoothed(s):
                     edge = halo[s][here] if moved else None
-                    wide = projected_ref[s, in_half : in_half + tile].astype(f32)
+                    wide = projected_ref[s, here].astype(f32)
                     return smooth(wide, columns[s][there], count, edge)
 
                 query_refs[part][here] = smoothed(0)
@@ -468,27 +506,25 @@
     out_shape += [shape_of((rows, 2 * tokens), f32) for _, rows in parts]
     if moved:
         out_shape += [shape_of((rows, tokens), bf16) for _, rows in parts]
-    inputs = [*projected, *(moved or messages), taps, filters, table]
+    inputs = [*projected, *(moved or alone), taps, filters, table]
     outs = pl.pallas_call(
         kernel,
         in_specs=[in_vmem] * len(inputs),
         out_specs=[in_vmem] * len(out_shape),
         out_shape=out_shape,
-        scratch_shapes=[pltpu.VMEM((half, 2 * tokens), f32)],
+        scratch_shapes=[pltpu.VMEM((max(rows for _, rows in parts), 2 * tokens), f32)],
         compiler_params=params,
         cost_estimate=estimate(0, 0),
         name="own_part",
     )(*inputs)
-    gated = list(outs[2 * number :]) if moved else messages
+    gated = list(outs[2 * number :]) if moved else alone
     return list(outs[:number]), list(outs[number : 2 * number]), gated
 
 
 def far_part(turn, begin, moved, total, filters, table, last, own):
     rows, tokens = total.shape[0], moved.shape[1]
     blocks = tokens // block_len
-    pairs = [[(b, turn * blocks + a - b) for b in range(blocks)] for a in range(blocks)]
-    if own:
-        pairs = [terms + [(blocks, a)] for a, terms in enumerate(pairs)]
+    far_pairs = [[(b, turn * blocks + a - b) for b in range(blocks)] for a in range(blocks)]
     channels_here = slice(begin, begin + rows)
 
     def kernel(*refs):
@@ -497,42 +533,50 @@
         moved_ref, total_ref, filters_ref, table_ref = take(4)
         own_refs = take(2) if own else None
         spec_ref = refs.pop()
+        sum_ref = refs.pop()
+        if last:
+            last_refs = take(4)
+            (out_ref,) = refs
+
+        def work(inside):
+            pieces = [moved_ref[:rows, block_lanes(b)] for b in range(blocks)] if inside else []
+            pairs = far_pairs if inside else [[] for _ in range(blocks)]
+            if last:
+                back_ref, query_ref, gated_ref, skip_ref = last_refs
+                query, gated = (
+                    [ref[:rows, block_lanes(a)] for a in range(blocks)]
+                    for ref in (query_ref, gated_ref)
+                )
+            if own:
+                first_ref, taps_ref = own_refs
+                key, value = first_ref[0], first_ref[1]
+                if inside:
+                    edges = halo_edges(moved_ref, taps_ref[:, :, channels_here])
+                    query[0] = query[0] + edges[0]
+                    key, value = key + edges[1], value + edges[2]
+                gated[0] = (key * value).astype(bf16)
+                pairs = [terms + [(len(pieces), a)] for a, terms in enumerate(pairs)]
+                pieces.append(gated[0])
+            if pieces:
+                block_spectra(pieces, table_ref, spec_ref, 0)
+            multiply_spectra(spec_ref, filters_ref, begin, pairs, total_ref, sum_ref)
+            if not last:
+                return
+            skip = column(skip_ref[...])[channels_here]
+            spectra = [sum_ref[:, spectrum_lanes(a)] for a in range(blocks)]
+            highs = [spectrum.astype(bf16) for spectrum in spectra]
+            lows = [(s - high.astype(f32)).astype(bf16) for s, high in zip(spectra, highs)]
+            both = dot(jnp.concatenate(highs, axis=0), back_ref[...])
+            small = dot(jnp.concatenate(lows, axis=0), back_ref[:, :block_len])
+            filtered = both[:, :block_len] + (both[:, block_len:] + small)
+            for a in range(blocks):
+                here = filtered[a * rows : (a + 1) * rows]
+                mixed = query[a] * (here + skip * gated[a].astype(f32))
+                out_ref[:, block_lanes(a)] = mixed.astype(bf16)
+
         inside = lax.axis_index("ctx") >= turn
-        pieces = [
-            jnp.where(inside, moved_ref[:rows, block_lanes(b)], jnp.zeros((), bf16))
-            for b in range(blocks)
-        ]
-        if last is None:
-            block_spectra(pieces, table_ref, spec_ref, 0)
-            multiply_spectra(spec_ref, filters_ref, begin, pairs, total_ref, refs[0])
-            return
-        sum_ref = refs.pop()
-        back_ref, query_ref, gated_ref, skip_ref = take(4)
-        out_ref = refs[-1]
-        query, gated = (
-            [ref[:rows, block_lanes(a)] for a in range(blocks)] for ref in (query_ref, gated_ref)
-        )
-        if own:
-            first_ref, taps_ref = own_refs
-            in_half = slice(begin % first_ref.shape[1], begin % first_ref.shape[1] + rows)
-            edges = halo_edges(moved_ref, taps_ref[:, :, channels_here], inside)
-            query[0] = query[0] + edges[0]
-            key, value = first_ref[0, in_half] + edges[1], first_ref[1, in_half] + edges[2]
-            gated[0] = (key * value).astype(bf16)
-            pieces.append(gated[0])
-        block_spectra(pieces, table_ref, spec_ref, 0)
-        multiply_spectra(spec_ref, filters_ref, begin, pairs, total_ref, sum_ref)
-        skip = column(skip_ref[...])[channels_here]
-        spectra = [sum_ref[:, spectrum_lanes(a)] for a in range(blocks)]
-        highs = [spectrum.astype(bf16) for spectrum in spectra]
-        lows = [(s - high.astype(f32)).astype(bf16) for s, high in zip(spectra, highs)]
-        both = dot(jnp.concatenate(highs, axis=0), back_ref[...])
-        small = dot(jnp.concatenate(lows, axis=0), back_ref[:, :block_len])
-        filtered = both[:, :block_len] + (both[:, block_len:] + small)
-        for a in range(blocks):
-            here = filtered[a * rows : (a + 1) * rows]
-            mixed = (query[a] * (here + skip * gated[a].astype(f32))).astype(bf16)
-            out_ref[:, block_lanes(a)] = mixed
+        pl.when(inside)(lambda: work(True))
+        pl.when(jnp.logical_not(inside))(lambda: work(False))
 
     args = [moved, total, filters, table]
     if own:
@@ -565,7 +609,7 @@
     def body(total, side_sum, extra_refs, outs):
         outs[0][...] = total(0).astype(bf16)
 
-    return body, [], [shape_of((channels, tokens), bf16)]
+    return body, [], [shape_of((channels, tokens), bf16)], None, False
 
 
 def shards(activations, norm_gain, w_in, w_short, long_filter, skip_gain, w_out):
@@ -578,17 +622,20 @@
     own = prepare(activations, norm_gain)
 
     filters = filter_spectra(long_filter, segments)
-    finish = [projection_finish(features, w_short, tokens, k) for k in range(2)]
-    results, (filters,) = gather_products(
-        [own], w_in, [filters], True, finish, "projection"
-    )
-    projected = [result[0] for result in results]
-    first_blocks = [result[1] for result in results]
-    messages = [message for result in results for message in result[2:]]
-    moving = [from_before(message) for message in messages]
+    last, running, (filters,) = gather_products([own], w_in, [filters], True, "projection")
+
+    def message(part, running):
+        (sent,) = last(message_finish(features, w_short, tokens, part), running)
+        return from_before(sent)
+
     exact = turns > 2
+    moving = [message(0, running)]
+    results = [last(projection_finish(features, w_short, tokens, k), running) for k in range(2)]
+    projected, first_blocks, gated = zip(*results)
+    later, gated = lax.optimization_barrier((running, gated))
+    moving.append(message(1, later))
     query, totals, gated = own_part(
-        projected, messages, moving if exact else None, w_short, filters, forward
+        projected, gated, moving if exact else None, w_short, filters, forward
     )
     if exact:
         moving = [from_before(part) for part in gated]
@@ -599,7 +646,7 @@
             if turn == turns - 1:
                 last = (inverse, query[k], gated[k], skip_gain)
                 if not exact:
-                    own_block = (first_blocks[2 * begin // channels], w_short)
+                    own_block = (first_blocks[k], w_short)
             done = far_part(
                 turn, begin, moving[k], totals[k], filters, forward, last, own_block
             )
@@ -609,10 +656,8 @@
             else:
                 mixed.append(done)
 
-    finish = [output_finish(channels, tokens)]
-    ((result,),), _ = gather_products(
-        mixed, w_out[None], [], False, finish, "output"
-    )
+    last, running, _ = gather_products(mixed, w_out[None], [], False, "output")
+    (result,) = last(output_finish(channels, tokens), running)
     return result
 
 

time: 76.3 us -> 75.1 us (0.984)
  waiting for transfers between devices: 26.3 us -> 23.4 us
  starting transfers between devices: 33.5 us -> 35.2 us
    ppermute x16, starting transfers between devices: 29.4 us -> 32 us  [along_ring(): return lax.ppermute(block, 'fsdp', pairs)]
    ppermute x16, waiting for transfers between devices: 21.3 us -> 19.2 us  [along_ring(): return lax.ppermute(block, 'fsdp', pairs)]
    pallas_call x2, Pallas kernels: 2.47 us -> 1.08 us  [far_part(): pl.pallas_call(kernel, in_specs=[in_vmem] * len(args), out_specs=in_vmem,...]
    pallas_call x11 -> x13, Pallas kernels: 10.5 us -> 11.8 us  [products(): pl.pallas_call(kernel, in_specs=[in_vmem] * (count + 1 + len(state) + len...]
    ppermute x2, waiting for transfers between devices: 3.48 us -> 2.66 us  [from_before(): lax.ppermute(block, 'ctx', [(i, (i + 1) % count) for i in range(count)])]
  transfers between devices with their start and end apart: 35 -> 35, of which waited for: 18 -> 17; matrix products, arithmetic and copies ran while one was open for 0% -> 0% of each run, Pallas kernels for 17% -> 17%
where the time goes in v8:
time: 75.1 us; the launch traced here: 74.9 us
  starting transfers between devices  35.2 us (47%)
  waiting for transfers between devices  23.4 us (31%)
  Pallas kernels  14.9 us (20%)
  local copies, waits for them, and re-layouts  1.14 us (2%)
    ppermute x16, starting transfers between devices, along_ring(): return lax.ppermute(block, 'fsdp', pairs)  32 us
    ppermute x16, waiting for transfers between devices, along_ring(): return lax.ppermute(block, 'fsdp', pairs)  19.2 us
    pallas_call x13, Pallas kernels, products(): pl.pallas_call(kernel, in_specs=[in_vmem] * (count + 1 + len(state) + len...  11.8 us
    ppermute x2, waiting for transfers between devices, from_before(): lax.ppermute(block, 'ctx', [(i, (i + 1) % count) for i in range(count)])  2.66 us
    ppermute x17, starting transfers between devices, other_core(): lax.ppermute(block, 'fsdp', [(i, i ^ 1) for i in range(2 * chip_count())])  1.77 us
    ppermute x17, waiting for transfers between devices, other_core(): lax.ppermute(block, 'fsdp', [(i, i ^ 1) for i in range(2 * chip_count())])  1.56 us
  transfers between devices with their start and end apart: 35, of which 17 were waited for; matrix products, arithmetic and copies ran while one was open for 0% of the time, Pallas kernels for 17%

profile of v8, /device:TPU:0, one launch (start us, length us, event | category | flops | bytes accessed | tf_op | source)
XLA Modules:
  0.0 74.9 jit_solution(16369069848335051338)
XLA Ops:
  1.8 2.6 %collective-permute-start = (bf16[264,640]{1,0:T(8,128)(2,1)S(1)}, bf16[264,640]{1,0:T(8,128)(2,1)S(1)}, u32[]{:S(2)}, u32[]{:S(2)}) collective-permute-start(bf16[264,640]{1,0:T(8,128)(2,1)S(1)} %prepare.1.refs_0_), channel_id=1, source_target_pairs={{0,8},{10,2},{8,16},{18,10},{16,24},{26,18},{24,28},{30,26},{28,20... | collective-permute-start | bytes 1013768 | tf_op jit(solution)/shard_map/projection_near_1_0/ppermute | solution.py:94
  4.4 1.6 %collective-permute-start.5 = (bf16[264,640]{1,0:T(8,128)(2,1)S(1)}, bf16[264,640]{1,0:T(8,128)(2,1)S(1)}, u32[]{:S(2)}, u32[]{:S(2)}) collective-permute-start(bf16[264,640]{1,0:T(8,128)(2,1)S(1)} %collective-permute-done.4.refs_1_), channel_id=1, source_target_pairs={{0,8},{10,2},{8,16},{18,10},{16,24},{26,18},{24,28},{30,26},{28,20... | collective-permute-start | bytes 1013768 | tf_op jit(solution)/shard_map/projection_far_1_0/ppermute | solution.py:94
  6.9 2.7 %collective-permute-done.refs_2_ = bf16[264,640]{1,0:T(8,128)(2,1)S(1)} collective-permute-done((bf16[264,640]{1,0:T(8,128)(2,1)S(1)}, bf16[264,640]{1,0:T(8,128)(2,1)S(1)}, u32[]{:S(2)}, u32[]{:S(2)}) %collective-permute-start) | collective-permute-done | bytes 337952 | tf_op jit(solution)/shard_map/projection_near_1_0/ppermute | solution.py:94
  9.5 2.1 %collective-permute-start.1 = (bf16[264,640]{1,0:T(8,128)(2,1)S(1)}, bf16[264,640]{1,0:T(8,128)(2,1)S(1)}, u32[]{:S(2)}, u32[]{:S(2)}) collective-permute-start(bf16[264,640]{1,0:T(8,128)(2,1)S(1)} %collective-permute-done.refs_2_), channel_id=1, source_target_pairs={{0,8},{10,2},{8,16},{18,10},{16,24},{26,18},{24,28},{30,26},{28,20... | collective-permute-start | bytes 1013768 | tf_op jit(solution)/shard_map/projection_near_2_0/ppermute | solution.py:94
  11.6 1.5 %collective-permute-done.5.refs_0_ = bf16[264,640]{1,0:T(8,128)(2,1)S(1)} collective-permute-done((bf16[264,640]{1,0:T(8,128)(2,1)S(1)}, bf16[264,640]{1,0:T(8,128)(2,1)S(1)}, u32[]{:S(2)}, u32[]{:S(2)}) %collective-permute-start.5) | collective-permute-done | bytes 337952 | tf_op jit(solution)/shard_map/projection_far_1_0/ppermute | solution.py:94
  13.2 2.1 %collective-permute-start.6 = (bf16[264,640]{1,0:T(8,128)(2,1)S(1)}, bf16[264,640]{1,0:T(8,128)(2,1)S(1)}, u32[]{:S(2)}, u32[]{:S(2)}) collective-permute-start(bf16[264,640]{1,0:T(8,128)(2,1)S(1)} %collective-permute-done.5.refs_0_), channel_id=1, source_target_pairs={{0,8},{10,2},{8,16},{18,10},{16,24},{26,18},{24,28},{30,26},{28,20... | collective-permute-start | bytes 1013768 | tf_op jit(solution)/shard_map/projection_far_2_0/ppermute | solution.py:94
  15.2 1.4 %projection_1.1 = (f32[3,256,640]{2,1,0:T(8,128)S(1)}, f32[8,640]{1,0:T(8,128)S(1)}) custom-call(bf16[264,640]{1,0:T(8,128)(2,1)S(1)} %prepare.1.refs_0_, bf16[264,640]{1,0:T(8,128)(2,1)S(1)} %collective-permute-done.4.refs_1_, bf16[264,640]{1,0:T(8,128)(2,1)S(1)} %collective-permute-done.refs_2_, bf16[264,640]{1,0:T(8,128)(2,1)S(1)} %collective-permute-done.9.refs_3_, ...), custom_call_target="tpu_custom_call" | custom-call | tf_op jit(solution)/shard_map/projection_1/pallas_call | solution.py:203
  17.3 2.1 %collective-permute-start.2 = (bf16[264,640]{1,0:T(8,128)(2,1)S(1)}, bf16[264,640]{1,0:T(8,128)(2,1)S(1)}, u32[]{:S(2)}, u32[]{:S(2)}) collective-permute-start(bf16[264,640]{1,0:T(8,128)(2,1)S(1)} %collective-permute-done.1.refs_2_), channel_id=1, source_target_pairs={{0,8},{10,2},{8,16},{18,10},{16,24},{26,18},{24,28},{30,26},{28,20... | collective-permute-start | bytes 1013768 | tf_op jit(solution)/shard_map/projection_near_3_0/ppermute | solution.py:94
  20.4 2.1 %collective-permute-start.13 = (bf16[264,640]{1,0:T(8,128)(2,1)S(1)}, bf16[264,640]{1,0:T(8,128)(2,1)S(1)}, u32[]{:S(2)}, u32[]{:S(2)}) collective-permute-start(bf16[264,640]{1,0:T(8,128)(2,1)S(1)} %collective-permute-done.6.refs_0_), channel_id=1, source_target_pairs={{0,8},{10,2},{8,16},{18,10},{16,24},{26,18},{24,28},{30,26},{28,20... | collective-permute-start | bytes 1013768 | tf_op jit(solution)/shard_map/projection_far_3_0/ppermute | solution.py:94
  22.5 1.6 %projection_2.1 = (f32[3,256,640]{2,1,0:T(8,128)S(1)}, f32[8,640]{1,0:T(8,128)S(1)}) custom-call(bf16[264,640]{1,0:T(8,128)(2,1)S(1)} %collective-permute-done.5.refs_0_, bf16[264,640]{1,0:T(8,128)(2,1)S(1)} %collective-permute-done.8.refs_1_, bf16[264,640]{1,0:T(8,128)(2,1)S(1)} %collective-permute-done.1.refs_2_, ...), custom_call_target="tpu_custom_call", output_to_operand_aliasing={{0}: (5, {}), {1}: (6, {})} | custom-call | tf_op jit(solution)/shard_map/projection_2/pallas_call | solution.py:203
  25.0 2.1 %collective-permute-start.3 = (bf16[264,640]{1,0:T(8,128)(2,1)S(1)}, bf16[264,640]{1,0:T(8,128)(2,1)S(1)}, u32[]{:S(2)}, u32[]{:S(2)}) collective-permute-start(bf16[264,640]{1,0:T(8,128)(2,1)S(1)} %collective-permute-done.2.refs_2_), channel_id=1, source_target_pairs={{0,8},{10,2},{8,16},{18,10},{16,24},{26,18},{24,28},{30,26},{28,20... | collective-permute-start | bytes 1013768 | tf_op jit(solution)/shard_map/projection_near_4_0/ppermute | solution.py:94
  28.1 1.6 %projection_3.1 = (f32[3,256,640]{2,1,0:T(8,128)S(1)}, f32[8,640]{1,0:T(8,128)S(1)}) custom-call(bf16[264,640]{1,0:T(8,128)(2,1)S(1)} %collective-permute-done.6.refs_0_, bf16[264,640]{1,0:T(8,128)(2,1)S(1)} %collective-permute-done.7.refs_1_, bf16[264,640]{1,0:T(8,128)(2,1)S(1)} %collective-permute-done.2.refs_2_, ...), custom_call_target="tpu_custom_call", output_to_operand_aliasing={{0}: (5, {}), {1}: (6, {})} | custom-call | tf_op jit(solution)/shard_map/projection_3/pallas_call | solution.py:203
  29.7 2.5 %collective-permute-done.3.refs_2_ = bf16[264,640]{1,0:T(8,128)(2,1)S(1)} collective-permute-done((bf16[264,640]{1,0:T(8,128)(2,1)S(1)}, bf16[264,640]{1,0:T(8,128)(2,1)S(1)}, u32[]{:S(2)}, u32[]{:S(2)}) %collective-permute-start.3) | collective-permute-done | bytes 337952 | tf_op jit(solution)/shard_map/projection_near_4_0/ppermute | solution.py:94
  32.2 1.2 %projection_4.1 = (f32[3,256,640]{2,1,0:T(8,128)S(1)}, f32[8,640]{1,0:T(8,128)S(1)}) custom-call(bf16[264,640]{1,0:T(8,128)(2,1)S(1)} %collective-permute-done.13.refs_0_, bf16[264,640]{1,0:T(8,128)(2,1)S(1)} %collective-permute-done.14.refs_1_, bf16[264,640]{1,0:T(8,128)(2,1)S(1)} %collective-permute-done.3.refs_2_, ...), custom_call_target="tpu_custom_call", output_to_operand_aliasing={{0}: (4, {}), {1}: (5, {})} | custom-call | flops 2000000000 | tf_op jit(solution)/shard_map/projection_4/pallas_call | solution.py:203
  34.5 1.3 %collective-permute-start.15 = (bf16[136,640]{1,0:T(8,128)(2,1)S(1)}, bf16[136,640]{1,0:T(8,128)(2,1)S(1)}, u32[]{:S(2)}, u32[]{:S(2)}) collective-permute-start(bf16[136,640]{1,0:T(8,128)(2,1)S(1)} %projection_last.4), channel_id=1, source_target_pairs={{0,1},{1,0},{2,3},{3,2},{4,5},{5,4},{6,7},{7,6},{8,9},{9,8},{10,11... | collective-permute-start | bytes 522248 | tf_op jit(solution)/shard_map/ppermute | solution.py:605
  39.0 2.5 %collective-permute-done.15.refs_0_ = bf16[136,640]{1,0:T(8,128)(2,1)S(1)} collective-permute-done((bf16[136,640]{1,0:T(8,128)(2,1)S(1)}, bf16[136,640]{1,0:T(8,128)(2,1)S(1)}, u32[]{:S(2)}, u32[]{:S(2)}) %collective-permute-start.15) | collective-permute-done | bytes 174112 | tf_op jit(solution)/shard_map/ppermute | solution.py:605
  42.1 2.4 %collective-permute-start.16 = (bf16[128,640]{1,0:T(8,128)(2,1)S(1)}, bf16[128,640]{1,0:T(8,128)(2,1)S(1)}, u32[]{:S(2)}, u32[]{:S(2)}) collective-permute-start(bf16[128,640]{1,0:T(8,128)(2,1)S(1)} %far_part_1_0.1.refs_0_), channel_id=1, source_target_pairs={{0,8},{10,2},{8,16},{18,10},{16,24},{26,18},{24,28},{30,26},{28,20... | collective-permute-start | bytes 491528 | tf_op jit(solution)/shard_map/output_near_1_0/ppermute | solution.py:94
  45.4 2.1 %collective-permute-start.18 = (bf16[128,640]{1,0:T(8,128)(2,1)S(1)}, bf16[128,640]{1,0:T(8,128)(2,1)S(1)}, u32[]{:S(2)}, u32[]{:S(2)}) collective-permute-start(bf16[128,640]{1,0:T(8,128)(2,1)S(1)} %far_part_1_128.1.refs_1_), channel_id=1, source_target_pairs={{0,8},{10,2},{8,16},{18,10},{16,24},{26,18},{24,28},{30,26},{28,20... | collective-permute-start | bytes 491528 | tf_op jit(solution)/shard_map/output_near_1_1/ppermute | solution.py:94
  47.5 1.6 %collective-permute-start.23 = (bf16[128,640]{1,0:T(8,128)(2,1)S(1)}, bf16[128,640]{1,0:T(8,128)(2,1)S(1)}, u32[]{:S(2)}, u32[]{:S(2)}) collective-permute-start(bf16[128,640]{1,0:T(8,128)(2,1)S(1)} %collective-permute-done.22.refs_2_), channel_id=1, source_target_pairs={{0,8},{10,2},{8,16},{18,10},{16,24},{26,18},{24,28},{30,26},{28,20... | collective-permute-start | bytes 491528 | tf_op jit(solution)/shard_map/output_far_1_0/ppermute | solution.py:94
  49.1 1.6 %collective-permute-start.25 = (bf16[128,640]{1,0:T(8,128)(2,1)S(1)}, bf16[128,640]{1,0:T(8,128)(2,1)S(1)}, u32[]{:S(2)}, u32[]{:S(2)}) collective-permute-start(bf16[128,640]{1,0:T(8,128)(2,1)S(1)} %collective-permute-done.24.refs_3_), channel_id=1, source_target_pairs={{0,8},{10,2},{8,16},{18,10},{16,24},{26,18},{24,28},{30,26},{28,20... | collective-permute-start | bytes 491528 | tf_op jit(solution)/shard_map/output_far_1_1/ppermute | solution.py:94
  50.9 2.1 %collective-permute-start.19 = (bf16[256,640]{1,0:T(8,128)(2,1)S(1)}, bf16[256,640]{1,0:T(8,128)(2,1)S(1)}, u32[]{:S(2)}, u32[]{:S(2)}) collective-permute-start(bf16[256,640]{1,0:T(8,128)(2,1)S(1)} %constant_dynamic-update-slice_fusion.refs_4_), channel_id=1, source_target_pairs={{0,8},{10,2},{8,16},{18,10},{16,24},{26,18},{24,28},{30,26},{28,20... | collective-permute-start | bytes 983048 | tf_op jit(solution)/shard_map/output_near_2_0/ppermute | solution.py:94
  53.0 1.6 %collective-permute-done.25 = bf16[128,640]{1,0:T(8,128)(2,1)S(1)} collective-permute-done((bf16[128,640]{1,0:T(8,128)(2,1)S(1)}, bf16[128,640]{1,0:T(8,128)(2,1)S(1)}, u32[]{:S(2)}, u32[]{:S(2)}) %collective-permute-start.25) | collective-permute-done | bytes 163872 | tf_op jit(solution)/shard_map/output_far_1_1/ppermute | solution.py:94
  54.6 1.8 %collective-permute-start.26 = (bf16[256,640]{1,0:T(8,128)(2,1)S(1)}, bf16[256,640]{1,0:T(8,128)(2,1)S(1)}, u32[]{:S(2)}, u32[]{:S(2)}) collective-permute-start(bf16[256,640]{1,0:T(8,128)(2,1)S(1)} %constant_dynamic-update-slice_fusion.2.refs_0_), channel_id=1, source_target_pairs={{0,8},{10,2},{8,16},{18,10},{16,24},{26,18},{24,28},{30,26},{28,20... | collective-permute-start | bytes 983048 | tf_op jit(solution)/shard_map/output_far_2_0/ppermute | solution.py:94
  57.0 1.1 %collective-permute-done.19.refs_2_ = bf16[256,640]{1,0:T(8,128)(2,1)S(1)} collective-permute-done((bf16[256,640]{1,0:T(8,128)(2,1)S(1)}, bf16[256,640]{1,0:T(8,128)(2,1)S(1)}, u32[]{:S(2)}, u32[]{:S(2)}) %collective-permute-start.19) | collective-permute-done | bytes 327712 | tf_op jit(solution)/shard_map/output_near_2_0/ppermute | solution.py:94
  58.1 2.0 %collective-permute-start.20 = (bf16[256,640]{1,0:T(8,128)(2,1)S(1)}, bf16[256,640]{1,0:T(8,128)(2,1)S(1)}, u32[]{:S(2)}, u32[]{:S(2)}) collective-permute-start(bf16[256,640]{1,0:T(8,128)(2,1)S(1)} %collective-permute-done.19.refs_2_), channel_id=1, source_target_pairs={{0,8},{10,2},{8,16},{18,10},{16,24},{26,18},{24,28},{30,26},{28,20... | collective-permute-start | bytes 983048 | tf_op jit(solution)/shard_map/output_near_3_0/ppermute | solution.py:94
  60.1 1.7 %collective-permute-done.26.refs_0_ = bf16[256,640]{1,0:T(8,128)(2,1)S(1)} collective-permute-done((bf16[256,640]{1,0:T(8,128)(2,1)S(1)}, bf16[256,640]{1,0:T(8,128)(2,1)S(1)}, u32[]{:S(2)}, u32[]{:S(2)}) %collective-permute-start.26) | collective-permute-done | bytes 327712 | tf_op jit(solution)/shard_map/output_far_2_0/ppermute | solution.py:94
  61.7 1.8 %collective-permute-start.33 = (bf16[256,640]{1,0:T(8,128)(2,1)S(1)}, bf16[256,640]{1,0:T(8,128)(2,1)S(1)}, u32[]{:S(2)}, u32[]{:S(2)}) collective-permute-start(bf16[256,640]{1,0:T(8,128)(2,1)S(1)} %collective-permute-done.26.refs_0_), channel_id=1, source_target_pairs={{0,8},{10,2},{8,16},{18,10},{16,24},{26,18},{24,28},{30,26},{28,20... | collective-permute-start | bytes 983048 | tf_op jit(solution)/shard_map/output_far_3_0/ppermute | solution.py:94
  64.2 1.0 %collective-permute-done.20.refs_2_ = bf16[256,640]{1,0:T(8,128)(2,1)S(1)} collective-permute-done((bf16[256,640]{1,0:T(8,128)(2,1)S(1)}, bf16[256,640]{1,0:T(8,128)(2,1)S(1)}, u32[]{:S(2)}, u32[]{:S(2)}) %collective-permute-start.20) | collective-permute-done | bytes 327712 | tf_op jit(solution)/shard_map/output_near_3_0/ppermute | solution.py:94
  65.2 1.9 %collective-permute-start.21 = (bf16[256,640]{1,0:T(8,128)(2,1)S(1)}, bf16[256,640]{1,0:T(8,128)(2,1)S(1)}, u32[]{:S(2)}, u32[]{:S(2)}) collective-permute-start(bf16[256,640]{1,0:T(8,128)(2,1)S(1)} %collective-permute-done.20.refs_2_), channel_id=1, source_target_pairs={{0,8},{10,2},{8,16},{18,10},{16,24},{26,18},{24,28},{30,26},{28,20... | collective-permute-start | bytes 983048 | tf_op jit(solution)/shard_map/output_near_4_0/ppermute | solution.py:94
  67.1 1.7 %collective-permute-done.33.refs_0_ = bf16[256,640]{1,0:T(8,128)(2,1)S(1)} collective-permute-done((bf16[256,640]{1,0:T(8,128)(2,1)S(1)}, bf16[256,640]{1,0:T(8,128)(2,1)S(1)}, u32[]{:S(2)}, u32[]{:S(2)}) %collective-permute-start.33) | collective-permute-done | bytes 327712 | tf_op jit(solution)/shard_map/output_far_3_0/ppermute | solution.py:94
  69.4 2.9 %collective-permute-done.21.refs_2_ = bf16[256,640]{1,0:T(8,128)(2,1)S(1)} collective-permute-done((bf16[256,640]{1,0:T(8,128)(2,1)S(1)}, bf16[256,640]{1,0:T(8,128)(2,1)S(1)}, u32[]{:S(2)}, u32[]{:S(2)}) %collective-permute-start.21) | collective-permute-done | bytes 327712 | tf_op jit(solution)/shard_map/output_near_4_0/ppermute | solution.py:94
  72.8 1.1 %collective-permute-done.32.refs_0_ = bf16[256,640]{1,0:T(8,128)(2,1)S(1)} collective-permute-done((bf16[256,640]{1,0:T(8,128)(2,1)S(1)}, bf16[256,640]{1,0:T(8,128)(2,1)S(1)}, u32[]{:S(2)}, u32[]{:S(2)}) %collective-permute-start.32) | collective-permute-done | bytes 327712 | tf_op jit(solution)/shard_map/output_core_near_4_0/ppermute | solution.py:98
  (84 shorter events, 15.4 us)
Async XLA Ops:
  1.8 7.7 %collective-permute-start = (bf16[264,640]{1,0:T(8,128)(2,1)S(1)}, bf16[264,640]{1,0:T(8,128)(2,1)S(1)}, u32[]{:S(2)}, u32[]{:S(2)}) collective-permute-start(bf16[264,640]{1,0:T(8,128)(2,1)S(1)} %prepare.1.refs_0_), channel_id=1, source_target_pairs={{0,8},{10,2},{8,16},{18,10},{16,24},{26,18},{24,28},{30,26},{28,20... | collective-permute-start | bytes 1013768 | tf_op jit(solution)/shard_map/projection_near_1_0/ppermute | solution.py:94
  4.4 8.7 %collective-permute-start.5 = (bf16[264,640]{1,0:T(8,128)(2,1)S(1)}, bf16[264,640]{1,0:T(8,128)(2,1)S(1)}, u32[]{:S(2)}, u32[]{:S(2)}) collective-permute-start(bf16[264,640]{1,0:T(8,128)(2,1)S(1)} %collective-permute-done.4.refs_1_), channel_id=1, source_target_pairs={{0,8},{10,2},{8,16},{18,10},{16,24},{26,18},{24,28},{30,26},{28,20... | collective-permute-start | bytes 1013768 | tf_op jit(solution)/shard_map/projection_far_1_0/ppermute | solution.py:94
  9.5 5.7 %collective-permute-start.9 = (bf16[264,640]{1,0:T(8,128)(2,1)S(1)}, bf16[264,640]{1,0:T(8,128)(2,1)S(1)}, u32[]{:S(2)}, u32[]{:S(2)}) collective-permute-start(bf16[264,640]{1,0:T(8,128)(2,1)S(1)} %collective-permute-done.refs_2_), channel_id=1, source_target_pairs={{0,2},{2,0},{4,6},{6,4},{8,10},{10,8},{12,14},{14,12},{16,18},{18,... | collective-permute-start | bytes 1013768 | tf_op jit(solution)/shard_map/projection_core_near_1_0/ppermute | solution.py:98
  9.5 7.2 %collective-permute-start.1 = (bf16[264,640]{1,0:T(8,128)(2,1)S(1)}, bf16[264,640]{1,0:T(8,128)(2,1)S(1)}, u32[]{:S(2)}, u32[]{:S(2)}) collective-permute-start(bf16[264,640]{1,0:T(8,128)(2,1)S(1)} %collective-permute-done.refs_2_), channel_id=1, source_target_pairs={{0,8},{10,2},{8,16},{18,10},{16,24},{26,18},{24,28},{30,26},{28,20... | collective-permute-start | bytes 1013768 | tf_op jit(solution)/shard_map/projection_near_2_0/ppermute | solution.py:94
  13.2 7.2 %collective-permute-start.6 = (bf16[264,640]{1,0:T(8,128)(2,1)S(1)}, bf16[264,640]{1,0:T(8,128)(2,1)S(1)}, u32[]{:S(2)}, u32[]{:S(2)}) collective-permute-start(bf16[264,640]{1,0:T(8,128)(2,1)S(1)} %collective-permute-done.5.refs_0_), channel_id=1, source_target_pairs={{0,8},{10,2},{8,16},{18,10},{16,24},{26,18},{24,28},{30,26},{28,20... | collective-permute-start | bytes 1013768 | tf_op jit(solution)/shard_map/projection_far_2_0/ppermute | solution.py:94
  16.8 5.7 %collective-permute-start.10 = (bf16[264,640]{1,0:T(8,128)(2,1)S(1)}, bf16[264,640]{1,0:T(8,128)(2,1)S(1)}, u32[]{:S(2)}, u32[]{:S(2)}) collective-permute-start(bf16[264,640]{1,0:T(8,128)(2,1)S(1)} %collective-permute-done.1.refs_2_), channel_id=1, source_target_pairs={{0,2},{2,0},{4,6},{6,4},{8,10},{10,8},{12,14},{14,12},{16,18},{18,... | collective-permute-start | bytes 1013768 | tf_op jit(solution)/shard_map/projection_core_near_2_0/ppermute | solution.py:98
  16.8 5.7 %collective-permute-start.8 = (bf16[264,640]{1,0:T(8,128)(2,1)S(1)}, bf16[264,640]{1,0:T(8,128)(2,1)S(1)}, u32[]{:S(2)}, u32[]{:S(2)}) collective-permute-start(bf16[264,640]{1,0:T(8,128)(2,1)S(1)} %collective-permute-done.5.refs_0_), channel_id=1, source_target_pairs={{0,2},{2,0},{4,6},{6,4},{8,10},{10,8},{12,14},{14,12},{16,18},{18,... | collective-permute-start | bytes 1013768 | tf_op jit(solution)/shard_map/projection_core_far_1_0/ppermute | solution.py:98
  17.3 7.2 %collective-permute-start.2 = (bf16[264,640]{1,0:T(8,128)(2,1)S(1)}, bf16[264,640]{1,0:T(8,128)(2,1)S(1)}, u32[]{:S(2)}, u32[]{:S(2)}) collective-permute-start(bf16[264,640]{1,0:T(8,128)(2,1)S(1)} %collective-permute-done.1.refs_2_), channel_id=1, source_target_pairs={{0,8},{10,2},{8,16},{18,10},{16,24},{26,18},{24,28},{30,26},{28,20... | collective-permute-start | bytes 1013768 | tf_op jit(solution)/shard_map/projection_near_3_0/ppermute | solution.py:94
  20.4 7.7 %collective-permute-start.13 = (bf16[264,640]{1,0:T(8,128)(2,1)S(1)}, bf16[264,640]{1,0:T(8,128)(2,1)S(1)}, u32[]{:S(2)}, u32[]{:S(2)}) collective-permute-start(bf16[264,640]{1,0:T(8,128)(2,1)S(1)} %collective-permute-done.6.refs_0_), channel_id=1, source_target_pairs={{0,8},{10,2},{8,16},{18,10},{16,24},{26,18},{24,28},{30,26},{28,20... | collective-permute-start | bytes 1013768 | tf_op jit(solution)/shard_map/projection_far_3_0/ppermute | solution.py:94
  24.5 3.6 %collective-permute-start.11 = (bf16[264,640]{1,0:T(8,128)(2,1)S(1)}, bf16[264,640]{1,0:T(8,128)(2,1)S(1)}, u32[]{:S(2)}, u32[]{:S(2)}) collective-permute-start(bf16[264,640]{1,0:T(8,128)(2,1)S(1)} %collective-permute-done.2.refs_2_), channel_id=1, source_target_pairs={{0,2},{2,0},{4,6},{6,4},{8,10},{10,8},{12,14},{14,12},{16,18},{18,... | collective-permute-start | bytes 1013768 | tf_op jit(solution)/shard_map/projection_core_near_3_0/ppermute | solution.py:98
  24.5 3.6 %collective-permute-start.7 = (bf16[264,640]{1,0:T(8,128)(2,1)S(1)}, bf16[264,640]{1,0:T(8,128)(2,1)S(1)}, u32[]{:S(2)}, u32[]{:S(2)}) collective-permute-start(bf16[264,640]{1,0:T(8,128)(2,1)S(1)} %collective-permute-done.6.refs_0_), channel_id=1, source_target_pairs={{0,2},{2,0},{4,6},{6,4},{8,10},{10,8},{12,14},{14,12},{16,18},{18,... | collective-permute-start | bytes 1013768 | tf_op jit(solution)/shard_map/projection_core_far_2_0/ppermute | solution.py:98
  25.0 7.2 %collective-permute-start.3 = (bf16[264,640]{1,0:T(8,128)(2,1)S(1)}, bf16[264,640]{1,0:T(8,128)(2,1)S(1)}, u32[]{:S(2)}, u32[]{:S(2)}) collective-permute-start(bf16[264,640]{1,0:T(8,128)(2,1)S(1)} %collective-permute-done.2.refs_2_), channel_id=1, source_target_pairs={{0,8},{10,2},{8,16},{18,10},{16,24},{26,18},{24,28},{30,26},{28,20... | collective-permute-start | bytes 1013768 | tf_op jit(solution)/shard_map/projection_near_4_0/ppermute | solution.py:94
  28.1 4.1 %collective-permute-start.14 = (bf16[264,640]{1,0:T(8,128)(2,1)S(1)}, bf16[264,640]{1,0:T(8,128)(2,1)S(1)}, u32[]{:S(2)}, u32[]{:S(2)}) collective-permute-start(bf16[264,640]{1,0:T(8,128)(2,1)S(1)} %collective-permute-done.13.refs_0_), channel_id=1, source_target_pairs={{0,2},{2,0},{4,6},{6,4},{8,10},{10,8},{12,14},{14,12},{16,18},{18,... | collective-permute-start | bytes 1013768 | tf_op jit(solution)/shard_map/projection_core_far_3_0/ppermute | solution.py:98
  34.5 7.0 %collective-permute-start.15 = (bf16[136,640]{1,0:T(8,128)(2,1)S(1)}, bf16[136,640]{1,0:T(8,128)(2,1)S(1)}, u32[]{:S(2)}, u32[]{:S(2)}) collective-permute-start(bf16[136,640]{1,0:T(8,128)(2,1)S(1)} %projection_last.4), channel_id=1, source_target_pairs={{0,1},{1,0},{2,3},{3,2},{4,5},{5,4},{6,7},{7,6},{8,9},{9,8},{10,11... | collective-permute-start | bytes 522248 | tf_op jit(solution)/shard_map/ppermute | solution.py:605
  37.9 6.9 %collective-permute-start.17 = (bf16[136,640]{1,0:T(8,128)(2,1)S(1)}, bf16[136,640]{1,0:T(8,128)(2,1)S(1)}, u32[]{:S(2)}, u32[]{:S(2)}) collective-permute-start(bf16[136,640]{1,0:T(8,128)(2,1)S(1)} %projection_last.7), channel_id=1, source_target_pairs={{0,1},{1,0},{2,3},{3,2},{4,5},{5,4},{6,7},{7,6},{8,9},{9,8},{10,11... | collective-permute-start | bytes 522248 | tf_op jit(solution)/shard_map/ppermute | solution.py:605
  42.1 5.4 %collective-permute-start.22 = (bf16[128,640]{1,0:T(8,128)(2,1)S(1)}, bf16[128,640]{1,0:T(8,128)(2,1)S(1)}, u32[]{:S(2)}, u32[]{:S(2)}) collective-permute-start(bf16[128,640]{1,0:T(8,128)(2,1)S(1)} %far_part_1_0.1.refs_0_), channel_id=1, source_target_pairs={{0,2},{2,0},{4,6},{6,4},{8,10},{10,8},{12,14},{14,12},{16,18},{18,... | collective-permute-start | bytes 491528 | tf_op jit(solution)/shard_map/output_core_own_0/ppermute | solution.py:98
  42.1 6.9 %collective-permute-start.16 = (bf16[128,640]{1,0:T(8,128)(2,1)S(1)}, bf16[128,640]{1,0:T(8,128)(2,1)S(1)}, u32[]{:S(2)}, u32[]{:S(2)}) collective-permute-start(bf16[128,640]{1,0:T(8,128)(2,1)S(1)} %far_part_1_0.1.refs_0_), channel_id=1, source_target_pairs={{0,8},{10,2},{8,16},{18,10},{16,24},{26,18},{24,28},{30,26},{28,20... | collective-permute-start | bytes 491528 | tf_op jit(solution)/shard_map/output_near_1_0/ppermute | solution.py:94
  45.3 3.8 %collective-permute-start.24 = (bf16[128,640]{1,0:T(8,128)(2,1)S(1)}, bf16[128,640]{1,0:T(8,128)(2,1)S(1)}, u32[]{:S(2)}, u32[]{:S(2)}) collective-permute-start(bf16[128,640]{1,0:T(8,128)(2,1)S(1)} %far_part_1_128.1.refs_1_), channel_id=1, source_target_pairs={{0,2},{2,0},{4,6},{6,4},{8,10},{10,8},{12,14},{14,12},{16,18},{18,... | collective-permute-start | bytes 491528 | tf_op jit(solution)/shard_map/output_core_own_1/ppermute | solution.py:98
  45.4 5.4 %collective-permute-start.18 = (bf16[128,640]{1,0:T(8,128)(2,1)S(1)}, bf16[128,640]{1,0:T(8,128)(2,1)S(1)}, u32[]{:S(2)}, u32[]{:S(2)}) collective-permute-start(bf16[128,640]{1,0:T(8,128)(2,1)S(1)} %far_part_1_128.1.refs_1_), channel_id=1, source_target_pairs={{0,8},{10,2},{8,16},{18,10},{16,24},{26,18},{24,28},{30,26},{28,20... | collective-permute-start | bytes 491528 | tf_op jit(solution)/shard_map/output_near_1_1/ppermute | solution.py:94
  47.5 5.5 %collective-permute-start.23 = (bf16[128,640]{1,0:T(8,128)(2,1)S(1)}, bf16[128,640]{1,0:T(8,128)(2,1)S(1)}, u32[]{:S(2)}, u32[]{:S(2)}) collective-permute-start(bf16[128,640]{1,0:T(8,128)(2,1)S(1)} %collective-permute-done.22.refs_2_), channel_id=1, source_target_pairs={{0,8},{10,2},{8,16},{18,10},{16,24},{26,18},{24,28},{30,26},{28,20... | collective-permute-start | bytes 491528 | tf_op jit(solution)/shard_map/output_far_1_0/ppermute | solution.py:94
  49.1 5.5 %collective-permute-start.25 = (bf16[128,640]{1,0:T(8,128)(2,1)S(1)}, bf16[128,640]{1,0:T(8,128)(2,1)S(1)}, u32[]{:S(2)}, u32[]{:S(2)}) collective-permute-start(bf16[128,640]{1,0:T(8,128)(2,1)S(1)} %collective-permute-done.24.refs_3_), channel_id=1, source_target_pairs={{0,8},{10,2},{8,16},{18,10},{16,24},{26,18},{24,28},{30,26},{28,20... | collective-permute-start | bytes 491528 | tf_op jit(solution)/shard_map/output_far_1_1/ppermute | solution.py:94
  50.8 5.6 %collective-permute-start.29 = (bf16[256,640]{1,0:T(8,128)(2,1)S(1)}, bf16[256,640]{1,0:T(8,128)(2,1)S(1)}, u32[]{:S(2)}, u32[]{:S(2)}) collective-permute-start(bf16[256,640]{1,0:T(8,128)(2,1)S(1)} %constant_dynamic-update-slice_fusion.refs_4_), channel_id=1, source_target_pairs={{0,2},{2,0},{4,6},{6,4},{8,10},{10,8},{12,14},{14,12},{16,18},{18,... | collective-permute-start | bytes 983048 | tf_op jit(solution)/shard_map/output_core_near_1_0/ppermute | solution.py:98
  50.9 7.2 %collective-permute-start.19 = (bf16[256,640]{1,0:T(8,128)(2,1)S(1)}, bf16[256,640]{1,0:T(8,128)(2,1)S(1)}, u32[]{:S(2)}, u32[]{:S(2)}) collective-permute-start(bf16[256,640]{1,0:T(8,128)(2,1)S(1)} %constant_dynamic-update-slice_fusion.refs_4_), channel_id=1, source_target_pairs={{0,8},{10,2},{8,16},{18,10},{16,24},{26,18},{24,28},{30,26},{28,20... | collective-permute-start | bytes 983048 | tf_op jit(solution)/shard_map/output_near_2_0/ppermute | solution.py:94
  54.6 7.1 %collective-permute-start.26 = (bf16[256,640]{1,0:T(8,128)(2,1)S(1)}, bf16[256,640]{1,0:T(8,128)(2,1)S(1)}, u32[]{:S(2)}, u32[]{:S(2)}) collective-permute-start(bf16[256,640]{1,0:T(8,128)(2,1)S(1)} %constant_dynamic-update-slice_fusion.2.refs_0_), channel_id=1, source_target_pairs={{0,8},{10,2},{8,16},{18,10},{16,24},{26,18},{24,28},{30,26},{28,20... | collective-permute-start | bytes 983048 | tf_op jit(solution)/shard_map/output_far_2_0/ppermute | solution.py:94
  56.4 7.2 %collective-permute-start.28 = (bf16[256,640]{1,0:T(8,128)(2,1)S(1)}, bf16[256,640]{1,0:T(8,128)(2,1)S(1)}, u32[]{:S(2)}, u32[]{:S(2)}) collective-permute-start(bf16[256,640]{1,0:T(8,128)(2,1)S(1)} %constant_dynamic-update-slice_fusion.2.refs_0_), channel_id=1, source_target_pairs={{0,2},{2,0},{4,6},{6,4},{8,10},{10,8},{12,14},{14,12},{16,18},{18,... | collective-permute-start | bytes 983048 | tf_op jit(solution)/shard_map/output_core_far_1_0/ppermute | solution.py:98
  58.1 5.5 %collective-permute-start.30 = (bf16[256,640]{1,0:T(8,128)(2,1)S(1)}, bf16[256,640]{1,0:T(8,128)(2,1)S(1)}, u32[]{:S(2)}, u32[]{:S(2)}) collective-permute-start(bf16[256,640]{1,0:T(8,128)(2,1)S(1)} %collective-permute-done.19.refs_2_), channel_id=1, source_target_pairs={{0,2},{2,0},{4,6},{6,4},{8,10},{10,8},{12,14},{14,12},{16,18},{18,... | collective-permute-start | bytes 983048 | tf_op jit(solution)/shard_map/output_core_near_2_0/ppermute | solution.py:98
  58.1 7.1 %collective-permute-start.20 = (bf16[256,640]{1,0:T(8,128)(2,1)S(1)}, bf16[256,640]{1,0:T(8,128)(2,1)S(1)}, u32[]{:S(2)}, u32[]{:S(2)}) collective-permute-start(bf16[256,640]{1,0:T(8,128)(2,1)S(1)} %collective-permute-done.19.refs_2_), channel_id=1, source_target_pairs={{0,8},{10,2},{8,16},{18,10},{16,24},{26,18},{24,28},{30,26},{28,20... | collective-permute-start | bytes 983048 | tf_op jit(solution)/shard_map/output_near_3_0/ppermute | solution.py:94
  61.7 7.1 %collective-permute-start.33 = (bf16[256,640]{1,0:T(8,128)(2,1)S(1)}, bf16[256,640]{1,0:T(8,128)(2,1)S(1)}, u32[]{:S(2)}, u32[]{:S(2)}) collective-permute-start(bf16[256,640]{1,0:T(8,128)(2,1)S(1)} %collective-permute-done.26.refs_0_), channel_id=1, source_target_pairs={{0,8},{10,2},{8,16},{18,10},{16,24},{26,18},{24,28},{30,26},{28,20... | collective-permute-start | bytes 983048 | tf_op jit(solution)/shard_map/output_far_3_0/ppermute | solution.py:94
  63.6 5.3 %collective-permute-start.27 = (bf16[256,640]{1,0:T(8,128)(2,1)S(1)}, bf16[256,640]{1,0:T(8,128)(2,1)S(1)}, u32[]{:S(2)}, u32[]{:S(2)}) collective-permute-start(bf16[256,640]{1,0:T(8,128)(2,1)S(1)} %collective-permute-done.26.refs_0_), channel_id=1, source_target_pairs={{0,2},{2,0},{4,6},{6,4},{8,10},{10,8},{12,14},{14,12},{16,18},{18,... | collective-permute-start | bytes 983048 | tf_op jit(solution)/shard_map/output_core_far_2_0/ppermute | solution.py:98
  65.2 3.6 %collective-permute-start.31 = (bf16[256,640]{1,0:T(8,128)(2,1)S(1)}, bf16[256,640]{1,0:T(8,128)(2,1)S(1)}, u32[]{:S(2)}, u32[]{:S(2)}) collective-permute-start(bf16[256,640]{1,0:T(8,128)(2,1)S(1)} %collective-permute-done.20.refs_2_), channel_id=1, source_target_pairs={{0,2},{2,0},{4,6},{6,4},{8,10},{10,8},{12,14},{14,12},{16,18},{18,... | collective-permute-start | bytes 983048 | tf_op jit(solution)/shard_map/output_core_near_3_0/ppermute | solution.py:98
  65.2 7.1 %collective-permute-start.21 = (bf16[256,640]{1,0:T(8,128)(2,1)S(1)}, bf16[256,640]{1,0:T(8,128)(2,1)S(1)}, u32[]{:S(2)}, u32[]{:S(2)}) collective-permute-start(bf16[256,640]{1,0:T(8,128)(2,1)S(1)} %collective-permute-done.20.refs_2_), channel_id=1, source_target_pairs={{0,8},{10,2},{8,16},{18,10},{16,24},{26,18},{24,28},{30,26},{28,20... | collective-permute-start | bytes 983048 | tf_op jit(solution)/shard_map/output_near_4_0/ppermute | solution.py:94
  68.8 3.5 %collective-permute-start.34 = (bf16[256,640]{1,0:T(8,128)(2,1)S(1)}, bf16[256,640]{1,0:T(8,128)(2,1)S(1)}, u32[]{:S(2)}, u32[]{:S(2)}) collective-permute-start(bf16[256,640]{1,0:T(8,128)(2,1)S(1)} %collective-permute-done.33.refs_0_), channel_id=1, source_target_pairs={{0,2},{2,0},{4,6},{6,4},{8,10},{10,8},{12,14},{14,12},{16,18},{18,... | collective-permute-start | bytes 983048 | tf_op jit(solution)/shard_map/output_core_far_3_0/ppermute | solution.py:98
  (14 other events, 67.5 us)

commit v9 on v8

--- a/solution.py
+++ b/solution.py
@@ -167,7 +167,7 @@
                 parts = sides + ([] if first_group else [state_refs[1][...]])
                 side_sum = sum(parts[1:], parts[0])
 
-            def total(stream, lanes=slice(None)):
+            def total(stream, lanes=slice(None), out_here=out_here):
                 left = []
                 for steps, other, _ in items:
                     block = chip_of[steps]
@@ -213,6 +213,25 @@
     )(*shards, weight, *state, *extras)
 
 
+def pass_on(near, far):
+    rows = near.shape[0] - side_rows
+
+    def kernel(near_ref, far_ref, out_ref):
+        out_ref[:rows] = near_ref[:rows]
+        below = pltpu.roll(far_ref[rows:].astype(f32), 2, 0)
+        out_ref[rows:] = (near_ref[rows:].astype(f32) + below).astype(bf16)
+
+    return pl.pallas_call(
+        kernel,
+        in_specs=[in_vmem, in_vmem],
+        out_specs=in_vmem,
+        out_shape=shape_of(near.shape, bf16),
+        compiler_params=params,
+        cost_estimate=estimate(0, 0),
+        name="pass_on",
+    )(near, far)
+
+
 def gather_products(own, weight, beside, side, name):
     chips = chip_count()
     last_step = chips // 2
@@ -229,6 +248,9 @@
 
     near, far = own, send(other_core, own, "core_own")
     items = [(0, 0, near), (0, 1, far)]
+    sibling = far
+    if side:
+        far = [far[0][: far[0].shape[0] - side_rows]]
     running = None
     for step in range(1, last_step + 1):
         near = joined(send(along_ring, near, f"near_{step}"))
@@ -241,6 +263,8 @@
         pair = [(step, 0, arrived), (chips - step, 1, theirs)]
         if step < last_step:
             running = products(items + pair, weight, running, side, None, 0, f"{name}_{step}")
+            if side and step == 1:
+                near = [pass_on(near[0], sibling[0])]
             far = joined(send(along_ring, far, f"far_{step}"))
             theirs = send(other_core, far, f"core_far_{step}")
             items = [(step, 1, far), (chips - step, 0, theirs)]
@@ -305,19 +329,21 @@
         (taps_ref,), (message_ref,) = extra_refs, outs
         factor = norm_factor(side_sum, features)
         projected = [(total(stream) * factor).astype(bf16) for stream in (1, 2)]
-        ends = [(total(0, last) * factor[:, last]).astype(bf16)]
-        ends += [wide[:, last] for wide in projected]
-        lines = [end.astype(f32).T[block_len - count + 1 :] for end in ends]
-        lines.append(jnp.zeros((side_rows - streams * (count - 1), rows), f32))
 
         def write(here, key, value):
             message_ref[here] = (key * value).astype(bf16)
 
         gate(projected, taps_ref, begin, write)
-        message_ref[rows:] = jnp.zeros((side_rows, tokens), bf16)
-        message_ref[rows:, :rows] = jnp.concatenate(lines, axis=0).astype(bf16)
-
-    out_shape = [shape_of((rows + side_rows, tokens), bf16)]
+        if part == 0:
+            lines = []
+            for stream in range(streams):
+                end = (total(stream, last, slice(0, channels)) * factor[:, last]).astype(bf16)
+                lines.append(end.astype(f32).T[block_len - count + 1 :])
+            lines.append(jnp.zeros((side_rows - streams * (count - 1), channels), f32))
+            message_ref[rows:] = jnp.zeros((side_rows, tokens), bf16)
+            message_ref[rows:, :channels] = jnp.concatenate(lines, axis=0).astype(bf16)
+
+    out_shape = [shape_of((rows + (side_rows if part == 0 else 0), tokens), bf16)]
     return body, [w_short], out_shape, parts[part], True
 
 
@@ -348,15 +374,15 @@
     return body, [w_short], out_shape, parts[part], False
 
 
-def halo_columns(message_ref, streams, count, inside):
-    rows = message_ref.shape[0] - side_rows
-    side = jnp.where(inside, message_ref[rows:, :rows].astype(f32), 0.0).T
+def halo_columns(message_ref, streams, count, channels, inside):
+    side = message_ref[message_ref.shape[0] - side_rows :, :channels].astype(f32)
+    side = jnp.where(inside, side, 0.0).T
     return [side[:, s * (count - 1) : (s + 1) * (count - 1)] for s in range(streams)]
 
 
-def halo_edges(message_ref, taps):
+def halo_edges(message_ref, taps, begin):
     streams, count, rows = taps.shape
-    side = message_ref[rows:, :rows].astype(f32)
+    side = message_ref[message_ref.shape[0] - side_rows :, begin : begin + rows].astype(f32)
     lines = []
     for s in range(streams):
         for token in range(count - 1):
@@ -479,10 +505,10 @@
         gated_refs = take(number) if moved else None
         (spec_ref,) = refs
         columns = [tap_columns(taps_ref[s]) for s in range(streams)]
+        if moved:
+            inside = lax.axis_index("ctx") > 0
+            halo = halo_columns(message_refs[0], streams, count, taps_ref.shape[2], inside)
         for part, (begin, rows) in enumerate(parts):
-            if moved:
-                inside = lax.axis_index("ctx") > 0
-                halo = halo_columns(message_refs[part], streams, count, inside)
             tile = math.gcd(rows, 64)
             for start in range(0, rows, tile):
                 here = slice(start, start + tile)
@@ -490,7 +516,7 @@
                 projected_ref = projected_refs[part]
 
                 def smoothed(s):
-                    edge = halo[s][here] if moved else None
+                    edge = halo[s][there] if moved else None
                     wide = projected_ref[s, here].astype(f32)
                     return smooth(wide, columns[s][there], count, edge)
 
@@ -531,7 +557,7 @@
         refs = list(refs)
         take = lambda n: take_from(refs, n)
         moved_ref, total_ref, filters_ref, table_ref = take(4)
-        own_refs = take(2) if own else None
+        own_refs = take(3) if own else None
         spec_ref = refs.pop()
         sum_ref = refs.pop()
         if last:
@@ -548,10 +574,10 @@
                     for ref in (query_ref, gated_ref)
                 )
             if own:
-                first_ref, taps_ref = own_refs
+                first_ref, taps_ref, halo_ref = own_refs
                 key, value = first_ref[0], first_ref[1]
                 if inside:
-                    edges = halo_edges(moved_ref, taps_ref[:, :, channels_here])
+                    edges = halo_edges(halo_ref, taps_ref[:, :, channels_here], begin)
                     query[0] = query[0] + edges[0]
                     key, value = key + edges[1], value + edges[2]
                 gated[0] = (key * value).astype(bf16)
@@ -646,7 +672,7 @@
             if turn == turns - 1:
                 last = (inverse, query[k], gated[k], skip_gain)
                 if not exact:
-                    own_block = (first_blocks[k], w_short)
+                    own_block = (first_blocks[k], w_short, moving[0])
             done = far_part(
                 turn, begin, moving[k], totals[k], filters, forward, last, own_block
             )

time: 75.1 us -> 74 us (0.985)
  starting transfers between devices: 35.2 us -> 34.1 us
  transfers between devices with their start and end apart: 35 -> 35, of which waited for: 17 -> 18; matrix products, arithmetic and copies ran while one was open for 0% -> 0% of each run, Pallas kernels for 17% -> 18%
where the time goes in v9:
time: 74 us; the launch traced here: 73.8 us
  starting transfers between devices  34.1 us (46%)
  waiting for transfers between devices  23.4 us (32%)
  Pallas kernels  14.9 us (20%)
  local copies, waits for them, and re-layouts  1.13 us (2%)
    ppermute x16, starting transfers between devices, along_ring(): return lax.ppermute(block, 'fsdp', pairs)  31.3 us
    ppermute x16, waiting for transfers between devices, along_ring(): return lax.ppermute(block, 'fsdp', pairs)  18.8 us
    pallas_call x13, Pallas kernels, products(): pl.pallas_call(kernel, in_specs=[in_vmem] * (count + 1 + len(state) + len...  11.8 us
    ppermute x2, waiting for transfers between devices, from_before(): lax.ppermute(block, 'ctx', [(i, (i + 1) % count) for i in range(count)])  2.89 us
    ppermute x17, waiting for transfers between devices, other_core(): lax.ppermute(block, 'fsdp', [(i, i ^ 1) for i in range(2 * chip_count())])  1.77 us
    ppermute x2, starting transfers between devices, from_before(): lax.ppermute(block, 'ctx', [(i, (i + 1) % count) for i in range(count)])  1.55 us
  transfers between devices with their start and end apart: 35, of which 18 were waited for; matrix products, arithmetic and copies ran while one was open for 0% of the time, Pallas kernels for 18%

profile of v9, /device:TPU:0, one launch (start us, length us, event | category | flops | bytes accessed | tf_op | source)
XLA Modules:
  0.0 73.8 jit_solution(8989929565052856478)
XLA Ops:
  1.8 2.6 %collective-permute-start = (bf16[264,640]{1,0:T(8,128)(2,1)S(1)}, bf16[264,640]{1,0:T(8,128)(2,1)S(1)}, u32[]{:S(2)}, u32[]{:S(2)}) collective-permute-start(bf16[264,640]{1,0:T(8,128)(2,1)S(1)} %prepare.1.refs_0_), channel_id=1, source_target_pairs={{0,8},{10,2},{8,16},{18,10},{16,24},{26,18},{24,28},{30,26},{28,20... | collective-permute-start | bytes 1013768 | tf_op jit(solution)/shard_map/projection_near_1_0/ppermute | solution.py:94
  4.5 1.6 %collective-permute-start.5 = (bf16[256,640]{1,0:T(8,128)(2,1)S(1)}, bf16[256,640]{1,0:T(8,128)(2,1)S(1)}, u32[]{:S(2)}, u32[]{:S(2)}) collective-permute-start(bf16[256,640]{1,0:T(8,128)(2,1)S(1)} %slice.4), channel_id=1, source_target_pairs={{0,8},{10,2},{8,16},{18,10},{16,24},{26,18},{24,28},{30,26},{28,20... | collective-permute-start | bytes 983048 | tf_op jit(solution)/shard_map/projection_far_1_0/ppermute | solution.py:94
  7.0 2.6 %collective-permute-done.near_ref.refs_2_ = bf16[264,640]{1,0:T(8,128)(2,1)S(1)} collective-permute-done((bf16[264,640]{1,0:T(8,128)(2,1)S(1)}, bf16[264,640]{1,0:T(8,128)(2,1)S(1)}, u32[]{:S(2)}, u32[]{:S(2)}) %collective-permute-start) | collective-permute-done | bytes 337952 | tf_op jit(solution)/shard_map/projection_near_1_0/ppermute | solution.py:94
  9.6 2.1 %collective-permute-start.2 = (bf16[264,640]{1,0:T(8,128)(2,1)S(1)}, bf16[264,640]{1,0:T(8,128)(2,1)S(1)}, u32[]{:S(2)}, u32[]{:S(2)}) collective-permute-start(bf16[264,640]{1,0:T(8,128)(2,1)S(1)} %pass_on.1), channel_id=1, source_target_pairs={{0,8},{10,2},{8,16},{18,10},{16,24},{26,18},{24,28},{30,26},{28,20... | collective-permute-start | bytes 1013768 | tf_op jit(solution)/shard_map/projection_near_2_0/ppermute | solution.py:94
  11.7 1.3 %collective-permute-done.5.refs_0_ = bf16[256,640]{1,0:T(8,128)(2,1)S(1)} collective-permute-done((bf16[256,640]{1,0:T(8,128)(2,1)S(1)}, bf16[256,640]{1,0:T(8,128)(2,1)S(1)}, u32[]{:S(2)}, u32[]{:S(2)}) %collective-permute-start.5) | collective-permute-done | bytes 327712 | tf_op jit(solution)/shard_map/projection_far_1_0/ppermute | solution.py:94
  13.0 2.1 %collective-permute-start.6 = (bf16[256,640]{1,0:T(8,128)(2,1)S(1)}, bf16[256,640]{1,0:T(8,128)(2,1)S(1)}, u32[]{:S(2)}, u32[]{:S(2)}) collective-permute-start(bf16[256,640]{1,0:T(8,128)(2,1)S(1)} %collective-permute-done.5.refs_0_), channel_id=1, source_target_pairs={{0,8},{10,2},{8,16},{18,10},{16,24},{26,18},{24,28},{30,26},{28,20... | collective-permute-start | bytes 983048 | tf_op jit(solution)/shard_map/projection_far_2_0/ppermute | solution.py:94
  15.1 1.4 %projection_1.1 = (f32[3,256,640]{2,1,0:T(8,128)S(1)}, f32[8,640]{1,0:T(8,128)S(1)}) custom-call(bf16[264,640]{1,0:T(8,128)(2,1)S(1)} %prepare.1.refs_0_, bf16[264,640]{1,0:T(8,128)(2,1)S(1)} %collective-permute-done.1.far_ref.refs_1_, bf16[264,640]{1,0:T(8,128)(2,1)S(1)} %collective-permute-done.near_ref.refs_2_, ...), custom_call_target="tpu_custom_call" | custom-call | tf_op jit(solution)/shard_map/projection_1/pallas_call | solution.py:203
  16.8 2.1 %collective-permute-start.3 = (bf16[264,640]{1,0:T(8,128)(2,1)S(1)}, bf16[264,640]{1,0:T(8,128)(2,1)S(1)}, u32[]{:S(2)}, u32[]{:S(2)}) collective-permute-start(bf16[264,640]{1,0:T(8,128)(2,1)S(1)} %collective-permute-done.2.refs_2_), channel_id=1, source_target_pairs={{0,8},{10,2},{8,16},{18,10},{16,24},{26,18},{24,28},{30,26},{28,20... | collective-permute-start | bytes 1013768 | tf_op jit(solution)/shard_map/projection_near_3_0/ppermute | solution.py:94
  19.0 1.3 %collective-permute-done.6.refs_0_ = bf16[256,640]{1,0:T(8,128)(2,1)S(1)} collective-permute-done((bf16[256,640]{1,0:T(8,128)(2,1)S(1)}, bf16[256,640]{1,0:T(8,128)(2,1)S(1)}, u32[]{:S(2)}, u32[]{:S(2)}) %collective-permute-start.6) | collective-permute-done | bytes 327712 | tf_op jit(solution)/shard_map/projection_far_2_0/ppermute | solution.py:94
  20.3 2.1 %collective-permute-start.13 = (bf16[256,640]{1,0:T(8,128)(2,1)S(1)}, bf16[256,640]{1,0:T(8,128)(2,1)S(1)}, u32[]{:S(2)}, u32[]{:S(2)}) collective-permute-start(bf16[256,640]{1,0:T(8,128)(2,1)S(1)} %collective-permute-done.6.refs_0_), channel_id=1, source_target_pairs={{0,8},{10,2},{8,16},{18,10},{16,24},{26,18},{24,28},{30,26},{28,20... | collective-permute-start | bytes 983048 | tf_op jit(solution)/shard_map/projection_far_3_0/ppermute | solution.py:94
  22.4 1.6 %projection_2.1 = (f32[3,256,640]{2,1,0:T(8,128)S(1)}, f32[8,640]{1,0:T(8,128)S(1)}) custom-call(bf16[256,640]{1,0:T(8,128)(2,1)S(1)} %collective-permute-done.5.refs_0_, bf16[256,640]{1,0:T(8,128)(2,1)S(1)} %collective-permute-done.8.refs_1_, bf16[264,640]{1,0:T(8,128)(2,1)S(1)} %collective-permute-done.2.refs_2_, ...), custom_call_target="tpu_custom_call", output_to_operand_aliasing={{0}: (5, {}), {1}: (6, {})} | custom-call | tf_op jit(solution)/shard_map/projection_2/pallas_call | solution.py:203
  24.0 2.0 %collective-permute-start.4 = (bf16[264,640]{1,0:T(8,128)(2,1)S(1)}, bf16[264,640]{1,0:T(8,128)(2,1)S(1)}, u32[]{:S(2)}, u32[]{:S(2)}) collective-permute-start(bf16[264,640]{1,0:T(8,128)(2,1)S(1)} %collective-permute-done.3.refs_2_), channel_id=1, source_target_pairs={{0,8},{10,2},{8,16},{18,10},{16,24},{26,18},{24,28},{30,26},{28,20... | collective-permute-start | bytes 1013768 | tf_op jit(solution)/shard_map/projection_near_4_0/ppermute | solution.py:94
  26.2 1.3 %collective-permute-done.13.refs_0_ = bf16[256,640]{1,0:T(8,128)(2,1)S(1)} collective-permute-done((bf16[256,640]{1,0:T(8,128)(2,1)S(1)}, bf16[256,640]{1,0:T(8,128)(2,1)S(1)}, u32[]{:S(2)}, u32[]{:S(2)}) %collective-permute-start.13) | collective-permute-done | bytes 327712 | tf_op jit(solution)/shard_map/projection_far_3_0/ppermute | solution.py:94
  27.7 1.6 %projection_3.1 = (f32[3,256,640]{2,1,0:T(8,128)S(1)}, f32[8,640]{1,0:T(8,128)S(1)}) custom-call(bf16[256,640]{1,0:T(8,128)(2,1)S(1)} %collective-permute-done.6.refs_0_, bf16[256,640]{1,0:T(8,128)(2,1)S(1)} %collective-permute-done.7.refs_1_, bf16[264,640]{1,0:T(8,128)(2,1)S(1)} %collective-permute-done.3.refs_2_, ...), custom_call_target="tpu_custom_call", output_to_operand_aliasing={{0}: (5, {}), {1}: (6, {})} | custom-call | tf_op jit(solution)/shard_map/projection_3/pallas_call | solution.py:203
  29.3 2.0 %collective-permute-done.4.refs_2_ = bf16[264,640]{1,0:T(8,128)(2,1)S(1)} collective-permute-done((bf16[264,640]{1,0:T(8,128)(2,1)S(1)}, bf16[264,640]{1,0:T(8,128)(2,1)S(1)}, u32[]{:S(2)}, u32[]{:S(2)}) %collective-permute-start.4) | collective-permute-done | bytes 337952 | tf_op jit(solution)/shard_map/projection_near_4_0/ppermute | solution.py:94
  31.3 1.2 %projection_4.1 = (f32[3,256,640]{2,1,0:T(8,128)S(1)}, f32[8,640]{1,0:T(8,128)S(1)}) custom-call(bf16[256,640]{1,0:T(8,128)(2,1)S(1)} %collective-permute-done.13.refs_0_, bf16[256,640]{1,0:T(8,128)(2,1)S(1)} %collective-permute-done.14.refs_1_, bf16[264,640]{1,0:T(8,128)(2,1)S(1)} %collective-permute-done.4.refs_2_, ...), custom_call_target="tpu_custom_call", output_to_operand_aliasing={{0}: (4, {}), {1}: (5, {})} | custom-call | flops 2000000000 | tf_op jit(solution)/shard_map/projection_4/pallas_call | solution.py:203
  33.7 1.1 %collective-permute-start.15 = (bf16[136,640]{1,0:T(8,128)(2,1)S(1)}, bf16[136,640]{1,0:T(8,128)(2,1)S(1)}, u32[]{:S(2)}, u32[]{:S(2)}) collective-permute-start(bf16[136,640]{1,0:T(8,128)(2,1)S(1)} %projection_last.4), channel_id=1, source_target_pairs={{0,1},{1,0},{2,3},{3,2},{4,5},{5,4},{6,7},{7,6},{8,9},{9,8},{10,11... | collective-permute-start | bytes 522248 | tf_op jit(solution)/shard_map/ppermute | solution.py:631
  38.2 2.8 %collective-permute-done.15.refs_0_.refs_6_ = bf16[136,640]{1,0:T(8,128)(2,1)S(1)} collective-permute-done((bf16[136,640]{1,0:T(8,128)(2,1)S(1)}, bf16[136,640]{1,0:T(8,128)(2,1)S(1)}, u32[]{:S(2)}, u32[]{:S(2)}) %collective-permute-start.15) | collective-permute-done | bytes 174112 | tf_op jit(solution)/shard_map/ppermute | solution.py:631
  41.6 2.0 %collective-permute-start.16 = (bf16[128,640]{1,0:T(8,128)(2,1)S(1)}, bf16[128,640]{1,0:T(8,128)(2,1)S(1)}, u32[]{:S(2)}, u32[]{:S(2)}) collective-permute-start(bf16[128,640]{1,0:T(8,128)(2,1)S(1)} %far_part_1_0.1.refs_0_), channel_id=1, source_target_pairs={{0,8},{10,2},{8,16},{18,10},{16,24},{26,18},{24,28},{30,26},{28,20... | collective-permute-start | bytes 491528 | tf_op jit(solution)/shard_map/output_near_1_0/ppermute | solution.py:94
  44.4 2.0 %collective-permute-start.18 = (bf16[128,640]{1,0:T(8,128)(2,1)S(1)}, bf16[128,640]{1,0:T(8,128)(2,1)S(1)}, u32[]{:S(2)}, u32[]{:S(2)}) collective-permute-start(bf16[128,640]{1,0:T(8,128)(2,1)S(1)} %far_part_1_128.1.refs_1_), channel_id=1, source_target_pairs={{0,8},{10,2},{8,16},{18,10},{16,24},{26,18},{24,28},{30,26},{28,20... | collective-permute-start | bytes 491528 | tf_op jit(solution)/shard_map/output_near_1_1/ppermute | solution.py:94
  46.4 1.6 %collective-permute-start.23 = (bf16[128,640]{1,0:T(8,128)(2,1)S(1)}, bf16[128,640]{1,0:T(8,128)(2,1)S(1)}, u32[]{:S(2)}, u32[]{:S(2)}) collective-permute-start(bf16[128,640]{1,0:T(8,128)(2,1)S(1)} %collective-permute-done.22.refs_2_), channel_id=1, source_target_pairs={{0,8},{10,2},{8,16},{18,10},{16,24},{26,18},{24,28},{30,26},{28,20... | collective-permute-start | bytes 491528 | tf_op jit(solution)/shard_map/output_far_1_0/ppermute | solution.py:94
  48.0 1.6 %collective-permute-start.25 = (bf16[128,640]{1,0:T(8,128)(2,1)S(1)}, bf16[128,640]{1,0:T(8,128)(2,1)S(1)}, u32[]{:S(2)}, u32[]{:S(2)}) collective-permute-start(bf16[128,640]{1,0:T(8,128)(2,1)S(1)} %collective-permute-done.24.refs_3_), channel_id=1, source_target_pairs={{0,8},{10,2},{8,16},{18,10},{16,24},{26,18},{24,28},{30,26},{28,20... | collective-permute-start | bytes 491528 | tf_op jit(solution)/shard_map/output_far_1_1/ppermute | solution.py:94
  49.8 2.0 %collective-permute-start.19 = (bf16[256,640]{1,0:T(8,128)(2,1)S(1)}, bf16[256,640]{1,0:T(8,128)(2,1)S(1)}, u32[]{:S(2)}, u32[]{:S(2)}) collective-permute-start(bf16[256,640]{1,0:T(8,128)(2,1)S(1)} %constant_dynamic-update-slice_fusion.refs_4_), channel_id=1, source_target_pairs={{0,8},{10,2},{8,16},{18,10},{16,24},{26,18},{24,28},{30,26},{28,20... | collective-permute-start | bytes 983048 | tf_op jit(solution)/shard_map/output_near_2_0/ppermute | solution.py:94
  51.9 1.6 %collective-permute-done.25 = bf16[128,640]{1,0:T(8,128)(2,1)S(1)} collective-permute-done((bf16[128,640]{1,0:T(8,128)(2,1)S(1)}, bf16[128,640]{1,0:T(8,128)(2,1)S(1)}, u32[]{:S(2)}, u32[]{:S(2)}) %collective-permute-start.25) | collective-permute-done | bytes 163872 | tf_op jit(solution)/shard_map/output_far_1_1/ppermute | solution.py:94
  53.5 1.8 %collective-permute-start.26 = (bf16[256,640]{1,0:T(8,128)(2,1)S(1)}, bf16[256,640]{1,0:T(8,128)(2,1)S(1)}, u32[]{:S(2)}, u32[]{:S(2)}) collective-permute-start(bf16[256,640]{1,0:T(8,128)(2,1)S(1)} %constant_dynamic-update-slice_fusion.2.refs_0_), channel_id=1, source_target_pairs={{0,8},{10,2},{8,16},{18,10},{16,24},{26,18},{24,28},{30,26},{28,20... | collective-permute-start | bytes 983048 | tf_op jit(solution)/shard_map/output_far_2_0/ppermute | solution.py:94
  57.0 2.0 %collective-permute-start.20 = (bf16[256,640]{1,0:T(8,128)(2,1)S(1)}, bf16[256,640]{1,0:T(8,128)(2,1)S(1)}, u32[]{:S(2)}, u32[]{:S(2)}) collective-permute-start(bf16[256,640]{1,0:T(8,128)(2,1)S(1)} %collective-permute-done.19.refs_2_), channel_id=1, source_target_pairs={{0,8},{10,2},{8,16},{18,10},{16,24},{26,18},{24,28},{30,26},{28,20... | collective-permute-start | bytes 983048 | tf_op jit(solution)/shard_map/output_near_3_0/ppermute | solution.py:94
  58.9 1.7 %collective-permute-done.26.refs_0_ = bf16[256,640]{1,0:T(8,128)(2,1)S(1)} collective-permute-done((bf16[256,640]{1,0:T(8,128)(2,1)S(1)}, bf16[256,640]{1,0:T(8,128)(2,1)S(1)}, u32[]{:S(2)}, u32[]{:S(2)}) %collective-permute-start.26) | collective-permute-done | bytes 327712 | tf_op jit(solution)/shard_map/output_far_2_0/ppermute | solution.py:94
  60.6 1.8 %collective-permute-start.33 = (bf16[256,640]{1,0:T(8,128)(2,1)S(1)}, bf16[256,640]{1,0:T(8,128)(2,1)S(1)}, u32[]{:S(2)}, u32[]{:S(2)}) collective-permute-start(bf16[256,640]{1,0:T(8,128)(2,1)S(1)} %collective-permute-done.26.refs_0_), channel_id=1, source_target_pairs={{0,8},{10,2},{8,16},{18,10},{16,24},{26,18},{24,28},{30,26},{28,20... | collective-permute-start | bytes 983048 | tf_op jit(solution)/shard_map/output_far_3_0/ppermute | solution.py:94
  64.1 1.9 %collective-permute-start.21 = (bf16[256,640]{1,0:T(8,128)(2,1)S(1)}, bf16[256,640]{1,0:T(8,128)(2,1)S(1)}, u32[]{:S(2)}, u32[]{:S(2)}) collective-permute-start(bf16[256,640]{1,0:T(8,128)(2,1)S(1)} %collective-permute-done.20.refs_2_), channel_id=1, source_target_pairs={{0,8},{10,2},{8,16},{18,10},{16,24},{26,18},{24,28},{30,26},{28,20... | collective-permute-start | bytes 983048 | tf_op jit(solution)/shard_map/output_near_4_0/ppermute | solution.py:94
  66.0 1.7 %collective-permute-done.33.refs_0_ = bf16[256,640]{1,0:T(8,128)(2,1)S(1)} collective-permute-done((bf16[256,640]{1,0:T(8,128)(2,1)S(1)}, bf16[256,640]{1,0:T(8,128)(2,1)S(1)}, u32[]{:S(2)}, u32[]{:S(2)}) %collective-permute-start.33) | collective-permute-done | bytes 327712 | tf_op jit(solution)/shard_map/output_far_3_0/ppermute | solution.py:94
  68.3 2.9 %collective-permute-done.21.refs_2_ = bf16[256,640]{1,0:T(8,128)(2,1)S(1)} collective-permute-done((bf16[256,640]{1,0:T(8,128)(2,1)S(1)}, bf16[256,640]{1,0:T(8,128)(2,1)S(1)}, u32[]{:S(2)}, u32[]{:S(2)}) %collective-permute-start.21) | collective-permute-done | bytes 327712 | tf_op jit(solution)/shard_map/output_near_4_0/ppermute | solution.py:94
  71.7 1.1 %collective-permute-done.32.refs_0_ = bf16[256,640]{1,0:T(8,128)(2,1)S(1)} collective-permute-done((bf16[256,640]{1,0:T(8,128)(2,1)S(1)}, bf16[256,640]{1,0:T(8,128)(2,1)S(1)}, u32[]{:S(2)}, u32[]{:S(2)}) %collective-permute-start.32) | collective-permute-done | bytes 327712 | tf_op jit(solution)/shard_map/output_core_near_4_0/ppermute | solution.py:98
  (86 shorter events, 15.2 us)
Async XLA Ops:
  1.3 3.2 %collective-permute-start.1 = (bf16[264,640]{1,0:T(8,128)(2,1)S(1)}, bf16[264,640]{1,0:T(8,128)(2,1)S(1)}, u32[]{:S(2)}, u32[]{:S(2)}) collective-permute-start(bf16[264,640]{1,0:T(8,128)(2,1)S(1)} %prepare.1.refs_0_), channel_id=1, source_target_pairs={{0,2},{2,0},{4,6},{6,4},{8,10},{10,8},{12,14},{14,12},{16,18},{18,... | collective-permute-start | bytes 1013768 | tf_op jit(solution)/shard_map/projection_core_own_0/ppermute | solution.py:98
  1.8 7.7 %collective-permute-start = (bf16[264,640]{1,0:T(8,128)(2,1)S(1)}, bf16[264,640]{1,0:T(8,128)(2,1)S(1)}, u32[]{:S(2)}, u32[]{:S(2)}) collective-permute-start(bf16[264,640]{1,0:T(8,128)(2,1)S(1)} %prepare.1.refs_0_), channel_id=1, source_target_pairs={{0,8},{10,2},{8,16},{18,10},{16,24},{26,18},{24,28},{30,26},{28,20... | collective-permute-start | bytes 1013768 | tf_op jit(solution)/shard_map/projection_near_1_0/ppermute | solution.py:94
  4.5 8.6 %collective-permute-start.5 = (bf16[256,640]{1,0:T(8,128)(2,1)S(1)}, bf16[256,640]{1,0:T(8,128)(2,1)S(1)}, u32[]{:S(2)}, u32[]{:S(2)}) collective-permute-start(bf16[256,640]{1,0:T(8,128)(2,1)S(1)} %slice.4), channel_id=1, source_target_pairs={{0,8},{10,2},{8,16},{18,10},{16,24},{26,18},{24,28},{30,26},{28,20... | collective-permute-start | bytes 983048 | tf_op jit(solution)/shard_map/projection_far_1_0/ppermute | solution.py:94
  9.5 5.6 %collective-permute-start.9 = (bf16[264,640]{1,0:T(8,128)(2,1)S(1)}, bf16[264,640]{1,0:T(8,128)(2,1)S(1)}, u32[]{:S(2)}, u32[]{:S(2)}) collective-permute-start(bf16[264,640]{1,0:T(8,128)(2,1)S(1)} %collective-permute-done.near_ref.refs_2_), channel_id=1, source_target_pairs={{0,2},{2,0},{4,6},{6,4},{8,10},{10,8},{12,14},{14,12},{16,18},{18,... | collective-permute-start | bytes 1013768 | tf_op jit(solution)/shard_map/projection_core_near_1_0/ppermute | solution.py:98
  9.6 7.2 %collective-permute-start.2 = (bf16[264,640]{1,0:T(8,128)(2,1)S(1)}, bf16[264,640]{1,0:T(8,128)(2,1)S(1)}, u32[]{:S(2)}, u32[]{:S(2)}) collective-permute-start(bf16[264,640]{1,0:T(8,128)(2,1)S(1)} %pass_on.1), channel_id=1, source_target_pairs={{0,8},{10,2},{8,16},{18,10},{16,24},{26,18},{24,28},{30,26},{28,20... | collective-permute-start | bytes 1013768 | tf_op jit(solution)/shard_map/projection_near_2_0/ppermute | solution.py:94
  13.0 7.3 %collective-permute-start.6 = (bf16[256,640]{1,0:T(8,128)(2,1)S(1)}, bf16[256,640]{1,0:T(8,128)(2,1)S(1)}, u32[]{:S(2)}, u32[]{:S(2)}) collective-permute-start(bf16[256,640]{1,0:T(8,128)(2,1)S(1)} %collective-permute-done.5.refs_0_), channel_id=1, source_target_pairs={{0,8},{10,2},{8,16},{18,10},{16,24},{26,18},{24,28},{30,26},{28,20... | collective-permute-start | bytes 983048 | tf_op jit(solution)/shard_map/projection_far_2_0/ppermute | solution.py:94
  16.8 5.6 %collective-permute-start.10 = (bf16[264,640]{1,0:T(8,128)(2,1)S(1)}, bf16[264,640]{1,0:T(8,128)(2,1)S(1)}, u32[]{:S(2)}, u32[]{:S(2)}) collective-permute-start(bf16[264,640]{1,0:T(8,128)(2,1)S(1)} %collective-permute-done.2.refs_2_), channel_id=1, source_target_pairs={{0,2},{2,0},{4,6},{6,4},{8,10},{10,8},{12,14},{14,12},{16,18},{18,... | collective-permute-start | bytes 1013768 | tf_op jit(solution)/shard_map/projection_core_near_2_0/ppermute | solution.py:98
  16.8 7.2 %collective-permute-start.3 = (bf16[264,640]{1,0:T(8,128)(2,1)S(1)}, bf16[264,640]{1,0:T(8,128)(2,1)S(1)}, u32[]{:S(2)}, u32[]{:S(2)}) collective-permute-start(bf16[264,640]{1,0:T(8,128)(2,1)S(1)} %collective-permute-done.2.refs_2_), channel_id=1, source_target_pairs={{0,8},{10,2},{8,16},{18,10},{16,24},{26,18},{24,28},{30,26},{28,20... | collective-permute-start | bytes 1013768 | tf_op jit(solution)/shard_map/projection_near_3_0/ppermute | solution.py:94
  18.9 3.5 %collective-permute-start.8 = (bf16[256,640]{1,0:T(8,128)(2,1)S(1)}, bf16[256,640]{1,0:T(8,128)(2,1)S(1)}, u32[]{:S(2)}, u32[]{:S(2)}) collective-permute-start(bf16[256,640]{1,0:T(8,128)(2,1)S(1)} %collective-permute-done.5.refs_0_), channel_id=1, source_target_pairs={{0,2},{2,0},{4,6},{6,4},{8,10},{10,8},{12,14},{14,12},{16,18},{18,... | collective-permute-start | bytes 983048 | tf_op jit(solution)/shard_map/projection_core_far_1_0/ppermute | solution.py:98
  20.3 7.2 %collective-permute-start.13 = (bf16[256,640]{1,0:T(8,128)(2,1)S(1)}, bf16[256,640]{1,0:T(8,128)(2,1)S(1)}, u32[]{:S(2)}, u32[]{:S(2)}) collective-permute-start(bf16[256,640]{1,0:T(8,128)(2,1)S(1)} %collective-permute-done.6.refs_0_), channel_id=1, source_target_pairs={{0,8},{10,2},{8,16},{18,10},{16,24},{26,18},{24,28},{30,26},{28,20... | collective-permute-start | bytes 983048 | tf_op jit(solution)/shard_map/projection_far_3_0/ppermute | solution.py:94
  24.0 3.7 %collective-permute-start.11 = (bf16[264,640]{1,0:T(8,128)(2,1)S(1)}, bf16[264,640]{1,0:T(8,128)(2,1)S(1)}, u32[]{:S(2)}, u32[]{:S(2)}) collective-permute-start(bf16[264,640]{1,0:T(8,128)(2,1)S(1)} %collective-permute-done.3.refs_2_), channel_id=1, source_target_pairs={{0,2},{2,0},{4,6},{6,4},{8,10},{10,8},{12,14},{14,12},{16,18},{18,... | collective-permute-start | bytes 1013768 | tf_op jit(solution)/shard_map/projection_core_near_3_0/ppermute | solution.py:98
  24.0 7.2 %collective-permute-start.4 = (bf16[264,640]{1,0:T(8,128)(2,1)S(1)}, bf16[264,640]{1,0:T(8,128)(2,1)S(1)}, u32[]{:S(2)}, u32[]{:S(2)}) collective-permute-start(bf16[264,640]{1,0:T(8,128)(2,1)S(1)} %collective-permute-done.3.refs_2_), channel_id=1, source_target_pairs={{0,8},{10,2},{8,16},{18,10},{16,24},{26,18},{24,28},{30,26},{28,20... | collective-permute-start | bytes 1013768 | tf_op jit(solution)/shard_map/projection_near_4_0/ppermute | solution.py:94
  27.5 3.8 %collective-permute-start.14 = (bf16[256,640]{1,0:T(8,128)(2,1)S(1)}, bf16[256,640]{1,0:T(8,128)(2,1)S(1)}, u32[]{:S(2)}, u32[]{:S(2)}) collective-permute-start(bf16[256,640]{1,0:T(8,128)(2,1)S(1)} %collective-permute-done.13.refs_0_), channel_id=1, source_target_pairs={{0,2},{2,0},{4,6},{6,4},{8,10},{10,8},{12,14},{14,12},{16,18},{18,... | collective-permute-start | bytes 983048 | tf_op jit(solution)/shard_map/projection_core_far_3_0/ppermute | solution.py:98
  33.7 7.3 %collective-permute-start.15 = (bf16[136,640]{1,0:T(8,128)(2,1)S(1)}, bf16[136,640]{1,0:T(8,128)(2,1)S(1)}, u32[]{:S(2)}, u32[]{:S(2)}) collective-permute-start(bf16[136,640]{1,0:T(8,128)(2,1)S(1)} %projection_last.4), channel_id=1, source_target_pairs={{0,1},{1,0},{2,3},{3,2},{4,5},{5,4},{6,7},{7,6},{8,9},{9,8},{10,11... | collective-permute-start | bytes 522248 | tf_op jit(solution)/shard_map/ppermute | solution.py:631
  36.8 6.9 %collective-permute-start.17 = (bf16[128,640]{1,0:T(8,128)(2,1)S(1)}, bf16[128,640]{1,0:T(8,128)(2,1)S(1)}, u32[]{:S(2)}, u32[]{:S(2)}) collective-permute-start(bf16[128,640]{1,0:T(8,128)(2,1)S(1)} %projection_last.7), channel_id=1, source_target_pairs={{0,1},{1,0},{2,3},{3,2},{4,5},{5,4},{6,7},{7,6},{8,9},{9,8},{10,11... | collective-permute-start | bytes 491528 | tf_op jit(solution)/shard_map/ppermute | solution.py:631
  41.6 4.8 %collective-permute-start.22 = (bf16[128,640]{1,0:T(8,128)(2,1)S(1)}, bf16[128,640]{1,0:T(8,128)(2,1)S(1)}, u32[]{:S(2)}, u32[]{:S(2)}) collective-permute-start(bf16[128,640]{1,0:T(8,128)(2,1)S(1)} %far_part_1_0.1.refs_0_), channel_id=1, source_target_pairs={{0,2},{2,0},{4,6},{6,4},{8,10},{10,8},{12,14},{14,12},{16,18},{18,... | collective-permute-start | bytes 491528 | tf_op jit(solution)/shard_map/output_core_own_0/ppermute | solution.py:98
  41.6 6.3 %collective-permute-start.16 = (bf16[128,640]{1,0:T(8,128)(2,1)S(1)}, bf16[128,640]{1,0:T(8,128)(2,1)S(1)}, u32[]{:S(2)}, u32[]{:S(2)}) collective-permute-start(bf16[128,640]{1,0:T(8,128)(2,1)S(1)} %far_part_1_0.1.refs_0_), channel_id=1, source_target_pairs={{0,8},{10,2},{8,16},{18,10},{16,24},{26,18},{24,28},{30,26},{28,20... | collective-permute-start | bytes 491528 | tf_op jit(solution)/shard_map/output_near_1_0/ppermute | solution.py:94
  44.3 3.7 %collective-permute-start.24 = (bf16[128,640]{1,0:T(8,128)(2,1)S(1)}, bf16[128,640]{1,0:T(8,128)(2,1)S(1)}, u32[]{:S(2)}, u32[]{:S(2)}) collective-permute-start(bf16[128,640]{1,0:T(8,128)(2,1)S(1)} %far_part_1_128.1.refs_1_), channel_id=1, source_target_pairs={{0,2},{2,0},{4,6},{6,4},{8,10},{10,8},{12,14},{14,12},{16,18},{18,... | collective-permute-start | bytes 491528 | tf_op jit(solution)/shard_map/output_core_own_1/ppermute | solution.py:98
  44.4 5.3 %collective-permute-start.18 = (bf16[128,640]{1,0:T(8,128)(2,1)S(1)}, bf16[128,640]{1,0:T(8,128)(2,1)S(1)}, u32[]{:S(2)}, u32[]{:S(2)}) collective-permute-start(bf16[128,640]{1,0:T(8,128)(2,1)S(1)} %far_part_1_128.1.refs_1_), channel_id=1, source_target_pairs={{0,8},{10,2},{8,16},{18,10},{16,24},{26,18},{24,28},{30,26},{28,20... | collective-permute-start | bytes 491528 | tf_op jit(solution)/shard_map/output_near_1_1/ppermute | solution.py:94
  46.4 5.5 %collective-permute-start.23 = (bf16[128,640]{1,0:T(8,128)(2,1)S(1)}, bf16[128,640]{1,0:T(8,128)(2,1)S(1)}, u32[]{:S(2)}, u32[]{:S(2)}) collective-permute-start(bf16[128,640]{1,0:T(8,128)(2,1)S(1)} %collective-permute-done.22.refs_2_), channel_id=1, source_target_pairs={{0,8},{10,2},{8,16},{18,10},{16,24},{26,18},{24,28},{30,26},{28,20... | collective-permute-start | bytes 491528 | tf_op jit(solution)/shard_map/output_far_1_0/ppermute | solution.py:94
  48.0 5.5 %collective-permute-start.25 = (bf16[128,640]{1,0:T(8,128)(2,1)S(1)}, bf16[128,640]{1,0:T(8,128)(2,1)S(1)}, u32[]{:S(2)}, u32[]{:S(2)}) collective-permute-start(bf16[128,640]{1,0:T(8,128)(2,1)S(1)} %collective-permute-done.24.refs_3_), channel_id=1, source_target_pairs={{0,8},{10,2},{8,16},{18,10},{16,24},{26,18},{24,28},{30,26},{28,20... | collective-permute-start | bytes 491528 | tf_op jit(solution)/shard_map/output_far_1_1/ppermute | solution.py:94
  49.7 5.5 %collective-permute-start.29 = (bf16[256,640]{1,0:T(8,128)(2,1)S(1)}, bf16[256,640]{1,0:T(8,128)(2,1)S(1)}, u32[]{:S(2)}, u32[]{:S(2)}) collective-permute-start(bf16[256,640]{1,0:T(8,128)(2,1)S(1)} %constant_dynamic-update-slice_fusion.refs_4_), channel_id=1, source_target_pairs={{0,2},{2,0},{4,6},{6,4},{8,10},{10,8},{12,14},{14,12},{16,18},{18,... | collective-permute-start | bytes 983048 | tf_op jit(solution)/shard_map/output_core_near_1_0/ppermute | solution.py:98
  49.8 7.1 %collective-permute-start.19 = (bf16[256,640]{1,0:T(8,128)(2,1)S(1)}, bf16[256,640]{1,0:T(8,128)(2,1)S(1)}, u32[]{:S(2)}, u32[]{:S(2)}) collective-permute-start(bf16[256,640]{1,0:T(8,128)(2,1)S(1)} %constant_dynamic-update-slice_fusion.refs_4_), channel_id=1, source_target_pairs={{0,8},{10,2},{8,16},{18,10},{16,24},{26,18},{24,28},{30,26},{28,20... | collective-permute-start | bytes 983048 | tf_op jit(solution)/shard_map/output_near_2_0/ppermute | solution.py:94
  53.5 7.1 %collective-permute-start.26 = (bf16[256,640]{1,0:T(8,128)(2,1)S(1)}, bf16[256,640]{1,0:T(8,128)(2,1)S(1)}, u32[]{:S(2)}, u32[]{:S(2)}) collective-permute-start(bf16[256,640]{1,0:T(8,128)(2,1)S(1)} %constant_dynamic-update-slice_fusion.2.refs_0_), channel_id=1, source_target_pairs={{0,8},{10,2},{8,16},{18,10},{16,24},{26,18},{24,28},{30,26},{28,20... | collective-permute-start | bytes 983048 | tf_op jit(solution)/shard_map/output_far_2_0/ppermute | solution.py:94
  55.3 7.2 %collective-permute-start.28 = (bf16[256,640]{1,0:T(8,128)(2,1)S(1)}, bf16[256,640]{1,0:T(8,128)(2,1)S(1)}, u32[]{:S(2)}, u32[]{:S(2)}) collective-permute-start(bf16[256,640]{1,0:T(8,128)(2,1)S(1)} %constant_dynamic-update-slice_fusion.2.refs_0_), channel_id=1, source_target_pairs={{0,2},{2,0},{4,6},{6,4},{8,10},{10,8},{12,14},{14,12},{16,18},{18,... | collective-permute-start | bytes 983048 | tf_op jit(solution)/shard_map/output_core_far_1_0/ppermute | solution.py:98
  57.0 5.5 %collective-permute-start.30 = (bf16[256,640]{1,0:T(8,128)(2,1)S(1)}, bf16[256,640]{1,0:T(8,128)(2,1)S(1)}, u32[]{:S(2)}, u32[]{:S(2)}) collective-permute-start(bf16[256,640]{1,0:T(8,128)(2,1)S(1)} %collective-permute-done.19.refs_2_), channel_id=1, source_target_pairs={{0,2},{2,0},{4,6},{6,4},{8,10},{10,8},{12,14},{14,12},{16,18},{18,... | collective-permute-start | bytes 983048 | tf_op jit(solution)/shard_map/output_core_near_2_0/ppermute | solution.py:98
  57.0 7.1 %collective-permute-start.20 = (bf16[256,640]{1,0:T(8,128)(2,1)S(1)}, bf16[256,640]{1,0:T(8,128)(2,1)S(1)}, u32[]{:S(2)}, u32[]{:S(2)}) collective-permute-start(bf16[256,640]{1,0:T(8,128)(2,1)S(1)} %collective-permute-done.19.refs_2_), channel_id=1, source_target_pairs={{0,8},{10,2},{8,16},{18,10},{16,24},{26,18},{24,28},{30,26},{28,20... | collective-permute-start | bytes 983048 | tf_op jit(solution)/shard_map/output_near_3_0/ppermute | solution.py:94
  60.6 7.1 %collective-permute-start.33 = (bf16[256,640]{1,0:T(8,128)(2,1)S(1)}, bf16[256,640]{1,0:T(8,128)(2,1)S(1)}, u32[]{:S(2)}, u32[]{:S(2)}) collective-permute-start(bf16[256,640]{1,0:T(8,128)(2,1)S(1)} %collective-permute-done.26.refs_0_), channel_id=1, source_target_pairs={{0,8},{10,2},{8,16},{18,10},{16,24},{26,18},{24,28},{30,26},{28,20... | collective-permute-start | bytes 983048 | tf_op jit(solution)/shard_map/output_far_3_0/ppermute | solution.py:94
  62.4 5.3 %collective-permute-start.27 = (bf16[256,640]{1,0:T(8,128)(2,1)S(1)}, bf16[256,640]{1,0:T(8,128)(2,1)S(1)}, u32[]{:S(2)}, u32[]{:S(2)}) collective-permute-start(bf16[256,640]{1,0:T(8,128)(2,1)S(1)} %collective-permute-done.26.refs_0_), channel_id=1, source_target_pairs={{0,2},{2,0},{4,6},{6,4},{8,10},{10,8},{12,14},{14,12},{16,18},{18,... | collective-permute-start | bytes 983048 | tf_op jit(solution)/shard_map/output_core_far_2_0/ppermute | solution.py:98
  64.1 3.6 %collective-permute-start.31 = (bf16[256,640]{1,0:T(8,128)(2,1)S(1)}, bf16[256,640]{1,0:T(8,128)(2,1)S(1)}, u32[]{:S(2)}, u32[]{:S(2)}) collective-permute-start(bf16[256,640]{1,0:T(8,128)(2,1)S(1)} %collective-permute-done.20.refs_2_), channel_id=1, source_target_pairs={{0,2},{2,0},{4,6},{6,4},{8,10},{10,8},{12,14},{14,12},{16,18},{18,... | collective-permute-start | bytes 983048 | tf_op jit(solution)/shard_map/output_core_near_3_0/ppermute | solution.py:98
  64.1 7.1 %collective-permute-start.21 = (bf16[256,640]{1,0:T(8,128)(2,1)S(1)}, bf16[256,640]{1,0:T(8,128)(2,1)S(1)}, u32[]{:S(2)}, u32[]{:S(2)}) collective-permute-start(bf16[256,640]{1,0:T(8,128)(2,1)S(1)} %collective-permute-done.20.refs_2_), channel_id=1, source_target_pairs={{0,8},{10,2},{8,16},{18,10},{16,24},{26,18},{24,28},{30,26},{28,20... | collective-permute-start | bytes 983048 | tf_op jit(solution)/shard_map/output_near_4_0/ppermute | solution.py:94
  67.7 3.5 %collective-permute-start.34 = (bf16[256,640]{1,0:T(8,128)(2,1)S(1)}, bf16[256,640]{1,0:T(8,128)(2,1)S(1)}, u32[]{:S(2)}, u32[]{:S(2)}) collective-permute-start(bf16[256,640]{1,0:T(8,128)(2,1)S(1)} %collective-permute-done.33.refs_0_), channel_id=1, source_target_pairs={{0,2},{2,0},{4,6},{6,4},{8,10},{10,8},{12,14},{14,12},{16,18},{18,... | collective-permute-start | bytes 983048 | tf_op jit(solution)/shard_map/output_core_far_3_0/ppermute | solution.py:98
  (14 other events, 60.0 us)

commit v10 on v9

--- a/solution.py
+++ b/solution.py
@@ -487,7 +487,21 @@
             total_ref[here, block_lanes(2 * a + 1)] = imag
 
 
-def own_part(projected, alone, moved, taps, filters, table):
+def mix(sum_ref, back_ref, query, gated, skip, out_ref):
+    rows = out_ref.shape[0]
+    spectra = [sum_ref[:, spectrum_lanes(a)] for a in range(len(query))]
+    highs = [spectrum.astype(bf16) for spectrum in spectra]
+    lows = [(s - high.astype(f32)).astype(bf16) for s, high in zip(spectra, highs)]
+    both = dot(jnp.concatenate(highs, axis=0), back_ref[...])
+    small = dot(jnp.concatenate(lows, axis=0), back_ref[:, :block_len])
+    filtered = both[:, :block_len] + (both[:, block_len:] + small)
+    for a in range(len(query)):
+        here = filtered[a * rows : (a + 1) * rows]
+        mixed = query[a] * (here + skip * gated[a].astype(f32))
+        out_ref[:, block_lanes(a)] = mixed.astype(bf16)
+
+
+def own_part(projected, alone, moved, taps, filters, table, inverse, skip):
     streams, _, tokens = projected[0].shape
     parts = channel_parts(taps.shape[2])
     number = len(parts)
@@ -500,9 +514,9 @@
         refs = list(refs)
         take = lambda n: take_from(refs, n)
         projected_refs, message_refs = take(number), take(number)
-        taps_ref, filters_ref, table_ref = take(3)
+        taps_ref, filters_ref, table_ref, back_ref, skip_ref = take(5)
         query_refs, total_refs = take(number), take(number)
-        gated_refs = take(number) if moved else None
+        gated_refs = take(number)
         (spec_ref,) = refs
         columns = [tap_columns(taps_ref[s]) for s in range(streams)]
         if moved:
@@ -527,12 +541,24 @@
             pieces = [source_ref[:rows, block_lanes(b)] for b in range(first, blocks)]
             block_spectra(pieces, table_ref, spec_ref, first)
             multiply_spectra(spec_ref, filters_ref, begin, pairs, None, total_refs[part])
+            if not moved:
+
+                @pl.when(lax.axis_index("ctx") == 0)
+                def _():
+                    lanes = [block_lanes(a) for a in range(blocks)]
+                    block_spectra([source_ref[:rows, lanes[0]]], table_ref, spec_ref, 0)
+                    sum_ref = total_refs[part]
+                    first_pairs = [[(0, a)] for a in range(blocks)]
+                    multiply_spectra(spec_ref, filters_ref, begin, first_pairs, sum_ref, sum_ref)
+                    query = [query_refs[part][:, at] for at in lanes]
+                    gated = [source_ref[:rows, at] for at in lanes]
+                    column_here = column(skip_ref[...])[begin : begin + rows]
+                    mix(sum_ref, back_ref, query, gated, column_here, gated_refs[part])
 
     out_shape = [shape_of((rows, tokens), f32) for _, rows in parts]
     out_shape += [shape_of((rows, 2 * tokens), f32) for _, rows in parts]
-    if moved:
-        out_shape += [shape_of((rows, tokens), bf16) for _, rows in parts]
-    inputs = [*projected, *(moved or alone), taps, filters, table]
+    out_shape += [shape_of((rows, tokens), bf16) for _, rows in parts]
+    inputs = [*projected, *(moved or alone), taps, filters, table, inverse, skip.reshape(1, -1)]
     outs = pl.pallas_call(
         kernel,
         in_specs=[in_vmem] * len(inputs),
@@ -543,7 +569,7 @@
         cost_estimate=estimate(0, 0),
         name="own_part",
     )(*inputs)
-    gated = list(outs[2 * number :]) if moved else alone
+    gated = list(outs[2 * number :])
     return list(outs[:number]), list(outs[number : 2 * number]), gated
 
 
@@ -557,7 +583,7 @@
         refs = list(refs)
         take = lambda n: take_from(refs, n)
         moved_ref, total_ref, filters_ref, table_ref = take(4)
-        own_refs = take(3) if own else None
+        own_refs = take(4) if own else None
         spec_ref = refs.pop()
         sum_ref = refs.pop()
         if last:
@@ -574,7 +600,10 @@
                     for ref in (query_ref, gated_ref)
                 )
             if own:
-                first_ref, taps_ref, halo_ref = own_refs
+                first_ref, taps_ref, halo_ref, ready_ref = own_refs
+                if not inside:
+                    out_ref[...] = ready_ref[...]
+                    return
                 key, value = first_ref[0], first_ref[1]
                 if inside:
                     edges = halo_edges(halo_ref, taps_ref[:, :, channels_here], begin)
@@ -588,17 +617,7 @@
             multiply_spectra(spec_ref, filters_ref, begin, pairs, total_ref, sum_ref)
             if not last:
                 return
-            skip = column(skip_ref[...])[channels_here]
-            spectra = [sum_ref[:, spectrum_lanes(a)] for a in range(blocks)]
-            highs = [spectrum.astype(bf16) for spectrum in spectra]
-            lows = [(s - high.astype(f32)).astype(bf16) for s, high in zip(spectra, highs)]
-            both = dot(jnp.concatenate(highs, axis=0), back_ref[...])
-            small = dot(jnp.concatenate(lows, axis=0), back_ref[:, :block_len])
-            filtered = both[:, :block_len] + (both[:, block_len:] + small)
-            for a in range(blocks):
-                here = filtered[a * rows : (a + 1) * rows]
-                mixed = query[a] * (here + skip * gated[a].astype(f32))
-                out_ref[:, block_lanes(a)] = mixed.astype(bf16)
+            mix(sum_ref, back_ref, query, gated, column(skip_ref[...])[channels_here], out_ref)
 
         inside = lax.axis_index("ctx") >= turn
         pl.when(inside)(lambda: work(True))
@@ -660,10 +679,11 @@
     projected, first_blocks, gated = zip(*results)
     later, gated = lax.optimization_barrier((running, gated))
     moving.append(message(1, later))
-    query, totals, gated = own_part(
-        projected, gated, moving if exact else None, w_short, filters, forward
+    query, totals, ready = own_part(
+        projected, gated, moving if exact else None, w_short, filters, forward, inverse, skip_gain
     )
     if exact:
+        gated = ready
         moving = [from_before(part) for part in gated]
     mixed = []
     for turn in range(1, turns):
@@ -672,7 +692,7 @@
             if turn == turns - 1:
                 last = (inverse, query[k], gated[k], skip_gain)
                 if not exact:
-                    own_block = (first_blocks[k], w_short, moving[0])
+                    own_block = (first_blocks[k], w_short, moving[0], ready[k])
             done = far_part(
                 turn, begin, moving[k], totals[k], filters, forward, last, own_block
             )

time: 74 us -> 73.4 us (level)
    pallas_call x1, Pallas kernels: 0.94 us -> 2 us  [own_part(): pl.pallas_call(kernel, in_specs=[in_vmem] * len(inputs), out_specs=[in_vm...]
    pallas_call x2, Pallas kernels: 1.08 us -> 0.03 us  [far_part(): pl.pallas_call(kernel, in_specs=[in_vmem] * len(args), out_specs=in_vmem,...]
where the time goes in v10:
time: 73.4 us; the launch traced here: 73.3 us
  starting transfers between devices  34.2 us (47%)
  waiting for transfers between devices  22.8 us (31%)
  Pallas kernels  14.9 us (20%)
  local copies, waits for them, and re-layouts  1.13 us (2%)
    ppermute x16, starting transfers between devices, along_ring(): return lax.ppermute(block, 'fsdp', pairs)  31.5 us
    ppermute x16, waiting for transfers between devices, along_ring(): return lax.ppermute(block, 'fsdp', pairs)  18.8 us
    pallas_call x13, Pallas kernels, products(): pl.pallas_call(kernel, in_specs=[in_vmem] * (count + 1 + len(state) + len...  11.8 us
    ppermute x2, waiting for transfers between devices, from_before(): lax.ppermute(block, 'ctx', [(i, (i + 1) % count) for i in range(count)])  2.26 us
    pallas_call x1, Pallas kernels, own_part(): pl.pallas_call(kernel, in_specs=[in_vmem] * len(inputs), out_specs=[in_vm...  2 us
    ppermute x17, waiting for transfers between devices, other_core(): lax.ppermute(block, 'fsdp', [(i, i ^ 1) for i in range(2 * chip_count())])  1.77 us
    ppermute x2, starting transfers between devices, from_before(): lax.ppermute(block, 'ctx', [(i, (i + 1) % count) for i in range(count)])  1.55 us
  transfers between devices with their start and end apart: 35, of which 18 were waited for; matrix products, arithmetic and copies ran while one was open for 0% of the time, Pallas kernels for 18%

profile of v10, /device:TPU:0, one launch (start us, length us, event | category | flops | bytes accessed | tf_op | source)
XLA Modules:
  0.0 73.3 jit_solution(15068059628910318786)
XLA Ops:
  1.8 2.6 %collective-permute-start = (bf16[264,640]{1,0:T(8,128)(2,1)S(1)}, bf16[264,640]{1,0:T(8,128)(2,1)S(1)}, u32[]{:S(2)}, u32[]{:S(2)}) collective-permute-start(bf16[264,640]{1,0:T(8,128)(2,1)S(1)} %prepare.1.refs_0_), channel_id=1, source_target_pairs={{0,8},{10,2},{8,16},{18,10},{16,24},{26,18},{24,28},{30,26},{28,20... | collective-permute-start | bytes 1013768 | tf_op jit(solution)/shard_map/projection_near_1_0/ppermute | solution.py:94
  4.5 1.6 %collective-permute-start.5 = (bf16[256,640]{1,0:T(8,128)(2,1)S(1)}, bf16[256,640]{1,0:T(8,128)(2,1)S(1)}, u32[]{:S(2)}, u32[]{:S(2)}) collective-permute-start(bf16[256,640]{1,0:T(8,128)(2,1)S(1)} %slice.4), channel_id=1, source_target_pairs={{0,8},{10,2},{8,16},{18,10},{16,24},{26,18},{24,28},{30,26},{28,20... | collective-permute-start | bytes 983048 | tf_op jit(solution)/shard_map/projection_far_1_0/ppermute | solution.py:94
  7.0 2.6 %collective-permute-done.near_ref.refs_2_ = bf16[264,640]{1,0:T(8,128)(2,1)S(1)} collective-permute-done((bf16[264,640]{1,0:T(8,128)(2,1)S(1)}, bf16[264,640]{1,0:T(8,128)(2,1)S(1)}, u32[]{:S(2)}, u32[]{:S(2)}) %collective-permute-start) | collective-permute-done | bytes 337952 | tf_op jit(solution)/shard_map/projection_near_1_0/ppermute | solution.py:94
  9.6 2.1 %collective-permute-start.2 = (bf16[264,640]{1,0:T(8,128)(2,1)S(1)}, bf16[264,640]{1,0:T(8,128)(2,1)S(1)}, u32[]{:S(2)}, u32[]{:S(2)}) collective-permute-start(bf16[264,640]{1,0:T(8,128)(2,1)S(1)} %pass_on.1), channel_id=1, source_target_pairs={{0,8},{10,2},{8,16},{18,10},{16,24},{26,18},{24,28},{30,26},{28,20... | collective-permute-start | bytes 1013768 | tf_op jit(solution)/shard_map/projection_near_2_0/ppermute | solution.py:94
  11.7 1.3 %collective-permute-done.5.refs_0_ = bf16[256,640]{1,0:T(8,128)(2,1)S(1)} collective-permute-done((bf16[256,640]{1,0:T(8,128)(2,1)S(1)}, bf16[256,640]{1,0:T(8,128)(2,1)S(1)}, u32[]{:S(2)}, u32[]{:S(2)}) %collective-permute-start.5) | collective-permute-done | bytes 327712 | tf_op jit(solution)/shard_map/projection_far_1_0/ppermute | solution.py:94
  13.0 2.1 %collective-permute-start.6 = (bf16[256,640]{1,0:T(8,128)(2,1)S(1)}, bf16[256,640]{1,0:T(8,128)(2,1)S(1)}, u32[]{:S(2)}, u32[]{:S(2)}) collective-permute-start(bf16[256,640]{1,0:T(8,128)(2,1)S(1)} %collective-permute-done.5.refs_0_), channel_id=1, source_target_pairs={{0,8},{10,2},{8,16},{18,10},{16,24},{26,18},{24,28},{30,26},{28,20... | collective-permute-start | bytes 983048 | tf_op jit(solution)/shard_map/projection_far_2_0/ppermute | solution.py:94
  15.1 1.4 %projection_1.1 = (f32[3,256,640]{2,1,0:T(8,128)S(1)}, f32[8,640]{1,0:T(8,128)S(1)}) custom-call(bf16[264,640]{1,0:T(8,128)(2,1)S(1)} %prepare.1.refs_0_, bf16[264,640]{1,0:T(8,128)(2,1)S(1)} %collective-permute-done.1.far_ref.refs_1_, bf16[264,640]{1,0:T(8,128)(2,1)S(1)} %collective-permute-done.near_ref.refs_2_, ...), custom_call_target="tpu_custom_call" | custom-call | tf_op jit(solution)/shard_map/projection_1/pallas_call | solution.py:203
  16.8 2.1 %collective-permute-start.3 = (bf16[264,640]{1,0:T(8,128)(2,1)S(1)}, bf16[264,640]{1,0:T(8,128)(2,1)S(1)}, u32[]{:S(2)}, u32[]{:S(2)}) collective-permute-start(bf16[264,640]{1,0:T(8,128)(2,1)S(1)} %collective-permute-done.2.refs_2_), channel_id=1, source_target_pairs={{0,8},{10,2},{8,16},{18,10},{16,24},{26,18},{24,28},{30,26},{28,20... | collective-permute-start | bytes 1013768 | tf_op jit(solution)/shard_map/projection_near_3_0/ppermute | solution.py:94
  19.0 1.3 %collective-permute-done.6.refs_0_ = bf16[256,640]{1,0:T(8,128)(2,1)S(1)} collective-permute-done((bf16[256,640]{1,0:T(8,128)(2,1)S(1)}, bf16[256,640]{1,0:T(8,128)(2,1)S(1)}, u32[]{:S(2)}, u32[]{:S(2)}) %collective-permute-start.6) | collective-permute-done | bytes 327712 | tf_op jit(solution)/shard_map/projection_far_2_0/ppermute | solution.py:94
  20.3 2.1 %collective-permute-start.13 = (bf16[256,640]{1,0:T(8,128)(2,1)S(1)}, bf16[256,640]{1,0:T(8,128)(2,1)S(1)}, u32[]{:S(2)}, u32[]{:S(2)}) collective-permute-start(bf16[256,640]{1,0:T(8,128)(2,1)S(1)} %collective-permute-done.6.refs_0_), channel_id=1, source_target_pairs={{0,8},{10,2},{8,16},{18,10},{16,24},{26,18},{24,28},{30,26},{28,20... | collective-permute-start | bytes 983048 | tf_op jit(solution)/shard_map/projection_far_3_0/ppermute | solution.py:94
  22.4 1.6 %projection_2.1 = (f32[3,256,640]{2,1,0:T(8,128)S(1)}, f32[8,640]{1,0:T(8,128)S(1)}) custom-call(bf16[256,640]{1,0:T(8,128)(2,1)S(1)} %collective-permute-done.5.refs_0_, bf16[256,640]{1,0:T(8,128)(2,1)S(1)} %collective-permute-done.8.refs_1_, bf16[264,640]{1,0:T(8,128)(2,1)S(1)} %collective-permute-done.2.refs_2_, ...), custom_call_target="tpu_custom_call", output_to_operand_aliasing={{0}: (5, {}), {1}: (6, {})} | custom-call | tf_op jit(solution)/shard_map/projection_2/pallas_call | solution.py:203
  24.0 2.0 %collective-permute-start.4 = (bf16[264,640]{1,0:T(8,128)(2,1)S(1)}, bf16[264,640]{1,0:T(8,128)(2,1)S(1)}, u32[]{:S(2)}, u32[]{:S(2)}) collective-permute-start(bf16[264,640]{1,0:T(8,128)(2,1)S(1)} %collective-permute-done.3.refs_2_), channel_id=1, source_target_pairs={{0,8},{10,2},{8,16},{18,10},{16,24},{26,18},{24,28},{30,26},{28,20... | collective-permute-start | bytes 1013768 | tf_op jit(solution)/shard_map/projection_near_4_0/ppermute | solution.py:94
  26.2 1.3 %collective-permute-done.13.refs_0_ = bf16[256,640]{1,0:T(8,128)(2,1)S(1)} collective-permute-done((bf16[256,640]{1,0:T(8,128)(2,1)S(1)}, bf16[256,640]{1,0:T(8,128)(2,1)S(1)}, u32[]{:S(2)}, u32[]{:S(2)}) %collective-permute-start.13) | collective-permute-done | bytes 327712 | tf_op jit(solution)/shard_map/projection_far_3_0/ppermute | solution.py:94
  27.7 1.6 %projection_3.1 = (f32[3,256,640]{2,1,0:T(8,128)S(1)}, f32[8,640]{1,0:T(8,128)S(1)}) custom-call(bf16[256,640]{1,0:T(8,128)(2,1)S(1)} %collective-permute-done.6.refs_0_, bf16[256,640]{1,0:T(8,128)(2,1)S(1)} %collective-permute-done.7.refs_1_, bf16[264,640]{1,0:T(8,128)(2,1)S(1)} %collective-permute-done.3.refs_2_, ...), custom_call_target="tpu_custom_call", output_to_operand_aliasing={{0}: (5, {}), {1}: (6, {})} | custom-call | tf_op jit(solution)/shard_map/projection_3/pallas_call | solution.py:203
  29.3 2.0 %collective-permute-done.4.refs_2_ = bf16[264,640]{1,0:T(8,128)(2,1)S(1)} collective-permute-done((bf16[264,640]{1,0:T(8,128)(2,1)S(1)}, bf16[264,640]{1,0:T(8,128)(2,1)S(1)}, u32[]{:S(2)}, u32[]{:S(2)}) %collective-permute-start.4) | collective-permute-done | bytes 337952 | tf_op jit(solution)/shard_map/projection_near_4_0/ppermute | solution.py:94
  31.3 1.2 %projection_4.1 = (f32[3,256,640]{2,1,0:T(8,128)S(1)}, f32[8,640]{1,0:T(8,128)S(1)}) custom-call(bf16[256,640]{1,0:T(8,128)(2,1)S(1)} %collective-permute-done.13.refs_0_, bf16[256,640]{1,0:T(8,128)(2,1)S(1)} %collective-permute-done.14.refs_1_, bf16[264,640]{1,0:T(8,128)(2,1)S(1)} %collective-permute-done.4.refs_2_, ...), custom_call_target="tpu_custom_call", output_to_operand_aliasing={{0}: (4, {}), {1}: (5, {})} | custom-call | flops 2000000000 | tf_op jit(solution)/shard_map/projection_4/pallas_call | solution.py:203
  33.7 1.1 %collective-permute-start.15 = (bf16[136,640]{1,0:T(8,128)(2,1)S(1)}, bf16[136,640]{1,0:T(8,128)(2,1)S(1)}, u32[]{:S(2)}, u32[]{:S(2)}) collective-permute-start(bf16[136,640]{1,0:T(8,128)(2,1)S(1)} %projection_last.4), channel_id=1, source_target_pairs={{0,1},{1,0},{2,3},{3,2},{4,5},{5,4},{6,7},{7,6},{8,9},{9,8},{10,11... | collective-permute-start | bytes 522248 | tf_op jit(solution)/shard_map/ppermute | solution.py:650
  37.3 2.0 %own_part.1 = (f32[128,640]{1,0:T(8,128)S(1)}, f32[128,640]{1,0:T(8,128)S(1)}, f32[128,1280]{1,0:T(8,128)S(1)}, f32[128,1280]{1,0:T(8,128)S(1)}, bf16[128,640]{1...) custom-call(bf16[3,128,640]{2,1,0:T(8,128)(2,1)S(1)} %get-tuple-element.64.refs_0_, ...), custom_call_target="tpu_custom_call" | custom-call | tf_op jit(solution)/shard_map/own_part/pallas_call | solution.py:562
  39.3 1.7 %collective-permute-done.15.refs_0_.refs_6_ = bf16[136,640]{1,0:T(8,128)(2,1)S(1)} collective-permute-done((bf16[136,640]{1,0:T(8,128)(2,1)S(1)}, bf16[136,640]{1,0:T(8,128)(2,1)S(1)}, u32[]{:S(2)}, u32[]{:S(2)}) %collective-permute-start.15) | collective-permute-done | bytes 174112 | tf_op jit(solution)/shard_map/ppermute | solution.py:650
  41.0 2.1 %collective-permute-start.16 = (bf16[128,640]{1,0:T(8,128)(2,1)S(1)}, bf16[128,640]{1,0:T(8,128)(2,1)S(1)}, u32[]{:S(2)}, u32[]{:S(2)}) collective-permute-start(bf16[128,640]{1,0:T(8,128)(2,1)S(1)} %far_part_1_0.1.refs_0_), channel_id=1, source_target_pairs={{0,8},{10,2},{8,16},{18,10},{16,24},{26,18},{24,28},{30,26},{28,20... | collective-permute-start | bytes 491528 | tf_op jit(solution)/shard_map/output_near_1_0/ppermute | solution.py:94
  43.8 2.0 %collective-permute-start.18 = (bf16[128,640]{1,0:T(8,128)(2,1)S(1)}, bf16[128,640]{1,0:T(8,128)(2,1)S(1)}, u32[]{:S(2)}, u32[]{:S(2)}) collective-permute-start(bf16[128,640]{1,0:T(8,128)(2,1)S(1)} %far_part_1_128.1.refs_1_), channel_id=1, source_target_pairs={{0,8},{10,2},{8,16},{18,10},{16,24},{26,18},{24,28},{30,26},{28,20... | collective-permute-start | bytes 491528 | tf_op jit(solution)/shard_map/output_near_1_1/ppermute | solution.py:94
  45.8 1.6 %collective-permute-start.23 = (bf16[128,640]{1,0:T(8,128)(2,1)S(1)}, bf16[128,640]{1,0:T(8,128)(2,1)S(1)}, u32[]{:S(2)}, u32[]{:S(2)}) collective-permute-start(bf16[128,640]{1,0:T(8,128)(2,1)S(1)} %collective-permute-done.22.refs_2_), channel_id=1, source_target_pairs={{0,8},{10,2},{8,16},{18,10},{16,24},{26,18},{24,28},{30,26},{28,20... | collective-permute-start | bytes 491528 | tf_op jit(solution)/shard_map/output_far_1_0/ppermute | solution.py:94
  47.5 1.6 %collective-permute-start.25 = (bf16[128,640]{1,0:T(8,128)(2,1)S(1)}, bf16[128,640]{1,0:T(8,128)(2,1)S(1)}, u32[]{:S(2)}, u32[]{:S(2)}) collective-permute-start(bf16[128,640]{1,0:T(8,128)(2,1)S(1)} %collective-permute-done.24.refs_3_), channel_id=1, source_target_pairs={{0,8},{10,2},{8,16},{18,10},{16,24},{26,18},{24,28},{30,26},{28,20... | collective-permute-start | bytes 491528 | tf_op jit(solution)/shard_map/output_far_1_1/ppermute | solution.py:94
  49.3 2.0 %collective-permute-start.19 = (bf16[256,640]{1,0:T(8,128)(2,1)S(1)}, bf16[256,640]{1,0:T(8,128)(2,1)S(1)}, u32[]{:S(2)}, u32[]{:S(2)}) collective-permute-start(bf16[256,640]{1,0:T(8,128)(2,1)S(1)} %constant_dynamic-update-slice_fusion.refs_4_), channel_id=1, source_target_pairs={{0,8},{10,2},{8,16},{18,10},{16,24},{26,18},{24,28},{30,26},{28,20... | collective-permute-start | bytes 983048 | tf_op jit(solution)/shard_map/output_near_2_0/ppermute | solution.py:94
  51.3 1.6 %collective-permute-done.25 = bf16[128,640]{1,0:T(8,128)(2,1)S(1)} collective-permute-done((bf16[128,640]{1,0:T(8,128)(2,1)S(1)}, bf16[128,640]{1,0:T(8,128)(2,1)S(1)}, u32[]{:S(2)}, u32[]{:S(2)}) %collective-permute-start.25) | collective-permute-done | bytes 163872 | tf_op jit(solution)/shard_map/output_far_1_1/ppermute | solution.py:94
  52.9 1.8 %collective-permute-start.26 = (bf16[256,640]{1,0:T(8,128)(2,1)S(1)}, bf16[256,640]{1,0:T(8,128)(2,1)S(1)}, u32[]{:S(2)}, u32[]{:S(2)}) collective-permute-start(bf16[256,640]{1,0:T(8,128)(2,1)S(1)} %constant_dynamic-update-slice_fusion.2.refs_0_), channel_id=1, source_target_pairs={{0,8},{10,2},{8,16},{18,10},{16,24},{26,18},{24,28},{30,26},{28,20... | collective-permute-start | bytes 983048 | tf_op jit(solution)/shard_map/output_far_2_0/ppermute | solution.py:94
  56.4 2.0 %collective-permute-start.20 = (bf16[256,640]{1,0:T(8,128)(2,1)S(1)}, bf16[256,640]{1,0:T(8,128)(2,1)S(1)}, u32[]{:S(2)}, u32[]{:S(2)}) collective-permute-start(bf16[256,640]{1,0:T(8,128)(2,1)S(1)} %collective-permute-done.19.refs_2_), channel_id=1, source_target_pairs={{0,8},{10,2},{8,16},{18,10},{16,24},{26,18},{24,28},{30,26},{28,20... | collective-permute-start | bytes 983048 | tf_op jit(solution)/shard_map/output_near_3_0/ppermute | solution.py:94
  58.4 1.7 %collective-permute-done.26.refs_0_ = bf16[256,640]{1,0:T(8,128)(2,1)S(1)} collective-permute-done((bf16[256,640]{1,0:T(8,128)(2,1)S(1)}, bf16[256,640]{1,0:T(8,128)(2,1)S(1)}, u32[]{:S(2)}, u32[]{:S(2)}) %collective-permute-start.26) | collective-permute-done | bytes 327712 | tf_op jit(solution)/shard_map/output_far_2_0/ppermute | solution.py:94
  60.1 1.8 %collective-permute-start.33 = (bf16[256,640]{1,0:T(8,128)(2,1)S(1)}, bf16[256,640]{1,0:T(8,128)(2,1)S(1)}, u32[]{:S(2)}, u32[]{:S(2)}) collective-permute-start(bf16[256,640]{1,0:T(8,128)(2,1)S(1)} %collective-permute-done.26.refs_0_), channel_id=1, source_target_pairs={{0,8},{10,2},{8,16},{18,10},{16,24},{26,18},{24,28},{30,26},{28,20... | collective-permute-start | bytes 983048 | tf_op jit(solution)/shard_map/output_far_3_0/ppermute | solution.py:94
  63.6 1.9 %collective-permute-start.21 = (bf16[256,640]{1,0:T(8,128)(2,1)S(1)}, bf16[256,640]{1,0:T(8,128)(2,1)S(1)}, u32[]{:S(2)}, u32[]{:S(2)}) collective-permute-start(bf16[256,640]{1,0:T(8,128)(2,1)S(1)} %collective-permute-done.20.refs_2_), channel_id=1, source_target_pairs={{0,8},{10,2},{8,16},{18,10},{16,24},{26,18},{24,28},{30,26},{28,20... | collective-permute-start | bytes 983048 | tf_op jit(solution)/shard_map/output_near_4_0/ppermute | solution.py:94
  65.5 1.7 %collective-permute-done.33.refs_0_ = bf16[256,640]{1,0:T(8,128)(2,1)S(1)} collective-permute-done((bf16[256,640]{1,0:T(8,128)(2,1)S(1)}, bf16[256,640]{1,0:T(8,128)(2,1)S(1)}, u32[]{:S(2)}, u32[]{:S(2)}) %collective-permute-start.33) | collective-permute-done | bytes 327712 | tf_op jit(solution)/shard_map/output_far_3_0/ppermute | solution.py:94
  67.8 2.9 %collective-permute-done.21.refs_2_ = bf16[256,640]{1,0:T(8,128)(2,1)S(1)} collective-permute-done((bf16[256,640]{1,0:T(8,128)(2,1)S(1)}, bf16[256,640]{1,0:T(8,128)(2,1)S(1)}, u32[]{:S(2)}, u32[]{:S(2)}) %collective-permute-start.21) | collective-permute-done | bytes 327712 | tf_op jit(solution)/shard_map/output_near_4_0/ppermute | solution.py:94
  (86 shorter events, 14.7 us)
Async XLA Ops:
  1.3 3.2 %collective-permute-start.1 = (bf16[264,640]{1,0:T(8,128)(2,1)S(1)}, bf16[264,640]{1,0:T(8,128)(2,1)S(1)}, u32[]{:S(2)}, u32[]{:S(2)}) collective-permute-start(bf16[264,640]{1,0:T(8,128)(2,1)S(1)} %prepare.1.refs_0_), channel_id=1, source_target_pairs={{0,2},{2,0},{4,6},{6,4},{8,10},{10,8},{12,14},{14,12},{16,18},{18,... | collective-permute-start | bytes 1013768 | tf_op jit(solution)/shard_map/projection_core_own_0/ppermute | solution.py:98
  1.8 7.7 %collective-permute-start = (bf16[264,640]{1,0:T(8,128)(2,1)S(1)}, bf16[264,640]{1,0:T(8,128)(2,1)S(1)}, u32[]{:S(2)}, u32[]{:S(2)}) collective-permute-start(bf16[264,640]{1,0:T(8,128)(2,1)S(1)} %prepare.1.refs_0_), channel_id=1, source_target_pairs={{0,8},{10,2},{8,16},{18,10},{16,24},{26,18},{24,28},{30,26},{28,20... | collective-permute-start | bytes 1013768 | tf_op jit(solution)/shard_map/projection_near_1_0/ppermute | solution.py:94
  4.5 8.6 %collective-permute-start.5 = (bf16[256,640]{1,0:T(8,128)(2,1)S(1)}, bf16[256,640]{1,0:T(8,128)(2,1)S(1)}, u32[]{:S(2)}, u32[]{:S(2)}) collective-permute-start(bf16[256,640]{1,0:T(8,128)(2,1)S(1)} %slice.4), channel_id=1, source_target_pairs={{0,8},{10,2},{8,16},{18,10},{16,24},{26,18},{24,28},{30,26},{28,20... | collective-permute-start | bytes 983048 | tf_op jit(solution)/shard_map/projection_far_1_0/ppermute | solution.py:94
  9.5 5.6 %collective-permute-start.9 = (bf16[264,640]{1,0:T(8,128)(2,1)S(1)}, bf16[264,640]{1,0:T(8,128)(2,1)S(1)}, u32[]{:S(2)}, u32[]{:S(2)}) collective-permute-start(bf16[264,640]{1,0:T(8,128)(2,1)S(1)} %collective-permute-done.near_ref.refs_2_), channel_id=1, source_target_pairs={{0,2},{2,0},{4,6},{6,4},{8,10},{10,8},{12,14},{14,12},{16,18},{18,... | collective-permute-start | bytes 1013768 | tf_op jit(solution)/shard_map/projection_core_near_1_0/ppermute | solution.py:98
  9.6 7.2 %collective-permute-start.2 = (bf16[264,640]{1,0:T(8,128)(2,1)S(1)}, bf16[264,640]{1,0:T(8,128)(2,1)S(1)}, u32[]{:S(2)}, u32[]{:S(2)}) collective-permute-start(bf16[264,640]{1,0:T(8,128)(2,1)S(1)} %pass_on.1), channel_id=1, source_target_pairs={{0,8},{10,2},{8,16},{18,10},{16,24},{26,18},{24,28},{30,26},{28,20... | collective-permute-start | bytes 1013768 | tf_op jit(solution)/shard_map/projection_near_2_0/ppermute | solution.py:94
  13.0 7.3 %collective-permute-start.6 = (bf16[256,640]{1,0:T(8,128)(2,1)S(1)}, bf16[256,640]{1,0:T(8,128)(2,1)S(1)}, u32[]{:S(2)}, u32[]{:S(2)}) collective-permute-start(bf16[256,640]{1,0:T(8,128)(2,1)S(1)} %collective-permute-done.5.refs_0_), channel_id=1, source_target_pairs={{0,8},{10,2},{8,16},{18,10},{16,24},{26,18},{24,28},{30,26},{28,20... | collective-permute-start | bytes 983048 | tf_op jit(solution)/shard_map/projection_far_2_0/ppermute | solution.py:94
  16.8 5.6 %collective-permute-start.10 = (bf16[264,640]{1,0:T(8,128)(2,1)S(1)}, bf16[264,640]{1,0:T(8,128)(2,1)S(1)}, u32[]{:S(2)}, u32[]{:S(2)}) collective-permute-start(bf16[264,640]{1,0:T(8,128)(2,1)S(1)} %collective-permute-done.2.refs_2_), channel_id=1, source_target_pairs={{0,2},{2,0},{4,6},{6,4},{8,10},{10,8},{12,14},{14,12},{16,18},{18,... | collective-permute-start | bytes 1013768 | tf_op jit(solution)/shard_map/projection_core_near_2_0/ppermute | solution.py:98
  16.8 7.2 %collective-permute-start.3 = (bf16[264,640]{1,0:T(8,128)(2,1)S(1)}, bf16[264,640]{1,0:T(8,128)(2,1)S(1)}, u32[]{:S(2)}, u32[]{:S(2)}) collective-permute-start(bf16[264,640]{1,0:T(8,128)(2,1)S(1)} %collective-permute-done.2.refs_2_), channel_id=1, source_target_pairs={{0,8},{10,2},{8,16},{18,10},{16,24},{26,18},{24,28},{30,26},{28,20... | collective-permute-start | bytes 1013768 | tf_op jit(solution)/shard_map/projection_near_3_0/ppermute | solution.py:94
  18.9 3.5 %collective-permute-start.8 = (bf16[256,640]{1,0:T(8,128)(2,1)S(1)}, bf16[256,640]{1,0:T(8,128)(2,1)S(1)}, u32[]{:S(2)}, u32[]{:S(2)}) collective-permute-start(bf16[256,640]{1,0:T(8,128)(2,1)S(1)} %collective-permute-done.5.refs_0_), channel_id=1, source_target_pairs={{0,2},{2,0},{4,6},{6,4},{8,10},{10,8},{12,14},{14,12},{16,18},{18,... | collective-permute-start | bytes 983048 | tf_op jit(solution)/shard_map/projection_core_far_1_0/ppermute | solution.py:98
  20.3 7.2 %collective-permute-start.13 = (bf16[256,640]{1,0:T(8,128)(2,1)S(1)}, bf16[256,640]{1,0:T(8,128)(2,1)S(1)}, u32[]{:S(2)}, u32[]{:S(2)}) collective-permute-start(bf16[256,640]{1,0:T(8,128)(2,1)S(1)} %collective-permute-done.6.refs_0_), channel_id=1, source_target_pairs={{0,8},{10,2},{8,16},{18,10},{16,24},{26,18},{24,28},{30,26},{28,20... | collective-permute-start | bytes 983048 | tf_op jit(solution)/shard_map/projection_far_3_0/ppermute | solution.py:94
  24.0 3.7 %collective-permute-start.11 = (bf16[264,640]{1,0:T(8,128)(2,1)S(1)}, bf16[264,640]{1,0:T(8,128)(2,1)S(1)}, u32[]{:S(2)}, u32[]{:S(2)}) collective-permute-start(bf16[264,640]{1,0:T(8,128)(2,1)S(1)} %collective-permute-done.3.refs_2_), channel_id=1, source_target_pairs={{0,2},{2,0},{4,6},{6,4},{8,10},{10,8},{12,14},{14,12},{16,18},{18,... | collective-permute-start | bytes 1013768 | tf_op jit(solution)/shard_map/projection_core_near_3_0/ppermute | solution.py:98
  24.0 7.2 %collective-permute-start.4 = (bf16[264,640]{1,0:T(8,128)(2,1)S(1)}, bf16[264,640]{1,0:T(8,128)(2,1)S(1)}, u32[]{:S(2)}, u32[]{:S(2)}) collective-permute-start(bf16[264,640]{1,0:T(8,128)(2,1)S(1)} %collective-permute-done.3.refs_2_), channel_id=1, source_target_pairs={{0,8},{10,2},{8,16},{18,10},{16,24},{26,18},{24,28},{30,26},{28,20... | collective-permute-start | bytes 1013768 | tf_op jit(solution)/shard_map/projection_near_4_0/ppermute | solution.py:94
  27.5 3.8 %collective-permute-start.14 = (bf16[256,640]{1,0:T(8,128)(2,1)S(1)}, bf16[256,640]{1,0:T(8,128)(2,1)S(1)}, u32[]{:S(2)}, u32[]{:S(2)}) collective-permute-start(bf16[256,640]{1,0:T(8,128)(2,1)S(1)} %collective-permute-done.13.refs_0_), channel_id=1, source_target_pairs={{0,2},{2,0},{4,6},{6,4},{8,10},{10,8},{12,14},{14,12},{16,18},{18,... | collective-permute-start | bytes 983048 | tf_op jit(solution)/shard_map/projection_core_far_3_0/ppermute | solution.py:98
  33.7 7.3 %collective-permute-start.15 = (bf16[136,640]{1,0:T(8,128)(2,1)S(1)}, bf16[136,640]{1,0:T(8,128)(2,1)S(1)}, u32[]{:S(2)}, u32[]{:S(2)}) collective-permute-start(bf16[136,640]{1,0:T(8,128)(2,1)S(1)} %projection_last.4), channel_id=1, source_target_pairs={{0,1},{1,0},{2,3},{3,2},{4,5},{5,4},{6,7},{7,6},{8,9},{9,8},{10,11... | collective-permute-start | bytes 522248 | tf_op jit(solution)/shard_map/ppermute | solution.py:650
  36.8 6.9 %collective-permute-start.17 = (bf16[128,640]{1,0:T(8,128)(2,1)S(1)}, bf16[128,640]{1,0:T(8,128)(2,1)S(1)}, u32[]{:S(2)}, u32[]{:S(2)}) collective-permute-start(bf16[128,640]{1,0:T(8,128)(2,1)S(1)} %projection_last.7), channel_id=1, source_target_pairs={{0,1},{1,0},{2,3},{3,2},{4,5},{5,4},{6,7},{7,6},{8,9},{9,8},{10,11... | collective-permute-start | bytes 491528 | tf_op jit(solution)/shard_map/ppermute | solution.py:650
  41.0 4.9 %collective-permute-start.22 = (bf16[128,640]{1,0:T(8,128)(2,1)S(1)}, bf16[128,640]{1,0:T(8,128)(2,1)S(1)}, u32[]{:S(2)}, u32[]{:S(2)}) collective-permute-start(bf16[128,640]{1,0:T(8,128)(2,1)S(1)} %far_part_1_0.1.refs_0_), channel_id=1, source_target_pairs={{0,2},{2,0},{4,6},{6,4},{8,10},{10,8},{12,14},{14,12},{16,18},{18,... | collective-permute-start | bytes 491528 | tf_op jit(solution)/shard_map/output_core_own_0/ppermute | solution.py:98
  41.0 6.4 %collective-permute-start.16 = (bf16[128,640]{1,0:T(8,128)(2,1)S(1)}, bf16[128,640]{1,0:T(8,128)(2,1)S(1)}, u32[]{:S(2)}, u32[]{:S(2)}) collective-permute-start(bf16[128,640]{1,0:T(8,128)(2,1)S(1)} %far_part_1_0.1.refs_0_), channel_id=1, source_target_pairs={{0,8},{10,2},{8,16},{18,10},{16,24},{26,18},{24,28},{30,26},{28,20... | collective-permute-start | bytes 491528 | tf_op jit(solution)/shard_map/output_near_1_0/ppermute | solution.py:94
  43.7 3.7 %collective-permute-start.24 = (bf16[128,640]{1,0:T(8,128)(2,1)S(1)}, bf16[128,640]{1,0:T(8,128)(2,1)S(1)}, u32[]{:S(2)}, u32[]{:S(2)}) collective-permute-start(bf16[128,640]{1,0:T(8,128)(2,1)S(1)} %far_part_1_128.1.refs_1_), channel_id=1, source_target_pairs={{0,2},{2,0},{4,6},{6,4},{8,10},{10,8},{12,14},{14,12},{16,18},{18,... | collective-permute-start | bytes 491528 | tf_op jit(solution)/shard_map/output_core_own_1/ppermute | solution.py:98
  43.8 5.4 %collective-permute-start.18 = (bf16[128,640]{1,0:T(8,128)(2,1)S(1)}, bf16[128,640]{1,0:T(8,128)(2,1)S(1)}, u32[]{:S(2)}, u32[]{:S(2)}) collective-permute-start(bf16[128,640]{1,0:T(8,128)(2,1)S(1)} %far_part_1_128.1.refs_1_), channel_id=1, source_target_pairs={{0,8},{10,2},{8,16},{18,10},{16,24},{26,18},{24,28},{30,26},{28,20... | collective-permute-start | bytes 491528 | tf_op jit(solution)/shard_map/output_near_1_1/ppermute | solution.py:94
  45.8 5.5 %collective-permute-start.23 = (bf16[128,640]{1,0:T(8,128)(2,1)S(1)}, bf16[128,640]{1,0:T(8,128)(2,1)S(1)}, u32[]{:S(2)}, u32[]{:S(2)}) collective-permute-start(bf16[128,640]{1,0:T(8,128)(2,1)S(1)} %collective-permute-done.22.refs_2_), channel_id=1, source_target_pairs={{0,8},{10,2},{8,16},{18,10},{16,24},{26,18},{24,28},{30,26},{28,20... | collective-permute-start | bytes 491528 | tf_op jit(solution)/shard_map/output_far_1_0/ppermute | solution.py:94
  47.5 5.5 %collective-permute-start.25 = (bf16[128,640]{1,0:T(8,128)(2,1)S(1)}, bf16[128,640]{1,0:T(8,128)(2,1)S(1)}, u32[]{:S(2)}, u32[]{:S(2)}) collective-permute-start(bf16[128,640]{1,0:T(8,128)(2,1)S(1)} %collective-permute-done.24.refs_3_), channel_id=1, source_target_pairs={{0,8},{10,2},{8,16},{18,10},{16,24},{26,18},{24,28},{30,26},{28,20... | collective-permute-start | bytes 491528 | tf_op jit(solution)/shard_map/output_far_1_1/ppermute | solution.py:94
  49.2 5.5 %collective-permute-start.29 = (bf16[256,640]{1,0:T(8,128)(2,1)S(1)}, bf16[256,640]{1,0:T(8,128)(2,1)S(1)}, u32[]{:S(2)}, u32[]{:S(2)}) collective-permute-start(bf16[256,640]{1,0:T(8,128)(2,1)S(1)} %constant_dynamic-update-slice_fusion.refs_4_), channel_id=1, source_target_pairs={{0,2},{2,0},{4,6},{6,4},{8,10},{10,8},{12,14},{14,12},{16,18},{18,... | collective-permute-start | bytes 983048 | tf_op jit(solution)/shard_map/output_core_near_1_0/ppermute | solution.py:98
  49.3 7.1 %collective-permute-start.19 = (bf16[256,640]{1,0:T(8,128)(2,1)S(1)}, bf16[256,640]{1,0:T(8,128)(2,1)S(1)}, u32[]{:S(2)}, u32[]{:S(2)}) collective-permute-start(bf16[256,640]{1,0:T(8,128)(2,1)S(1)} %constant_dynamic-update-slice_fusion.refs_4_), channel_id=1, source_target_pairs={{0,8},{10,2},{8,16},{18,10},{16,24},{26,18},{24,28},{30,26},{28,20... | collective-permute-start | bytes 983048 | tf_op jit(solution)/shard_map/output_near_2_0/ppermute | solution.py:94
  52.9 7.1 %collective-permute-start.26 = (bf16[256,640]{1,0:T(8,128)(2,1)S(1)}, bf16[256,640]{1,0:T(8,128)(2,1)S(1)}, u32[]{:S(2)}, u32[]{:S(2)}) collective-permute-start(bf16[256,640]{1,0:T(8,128)(2,1)S(1)} %constant_dynamic-update-slice_fusion.2.refs_0_), channel_id=1, source_target_pairs={{0,8},{10,2},{8,16},{18,10},{16,24},{26,18},{24,28},{30,26},{28,20... | collective-permute-start | bytes 983048 | tf_op jit(solution)/shard_map/output_far_2_0/ppermute | solution.py:94
  54.7 7.2 %collective-permute-start.28 = (bf16[256,640]{1,0:T(8,128)(2,1)S(1)}, bf16[256,640]{1,0:T(8,128)(2,1)S(1)}, u32[]{:S(2)}, u32[]{:S(2)}) collective-permute-start(bf16[256,640]{1,0:T(8,128)(2,1)S(1)} %constant_dynamic-update-slice_fusion.2.refs_0_), channel_id=1, source_target_pairs={{0,2},{2,0},{4,6},{6,4},{8,10},{10,8},{12,14},{14,12},{16,18},{18,... | collective-permute-start | bytes 983048 | tf_op jit(solution)/shard_map/output_core_far_1_0/ppermute | solution.py:98
  56.4 5.5 %collective-permute-start.30 = (bf16[256,640]{1,0:T(8,128)(2,1)S(1)}, bf16[256,640]{1,0:T(8,128)(2,1)S(1)}, u32[]{:S(2)}, u32[]{:S(2)}) collective-permute-start(bf16[256,640]{1,0:T(8,128)(2,1)S(1)} %collective-permute-done.19.refs_2_), channel_id=1, source_target_pairs={{0,2},{2,0},{4,6},{6,4},{8,10},{10,8},{12,14},{14,12},{16,18},{18,... | collective-permute-start | bytes 983048 | tf_op jit(solution)/shard_map/output_core_near_2_0/ppermute | solution.py:98
  56.4 7.1 %collective-permute-start.20 = (bf16[256,640]{1,0:T(8,128)(2,1)S(1)}, bf16[256,640]{1,0:T(8,128)(2,1)S(1)}, u32[]{:S(2)}, u32[]{:S(2)}) collective-permute-start(bf16[256,640]{1,0:T(8,128)(2,1)S(1)} %collective-permute-done.19.refs_2_), channel_id=1, source_target_pairs={{0,8},{10,2},{8,16},{18,10},{16,24},{26,18},{24,28},{30,26},{28,20... | collective-permute-start | bytes 983048 | tf_op jit(solution)/shard_map/output_near_3_0/ppermute | solution.py:94
  60.1 7.1 %collective-permute-start.33 = (bf16[256,640]{1,0:T(8,128)(2,1)S(1)}, bf16[256,640]{1,0:T(8,128)(2,1)S(1)}, u32[]{:S(2)}, u32[]{:S(2)}) collective-permute-start(bf16[256,640]{1,0:T(8,128)(2,1)S(1)} %collective-permute-done.26.refs_0_), channel_id=1, source_target_pairs={{0,8},{10,2},{8,16},{18,10},{16,24},{26,18},{24,28},{30,26},{28,20... | collective-permute-start | bytes 983048 | tf_op jit(solution)/shard_map/output_far_3_0/ppermute | solution.py:94
  61.9 5.3 %collective-permute-start.27 = (bf16[256,640]{1,0:T(8,128)(2,1)S(1)}, bf16[256,640]{1,0:T(8,128)(2,1)S(1)}, u32[]{:S(2)}, u32[]{:S(2)}) collective-permute-start(bf16[256,640]{1,0:T(8,128)(2,1)S(1)} %collective-permute-done.26.refs_0_), channel_id=1, source_target_pairs={{0,2},{2,0},{4,6},{6,4},{8,10},{10,8},{12,14},{14,12},{16,18},{18,... | collective-permute-start | bytes 983048 | tf_op jit(solution)/shard_map/output_core_far_2_0/ppermute | solution.py:98
  63.6 3.6 %collective-permute-start.31 = (bf16[256,640]{1,0:T(8,128)(2,1)S(1)}, bf16[256,640]{1,0:T(8,128)(2,1)S(1)}, u32[]{:S(2)}, u32[]{:S(2)}) collective-permute-start(bf16[256,640]{1,0:T(8,128)(2,1)S(1)} %collective-permute-done.20.refs_2_), channel_id=1, source_target_pairs={{0,2},{2,0},{4,6},{6,4},{8,10},{10,8},{12,14},{14,12},{16,18},{18,... | collective-permute-start | bytes 983048 | tf_op jit(solution)/shard_map/output_core_near_3_0/ppermute | solution.py:98
  63.6 7.1 %collective-permute-start.21 = (bf16[256,640]{1,0:T(8,128)(2,1)S(1)}, bf16[256,640]{1,0:T(8,128)(2,1)S(1)}, u32[]{:S(2)}, u32[]{:S(2)}) collective-permute-start(bf16[256,640]{1,0:T(8,128)(2,1)S(1)} %collective-permute-done.20.refs_2_), channel_id=1, source_target_pairs={{0,8},{10,2},{8,16},{18,10},{16,24},{26,18},{24,28},{30,26},{28,20... | collective-permute-start | bytes 983048 | tf_op jit(solution)/shard_map/output_near_4_0/ppermute | solution.py:94
  67.1 3.5 %collective-permute-start.34 = (bf16[256,640]{1,0:T(8,128)(2,1)S(1)}, bf16[256,640]{1,0:T(8,128)(2,1)S(1)}, u32[]{:S(2)}, u32[]{:S(2)}) collective-permute-start(bf16[256,640]{1,0:T(8,128)(2,1)S(1)} %collective-permute-done.33.refs_0_), channel_id=1, source_target_pairs={{0,2},{2,0},{4,6},{6,4},{8,10},{10,8},{12,14},{14,12},{16,18},{18,... | collective-permute-start | bytes 983048 | tf_op jit(solution)/shard_map/output_core_far_3_0/ppermute | solution.py:98
  (14 other events, 54.1 us)

commit v11 on v10

--- a/solution.py
+++ b/solution.py
@@ -677,8 +677,7 @@
     moving = [message(0, running)]
     results = [last(projection_finish(features, w_short, tokens, k), running) for k in range(2)]
     projected, first_blocks, gated = zip(*results)
-    later, gated = lax.optimization_barrier((running, gated))
-    moving.append(message(1, later))
+    moving.append(message(1, running))
     query, totals, ready = own_part(
         projected, gated, moving if exact else None, w_short, filters, forward, inverse, skip_gain
     )

time: 73.4 us -> 73.4 us (level)
  no operation moved by 1% of the time
where the time goes in v11:
time: 73.4 us; the launch traced here: 73.3 us
  starting transfers between devices  34 us (46%)
  waiting for transfers between devices  22.7 us (31%)
  Pallas kernels  14.9 us (20%)
  local copies, waits for them, and re-layouts  1.39 us (2%)
    ppermute x16, starting transfers between devices, along_ring(): return lax.ppermute(block, 'fsdp', pairs)  31.4 us
    ppermute x16, waiting for transfers between devices, along_ring(): return lax.ppermute(block, 'fsdp', pairs)  18.8 us
    pallas_call x13, Pallas kernels, products(): pl.pallas_call(kernel, in_specs=[in_vmem] * (count + 1 + len(state) + len...  11.8 us
    ppermute x2, waiting for transfers between devices, from_before(): lax.ppermute(block, 'ctx', [(i, (i + 1) % count) for i in range(count)])  2.17 us
    pallas_call x1, Pallas kernels, own_part(): pl.pallas_call(kernel, in_specs=[in_vmem] * len(inputs), out_specs=[in_vm...  2 us
    ppermute x17, waiting for transfers between devices, other_core(): lax.ppermute(block, 'fsdp', [(i, i ^ 1) for i in range(2 * chip_count())])  1.77 us
    ppermute x2, starting transfers between devices, from_before(): lax.ppermute(block, 'ctx', [(i, (i + 1) % count) for i in range(count)])  1.47 us
  transfers between devices with their start and end apart: 35, of which 18 were waited for; matrix products, arithmetic and copies ran while one was open for 0% of the time, Pallas kernels for 18%

profile of v11, /device:TPU:0, one launch (start us, length us, event | category | flops | bytes accessed | tf_op | source)
XLA Modules:
  0.0 73.3 jit_solution(6451586601716133880)
XLA Ops:
  1.8 2.6 %collective-permute-start = (bf16[264,640]{1,0:T(8,128)(2,1)S(1)}, bf16[264,640]{1,0:T(8,128)(2,1)S(1)}, u32[]{:S(2)}, u32[]{:S(2)}) collective-permute-start(bf16[264,640]{1,0:T(8,128)(2,1)S(1)} %prepare.1.refs_0_), channel_id=1, source_target_pairs={{0,8},{10,2},{8,16},{18,10},{16,24},{26,18},{24,28},{30,26},{28,20... | collective-permute-start | bytes 1013768 | tf_op jit(solution)/shard_map/projection_near_1_0/ppermute | solution.py:94
  4.5 1.6 %collective-permute-start.5 = (bf16[256,640]{1,0:T(8,128)(2,1)S(1)}, bf16[256,640]{1,0:T(8,128)(2,1)S(1)}, u32[]{:S(2)}, u32[]{:S(2)}) collective-permute-start(bf16[256,640]{1,0:T(8,128)(2,1)S(1)} %slice.4), channel_id=1, source_target_pairs={{0,8},{10,2},{8,16},{18,10},{16,24},{26,18},{24,28},{30,26},{28,20... | collective-permute-start | bytes 983048 | tf_op jit(solution)/shard_map/projection_far_1_0/ppermute | solution.py:94
  7.0 2.6 %collective-permute-done.near_ref.refs_2_ = bf16[264,640]{1,0:T(8,128)(2,1)S(1)} collective-permute-done((bf16[264,640]{1,0:T(8,128)(2,1)S(1)}, bf16[264,640]{1,0:T(8,128)(2,1)S(1)}, u32[]{:S(2)}, u32[]{:S(2)}) %collective-permute-start) | collective-permute-done | bytes 337952 | tf_op jit(solution)/shard_map/projection_near_1_0/ppermute | solution.py:94
  9.6 2.1 %collective-permute-start.2 = (bf16[264,640]{1,0:T(8,128)(2,1)S(1)}, bf16[264,640]{1,0:T(8,128)(2,1)S(1)}, u32[]{:S(2)}, u32[]{:S(2)}) collective-permute-start(bf16[264,640]{1,0:T(8,128)(2,1)S(1)} %pass_on.1), channel_id=1, source_target_pairs={{0,8},{10,2},{8,16},{18,10},{16,24},{26,18},{24,28},{30,26},{28,20... | collective-permute-start | bytes 1013768 | tf_op jit(solution)/shard_map/projection_near_2_0/ppermute | solution.py:94
  11.7 1.3 %collective-permute-done.5.refs_0_ = bf16[256,640]{1,0:T(8,128)(2,1)S(1)} collective-permute-done((bf16[256,640]{1,0:T(8,128)(2,1)S(1)}, bf16[256,640]{1,0:T(8,128)(2,1)S(1)}, u32[]{:S(2)}, u32[]{:S(2)}) %collective-permute-start.5) | collective-permute-done | bytes 327712 | tf_op jit(solution)/shard_map/projection_far_1_0/ppermute | solution.py:94
  13.0 2.1 %collective-permute-start.6 = (bf16[256,640]{1,0:T(8,128)(2,1)S(1)}, bf16[256,640]{1,0:T(8,128)(2,1)S(1)}, u32[]{:S(2)}, u32[]{:S(2)}) collective-permute-start(bf16[256,640]{1,0:T(8,128)(2,1)S(1)} %collective-permute-done.5.refs_0_), channel_id=1, source_target_pairs={{0,8},{10,2},{8,16},{18,10},{16,24},{26,18},{24,28},{30,26},{28,20... | collective-permute-start | bytes 983048 | tf_op jit(solution)/shard_map/projection_far_2_0/ppermute | solution.py:94
  15.1 1.4 %projection_1.1 = (f32[3,256,640]{2,1,0:T(8,128)S(1)}, f32[8,640]{1,0:T(8,128)S(1)}) custom-call(bf16[264,640]{1,0:T(8,128)(2,1)S(1)} %prepare.1.refs_0_, bf16[264,640]{1,0:T(8,128)(2,1)S(1)} %collective-permute-done.1.far_ref.refs_1_, bf16[264,640]{1,0:T(8,128)(2,1)S(1)} %collective-permute-done.near_ref.refs_2_, ...), custom_call_target="tpu_custom_call" | custom-call | tf_op jit(solution)/shard_map/projection_1/pallas_call | solution.py:203
  16.8 2.1 %collective-permute-start.3 = (bf16[264,640]{1,0:T(8,128)(2,1)S(1)}, bf16[264,640]{1,0:T(8,128)(2,1)S(1)}, u32[]{:S(2)}, u32[]{:S(2)}) collective-permute-start(bf16[264,640]{1,0:T(8,128)(2,1)S(1)} %collective-permute-done.2.refs_2_), channel_id=1, source_target_pairs={{0,8},{10,2},{8,16},{18,10},{16,24},{26,18},{24,28},{30,26},{28,20... | collective-permute-start | bytes 1013768 | tf_op jit(solution)/shard_map/projection_near_3_0/ppermute | solution.py:94
  19.0 1.3 %collective-permute-done.6.refs_0_ = bf16[256,640]{1,0:T(8,128)(2,1)S(1)} collective-permute-done((bf16[256,640]{1,0:T(8,128)(2,1)S(1)}, bf16[256,640]{1,0:T(8,128)(2,1)S(1)}, u32[]{:S(2)}, u32[]{:S(2)}) %collective-permute-start.6) | collective-permute-done | bytes 327712 | tf_op jit(solution)/shard_map/projection_far_2_0/ppermute | solution.py:94
  20.3 2.1 %collective-permute-start.13 = (bf16[256,640]{1,0:T(8,128)(2,1)S(1)}, bf16[256,640]{1,0:T(8,128)(2,1)S(1)}, u32[]{:S(2)}, u32[]{:S(2)}) collective-permute-start(bf16[256,640]{1,0:T(8,128)(2,1)S(1)} %collective-permute-done.6.refs_0_), channel_id=1, source_target_pairs={{0,8},{10,2},{8,16},{18,10},{16,24},{26,18},{24,28},{30,26},{28,20... | collective-permute-start | bytes 983048 | tf_op jit(solution)/shard_map/projection_far_3_0/ppermute | solution.py:94
  22.4 1.6 %projection_2.1 = (f32[3,256,640]{2,1,0:T(8,128)S(1)}, f32[8,640]{1,0:T(8,128)S(1)}) custom-call(bf16[256,640]{1,0:T(8,128)(2,1)S(1)} %collective-permute-done.5.refs_0_, bf16[256,640]{1,0:T(8,128)(2,1)S(1)} %collective-permute-done.8.refs_1_, bf16[264,640]{1,0:T(8,128)(2,1)S(1)} %collective-permute-done.2.refs_2_, ...), custom_call_target="tpu_custom_call", output_to_operand_aliasing={{0}: (5, {}), {1}: (6, {})} | custom-call | tf_op jit(solution)/shard_map/projection_2/pallas_call | solution.py:203
  24.0 2.0 %collective-permute-start.4 = (bf16[264,640]{1,0:T(8,128)(2,1)S(1)}, bf16[264,640]{1,0:T(8,128)(2,1)S(1)}, u32[]{:S(2)}, u32[]{:S(2)}) collective-permute-start(bf16[264,640]{1,0:T(8,128)(2,1)S(1)} %collective-permute-done.3.refs_2_), channel_id=1, source_target_pairs={{0,8},{10,2},{8,16},{18,10},{16,24},{26,18},{24,28},{30,26},{28,20... | collective-permute-start | bytes 1013768 | tf_op jit(solution)/shard_map/projection_near_4_0/ppermute | solution.py:94
  26.2 1.3 %collective-permute-done.13.refs_0_ = bf16[256,640]{1,0:T(8,128)(2,1)S(1)} collective-permute-done((bf16[256,640]{1,0:T(8,128)(2,1)S(1)}, bf16[256,640]{1,0:T(8,128)(2,1)S(1)}, u32[]{:S(2)}, u32[]{:S(2)}) %collective-permute-start.13) | collective-permute-done | bytes 327712 | tf_op jit(solution)/shard_map/projection_far_3_0/ppermute | solution.py:94
  27.7 1.6 %projection_3.1 = (f32[3,256,640]{2,1,0:T(8,128)S(1)}, f32[8,640]{1,0:T(8,128)S(1)}) custom-call(bf16[256,640]{1,0:T(8,128)(2,1)S(1)} %collective-permute-done.6.refs_0_, bf16[256,640]{1,0:T(8,128)(2,1)S(1)} %collective-permute-done.7.refs_1_, bf16[264,640]{1,0:T(8,128)(2,1)S(1)} %collective-permute-done.3.refs_2_, ...), custom_call_target="tpu_custom_call", output_to_operand_aliasing={{0}: (5, {}), {1}: (6, {})} | custom-call | tf_op jit(solution)/shard_map/projection_3/pallas_call | solution.py:203
  29.3 2.0 %collective-permute-done.4.refs_2_ = bf16[264,640]{1,0:T(8,128)(2,1)S(1)} collective-permute-done((bf16[264,640]{1,0:T(8,128)(2,1)S(1)}, bf16[264,640]{1,0:T(8,128)(2,1)S(1)}, u32[]{:S(2)}, u32[]{:S(2)}) %collective-permute-start.4) | collective-permute-done | bytes 337952 | tf_op jit(solution)/shard_map/projection_near_4_0/ppermute | solution.py:94
  31.3 1.2 %projection_4.1 = (f32[3,256,640]{2,1,0:T(8,128)S(1)}, f32[8,640]{1,0:T(8,128)S(1)}) custom-call(bf16[256,640]{1,0:T(8,128)(2,1)S(1)} %collective-permute-done.13.refs_0_, bf16[256,640]{1,0:T(8,128)(2,1)S(1)} %collective-permute-done.14.refs_1_, bf16[264,640]{1,0:T(8,128)(2,1)S(1)} %collective-permute-done.4.refs_2_, ...), custom_call_target="tpu_custom_call", output_to_operand_aliasing={{0}: (4, {}), {1}: (5, {})} | custom-call | flops 2000000000 | tf_op jit(solution)/shard_map/projection_4/pallas_call | solution.py:203
  33.7 1.1 %collective-permute-start.15 = (bf16[136,640]{1,0:T(8,128)(2,1)S(1)}, bf16[136,640]{1,0:T(8,128)(2,1)S(1)}, u32[]{:S(2)}, u32[]{:S(2)}) collective-permute-start(bf16[136,640]{1,0:T(8,128)(2,1)S(1)} %projection_last.4), channel_id=1, source_target_pairs={{0,1},{1,0},{2,3},{3,2},{4,5},{5,4},{6,7},{7,6},{8,9},{9,8},{10,11... | collective-permute-start | bytes 522248 | tf_op jit(solution)/shard_map/ppermute | solution.py:650
  37.4 2.0 %own_part.1 = (f32[128,640]{1,0:T(8,128)S(1)}, f32[128,640]{1,0:T(8,128)S(1)}, f32[128,1280]{1,0:T(8,128)S(1)}, f32[128,1280]{1,0:T(8,128)S(1)}, bf16[128,640]{1...) custom-call(bf16[3,128,640]{2,1,0:T(8,128)(2,1)S(1)} %get-tuple-element.60.refs_0_, ...), custom_call_target="tpu_custom_call" | custom-call | tf_op jit(solution)/shard_map/own_part/pallas_call | solution.py:562
  39.4 1.6 %collective-permute-done.15.refs_0_.refs_6_ = bf16[136,640]{1,0:T(8,128)(2,1)S(1)} collective-permute-done((bf16[136,640]{1,0:T(8,128)(2,1)S(1)}, bf16[136,640]{1,0:T(8,128)(2,1)S(1)}, u32[]{:S(2)}, u32[]{:S(2)}) %collective-permute-start.15) | collective-permute-done | bytes 174112 | tf_op jit(solution)/shard_map/ppermute | solution.py:650
  41.1 2.0 %collective-permute-start.16 = (bf16[128,640]{1,0:T(8,128)(2,1)S(1)}, bf16[128,640]{1,0:T(8,128)(2,1)S(1)}, u32[]{:S(2)}, u32[]{:S(2)}) collective-permute-start(bf16[128,640]{1,0:T(8,128)(2,1)S(1)} %far_part_1_0.1.refs_0_), channel_id=1, source_target_pairs={{0,8},{10,2},{8,16},{18,10},{16,24},{26,18},{24,28},{30,26},{28,20... | collective-permute-start | bytes 491528 | tf_op jit(solution)/shard_map/output_near_1_0/ppermute | solution.py:94
  43.8 2.0 %collective-permute-start.18 = (bf16[128,640]{1,0:T(8,128)(2,1)S(1)}, bf16[128,640]{1,0:T(8,128)(2,1)S(1)}, u32[]{:S(2)}, u32[]{:S(2)}) collective-permute-start(bf16[128,640]{1,0:T(8,128)(2,1)S(1)} %far_part_1_128.1.refs_1_), channel_id=1, source_target_pairs={{0,8},{10,2},{8,16},{18,10},{16,24},{26,18},{24,28},{30,26},{28,20... | collective-permute-start | bytes 491528 | tf_op jit(solution)/shard_map/output_near_1_1/ppermute | solution.py:94
  45.8 1.6 %collective-permute-start.23 = (bf16[128,640]{1,0:T(8,128)(2,1)S(1)}, bf16[128,640]{1,0:T(8,128)(2,1)S(1)}, u32[]{:S(2)}, u32[]{:S(2)}) collective-permute-start(bf16[128,640]{1,0:T(8,128)(2,1)S(1)} %collective-permute-done.22.refs_2_), channel_id=1, source_target_pairs={{0,8},{10,2},{8,16},{18,10},{16,24},{26,18},{24,28},{30,26},{28,20... | collective-permute-start | bytes 491528 | tf_op jit(solution)/shard_map/output_far_1_0/ppermute | solution.py:94
  47.5 1.6 %collective-permute-start.25 = (bf16[128,640]{1,0:T(8,128)(2,1)S(1)}, bf16[128,640]{1,0:T(8,128)(2,1)S(1)}, u32[]{:S(2)}, u32[]{:S(2)}) collective-permute-start(bf16[128,640]{1,0:T(8,128)(2,1)S(1)} %collective-permute-done.24.refs_3_), channel_id=1, source_target_pairs={{0,8},{10,2},{8,16},{18,10},{16,24},{26,18},{24,28},{30,26},{28,20... | collective-permute-start | bytes 491528 | tf_op jit(solution)/shard_map/output_far_1_1/ppermute | solution.py:94
  49.3 2.0 %collective-permute-start.19 = (bf16[256,640]{1,0:T(8,128)(2,1)S(1)}, bf16[256,640]{1,0:T(8,128)(2,1)S(1)}, u32[]{:S(2)}, u32[]{:S(2)}) collective-permute-start(bf16[256,640]{1,0:T(8,128)(2,1)S(1)} %constant_dynamic-update-slice_fusion.refs_4_), channel_id=1, source_target_pairs={{0,8},{10,2},{8,16},{18,10},{16,24},{26,18},{24,28},{30,26},{28,20... | collective-permute-start | bytes 983048 | tf_op jit(solution)/shard_map/output_near_2_0/ppermute | solution.py:94
  51.3 1.6 %collective-permute-done.25 = bf16[128,640]{1,0:T(8,128)(2,1)S(1)} collective-permute-done((bf16[128,640]{1,0:T(8,128)(2,1)S(1)}, bf16[128,640]{1,0:T(8,128)(2,1)S(1)}, u32[]{:S(2)}, u32[]{:S(2)}) %collective-permute-start.25) | collective-permute-done | bytes 163872 | tf_op jit(solution)/shard_map/output_far_1_1/ppermute | solution.py:94
  52.9 1.8 %collective-permute-start.26 = (bf16[256,640]{1,0:T(8,128)(2,1)S(1)}, bf16[256,640]{1,0:T(8,128)(2,1)S(1)}, u32[]{:S(2)}, u32[]{:S(2)}) collective-permute-start(bf16[256,640]{1,0:T(8,128)(2,1)S(1)} %constant_dynamic-update-slice_fusion.2.refs_0_), channel_id=1, source_target_pairs={{0,8},{10,2},{8,16},{18,10},{16,24},{26,18},{24,28},{30,26},{28,20... | collective-permute-start | bytes 983048 | tf_op jit(solution)/shard_map/output_far_2_0/ppermute | solution.py:94
  56.4 2.0 %collective-permute-start.20 = (bf16[256,640]{1,0:T(8,128)(2,1)S(1)}, bf16[256,640]{1,0:T(8,128)(2,1)S(1)}, u32[]{:S(2)}, u32[]{:S(2)}) collective-permute-start(bf16[256,640]{1,0:T(8,128)(2,1)S(1)} %collective-permute-done.19.refs_2_), channel_id=1, source_target_pairs={{0,8},{10,2},{8,16},{18,10},{16,24},{26,18},{24,28},{30,26},{28,20... | collective-permute-start | bytes 983048 | tf_op jit(solution)/shard_map/output_near_3_0/ppermute | solution.py:94
  58.4 1.7 %collective-permute-done.26.refs_0_ = bf16[256,640]{1,0:T(8,128)(2,1)S(1)} collective-permute-done((bf16[256,640]{1,0:T(8,128)(2,1)S(1)}, bf16[256,640]{1,0:T(8,128)(2,1)S(1)}, u32[]{:S(2)}, u32[]{:S(2)}) %collective-permute-start.26) | collective-permute-done | bytes 327712 | tf_op jit(solution)/shard_map/output_far_2_0/ppermute | solution.py:94
  60.1 1.8 %collective-permute-start.33 = (bf16[256,640]{1,0:T(8,128)(2,1)S(1)}, bf16[256,640]{1,0:T(8,128)(2,1)S(1)}, u32[]{:S(2)}, u32[]{:S(2)}) collective-permute-start(bf16[256,640]{1,0:T(8,128)(2,1)S(1)} %collective-permute-done.26.refs_0_), channel_id=1, source_target_pairs={{0,8},{10,2},{8,16},{18,10},{16,24},{26,18},{24,28},{30,26},{28,20... | collective-permute-start | bytes 983048 | tf_op jit(solution)/shard_map/output_far_3_0/ppermute | solution.py:94
  63.6 1.9 %collective-permute-start.21 = (bf16[256,640]{1,0:T(8,128)(2,1)S(1)}, bf16[256,640]{1,0:T(8,128)(2,1)S(1)}, u32[]{:S(2)}, u32[]{:S(2)}) collective-permute-start(bf16[256,640]{1,0:T(8,128)(2,1)S(1)} %collective-permute-done.20.refs_2_), channel_id=1, source_target_pairs={{0,8},{10,2},{8,16},{18,10},{16,24},{26,18},{24,28},{30,26},{28,20... | collective-permute-start | bytes 983048 | tf_op jit(solution)/shard_map/output_near_4_0/ppermute | solution.py:94
  65.5 1.7 %collective-permute-done.33.refs_0_ = bf16[256,640]{1,0:T(8,128)(2,1)S(1)} collective-permute-done((bf16[256,640]{1,0:T(8,128)(2,1)S(1)}, bf16[256,640]{1,0:T(8,128)(2,1)S(1)}, u32[]{:S(2)}, u32[]{:S(2)}) %collective-permute-start.33) | collective-permute-done | bytes 327712 | tf_op jit(solution)/shard_map/output_far_3_0/ppermute | solution.py:94
  67.8 2.9 %collective-permute-done.21.refs_2_ = bf16[256,640]{1,0:T(8,128)(2,1)S(1)} collective-permute-done((bf16[256,640]{1,0:T(8,128)(2,1)S(1)}, bf16[256,640]{1,0:T(8,128)(2,1)S(1)}, u32[]{:S(2)}, u32[]{:S(2)}) %collective-permute-start.21) | collective-permute-done | bytes 327712 | tf_op jit(solution)/shard_map/output_near_4_0/ppermute | solution.py:94
  (86 shorter events, 14.9 us)
Async XLA Ops:
  1.3 3.2 %collective-permute-start.1 = (bf16[264,640]{1,0:T(8,128)(2,1)S(1)}, bf16[264,640]{1,0:T(8,128)(2,1)S(1)}, u32[]{:S(2)}, u32[]{:S(2)}) collective-permute-start(bf16[264,640]{1,0:T(8,128)(2,1)S(1)} %prepare.1.refs_0_), channel_id=1, source_target_pairs={{0,2},{2,0},{4,6},{6,4},{8,10},{10,8},{12,14},{14,12},{16,18},{18,... | collective-permute-start | bytes 1013768 | tf_op jit(solution)/shard_map/projection_core_own_0/ppermute | solution.py:98
  1.8 7.7 %collective-permute-start = (bf16[264,640]{1,0:T(8,128)(2,1)S(1)}, bf16[264,640]{1,0:T(8,128)(2,1)S(1)}, u32[]{:S(2)}, u32[]{:S(2)}) collective-permute-start(bf16[264,640]{1,0:T(8,128)(2,1)S(1)} %prepare.1.refs_0_), channel_id=1, source_target_pairs={{0,8},{10,2},{8,16},{18,10},{16,24},{26,18},{24,28},{30,26},{28,20... | collective-permute-start | bytes 1013768 | tf_op jit(solution)/shard_map/projection_near_1_0/ppermute | solution.py:94
  4.5 8.6 %collective-permute-start.5 = (bf16[256,640]{1,0:T(8,128)(2,1)S(1)}, bf16[256,640]{1,0:T(8,128)(2,1)S(1)}, u32[]{:S(2)}, u32[]{:S(2)}) collective-permute-start(bf16[256,640]{1,0:T(8,128)(2,1)S(1)} %slice.4), channel_id=1, source_target_pairs={{0,8},{10,2},{8,16},{18,10},{16,24},{26,18},{24,28},{30,26},{28,20... | collective-permute-start | bytes 983048 | tf_op jit(solution)/shard_map/projection_far_1_0/ppermute | solution.py:94
  9.5 5.6 %collective-permute-start.9 = (bf16[264,640]{1,0:T(8,128)(2,1)S(1)}, bf16[264,640]{1,0:T(8,128)(2,1)S(1)}, u32[]{:S(2)}, u32[]{:S(2)}) collective-permute-start(bf16[264,640]{1,0:T(8,128)(2,1)S(1)} %collective-permute-done.near_ref.refs_2_), channel_id=1, source_target_pairs={{0,2},{2,0},{4,6},{6,4},{8,10},{10,8},{12,14},{14,12},{16,18},{18,... | collective-permute-start | bytes 1013768 | tf_op jit(solution)/shard_map/projection_core_near_1_0/ppermute | solution.py:98
  9.6 7.2 %collective-permute-start.2 = (bf16[264,640]{1,0:T(8,128)(2,1)S(1)}, bf16[264,640]{1,0:T(8,128)(2,1)S(1)}, u32[]{:S(2)}, u32[]{:S(2)}) collective-permute-start(bf16[264,640]{1,0:T(8,128)(2,1)S(1)} %pass_on.1), channel_id=1, source_target_pairs={{0,8},{10,2},{8,16},{18,10},{16,24},{26,18},{24,28},{30,26},{28,20... | collective-permute-start | bytes 1013768 | tf_op jit(solution)/shard_map/projection_near_2_0/ppermute | solution.py:94
  13.0 7.3 %collective-permute-start.6 = (bf16[256,640]{1,0:T(8,128)(2,1)S(1)}, bf16[256,640]{1,0:T(8,128)(2,1)S(1)}, u32[]{:S(2)}, u32[]{:S(2)}) collective-permute-start(bf16[256,640]{1,0:T(8,128)(2,1)S(1)} %collective-permute-done.5.refs_0_), channel_id=1, source_target_pairs={{0,8},{10,2},{8,16},{18,10},{16,24},{26,18},{24,28},{30,26},{28,20... | collective-permute-start | bytes 983048 | tf_op jit(solution)/shard_map/projection_far_2_0/ppermute | solution.py:94
  16.8 5.6 %collective-permute-start.10 = (bf16[264,640]{1,0:T(8,128)(2,1)S(1)}, bf16[264,640]{1,0:T(8,128)(2,1)S(1)}, u32[]{:S(2)}, u32[]{:S(2)}) collective-permute-start(bf16[264,640]{1,0:T(8,128)(2,1)S(1)} %collective-permute-done.2.refs_2_), channel_id=1, source_target_pairs={{0,2},{2,0},{4,6},{6,4},{8,10},{10,8},{12,14},{14,12},{16,18},{18,... | collective-permute-start | bytes 1013768 | tf_op jit(solution)/shard_map/projection_core_near_2_0/ppermute | solution.py:98
  16.8 7.2 %collective-permute-start.3 = (bf16[264,640]{1,0:T(8,128)(2,1)S(1)}, bf16[264,640]{1,0:T(8,128)(2,1)S(1)}, u32[]{:S(2)}, u32[]{:S(2)}) collective-permute-start(bf16[264,640]{1,0:T(8,128)(2,1)S(1)} %collective-permute-done.2.refs_2_), channel_id=1, source_target_pairs={{0,8},{10,2},{8,16},{18,10},{16,24},{26,18},{24,28},{30,26},{28,20... | collective-permute-start | bytes 1013768 | tf_op jit(solution)/shard_map/projection_near_3_0/ppermute | solution.py:94
  18.9 3.5 %collective-permute-start.8 = (bf16[256,640]{1,0:T(8,128)(2,1)S(1)}, bf16[256,640]{1,0:T(8,128)(2,1)S(1)}, u32[]{:S(2)}, u32[]{:S(2)}) collective-permute-start(bf16[256,640]{1,0:T(8,128)(2,1)S(1)} %collective-permute-done.5.refs_0_), channel_id=1, source_target_pairs={{0,2},{2,0},{4,6},{6,4},{8,10},{10,8},{12,14},{14,12},{16,18},{18,... | collective-permute-start | bytes 983048 | tf_op jit(solution)/shard_map/projection_core_far_1_0/ppermute | solution.py:98
  20.3 7.2 %collective-permute-start.13 = (bf16[256,640]{1,0:T(8,128)(2,1)S(1)}, bf16[256,640]{1,0:T(8,128)(2,1)S(1)}, u32[]{:S(2)}, u32[]{:S(2)}) collective-permute-start(bf16[256,640]{1,0:T(8,128)(2,1)S(1)} %collective-permute-done.6.refs_0_), channel_id=1, source_target_pairs={{0,8},{10,2},{8,16},{18,10},{16,24},{26,18},{24,28},{30,26},{28,20... | collective-permute-start | bytes 983048 | tf_op jit(solution)/shard_map/projection_far_3_0/ppermute | solution.py:94
  24.0 3.7 %collective-permute-start.11 = (bf16[264,640]{1,0:T(8,128)(2,1)S(1)}, bf16[264,640]{1,0:T(8,128)(2,1)S(1)}, u32[]{:S(2)}, u32[]{:S(2)}) collective-permute-start(bf16[264,640]{1,0:T(8,128)(2,1)S(1)} %collective-permute-done.3.refs_2_), channel_id=1, source_target_pairs={{0,2},{2,0},{4,6},{6,4},{8,10},{10,8},{12,14},{14,12},{16,18},{18,... | collective-permute-start | bytes 1013768 | tf_op jit(solution)/shard_map/projection_core_near_3_0/ppermute | solution.py:98
  24.0 7.2 %collective-permute-start.4 = (bf16[264,640]{1,0:T(8,128)(2,1)S(1)}, bf16[264,640]{1,0:T(8,128)(2,1)S(1)}, u32[]{:S(2)}, u32[]{:S(2)}) collective-permute-start(bf16[264,640]{1,0:T(8,128)(2,1)S(1)} %collective-permute-done.3.refs_2_), channel_id=1, source_target_pairs={{0,8},{10,2},{8,16},{18,10},{16,24},{26,18},{24,28},{30,26},{28,20... | collective-permute-start | bytes 1013768 | tf_op jit(solution)/shard_map/projection_near_4_0/ppermute | solution.py:94
  27.5 3.8 %collective-permute-start.14 = (bf16[256,640]{1,0:T(8,128)(2,1)S(1)}, bf16[256,640]{1,0:T(8,128)(2,1)S(1)}, u32[]{:S(2)}, u32[]{:S(2)}) collective-permute-start(bf16[256,640]{1,0:T(8,128)(2,1)S(1)} %collective-permute-done.13.refs_0_), channel_id=1, source_target_pairs={{0,2},{2,0},{4,6},{6,4},{8,10},{10,8},{12,14},{14,12},{16,18},{18,... | collective-permute-start | bytes 983048 | tf_op jit(solution)/shard_map/projection_core_far_3_0/ppermute | solution.py:98
  33.7 7.3 %collective-permute-start.15 = (bf16[136,640]{1,0:T(8,128)(2,1)S(1)}, bf16[136,640]{1,0:T(8,128)(2,1)S(1)}, u32[]{:S(2)}, u32[]{:S(2)}) collective-permute-start(bf16[136,640]{1,0:T(8,128)(2,1)S(1)} %projection_last.4), channel_id=1, source_target_pairs={{0,1},{1,0},{2,3},{3,2},{4,5},{5,4},{6,7},{7,6},{8,9},{9,8},{10,11... | collective-permute-start | bytes 522248 | tf_op jit(solution)/shard_map/ppermute | solution.py:650
  35.4 8.3 %collective-permute-start.17 = (bf16[128,640]{1,0:T(8,128)(2,1)S(1)}, bf16[128,640]{1,0:T(8,128)(2,1)S(1)}, u32[]{:S(2)}, u32[]{:S(2)}) collective-permute-start(bf16[128,640]{1,0:T(8,128)(2,1)S(1)} %projection_last.7), channel_id=1, source_target_pairs={{0,1},{1,0},{2,3},{3,2},{4,5},{5,4},{6,7},{7,6},{8,9},{9,8},{10,11... | collective-permute-start | bytes 491528 | tf_op jit(solution)/shard_map/ppermute | solution.py:650
  41.0 4.8 %collective-permute-start.22 = (bf16[128,640]{1,0:T(8,128)(2,1)S(1)}, bf16[128,640]{1,0:T(8,128)(2,1)S(1)}, u32[]{:S(2)}, u32[]{:S(2)}) collective-permute-start(bf16[128,640]{1,0:T(8,128)(2,1)S(1)} %far_part_1_0.1.refs_0_), channel_id=1, source_target_pairs={{0,2},{2,0},{4,6},{6,4},{8,10},{10,8},{12,14},{14,12},{16,18},{18,... | collective-permute-start | bytes 491528 | tf_op jit(solution)/shard_map/output_core_own_0/ppermute | solution.py:98
  41.1 6.3 %collective-permute-start.16 = (bf16[128,640]{1,0:T(8,128)(2,1)S(1)}, bf16[128,640]{1,0:T(8,128)(2,1)S(1)}, u32[]{:S(2)}, u32[]{:S(2)}) collective-permute-start(bf16[128,640]{1,0:T(8,128)(2,1)S(1)} %far_part_1_0.1.refs_0_), channel_id=1, source_target_pairs={{0,8},{10,2},{8,16},{18,10},{16,24},{26,18},{24,28},{30,26},{28,20... | collective-permute-start | bytes 491528 | tf_op jit(solution)/shard_map/output_near_1_0/ppermute | solution.py:94
  43.7 3.7 %collective-permute-start.24 = (bf16[128,640]{1,0:T(8,128)(2,1)S(1)}, bf16[128,640]{1,0:T(8,128)(2,1)S(1)}, u32[]{:S(2)}, u32[]{:S(2)}) collective-permute-start(bf16[128,640]{1,0:T(8,128)(2,1)S(1)} %far_part_1_128.1.refs_1_), channel_id=1, source_target_pairs={{0,2},{2,0},{4,6},{6,4},{8,10},{10,8},{12,14},{14,12},{16,18},{18,... | collective-permute-start | bytes 491528 | tf_op jit(solution)/shard_map/output_core_own_1/ppermute | solution.py:98
  43.8 5.4 %collective-permute-start.18 = (bf16[128,640]{1,0:T(8,128)(2,1)S(1)}, bf16[128,640]{1,0:T(8,128)(2,1)S(1)}, u32[]{:S(2)}, u32[]{:S(2)}) collective-permute-start(bf16[128,640]{1,0:T(8,128)(2,1)S(1)} %far_part_1_128.1.refs_1_), channel_id=1, source_target_pairs={{0,8},{10,2},{8,16},{18,10},{16,24},{26,18},{24,28},{30,26},{28,20... | collective-permute-start | bytes 491528 | tf_op jit(solution)/shard_map/output_near_1_1/ppermute | solution.py:94
  45.8 5.5 %collective-permute-start.23 = (bf16[128,640]{1,0:T(8,128)(2,1)S(1)}, bf16[128,640]{1,0:T(8,128)(2,1)S(1)}, u32[]{:S(2)}, u32[]{:S(2)}) collective-permute-start(bf16[128,640]{1,0:T(8,128)(2,1)S(1)} %collective-permute-done.22.refs_2_), channel_id=1, source_target_pairs={{0,8},{10,2},{8,16},{18,10},{16,24},{26,18},{24,28},{30,26},{28,20... | collective-permute-start | bytes 491528 | tf_op jit(solution)/shard_map/output_far_1_0/ppermute | solution.py:94
  47.5 5.5 %collective-permute-start.25 = (bf16[128,640]{1,0:T(8,128)(2,1)S(1)}, bf16[128,640]{1,0:T(8,128)(2,1)S(1)}, u32[]{:S(2)}, u32[]{:S(2)}) collective-permute-start(bf16[128,640]{1,0:T(8,128)(2,1)S(1)} %collective-permute-done.24.refs_3_), channel_id=1, source_target_pairs={{0,8},{10,2},{8,16},{18,10},{16,24},{26,18},{24,28},{30,26},{28,20... | collective-permute-start | bytes 491528 | tf_op jit(solution)/shard_map/output_far_1_1/ppermute | solution.py:94
  49.2 5.5 %collective-permute-start.29 = (bf16[256,640]{1,0:T(8,128)(2,1)S(1)}, bf16[256,640]{1,0:T(8,128)(2,1)S(1)}, u32[]{:S(2)}, u32[]{:S(2)}) collective-permute-start(bf16[256,640]{1,0:T(8,128)(2,1)S(1)} %constant_dynamic-update-slice_fusion.refs_4_), channel_id=1, source_target_pairs={{0,2},{2,0},{4,6},{6,4},{8,10},{10,8},{12,14},{14,12},{16,18},{18,... | collective-permute-start | bytes 983048 | tf_op jit(solution)/shard_map/output_core_near_1_0/ppermute | solution.py:98
  49.3 7.1 %collective-permute-start.19 = (bf16[256,640]{1,0:T(8,128)(2,1)S(1)}, bf16[256,640]{1,0:T(8,128)(2,1)S(1)}, u32[]{:S(2)}, u32[]{:S(2)}) collective-permute-start(bf16[256,640]{1,0:T(8,128)(2,1)S(1)} %constant_dynamic-update-slice_fusion.refs_4_), channel_id=1, source_target_pairs={{0,8},{10,2},{8,16},{18,10},{16,24},{26,18},{24,28},{30,26},{28,20... | collective-permute-start | bytes 983048 | tf_op jit(solution)/shard_map/output_near_2_0/ppermute | solution.py:94
  52.9 7.1 %collective-permute-start.26 = (bf16[256,640]{1,0:T(8,128)(2,1)S(1)}, bf16[256,640]{1,0:T(8,128)(2,1)S(1)}, u32[]{:S(2)}, u32[]{:S(2)}) collective-permute-start(bf16[256,640]{1,0:T(8,128)(2,1)S(1)} %constant_dynamic-update-slice_fusion.2.refs_0_), channel_id=1, source_target_pairs={{0,8},{10,2},{8,16},{18,10},{16,24},{26,18},{24,28},{30,26},{28,20... | collective-permute-start | bytes 983048 | tf_op jit(solution)/shard_map/output_far_2_0/ppermute | solution.py:94
  54.7 7.2 %collective-permute-start.28 = (bf16[256,640]{1,0:T(8,128)(2,1)S(1)}, bf16[256,640]{1,0:T(8,128)(2,1)S(1)}, u32[]{:S(2)}, u32[]{:S(2)}) collective-permute-start(bf16[256,640]{1,0:T(8,128)(2,1)S(1)} %constant_dynamic-update-slice_fusion.2.refs_0_), channel_id=1, source_target_pairs={{0,2},{2,0},{4,6},{6,4},{8,10},{10,8},{12,14},{14,12},{16,18},{18,... | collective-permute-start | bytes 983048 | tf_op jit(solution)/shard_map/output_core_far_1_0/ppermute | solution.py:98
  56.4 5.5 %collective-permute-start.30 = (bf16[256,640]{1,0:T(8,128)(2,1)S(1)}, bf16[256,640]{1,0:T(8,128)(2,1)S(1)}, u32[]{:S(2)}, u32[]{:S(2)}) collective-permute-start(bf16[256,640]{1,0:T(8,128)(2,1)S(1)} %collective-permute-done.19.refs_2_), channel_id=1, source_target_pairs={{0,2},{2,0},{4,6},{6,4},{8,10},{10,8},{12,14},{14,12},{16,18},{18,... | collective-permute-start | bytes 983048 | tf_op jit(solution)/shard_map/output_core_near_2_0/ppermute | solution.py:98
  56.4 7.1 %collective-permute-start.20 = (bf16[256,640]{1,0:T(8,128)(2,1)S(1)}, bf16[256,640]{1,0:T(8,128)(2,1)S(1)}, u32[]{:S(2)}, u32[]{:S(2)}) collective-permute-start(bf16[256,640]{1,0:T(8,128)(2,1)S(1)} %collective-permute-done.19.refs_2_), channel_id=1, source_target_pairs={{0,8},{10,2},{8,16},{18,10},{16,24},{26,18},{24,28},{30,26},{28,20... | collective-permute-start | bytes 983048 | tf_op jit(solution)/shard_map/output_near_3_0/ppermute | solution.py:94
  60.1 7.1 %collective-permute-start.33 = (bf16[256,640]{1,0:T(8,128)(2,1)S(1)}, bf16[256,640]{1,0:T(8,128)(2,1)S(1)}, u32[]{:S(2)}, u32[]{:S(2)}) collective-permute-start(bf16[256,640]{1,0:T(8,128)(2,1)S(1)} %collective-permute-done.26.refs_0_), channel_id=1, source_target_pairs={{0,8},{10,2},{8,16},{18,10},{16,24},{26,18},{24,28},{30,26},{28,20... | collective-permute-start | bytes 983048 | tf_op jit(solution)/shard_map/output_far_3_0/ppermute | solution.py:94
  61.9 5.3 %collective-permute-start.27 = (bf16[256,640]{1,0:T(8,128)(2,1)S(1)}, bf16[256,640]{1,0:T(8,128)(2,1)S(1)}, u32[]{:S(2)}, u32[]{:S(2)}) collective-permute-start(bf16[256,640]{1,0:T(8,128)(2,1)S(1)} %collective-permute-done.26.refs_0_), channel_id=1, source_target_pairs={{0,2},{2,0},{4,6},{6,4},{8,10},{10,8},{12,14},{14,12},{16,18},{18,... | collective-permute-start | bytes 983048 | tf_op jit(solution)/shard_map/output_core_far_2_0/ppermute | solution.py:98
  63.6 3.6 %collective-permute-start.31 = (bf16[256,640]{1,0:T(8,128)(2,1)S(1)}, bf16[256,640]{1,0:T(8,128)(2,1)S(1)}, u32[]{:S(2)}, u32[]{:S(2)}) collective-permute-start(bf16[256,640]{1,0:T(8,128)(2,1)S(1)} %collective-permute-done.20.refs_2_), channel_id=1, source_target_pairs={{0,2},{2,0},{4,6},{6,4},{8,10},{10,8},{12,14},{14,12},{16,18},{18,... | collective-permute-start | bytes 983048 | tf_op jit(solution)/shard_map/output_core_near_3_0/ppermute | solution.py:98
  63.6 7.1 %collective-permute-start.21 = (bf16[256,640]{1,0:T(8,128)(2,1)S(1)}, bf16[256,640]{1,0:T(8,128)(2,1)S(1)}, u32[]{:S(2)}, u32[]{:S(2)}) collective-permute-start(bf16[256,640]{1,0:T(8,128)(2,1)S(1)} %collective-permute-done.20.refs_2_), channel_id=1, source_target_pairs={{0,8},{10,2},{8,16},{18,10},{16,24},{26,18},{24,28},{30,26},{28,20... | collective-permute-start | bytes 983048 | tf_op jit(solution)/shard_map/output_near_4_0/ppermute | solution.py:94
  67.1 3.5 %collective-permute-start.34 = (bf16[256,640]{1,0:T(8,128)(2,1)S(1)}, bf16[256,640]{1,0:T(8,128)(2,1)S(1)}, u32[]{:S(2)}, u32[]{:S(2)}) collective-permute-start(bf16[256,640]{1,0:T(8,128)(2,1)S(1)} %collective-permute-done.33.refs_0_), channel_id=1, source_target_pairs={{0,2},{2,0},{4,6},{6,4},{8,10},{10,8},{12,14},{14,12},{16,18},{18,... | collective-permute-start | bytes 983048 | tf_op jit(solution)/shard_map/output_core_far_3_0/ppermute | solution.py:98
  (14 other events, 53.6 us)
